TPU v7x, 512 devices: a whole 4x8x8 slice. The times are simulated.
512 devices in a mesh: gx: 32 (over y, x), gy: 16 (over z, core).
Axes of the slice: x: 4, y: 8, z: 8, core: 2. Of those that a mesh axis runs over, the one named last changes fastest.
Arguments:
- rhs: float32 [24, 256, 128, 128], P(None, 'gx', 'gy'), may hold values from -8 to 8
- shift: float32 [256, 128, 128], P('gx', 'gy'), may hold values from 0.05 to 2
- slots: int32 [32, 16], P('gx', 'gy'), may hold values from 0 to 15, each once within a row
- coarse_inverse: float32 [32, 16, 128, 2048], P('gx', 'gy'), may hold values from -16 to 16
Outputs:
- corrected: float32 [24, 256, 128, 128], P(None, 'gx', 'gy')
Inputs may be any that keep to these rules, and one draw needn't show every extreme that they name: Each row of slots holds every number 0 to 15 once.
All inputs are finite; a program needn't handle non-finite values.
Results may differ from a plain program's by a relative error of at most 0.0001.
Values sent between devices are 32-bit elements; how exact they have to be, the bound alone decides.
No kernel may reach another device: no remote copies, remote signals or barrier semaphores. Data moves between devices by JAX's collectives and lax.ppermute only.
A program may use at most 64 MiB of HBM per device.

v0:
```python
import jax
import jax.numpy as jnp
from jax import lax
from jax.sharding import PartitionSpec as P

DEGREE = 3


THETA = 8.0
DELTA = 6.5


def with_halo(cells, sides, width):
    for axis, dim in sides:
        count = lax.axis_size(axis)
        ends = count - 1
        head = lax.slice_in_dim(cells, 0, width, axis=dim)
        tail = lax.slice_in_dim(cells, cells.shape[dim] - width, cells.shape[dim], axis=dim)
        cells = jnp.concatenate(
            [
                lax.ppermute(tail, axis, [(i, (i + 1) % count) for i in range(ends)]),
                cells,
                lax.ppermute(head, axis, [((i + 1) % count, i) for i in range(ends)]),
            ],
            axis=dim,
        )
    return cells


def restrict(v):
    xs, ys, zs = v.shape[-3:]
    return v.reshape(v.shape[:-3] + (xs // 2, 2, ys // 2, 2, zs)).mean(axis=(-4, -2))


def prolong(v):
    return jnp.repeat(jnp.repeat(v, 2, axis=-3), 2, axis=-2)


def stencil(padded, level_shift):
    centre = padded[:, 1:-1, 1:-1]
    zpadded = jnp.pad(centre, ((0, 0), (0, 0), (0, 0), (1, 1)))
    beside = padded[:, 2:, 1:-1] + padded[:, :-2, 1:-1]
    beside = beside + padded[:, 1:-1, 2:] + padded[:, 1:-1, :-2]
    beside = beside + zpadded[..., 2:] + zpadded[..., :-2]
    return (6.0 + level_shift) * centre - beside


def chebyshev(right, apply_op, indicator):
    sigma = THETA / DELTA
    rho = 1.0 / sigma
    step_dir = right / THETA
    iterate = step_dir
    for turn in range(DEGREE - 1):
        rho_new = 1.0 / (2.0 * sigma - rho)
        step_dir = rho_new * rho * step_dir + 2.0 * rho_new / DELTA * (right - apply_op(iterate))
        step_dir = step_dir * indicator
        iterate = iterate + step_dir
        rho = rho_new
    return iterate


def faces_apply(field, level_shift):
    padded = with_halo(field, (("gx", 1), ("gy", 2)), 1)
    return stencil(padded, level_shift)


def residual_apply(field, level_shift):
    padded = with_halo(field, (("gx", 1), ("gy", 2)), 1)
    return stencil(padded, level_shift)


def smooth(right, level_shift):

    def apply_op(field):
        return faces_apply(field, level_shift)

    return chebyshev(right, apply_op, 1.0)


def body(rhs, shift, slots, coarse_inverse):
    high = lax.Precision.HIGHEST
    shifts = [shift, restrict(shift), restrict(restrict(shift))]
    coeff_list = []
    for level in range(3):
        coeff_list.append(None)
    current = rhs
    iterates = []
    rights = []
    for level in range(3):
        iterate = smooth(current, shifts[level])
        leftover = current - residual_apply(iterate, shifts[level])
        iterates.append(iterate)
        rights.append(current)
        current = restrict(leftover) if level < 2 else leftover.mean(axis=(1, 2))
    count = lax.axis_size("gy")
    channels = current.shape[0]
    depth = current.shape[1]
    blocks = lax.all_gather(current[None], "gy", axis=0, tiled=True)
    slot_all = lax.all_gather(slots, "gy", axis=1, tiled=True)
    places = (slot_all[0][None, :] == jnp.arange(count, dtype=jnp.int32)[:, None]).astype(
        jnp.float32
    )
    ordered = jnp.einsum("mj,jck->mck", places, blocks, precision=high)
    flat = ordered.transpose(1, 0, 2).reshape(channels, count * depth)
    solved = lax.dot_general(
        flat,
        coarse_inverse[0, 0],
        (((1,), (1,)), ((), ())),
        precision=high,
        preferred_element_type=jnp.float32,
    )
    back = lax.all_gather(solved[None], "gy", axis=0, tiled=True)
    owned = (jnp.arange(count, dtype=jnp.int32) == slots[0, 0]).astype(jnp.float32)
    coarse_fix = jnp.einsum("j,jck->ck", owned, back, precision=high)
    upward = coarse_fix[:, None, None, :]
    for level in (2, 1, 0):
        iterate = iterates[level] + upward
        leftover = rights[level] - residual_apply(iterate, shifts[level])
        iterate = iterate + smooth(leftover, shifts[level])
        upward = prolong(iterate)
    return iterate


def solution(mesh):
    return jax.shard_map(
        body,
        mesh=mesh,
        in_specs=(
            P(None, "gx", "gy", None),
            P("gx", "gy", None),
            P("gx", "gy"),
            P("gx", "gy", None, None),
        ),
        out_specs=P(None, "gx", "gy", None),
        check_vma=False,
    )
```

profile of v0, /device:TPU:223, one launch (start us, length us, event | category | flops | bytes accessed | tf_op | source)
XLA Modules:
  0.0 422.3 jit_solution(15996848357323049548)
XLA Ops:
  8.2 6.7 %collective-permute-done = f32[24,1,8,128]{3,0,2,1:T(8,128)S(1)} collective-permute-done((f32[24,1,8,128]{3,0,2,1:T(8,128)S(1)}, f32[24,1,8,128]{3,0,2,1:T(8,128)S(1)}, u32[]{:S(2)}, u32[]{:S(2)}) %collective-permute-start) | collective-permute-done | bytes 98336 | tf_op jit(solution)/shard_map/ppermute | solution.py:23
  19.0 5.1 %collective-permute-start.3 = (f32[24,10,1,128]{3,0,2,1:T(8,128)S(1)}, f32[24,10,1,128]{3,0,2,1:T(8,128)S(1)}, u32[]{:S(2)}, u32[]{:S(2)}) collective-permute-start(f32[24,10,1,128]{3,0,2,1:T(8,128)S(1)} %get-tuple-element.34), channel_id=1, source_target_pairs={{0,1},{1,2},{2,3},{3,4},{4,5},{5,6},{6,7},{7,8},{8,9},{9,10},{10,1... | collective-permute-start | bytes 368648 | tf_op jit(solution)/shard_map/ppermute | solution.py:21
  32.8 5.2 %collective-permute-done.4 = f32[24,1,8,128]{3,0,2,1:T(8,128)S(1)} collective-permute-done((f32[24,1,8,128]{3,0,2,1:T(8,128)S(1)}, f32[24,1,8,128]{3,0,2,1:T(8,128)S(1)}, u32[]{:S(2)}, u32[]{:S(2)}) %collective-permute-start.4) | collective-permute-done | bytes 98336 | tf_op jit(solution)/shard_map/ppermute | solution.py:23
  40.4 5.6 %collective-permute-start.7 = (f32[24,10,1,128]{3,0,2,1:T(8,128)S(1)}, f32[24,10,1,128]{3,0,2,1:T(8,128)S(1)}, u32[]{:S(2)}, u32[]{:S(2)}) collective-permute-start(f32[24,10,1,128]{3,0,2,1:T(8,128)S(1)} %get-tuple-element.32), channel_id=1, source_target_pairs={{0,1},{1,2},{2,3},{3,4},{4,5},{5,6},{6,7},{7,8},{8,9},{9,10},{10,1... | collective-permute-start | bytes 368648 | tf_op jit(solution)/shard_map/ppermute | solution.py:21
  54.2 5.2 %collective-permute-done.8 = f32[24,1,8,128]{3,0,2,1:T(8,128)S(1)} collective-permute-done((f32[24,1,8,128]{3,0,2,1:T(8,128)S(1)}, f32[24,1,8,128]{3,0,2,1:T(8,128)S(1)}, u32[]{:S(2)}, u32[]{:S(2)}) %collective-permute-start.8) | collective-permute-done | bytes 98336 | tf_op jit(solution)/shard_map/ppermute | solution.py:23
  61.4 6.4 %collective-permute-start.11 = (f32[24,10,1,128]{3,0,2,1:T(8,128)S(1)}, f32[24,10,1,128]{3,0,2,1:T(8,128)S(1)}, u32[]{:S(2)}, u32[]{:S(2)}) collective-permute-start(f32[24,10,1,128]{3,0,2,1:T(8,128)S(1)} %get-tuple-element.30), channel_id=1, source_target_pairs={{0,1},{1,2},{2,3},{3,4},{4,5},{5,6},{6,7},{7,8},{8,9},{9,10},{10,1... | collective-permute-start | bytes 368648 | tf_op jit(solution)/shard_map/ppermute | solution.py:21
  77.8 4.7 %collective-permute-done.12 = f32[24,1,4,128]{3,0,2,1:T(8,128)S(1)} collective-permute-done((f32[24,1,4,128]{3,0,2,1:T(8,128)S(1)}, f32[24,1,4,128]{3,0,2,1:T(8,128)S(1)}, u32[]{:S(2)}, u32[]{:S(2)}) %collective-permute-start.12) | collective-permute-done | bytes 49184 | tf_op jit(solution)/shard_map/ppermute | solution.py:23
  84.5 6.7 %collective-permute-start.15 = (f32[24,6,1,128]{3,0,2,1:T(8,128)S(1)}, f32[24,6,1,128]{3,0,2,1:T(8,128)S(1)}, u32[]{:S(2)}, u32[]{:S(2)}) collective-permute-start(f32[24,6,1,128]{3,0,2,1:T(8,128)S(1)} %get-tuple-element.58), channel_id=1, source_target_pairs={{0,1},{1,2},{2,3},{3,4},{4,5},{5,6},{6,7},{7,8},{8,9},{9,10},{10,1... | collective-permute-start | bytes 221192 | tf_op jit(solution)/shard_map/ppermute | solution.py:21
  98.1 4.8 %collective-permute-done.16 = f32[24,1,4,128]{3,0,2,1:T(8,128)S(1)} collective-permute-done((f32[24,1,4,128]{3,0,2,1:T(8,128)S(1)}, f32[24,1,4,128]{3,0,2,1:T(8,128)S(1)}, u32[]{:S(2)}, u32[]{:S(2)}) %collective-permute-start.16) | collective-permute-done | bytes 49184 | tf_op jit(solution)/shard_map/ppermute | solution.py:23
  104.8 6.6 %collective-permute-start.19 = (f32[24,6,1,128]{3,0,2,1:T(8,128)S(1)}, f32[24,6,1,128]{3,0,2,1:T(8,128)S(1)}, u32[]{:S(2)}, u32[]{:S(2)}) collective-permute-start(f32[24,6,1,128]{3,0,2,1:T(8,128)S(1)} %get-tuple-element.56), channel_id=1, source_target_pairs={{0,1},{1,2},{2,3},{3,4},{4,5},{5,6},{6,7},{7,8},{8,9},{9,10},{10,1... | collective-permute-start | bytes 221192 | tf_op jit(solution)/shard_map/ppermute | solution.py:21
  118.3 4.8 %collective-permute-done.20 = f32[24,1,4,128]{3,0,2,1:T(8,128)S(1)} collective-permute-done((f32[24,1,4,128]{3,0,2,1:T(8,128)S(1)}, f32[24,1,4,128]{3,0,2,1:T(8,128)S(1)}, u32[]{:S(2)}, u32[]{:S(2)}) %collective-permute-start.20) | collective-permute-done | bytes 49184 | tf_op jit(solution)/shard_map/ppermute | solution.py:23
  125.0 6.6 %collective-permute-start.23 = (f32[24,6,1,128]{3,0,2,1:T(8,128)S(1)}, f32[24,6,1,128]{3,0,2,1:T(8,128)S(1)}, u32[]{:S(2)}, u32[]{:S(2)}) collective-permute-start(f32[24,6,1,128]{3,0,2,1:T(8,128)S(1)} %get-tuple-element.54), channel_id=1, source_target_pairs={{0,1},{1,2},{2,3},{3,4},{4,5},{5,6},{6,7},{7,8},{8,9},{9,10},{10,1... | collective-permute-start | bytes 221192 | tf_op jit(solution)/shard_map/ppermute | solution.py:21
  145.1 6.6 %collective-permute-start.27 = (f32[24,4,1,128]{3,0,2,1:T(8,128)S(1)}, f32[24,4,1,128]{3,0,2,1:T(8,128)S(1)}, u32[]{:S(2)}, u32[]{:S(2)}) collective-permute-start(f32[24,4,1,128]{3,0,2,1:T(8,128)S(1)} %get-tuple-element.82), channel_id=1, source_target_pairs={{0,1},{1,2},{2,3},{3,4},{4,5},{5,6},{6,7},{7,8},{8,9},{9,10},{10,1... | collective-permute-start | bytes 147464 | tf_op jit(solution)/shard_map/ppermute | solution.py:21
  164.8 6.6 %collective-permute-start.31 = (f32[24,4,1,128]{3,0,2,1:T(8,128)S(1)}, f32[24,4,1,128]{3,0,2,1:T(8,128)S(1)}, u32[]{:S(2)}, u32[]{:S(2)}) collective-permute-start(f32[24,4,1,128]{3,0,2,1:T(8,128)S(1)} %get-tuple-element.80), channel_id=1, source_target_pairs={{0,1},{1,2},{2,3},{3,4},{4,5},{5,6},{6,7},{7,8},{8,9},{9,10},{10,1... | collective-permute-start | bytes 147464 | tf_op jit(solution)/shard_map/ppermute | solution.py:21
  184.4 6.6 %collective-permute-start.35 = (f32[24,4,1,128]{3,0,2,1:T(8,128)S(1)}, f32[24,4,1,128]{3,0,2,1:T(8,128)S(1)}, u32[]{:S(2)}, u32[]{:S(2)}) collective-permute-start(f32[24,4,1,128]{3,0,2,1:T(8,128)S(1)} %get-tuple-element.78), channel_id=1, source_target_pairs={{0,1},{1,2},{2,3},{3,4},{4,5},{5,6},{6,7},{7,8},{8,9},{9,10},{10,1... | collective-permute-start | bytes 147464 | tf_op jit(solution)/shard_map/ppermute | solution.py:21
  193.7 8.8 %all-reduce.18 = s32[16]{0:T(128)S(1)} all-reduce(s32[16]{0:T(128)S(1)} %bitcast_dynamic-update-slice_fusion), channel_id=1, replica_groups=mesh['gx'=32,'gy'=16] {'gy'}, use_global_device_ids=true, to_apply=%add.18 | all-reduce | flops 16 | bytes 128
  202.6 18.2 %all-gather = f32[384,128]{1,0:T(8,128)S(1)} all-gather(f32[24,128]{1,0:T(8,128)S(1)} %broadcast_multiply_fusion.6), channel_id=2, replica_groups=mesh['gx'=32,'gy'=16] {'gy'}, dimensions={0}, use_global_device_ids=true | all-gather | bytes 208896 | tf_op jit(solution)/shard_map/all_gather | solution.py:98
  222.0 15.5 %all-gather.1 = f32[384,128]{1,0:T(8,128)S(1)} all-gather(f32[24,128]{1,0:T(8,128)S(1)} %fusion), channel_id=3, replica_groups=mesh['gx'=32,'gy'=16] {'gy'}, dimensions={0}, use_global_device_ids=true | all-gather | bytes 208896 | tf_op jit(solution)/shard_map/all_gather | solution.py:112
  269.2 5.1 %collective-permute-start.43 = (f32[24,4,1,128]{3,0,2,1:T(8,128)S(1)}, f32[24,4,1,128]{3,0,2,1:T(8,128)S(1)}, u32[]{:S(2)}, u32[]{:S(2)}) collective-permute-start(f32[24,4,1,128]{3,0,2,1:T(8,128)S(1)} %get-tuple-element.74), channel_id=1, source_target_pairs={{0,1},{1,2},{2,3},{3,4},{4,5},{5,6},{6,7},{7,8},{8,9},{9,10},{10,1... | collective-permute-start | bytes 147464 | tf_op jit(solution)/shard_map/ppermute | solution.py:21
  287.7 6.3 %collective-permute-start.47 = (f32[24,4,1,128]{3,0,2,1:T(8,128)S(1)}, f32[24,4,1,128]{3,0,2,1:T(8,128)S(1)}, u32[]{:S(2)}, u32[]{:S(2)}) collective-permute-start(f32[24,4,1,128]{3,0,2,1:T(8,128)S(1)} %get-tuple-element.72), channel_id=1, source_target_pairs={{0,1},{1,2},{2,3},{3,4},{4,5},{5,6},{6,7},{7,8},{8,9},{9,10},{10,1... | collective-permute-start | bytes 147464 | tf_op jit(solution)/shard_map/ppermute | solution.py:21
  300.7 4.8 %collective-permute-done.48 = f32[24,1,4,128]{3,0,2,1:T(8,128)S(1)} collective-permute-done((f32[24,1,4,128]{3,0,2,1:T(8,128)S(1)}, f32[24,1,4,128]{3,0,2,1:T(8,128)S(1)}, u32[]{:S(2)}, u32[]{:S(2)}) %collective-permute-start.48) | collective-permute-done | bytes 49184 | tf_op jit(solution)/shard_map/ppermute | solution.py:23
  307.4 6.6 %collective-permute-start.51 = (f32[24,6,1,128]{3,0,2,1:T(8,128)S(1)}, f32[24,6,1,128]{3,0,2,1:T(8,128)S(1)}, u32[]{:S(2)}, u32[]{:S(2)}) collective-permute-start(f32[24,6,1,128]{3,0,2,1:T(8,128)S(1)} %get-tuple-element.52), channel_id=1, source_target_pairs={{0,1},{1,2},{2,3},{3,4},{4,5},{5,6},{6,7},{7,8},{8,9},{9,10},{10,1... | collective-permute-start | bytes 221192 | tf_op jit(solution)/shard_map/ppermute | solution.py:21
  320.9 4.8 %collective-permute-done.52 = f32[24,1,4,128]{3,0,2,1:T(8,128)S(1)} collective-permute-done((f32[24,1,4,128]{3,0,2,1:T(8,128)S(1)}, f32[24,1,4,128]{3,0,2,1:T(8,128)S(1)}, u32[]{:S(2)}, u32[]{:S(2)}) %collective-permute-start.52) | collective-permute-done | bytes 49184 | tf_op jit(solution)/shard_map/ppermute | solution.py:23
  327.6 6.6 %collective-permute-start.55 = (f32[24,6,1,128]{3,0,2,1:T(8,128)S(1)}, f32[24,6,1,128]{3,0,2,1:T(8,128)S(1)}, u32[]{:S(2)}, u32[]{:S(2)}) collective-permute-start(f32[24,6,1,128]{3,0,2,1:T(8,128)S(1)} %get-tuple-element.50), channel_id=1, source_target_pairs={{0,1},{1,2},{2,3},{3,4},{4,5},{5,6},{6,7},{7,8},{8,9},{9,10},{10,1... | collective-permute-start | bytes 221192 | tf_op jit(solution)/shard_map/ppermute | solution.py:21
  341.2 4.8 %collective-permute-done.56 = f32[24,1,4,128]{3,0,2,1:T(8,128)S(1)} collective-permute-done((f32[24,1,4,128]{3,0,2,1:T(8,128)S(1)}, f32[24,1,4,128]{3,0,2,1:T(8,128)S(1)}, u32[]{:S(2)}, u32[]{:S(2)}) %collective-permute-start.56) | collective-permute-done | bytes 49184 | tf_op jit(solution)/shard_map/ppermute | solution.py:23
  347.9 6.6 %collective-permute-start.59 = (f32[24,6,1,128]{3,0,2,1:T(8,128)S(1)}, f32[24,6,1,128]{3,0,2,1:T(8,128)S(1)}, u32[]{:S(2)}, u32[]{:S(2)}) collective-permute-start(f32[24,6,1,128]{3,0,2,1:T(8,128)S(1)} %get-tuple-element.48), channel_id=1, source_target_pairs={{0,1},{1,2},{2,3},{3,4},{4,5},{5,6},{6,7},{7,8},{8,9},{9,10},{10,1... | collective-permute-start | bytes 221192 | tf_op jit(solution)/shard_map/ppermute | solution.py:21
  362.0 5.0 %collective-permute-done.60 = f32[24,1,8,128]{3,0,2,1:T(8,128)S(1)} collective-permute-done((f32[24,1,8,128]{3,0,2,1:T(8,128)S(1)}, f32[24,1,8,128]{3,0,2,1:T(8,128)S(1)}, u32[]{:S(2)}, u32[]{:S(2)}) %collective-permute-start.60) | collective-permute-done | bytes 98336 | tf_op jit(solution)/shard_map/ppermute | solution.py:23
  368.9 6.8 %collective-permute-start.63 = (f32[24,10,1,128]{3,0,2,1:T(8,128)S(1)}, f32[24,10,1,128]{3,0,2,1:T(8,128)S(1)}, u32[]{:S(2)}, u32[]{:S(2)}) collective-permute-start(f32[24,10,1,128]{3,0,2,1:T(8,128)S(1)} %get-tuple-element.28), channel_id=1, source_target_pairs={{0,1},{1,2},{2,3},{3,4},{4,5},{5,6},{6,7},{7,8},{8,9},{9,10},{10,1... | collective-permute-start | bytes 368648 | tf_op jit(solution)/shard_map/ppermute | solution.py:21
  383.7 5.0 %collective-permute-done.64 = f32[24,1,8,128]{3,0,2,1:T(8,128)S(1)} collective-permute-done((f32[24,1,8,128]{3,0,2,1:T(8,128)S(1)}, f32[24,1,8,128]{3,0,2,1:T(8,128)S(1)}, u32[]{:S(2)}, u32[]{:S(2)}) %collective-permute-start.64) | collective-permute-done | bytes 98336 | tf_op jit(solution)/shard_map/ppermute | solution.py:23
  390.6 6.7 %collective-permute-start.67 = (f32[24,10,1,128]{3,0,2,1:T(8,128)S(1)}, f32[24,10,1,128]{3,0,2,1:T(8,128)S(1)}, u32[]{:S(2)}, u32[]{:S(2)}) collective-permute-start(f32[24,10,1,128]{3,0,2,1:T(8,128)S(1)} %get-tuple-element.26), channel_id=1, source_target_pairs={{0,1},{1,2},{2,3},{3,4},{4,5},{5,6},{6,7},{7,8},{8,9},{9,10},{10,1... | collective-permute-start | bytes 368648 | tf_op jit(solution)/shard_map/ppermute | solution.py:21
  405.4 5.0 %collective-permute-done.68 = f32[24,1,8,128]{3,0,2,1:T(8,128)S(1)} collective-permute-done((f32[24,1,8,128]{3,0,2,1:T(8,128)S(1)}, f32[24,1,8,128]{3,0,2,1:T(8,128)S(1)}, u32[]{:S(2)}, u32[]{:S(2)}) %collective-permute-start.68) | collective-permute-done | bytes 98336 | tf_op jit(solution)/shard_map/ppermute | solution.py:23
  412.3 6.7 %collective-permute-start.71 = (f32[24,10,1,128]{3,0,2,1:T(8,128)S(1)}, f32[24,10,1,128]{3,0,2,1:T(8,128)S(1)}, u32[]{:S(2)}, u32[]{:S(2)}) collective-permute-start(f32[24,10,1,128]{3,0,2,1:T(8,128)S(1)} %get-tuple-element.24), channel_id=1, source_target_pairs={{0,1},{1,2},{2,3},{3,4},{4,5},{5,6},{6,7},{7,8},{8,9},{9,10},{10,1... | collective-permute-start | bytes 368648 | tf_op jit(solution)/shard_map/ppermute | solution.py:21
  (206 shorter events, 208.8 us)
Async XLA Ops:
  6.3 8.7 %collective-permute-start = (f32[24,1,8,128]{3,0,2,1:T(8,128)S(1)}, f32[24,1,8,128]{3,0,2,1:T(8,128)S(1)}, u32[]{:S(2)}, u32[]{:S(2)}) collective-permute-start(f32[24,1,8,128]{3,0,2,1:T(8,128)S(1)} %get-tuple-element.46), channel_id=1, source_target_pairs={{16,0},{32,16},{48,32},{64,48},{80,64},{96,80},{112,96},{128,112},... | collective-permute-start | bytes 294920 | tf_op jit(solution)/shard_map/ppermute | solution.py:23
  15.0 9.8 %collective-permute-start.2 = (f32[24,10,1,128]{3,0,2,1:T(8,128)S(1)}, f32[24,10,1,128]{3,0,2,1:T(8,128)S(1)}, u32[]{:S(2)}, u32[]{:S(2)}) collective-permute-start(f32[24,10,1,128]{3,0,2,1:T(8,128)S(1)} %get-tuple-element.33), channel_id=1, source_target_pairs={{1,0},{2,1},{3,2},{4,3},{5,4},{6,5},{7,6},{8,7},{9,8},{10,9},{11,1... | collective-permute-start | bytes 368648 | tf_op jit(solution)/shard_map/ppermute | solution.py:23
  28.6 9.4 %collective-permute-start.4 = (f32[24,1,8,128]{3,0,2,1:T(8,128)S(1)}, f32[24,1,8,128]{3,0,2,1:T(8,128)S(1)}, u32[]{:S(2)}, u32[]{:S(2)}) collective-permute-start(f32[24,1,8,128]{3,0,2,1:T(8,128)S(1)} %get-tuple-element.44), channel_id=1, source_target_pairs={{16,0},{32,16},{48,32},{64,48},{80,64},{96,80},{112,96},{128,112},... | collective-permute-start | bytes 294920 | tf_op jit(solution)/shard_map/ppermute | solution.py:23
  38.1 8.5 %collective-permute-start.6 = (f32[24,10,1,128]{3,0,2,1:T(8,128)S(1)}, f32[24,10,1,128]{3,0,2,1:T(8,128)S(1)}, u32[]{:S(2)}, u32[]{:S(2)}) collective-permute-start(f32[24,10,1,128]{3,0,2,1:T(8,128)S(1)} %get-tuple-element.31), channel_id=1, source_target_pairs={{1,0},{2,1},{3,2},{4,3},{5,4},{6,5},{7,6},{8,7},{9,8},{10,9},{11,1... | collective-permute-start | bytes 368648 | tf_op jit(solution)/shard_map/ppermute | solution.py:23
  50.5 9.0 %collective-permute-start.8 = (f32[24,1,8,128]{3,0,2,1:T(8,128)S(1)}, f32[24,1,8,128]{3,0,2,1:T(8,128)S(1)}, u32[]{:S(2)}, u32[]{:S(2)}) collective-permute-start(f32[24,1,8,128]{3,0,2,1:T(8,128)S(1)} %get-tuple-element.42), channel_id=1, source_target_pairs={{16,0},{32,16},{48,32},{64,48},{80,64},{96,80},{112,96},{128,112},... | collective-permute-start | bytes 294920 | tf_op jit(solution)/shard_map/ppermute | solution.py:23
  59.5 9.0 %collective-permute-start.10 = (f32[24,10,1,128]{3,0,2,1:T(8,128)S(1)}, f32[24,10,1,128]{3,0,2,1:T(8,128)S(1)}, u32[]{:S(2)}, u32[]{:S(2)}) collective-permute-start(f32[24,10,1,128]{3,0,2,1:T(8,128)S(1)} %get-tuple-element.29), channel_id=1, source_target_pairs={{1,0},{2,1},{3,2},{4,3},{5,4},{6,5},{7,6},{8,7},{9,8},{10,9},{11,1... | collective-permute-start | bytes 368648 | tf_op jit(solution)/shard_map/ppermute | solution.py:23
  61.4 8.3 %collective-permute-start.11 = (f32[24,10,1,128]{3,0,2,1:T(8,128)S(1)}, f32[24,10,1,128]{3,0,2,1:T(8,128)S(1)}, u32[]{:S(2)}, u32[]{:S(2)}) collective-permute-start(f32[24,10,1,128]{3,0,2,1:T(8,128)S(1)} %get-tuple-element.30), channel_id=1, source_target_pairs={{0,1},{1,2},{2,3},{3,4},{4,5},{5,6},{6,7},{7,8},{8,9},{9,10},{10,1... | collective-permute-start | bytes 368648 | tf_op jit(solution)/shard_map/ppermute | solution.py:21
  74.4 8.2 %collective-permute-start.12 = (f32[24,1,4,128]{3,0,2,1:T(8,128)S(1)}, f32[24,1,4,128]{3,0,2,1:T(8,128)S(1)}, u32[]{:S(2)}, u32[]{:S(2)}) collective-permute-start(f32[24,1,4,128]{3,0,2,1:T(8,128)S(1)} %get-tuple-element.70), channel_id=1, source_target_pairs={{16,0},{32,16},{48,32},{64,48},{80,64},{96,80},{112,96},{128,112},... | collective-permute-start | bytes 147464 | tf_op jit(solution)/shard_map/ppermute | solution.py:23
  82.5 8.7 %collective-permute-start.14 = (f32[24,6,1,128]{3,0,2,1:T(8,128)S(1)}, f32[24,6,1,128]{3,0,2,1:T(8,128)S(1)}, u32[]{:S(2)}, u32[]{:S(2)}) collective-permute-start(f32[24,6,1,128]{3,0,2,1:T(8,128)S(1)} %get-tuple-element.57), channel_id=1, source_target_pairs={{1,0},{2,1},{3,2},{4,3},{5,4},{6,5},{7,6},{8,7},{9,8},{10,9},{11,1... | collective-permute-start | bytes 221192 | tf_op jit(solution)/shard_map/ppermute | solution.py:23
  102.8 8.7 %collective-permute-start.18 = (f32[24,6,1,128]{3,0,2,1:T(8,128)S(1)}, f32[24,6,1,128]{3,0,2,1:T(8,128)S(1)}, u32[]{:S(2)}, u32[]{:S(2)}) collective-permute-start(f32[24,6,1,128]{3,0,2,1:T(8,128)S(1)} %get-tuple-element.55), channel_id=1, source_target_pairs={{1,0},{2,1},{3,2},{4,3},{5,4},{6,5},{7,6},{8,7},{9,8},{10,9},{11,1... | collective-permute-start | bytes 221192 | tf_op jit(solution)/shard_map/ppermute | solution.py:23
  114.9 8.2 %collective-permute-start.20 = (f32[24,1,4,128]{3,0,2,1:T(8,128)S(1)}, f32[24,1,4,128]{3,0,2,1:T(8,128)S(1)}, u32[]{:S(2)}, u32[]{:S(2)}) collective-permute-start(f32[24,1,4,128]{3,0,2,1:T(8,128)S(1)} %get-tuple-element.66), channel_id=1, source_target_pairs={{16,0},{32,16},{48,32},{64,48},{80,64},{96,80},{112,96},{128,112},... | collective-permute-start | bytes 147464 | tf_op jit(solution)/shard_map/ppermute | solution.py:23
  123.1 8.7 %collective-permute-start.22 = (f32[24,6,1,128]{3,0,2,1:T(8,128)S(1)}, f32[24,6,1,128]{3,0,2,1:T(8,128)S(1)}, u32[]{:S(2)}, u32[]{:S(2)}) collective-permute-start(f32[24,6,1,128]{3,0,2,1:T(8,128)S(1)} %get-tuple-element.53), channel_id=1, source_target_pairs={{1,0},{2,1},{3,2},{4,3},{5,4},{6,5},{7,6},{8,7},{9,8},{10,9},{11,1... | collective-permute-start | bytes 221192 | tf_op jit(solution)/shard_map/ppermute | solution.py:23
  143.1 8.6 %collective-permute-start.26 = (f32[24,4,1,128]{3,0,2,1:T(8,128)S(1)}, f32[24,4,1,128]{3,0,2,1:T(8,128)S(1)}, u32[]{:S(2)}, u32[]{:S(2)}) collective-permute-start(f32[24,4,1,128]{3,0,2,1:T(8,128)S(1)} %get-tuple-element.81), channel_id=1, source_target_pairs={{1,0},{2,1},{3,2},{4,3},{5,4},{6,5},{7,6},{8,7},{9,8},{10,9},{11,1... | collective-permute-start | bytes 147464 | tf_op jit(solution)/shard_map/ppermute | solution.py:23
  162.8 8.5 %collective-permute-start.30 = (f32[24,4,1,128]{3,0,2,1:T(8,128)S(1)}, f32[24,4,1,128]{3,0,2,1:T(8,128)S(1)}, u32[]{:S(2)}, u32[]{:S(2)}) collective-permute-start(f32[24,4,1,128]{3,0,2,1:T(8,128)S(1)} %get-tuple-element.79), channel_id=1, source_target_pairs={{1,0},{2,1},{3,2},{4,3},{5,4},{6,5},{7,6},{8,7},{9,8},{10,9},{11,1... | collective-permute-start | bytes 147464 | tf_op jit(solution)/shard_map/ppermute | solution.py:23
  182.5 20.0 %collective-permute-start.34 = (f32[24,4,1,128]{3,0,2,1:T(8,128)S(1)}, f32[24,4,1,128]{3,0,2,1:T(8,128)S(1)}, u32[]{:S(2)}, u32[]{:S(2)}) collective-permute-start(f32[24,4,1,128]{3,0,2,1:T(8,128)S(1)} %get-tuple-element.77), channel_id=1, source_target_pairs={{1,0},{2,1},{3,2},{4,3},{5,4},{6,5},{7,6},{8,7},{9,8},{10,9},{11,1... | collective-permute-start | bytes 147464 | tf_op jit(solution)/shard_map/ppermute | solution.py:23
  184.4 18.1 %collective-permute-start.35 = (f32[24,4,1,128]{3,0,2,1:T(8,128)S(1)}, f32[24,4,1,128]{3,0,2,1:T(8,128)S(1)}, u32[]{:S(2)}, u32[]{:S(2)}) collective-permute-start(f32[24,4,1,128]{3,0,2,1:T(8,128)S(1)} %get-tuple-element.78), channel_id=1, source_target_pairs={{0,1},{1,2},{2,3},{3,4},{4,5},{5,6},{6,7},{7,8},{8,9},{9,10},{10,1... | collective-permute-start | bytes 147464 | tf_op jit(solution)/shard_map/ppermute | solution.py:21
  265.8 8.5 %collective-permute-start.42 = (f32[24,4,1,128]{3,0,2,1:T(8,128)S(1)}, f32[24,4,1,128]{3,0,2,1:T(8,128)S(1)}, u32[]{:S(2)}, u32[]{:S(2)}) collective-permute-start(f32[24,4,1,128]{3,0,2,1:T(8,128)S(1)} %get-tuple-element.73), channel_id=1, source_target_pairs={{1,0},{2,1},{3,2},{4,3},{5,4},{6,5},{7,6},{8,7},{9,8},{10,9},{11,1... | collective-permute-start | bytes 147464 | tf_op jit(solution)/shard_map/ppermute | solution.py:23
  285.5 8.5 %collective-permute-start.46 = (f32[24,4,1,128]{3,0,2,1:T(8,128)S(1)}, f32[24,4,1,128]{3,0,2,1:T(8,128)S(1)}, u32[]{:S(2)}, u32[]{:S(2)}) collective-permute-start(f32[24,4,1,128]{3,0,2,1:T(8,128)S(1)} %get-tuple-element.71), channel_id=1, source_target_pairs={{1,0},{2,1},{3,2},{4,3},{5,4},{6,5},{7,6},{8,7},{9,8},{10,9},{11,1... | collective-permute-start | bytes 147464 | tf_op jit(solution)/shard_map/ppermute | solution.py:23
  305.5 8.6 %collective-permute-start.50 = (f32[24,6,1,128]{3,0,2,1:T(8,128)S(1)}, f32[24,6,1,128]{3,0,2,1:T(8,128)S(1)}, u32[]{:S(2)}, u32[]{:S(2)}) collective-permute-start(f32[24,6,1,128]{3,0,2,1:T(8,128)S(1)} %get-tuple-element.51), channel_id=1, source_target_pairs={{1,0},{2,1},{3,2},{4,3},{5,4},{6,5},{7,6},{8,7},{9,8},{10,9},{11,1... | collective-permute-start | bytes 221192 | tf_op jit(solution)/shard_map/ppermute | solution.py:23
  317.5 8.2 %collective-permute-start.52 = (f32[24,1,4,128]{3,0,2,1:T(8,128)S(1)}, f32[24,1,4,128]{3,0,2,1:T(8,128)S(1)}, u32[]{:S(2)}, u32[]{:S(2)}) collective-permute-start(f32[24,1,4,128]{3,0,2,1:T(8,128)S(1)} %get-tuple-element.62), channel_id=1, source_target_pairs={{16,0},{32,16},{48,32},{64,48},{80,64},{96,80},{112,96},{128,112},... | collective-permute-start | bytes 147464 | tf_op jit(solution)/shard_map/ppermute | solution.py:23
  325.7 8.7 %collective-permute-start.54 = (f32[24,6,1,128]{3,0,2,1:T(8,128)S(1)}, f32[24,6,1,128]{3,0,2,1:T(8,128)S(1)}, u32[]{:S(2)}, u32[]{:S(2)}) collective-permute-start(f32[24,6,1,128]{3,0,2,1:T(8,128)S(1)} %get-tuple-element.49), channel_id=1, source_target_pairs={{1,0},{2,1},{3,2},{4,3},{5,4},{6,5},{7,6},{8,7},{9,8},{10,9},{11,1... | collective-permute-start | bytes 221192 | tf_op jit(solution)/shard_map/ppermute | solution.py:23
  337.8 8.2 %collective-permute-start.56 = (f32[24,1,4,128]{3,0,2,1:T(8,128)S(1)}, f32[24,1,4,128]{3,0,2,1:T(8,128)S(1)}, u32[]{:S(2)}, u32[]{:S(2)}) collective-permute-start(f32[24,1,4,128]{3,0,2,1:T(8,128)S(1)} %get-tuple-element.60), channel_id=1, source_target_pairs={{16,0},{32,16},{48,32},{64,48},{80,64},{96,80},{112,96},{128,112},... | collective-permute-start | bytes 147464 | tf_op jit(solution)/shard_map/ppermute | solution.py:23
  346.0 8.7 %collective-permute-start.58 = (f32[24,6,1,128]{3,0,2,1:T(8,128)S(1)}, f32[24,6,1,128]{3,0,2,1:T(8,128)S(1)}, u32[]{:S(2)}, u32[]{:S(2)}) collective-permute-start(f32[24,6,1,128]{3,0,2,1:T(8,128)S(1)} %get-tuple-element.47), channel_id=1, source_target_pairs={{1,0},{2,1},{3,2},{4,3},{5,4},{6,5},{7,6},{8,7},{9,8},{10,9},{11,1... | collective-permute-start | bytes 221192 | tf_op jit(solution)/shard_map/ppermute | solution.py:23
  358.3 8.7 %collective-permute-start.60 = (f32[24,1,8,128]{3,0,2,1:T(8,128)S(1)}, f32[24,1,8,128]{3,0,2,1:T(8,128)S(1)}, u32[]{:S(2)}, u32[]{:S(2)}) collective-permute-start(f32[24,1,8,128]{3,0,2,1:T(8,128)S(1)} %get-tuple-element.40), channel_id=1, source_target_pairs={{16,0},{32,16},{48,32},{64,48},{80,64},{96,80},{112,96},{128,112},... | collective-permute-start | bytes 294920 | tf_op jit(solution)/shard_map/ppermute | solution.py:23
  367.0 9.2 %collective-permute-start.62 = (f32[24,10,1,128]{3,0,2,1:T(8,128)S(1)}, f32[24,10,1,128]{3,0,2,1:T(8,128)S(1)}, u32[]{:S(2)}, u32[]{:S(2)}) collective-permute-start(f32[24,10,1,128]{3,0,2,1:T(8,128)S(1)} %get-tuple-element.27), channel_id=1, source_target_pairs={{1,0},{2,1},{3,2},{4,3},{5,4},{6,5},{7,6},{8,7},{9,8},{10,9},{11,1... | collective-permute-start | bytes 368648 | tf_op jit(solution)/shard_map/ppermute | solution.py:23
  368.9 8.5 %collective-permute-start.63 = (f32[24,10,1,128]{3,0,2,1:T(8,128)S(1)}, f32[24,10,1,128]{3,0,2,1:T(8,128)S(1)}, u32[]{:S(2)}, u32[]{:S(2)}) collective-permute-start(f32[24,10,1,128]{3,0,2,1:T(8,128)S(1)} %get-tuple-element.28), channel_id=1, source_target_pairs={{0,1},{1,2},{2,3},{3,4},{4,5},{5,6},{6,7},{7,8},{8,9},{9,10},{10,1... | collective-permute-start | bytes 368648 | tf_op jit(solution)/shard_map/ppermute | solution.py:21
  380.0 8.7 %collective-permute-start.64 = (f32[24,1,8,128]{3,0,2,1:T(8,128)S(1)}, f32[24,1,8,128]{3,0,2,1:T(8,128)S(1)}, u32[]{:S(2)}, u32[]{:S(2)}) collective-permute-start(f32[24,1,8,128]{3,0,2,1:T(8,128)S(1)} %get-tuple-element.38), channel_id=1, source_target_pairs={{16,0},{32,16},{48,32},{64,48},{80,64},{96,80},{112,96},{128,112},... | collective-permute-start | bytes 294920 | tf_op jit(solution)/shard_map/ppermute | solution.py:23
  388.7 9.3 %collective-permute-start.66 = (f32[24,10,1,128]{3,0,2,1:T(8,128)S(1)}, f32[24,10,1,128]{3,0,2,1:T(8,128)S(1)}, u32[]{:S(2)}, u32[]{:S(2)}) collective-permute-start(f32[24,10,1,128]{3,0,2,1:T(8,128)S(1)} %get-tuple-element.25), channel_id=1, source_target_pairs={{1,0},{2,1},{3,2},{4,3},{5,4},{6,5},{7,6},{8,7},{9,8},{10,9},{11,1... | collective-permute-start | bytes 368648 | tf_op jit(solution)/shard_map/ppermute | solution.py:23
  390.6 8.6 %collective-permute-start.67 = (f32[24,10,1,128]{3,0,2,1:T(8,128)S(1)}, f32[24,10,1,128]{3,0,2,1:T(8,128)S(1)}, u32[]{:S(2)}, u32[]{:S(2)}) collective-permute-start(f32[24,10,1,128]{3,0,2,1:T(8,128)S(1)} %get-tuple-element.26), channel_id=1, source_target_pairs={{0,1},{1,2},{2,3},{3,4},{4,5},{5,6},{6,7},{7,8},{8,9},{9,10},{10,1... | collective-permute-start | bytes 368648 | tf_op jit(solution)/shard_map/ppermute | solution.py:21
  401.6 8.7 %collective-permute-start.68 = (f32[24,1,8,128]{3,0,2,1:T(8,128)S(1)}, f32[24,1,8,128]{3,0,2,1:T(8,128)S(1)}, u32[]{:S(2)}, u32[]{:S(2)}) collective-permute-start(f32[24,1,8,128]{3,0,2,1:T(8,128)S(1)} %get-tuple-element.36), channel_id=1, source_target_pairs={{16,0},{32,16},{48,32},{64,48},{80,64},{96,80},{112,96},{128,112},... | collective-permute-start | bytes 294920 | tf_op jit(solution)/shard_map/ppermute | solution.py:23
  410.3 9.3 %collective-permute-start.70 = (f32[24,10,1,128]{3,0,2,1:T(8,128)S(1)}, f32[24,10,1,128]{3,0,2,1:T(8,128)S(1)}, u32[]{:S(2)}, u32[]{:S(2)}) collective-permute-start(f32[24,10,1,128]{3,0,2,1:T(8,128)S(1)} %get-tuple-element.23), channel_id=1, source_target_pairs={{1,0},{2,1},{3,2},{4,3},{5,4},{6,5},{7,6},{8,7},{9,8},{10,9},{11,1... | collective-permute-start | bytes 368648 | tf_op jit(solution)/shard_map/ppermute | solution.py:23
  412.3 8.6 %collective-permute-start.71 = (f32[24,10,1,128]{3,0,2,1:T(8,128)S(1)}, f32[24,10,1,128]{3,0,2,1:T(8,128)S(1)}, u32[]{:S(2)}, u32[]{:S(2)}) collective-permute-start(f32[24,10,1,128]{3,0,2,1:T(8,128)S(1)} %get-tuple-element.24), channel_id=1, source_target_pairs={{0,1},{1,2},{2,3},{3,4},{4,5},{5,6},{6,7},{7,8},{8,9},{9,10},{10,1... | collective-permute-start | bytes 368648 | tf_op jit(solution)/shard_map/ppermute | solution.py:21
  (43 other events, 534.3 us)
where the time goes:
time: 425 us; the launch traced here: 422 us
  starting transfers between devices  249 us (59%)
  waiting for transfers between devices  115 us (27%)
  blocking collectives  42.5 us (10%)
  other arithmetic  9.6 us (2%)
    ppermute x36, starting transfers between devices, with_halo(): lax.ppermute(tail, axis, [(i, (i + 1) % count) for i in range(ends)])  149 us
    ppermute x36, starting transfers between devices, with_halo(): lax.ppermute(head, axis, [((i + 1) % count, i) for i in range(ends)])  99.2 us
    ppermute x36, waiting for transfers between devices, with_halo(): lax.ppermute(head, axis, [((i + 1) % count, i) for i in range(ends)])  91.8 us
    ppermute x36, waiting for transfers between devices, with_halo(): lax.ppermute(tail, axis, [(i, (i + 1) % count) for i in range(ends)])  23.1 us
    all_gather x1, blocking collectives, body(): blocks = lax.all_gather(current[None], 'gy', axis=0, tiled=True)  18.2 us
    all_gather x1, blocking collectives, body(): back = lax.all_gather(solved[None], 'gy', axis=0, tiled=True)  15.5 us
    unnamed x1, blocking collectives  8.83 us
  transfers between devices with their start and end apart: 72, of which 52 were waited for; matrix products, arithmetic and copies ran while one was open for 0% of the time, Pallas kernels for 0%

commit v1 on v0

v1 whole, which is shorter than its diff:
```python
import functools
import math

import jax
import jax.numpy as jnp
from jax import lax
from jax.experimental import pallas as pl
from jax.experimental.pallas import tpu as pltpu
from jax.sharding import PartitionSpec as P

THETA = 8.0
DELTA = 6.5
ROOTS = tuple(THETA + DELTA * math.cos(math.pi * (2 * k + 1) / 6) for k in range(3))
HALO = 3


def swap(x, axis, dist, odd):
    count = lax.axis_size(axis)
    pairs = []
    for i in range(count - dist):
        if (i // dist) % 2 == odd:
            pairs += [(i, i + dist), (i + dist, i)]
    return lax.ppermute(x, axis, pairs)


def parity(axis, dist):
    return lax.rem(lax.div(lax.axis_index(axis), dist), 2)


def swap_ends(low, high, axis, dist):
    even = parity(axis, dist) == 0
    first = swap(jnp.where(even, high, low), axis, dist, 0)
    second = swap(jnp.where(even, low, high), axis, dist, 1)
    return first, second


def in_order(first, second, axis, dist):
    even = parity(axis, dist) == 0
    return jnp.where(even, second, first), jnp.where(even, first, second)


def cells(x):
    return x.reshape((-1,) + x.shape[-2:])


def z_neighbours(v):
    lane = lax.broadcasted_iota(jnp.int32, v.shape, 1)
    below = jnp.where(lane == 0, 0.0, pltpu.roll(v, 1, 1))
    above = jnp.where(lane == v.shape[1] - 1, 0.0, pltpu.roll(v, v.shape[1] - 1, 1))
    return below + above


def inside(at, size):
    return jnp.where((at >= 0) & (at < size), 1.0, 0.0).astype(jnp.float32)


def beside(src, x, y):
    centre = src[x, y]
    total = (src[x - 1, y] + src[x + 1, y]) + (src[x, y - 1] + src[x, y + 1])
    return total + z_neighbours(centre), centre


def factor_cell(src, x, y, shift_row, root, mask):
    total, centre = beside(src, x, y)
    scale = mask * (1.0 / root)
    return (scale * ((root - 6.0) - shift_row)) * centre + scale * total


def factor(src, dst, shift, shift_at, size, root, masks):
    def row(x, carry):
        row_mask = masks(x, None)
        for y in range(size):
            shift_row = shift[x + shift_at, pl.ds(y + shift_at, 1), :]
            mask = row_mask * masks(None, y)
            dst[x, y] = factor_cell(src, x + 1, y + 1, shift_row, root, mask)
        return carry

    lax.fori_loop(0, size, row, 0)


def masks_of(where, reach, grid):
    def masks(x, y):
        if x is not None:
            return inside(where[0] + x - reach, grid[0])
        return inside(where[1] + y - reach, grid[1])

    return masks


def put_columns(dst, centre, pieces, where, rows, width, reach):
    def row(x, carry):
        for y in range(width):
            dst[x, reach + y] = centre[x, y]
        for ref, base, columns, dist, odd in pieces:
            gap = 0 if dist == 1 else reach - columns
            right, left = reach + width + gap, reach - columns - gap
            if odd:
                right, left = left, right
            at = jnp.where(where[1 + dist] == 0, right, left)
            for k in range(columns):
                dst[x, at + k] = ref[base + x * columns + k]
        return carry

    lax.fori_loop(0, rows, row, 0)


def down_kernel(n, grid, layout, where, rows, *refs):
    sides = refs[: len(layout)]
    shift, iterate, leftover, coarser, pad, one, two = refs[len(layout) :]
    pieces = [(ref,) + piece for ref, piece in zip(sides, layout)]
    put_columns(pad, rows, pieces, where, n + 2 * HALO, n, HALO)
    factor(pad, one, shift, 0, n + 4, ROOTS[0], masks_of(where, 2, grid))
    factor(one, two, shift, 1, n + 2, ROOTS[1], masks_of(where, 1, grid))

    def row(x, carry):
        for y in range(n):
            shift_row = shift[x + 2, pl.ds(y + 2, 1), :]
            leftover[x, y] = factor_cell(two, x + 1, y + 1, shift_row, ROOTS[2], 1.0)
            iterate[x, y] = (
                pad[x + 3, y + 3] * (1.0 / ROOTS[0])
                + one[x + 2, y + 2] * (1.0 / ROOTS[1])
                + two[x + 1, y + 1] * (1.0 / ROOTS[2])
            )
        return carry

    lax.fori_loop(0, n, row, 0)

    def coarse_row(x, carry):
        for y in range(n // 2):
            near = leftover[2 * x, 2 * y] + leftover[2 * x, 2 * y + 1]
            far = leftover[2 * x + 1, 2 * y] + leftover[2 * x + 1, 2 * y + 1]
            coarser[x, y] = 0.25 * (near + far)
        return carry

    lax.fori_loop(0, n // 2, coarse_row, 0)


def up_kernel(n, grid, layout, where, coarse_rows, *refs):
    half = n // 2
    sides = refs[: len(layout)]
    shift, iterate, leftover_rows, left_first, left_second, result, coarse, start, one = refs[len(layout) :]
    if layout[0] is None:
        for k in range(5):
            coarse[2, k] = coarse_rows[k]
            for ref, dist, odd in zip(sides, (1, 1, 2, 2), (0, 1, 0, 1)):
                ahead, behind = (2 - dist, 2 + dist) if odd else (2 + dist, 2 - dist)
                coarse[jnp.where(where[3 + dist] == 0, ahead, behind), k] = ref[k]
    else:
        put_columns(coarse, coarse_rows, [(ref,) + piece for ref, piece in zip(sides, layout)], where, half + 4, half, 2)
    put_columns(
        start, leftover_rows, [(left_first, where[6], 2, 1, 0), (left_second, where[6], 2, 1, 1)], where, n + 4, n, 2
    )
    outer = masks_of(where, 2, grid)

    def first_row(x, carry):
        row_mask = outer(x, None)
        here, before, after = (x + 2) // 2, (x + 1) // 2, (x + 3) // 2
        for y in range(n + 4):
            at, left, right = (y + 2) // 2, (y + 1) // 2, (y + 3) // 2
            centre = coarse[here, at]
            total = (coarse[before, at] + coarse[after, at]) + (coarse[here, left] + coarse[here, right])
            total = total + z_neighbours(centre)
            shift_row = shift[x, pl.ds(y, 1), :]
            mask = row_mask * outer(None, y)
            start[x, y] = mask * ((start[x, y] - (6.0 + shift_row) * centre) + total)
        return carry

    lax.fori_loop(0, n + 4, first_row, 0)
    factor(start, one, shift, 1, n + 2, ROOTS[0], masks_of(where, 1, grid))

    def row(x, carry):
        for y in range(n):
            shift_row = shift[x + 2, pl.ds(y + 2, 1), :]
            two = factor_cell(one, x + 1, y + 1, shift_row, ROOTS[1], 1.0)
            step = (
                start[x + 2, y + 2] * (1.0 / ROOTS[0]) + one[x + 1, y + 1] * (1.0 / ROOTS[1]) + two * (1.0 / ROOTS[2])
            )
            result[x, y] = (iterate[x, y] + coarse[x // 2 + 2, y // 2 + 2]) + step
        return carry

    lax.fori_loop(0, n, row, 0)


VMEM = pl.BlockSpec(memory_space=pltpu.VMEM)
SMEM = pl.BlockSpec(memory_space=pltpu.SMEM)


def call(kernel, where, operands, outs, scratch, name):
    tail = operands[0].shape[-2:]
    return pl.pallas_call(
        kernel,
        out_shape=[jax.ShapeDtypeStruct(out + tail, jnp.float32) for out in outs],
        in_specs=[SMEM] + [VMEM] * len(operands),
        out_specs=[VMEM] * len(outs),
        scratch_shapes=[pltpu.VMEM(own + tail, jnp.float32) for own in scratch],
        compiler_params=pltpu.CompilerParams(vmem_limit_bytes=32 * 1024 * 1024),
        name=name,
    )(where, *operands)


def place(n, offset=0):
    return jnp.stack(
        [
            lax.axis_index("gx") * n,
            lax.axis_index("gy") * n,
            parity("gy", 1),
            parity("gy", 2),
            parity("gx", 1),
            parity("gx", 2),
            jnp.int32(offset),
        ]
    ).astype(jnp.int32)


def grid_of(n):
    return (lax.axis_size("gx") * n, lax.axis_size("gy") * n)


def down(n, rows, sides, layout, shift):
    wide = n + 2 * HALO
    return call(
        functools.partial(down_kernel, n, grid_of(n), layout),
        place(n),
        [rows, *sides, shift],
        [(n, n), (n, n), (n // 2, n // 2)],
        [(wide, wide), (n + 4, n + 4), (n + 2, n + 2)],
        "down_%d" % n,
    )


def up(n, coarse_rows, sides, layout, shift, iterate, leftover_rows, left, offset):
    return call(
        functools.partial(up_kernel, n, grid_of(n), layout),
        place(n, offset),
        [coarse_rows, *sides, shift, iterate, leftover_rows, *left],
        [(n, n)],
        [(n // 2 + 4, n // 2 + 4), (n + 4, n + 4), (n + 2, n + 2)],
        "up_%d" % n,
    )[0]


def gx_rows(v, width):
    first, second = swap_ends(v[:width], v[v.shape[0] - width :], "gx", 1)
    before, after = in_order(first, second, "gx", 1)
    return jnp.concatenate([before, v, after], axis=0)


def gy_sides(rows, width):
    first, second = swap_ends(cells(rows[:, :width]), cells(rows[:, rows.shape[1] - width :]), "gy", 1)
    return [first, second]


BOTH = [(0, HALO, 1, 0), (0, HALO, 1, 1)]
BOTH_TWO = [(0, 2, 1, 0), (0, 2, 1, 1)]


def restrict_shift(v):
    xs, ys, zs = v.shape
    return v.reshape(xs // 2, 2, ys // 2, 2, zs).mean(axis=(1, 3))


def body(rhs, shift, slots, coarse_inverse):
    high = lax.Precision.HIGHEST
    right = jnp.transpose(rhs, (1, 2, 0, 3))
    n = right.shape[0]
    chans, depth = right.shape[2:]

    def with_shift(strip, block):
        flat = block.reshape(-1, depth)
        extra = -flat.shape[0] % chans
        flat = jnp.pad(flat, ((0, extra), (0, 0)))
        return jnp.concatenate([cells(strip), flat.reshape(-1, chans, depth)], axis=0)

    def shift_of(message, count, shape):
        flat = message[count:].reshape(-1, depth)
        return flat[: shape[0] * shape[1]].reshape(shape + (depth,))

    first, second = swap_ends(with_shift(right[:HALO], shift), with_shift(right[n - HALO :], shift), "gx", 1)
    before, after = in_order(first, second, "gx", 1)
    strip = HALO * n
    rows = jnp.concatenate(
        [before[:strip].reshape(HALO, n, chans, depth), right, after[:strip].reshape(HALO, n, chans, depth)], axis=0
    )
    shift_rows = jnp.concatenate([shift_of(before, strip, (n, n)), shift, shift_of(after, strip, (n, n))], axis=0)
    low, up_end = rows[:, :HALO], rows[:, n - HALO :]
    sides = swap_ends(with_shift(low, shift_rows), with_shift(up_end, shift_rows), "gy", 1)
    before, after = in_order(*sides, "gy", 1)
    strip = HALO * (n + 2 * HALO)
    shift_wide = jnp.concatenate(
        [shift_of(before, strip, (3 * n, n)), shift_rows, shift_of(after, strip, (3 * n, n))], axis=1
    )
    shift_one = restrict_shift(shift_wide)
    shift_two = restrict_shift(shift_one)
    shifts = [shift_wide[n - 2 : 2 * n + 2, n - 2 : 2 * n + 2], shift_one[2:-2, 2:-2], shift_two]

    x0, q0, b1 = down(n, rows, list(sides), BOTH, shifts[0])
    rows = gx_rows(b1, HALO)
    x1, q1, b2 = down(n // 2, rows, gy_sides(rows, HALO), BOTH, shifts[1])

    near = swap_ends(b2, b2, "gx", 1)
    far = swap_ends(b2[:1], b2[1:], "gx", 2)
    (before, after), (before_far, after_far) = in_order(*near, "gx", 1), in_order(*far, "gx", 2)
    rows = jnp.concatenate([before_far, before, b2, after, after_far], axis=0)
    near = swap_ends(cells(rows), cells(rows), "gy", 1)
    far = swap_ends(cells(rows[:, :1]), cells(rows[:, 1:]), "gy", 2)
    layout = [(0, 2, 1, 0), (0, 2, 1, 1), (0, 1, 2, 0), (0, 1, 2, 1)]
    x2, q2, b3 = down(n // 4, rows, [*near, *far], layout, shifts[2])

    lefts = [q0, q1, q2]
    low = jnp.concatenate([cells(q[:2]) for q in lefts], axis=0)
    up_end = jnp.concatenate([cells(q[-2:]) for q in lefts], axis=0)
    first, second = swap_ends(low, up_end, "gx", 1)
    before, after = in_order(first, second, "gx", 1)
    left_rows, at = [], 0
    for q in lefts:
        wide = 2 * q.shape[1]
        shape = (2,) + q.shape[1:]
        left_rows.append(
            jnp.concatenate([before[at : at + wide].reshape(shape), q, after[at : at + wide].reshape(shape)], axis=0)
        )
        at += wide
    low = jnp.concatenate([cells(q[:, :2]) for q in left_rows], axis=0)
    up_end = jnp.concatenate([cells(q[:, -2:]) for q in left_rows], axis=0)
    left_sides = swap_ends(low, up_end, "gy", 1)
    offsets = [0, 2 * (n + 4), 2 * (n + 4) + 2 * (n // 2 + 4)]

    count = lax.axis_size("gy")
    me = lax.axis_index("gy")
    slot = jnp.broadcast_to(slots.astype(jnp.float32), (8, depth))
    shares = lax.all_gather(jnp.concatenate([b3[0, 0], slot], axis=0)[None], "gy", axis=0, tiled=True)
    blocks = shares[:, :chans]
    slot_all = shares[:, chans, 0].astype(jnp.int32)
    places = (slot_all[None, :] == jnp.arange(count, dtype=jnp.int32)[:, None]).astype(jnp.float32)
    ordered = jnp.einsum("mj,jck->mck", places, blocks, precision=high)
    flat = ordered.transpose(1, 0, 2).reshape(chans, count * depth)
    solved = lax.dot_general(
        flat, coarse_inverse[0, 0], (((1,), (1,)), ((), ())), precision=high, preferred_element_type=jnp.float32
    )
    back = lax.all_gather(solved[None], "gy", axis=0, tiled=True)
    beside_me = me + jnp.arange(-2, 3, dtype=jnp.int32)
    wanted = (beside_me[:, None] == jnp.arange(count, dtype=jnp.int32)[None, :]).astype(jnp.float32)
    chosen = jnp.einsum("wj,mj->wm", wanted, places, precision=high)
    fix = jnp.einsum("wm,mck->wck", chosen, back, precision=high)
    lines = [*swap_ends(fix, fix, "gx", 1), *swap_ends(fix, fix, "gx", 2)]

    x2 = up(n // 4, fix, lines, [None] * 4, shifts[2], x2, left_rows[2], left_sides, offsets[2])
    rows = gx_rows(x2, 2)
    x1 = up(n // 2, rows, gy_sides(rows, 2), BOTH_TWO, shifts[1], x1, left_rows[1], left_sides, offsets[1])
    rows = gx_rows(x1, 2)
    x0 = up(n, rows, gy_sides(rows, 2), BOTH_TWO, shifts[0], x0, left_rows[0], left_sides, offsets[0])
    return jnp.transpose(x0, (2, 0, 1, 3))


def solution(mesh):
    return jax.shard_map(
        body,
        mesh=mesh,
        in_specs=(
            P(None, "gx", "gy", None),
            P("gx", "gy", None),
            P("gx", "gy"),
            P("gx", "gy", None, None),
        ),
        out_specs=P(None, "gx", "gy", None),
        check_vma=False,
    )
```

time: 425 us -> 247 us (0.58)
  the two profiles are of different devices: /device:TPU:223 before, /device:TPU:31 now
where the time goes in v1:
time: 247 us; the launch traced here: 245 us
  starting transfers between devices  103 us (42%)
  waiting for transfers between devices  46.2 us (19%)
  blocking collectives  45.2 us (18%)
  Pallas kernels  20.8 us (8%)
  local copies, waits for them, and re-layouts  16.2 us (7%)
  other arithmetic  10.8 us (4%)
    ppermute x32, starting transfers between devices, swap(): return lax.ppermute(x, axis, pairs)  103 us
    ppermute x32, waiting for transfers between devices, swap(): return lax.ppermute(x, axis, pairs)  46.2 us
    all_gather x1, blocking collectives, body(): lax.all_gather(jnp.concatenate([b3[0, 0], slot], axis=0)[None], 'gy', axi...  25 us
    pallas_call x6, Pallas kernels, call(): pl.pallas_call(kernel, out_shape=[jax.ShapeDtypeStruct(out + tail, jnp.fl...  20.8 us
    all_gather x1, blocking collectives, body(): back = lax.all_gather(solved[None], 'gy', axis=0, tiled=True)  20.2 us
    unnamed x51, local copies, waits for them, and re-layouts  12.7 us
  transfers between devices with their start and end apart: 32, of which 16 were waited for; matrix products, arithmetic and copies ran while one was open for 2% of the time, Pallas kernels for 0%

profile of v1, /device:TPU:31, one launch (start us, length us, event | category | flops | bytes accessed | tf_op | source)
XLA Modules:
  0.0 245.4 jit_solution(10658429761762383761)
XLA Ops:
  1.8 4.3 %collective-permute-start = (f32[27,24,128]{2,1,0:T(8,128)S(1)}, f32[27,24,128]{2,1,0:T(8,128)S(1)}, u32[]{:S(2)}, u32[]{:S(2)}) collective-permute-start(f32[27,24,128]{2,1,0:T(8,128)S(1)} %get-tuple-element.43), channel_id=1, source_target_pairs={{16,32},{32,16},{48,64},{64,48},{80,96},{96,80},{112,128},{128,112... | collective-permute-start | bytes 995336 | tf_op jit(solution)/shard_map/ppermute | solution.py:23
  8.1 7.6 %collective-permute-done = f32[27,24,128]{2,1,0:T(8,128)S(1)} collective-permute-done((f32[27,24,128]{2,1,0:T(8,128)S(1)}, f32[27,24,128]{2,1,0:T(8,128)S(1)}, u32[]{:S(2)}, u32[]{:S(2)}) %collective-permute-start) | collective-permute-done | bytes 331808 | tf_op jit(solution)/shard_map/ppermute | solution.py:23
  19.6 3.8 %collective-permute-start.2 = (f32[50,24,128]{2,1,0:T(8,128)}, f32[50,24,128]{2,1,0:T(8,128)S(1)}, u32[]{:S(2)}, u32[]{:S(2)}) collective-permute-start(f32[50,24,128]{2,1,0:T(8,128)} %get-tuple-element.32), channel_id=1, source_target_pairs={{0,1},{1,0},{2,3},{3,2},{4,5},{5,4},{6,7},{7,6},{8,9},{9,8},{10,11... | collective-permute-start | bytes 1843208 | tf_op jit(solution)/shard_map/ppermute | solution.py:23
  23.4 3.9 %collective-permute-start.3 = (f32[50,24,128]{2,1,0:T(8,128)}, f32[50,24,128]{2,1,0:T(8,128)}, u32[]{:S(2)}, u32[]{:S(2)}) collective-permute-start(f32[50,24,128]{2,1,0:T(8,128)} %get-tuple-element.31), channel_id=1, source_target_pairs={{1,2},{2,1},{3,4},{4,3},{5,6},{6,5},{7,8},{8,7},{9,10},{10,9},{11,... | collective-permute-start | bytes 1843208 | tf_op jit(solution)/shard_map/ppermute | solution.py:23
  27.4 8.0 %collective-permute-done.3.refs_1_ = f32[50,24,128]{2,1,0:T(8,128)} collective-permute-done((f32[50,24,128]{2,1,0:T(8,128)}, f32[50,24,128]{2,1,0:T(8,128)}, u32[]{:S(2)}, u32[]{:S(2)}) %collective-permute-start.3) | collective-permute-done | bytes 614432 | tf_op jit(solution)/shard_map/ppermute | solution.py:23
  39.1 5.6 %down_8.1 = (f32[8,8,24,128]{3,2,1,0:T(8,128)S(1)}, f32[8,8,24,128]{3,2,1,0:T(8,128)S(1)}, f32[4,4,24,128]{3,2,1,0:T(8,128)S(1)}) custom-call(s32[7]{0:T(128)S(1)} %stack.36.where, f32[14,8,24,128]{3,2,1,0:T(8,128)S(1)} %pad_maximum_fusion.rows, f32[50,24,128]{2,1,0:T(8,128)S(1)} %copy-done.8, f32[50,24,128]{2,1,0:T(8,128)} %collective-permute-done.3.refs_1_, ...), custom_call_target="tpu_custom_call" | custom-call | tf_op jit(solution)/shard_map/down_8/pallas_call | solution.py:190
  45.6 4.3 %collective-permute-start.4 = (f32[3,4,24,128]{3,2,1,0:T(8,128)S(1)}, f32[3,4,24,128]{3,2,1,0:T(8,128)S(1)}, u32[]{:S(2)}, u32[]{:S(2)}) collective-permute-start(f32[3,4,24,128]{3,2,1,0:T(8,128)S(1)} %get-tuple-element.61), channel_id=1, source_target_pairs={{16,32},{32,16},{48,64},{64,48},{80,96},{96,80},{112,128},{128,112... | collective-permute-start | bytes 442376 | tf_op jit(solution)/shard_map/ppermute | solution.py:23
  58.7 6.2 %collective-permute-start.7 = (f32[30,24,128]{2,1,0:T(8,128)}, f32[30,24,128]{2,1,0:T(8,128)S(1)}, u32[]{:S(2)}, u32[]{:S(2)}) collective-permute-start(f32[30,24,128]{2,1,0:T(8,128)} %bitcast.27), channel_id=1, source_target_pairs={{1,2},{2,1},{3,4},{4,3},{5,6},{6,5},{7,8},{8,7},{9,10},{10,9},{11,... | collective-permute-start | bytes 1105928 | tf_op jit(solution)/shard_map/ppermute | solution.py:23
  65.1 5.2 %collective-permute-done.7.refs_1_ = f32[30,24,128]{2,1,0:T(8,128)S(1)} collective-permute-done((f32[30,24,128]{2,1,0:T(8,128)}, f32[30,24,128]{2,1,0:T(8,128)S(1)}, u32[]{:S(2)}, u32[]{:S(2)}) %collective-permute-start.7) | collective-permute-done | bytes 368672 | tf_op jit(solution)/shard_map/ppermute | solution.py:23
  72.0 2.7 %down_4.1 = (f32[4,4,24,128]{3,2,1,0:T(8,128)S(1)}, f32[4,4,24,128]{3,2,1,0:T(8,128)S(1)}, f32[2,2,24,128]{3,2,1,0:T(8,128)S(1)}) custom-call(s32[7]{0:T(128)S(1)} %stack.86.where, f32[10,4,24,128]{3,2,1,0:T(8,128)S(1)} %pad_maximum_fusion.6.rows, f32[30,24,128]{2,1,0:T(8,128)S(1)} %collective-permute-done.6.refs_0_, f32[30,24,128]{2,1,0:T(8,128)S(1)} %copy-done.12, ...), custom_call_target="tpu_custom_call" | custom-call | tf_op jit(solution)/shard_map/down_4/pallas_call | solution.py:190
  74.8 4.1 %collective-permute-start.8 = (f32[1,2,24,128]{3,2,1,0:T(8,128)S(1)}, f32[1,2,24,128]{3,2,1,0:T(8,128)S(1)}, u32[]{:S(2)}, u32[]{:S(2)}) collective-permute-start(f32[1,2,24,128]{3,2,1,0:T(8,128)S(1)} %get-tuple-element.66), channel_id=1, source_target_pairs={{32,64},{64,32},{48,80},{80,48},{96,128},{128,96},{112,144},{144,1... | collective-permute-start | bytes 73736 | tf_op jit(solution)/shard_map/ppermute | solution.py:23
  80.8 4.3 %collective-permute-start.10 = (f32[2,2,24,128]{3,2,1,0:T(8,128)S(1)}, f32[2,2,24,128]{3,2,1,0:T(8,128)S(1)}, u32[]{:S(2)}, u32[]{:S(2)}) collective-permute-start(f32[2,2,24,128]{3,2,1,0:T(8,128)S(1)} %get-tuple-element.15), channel_id=1, source_target_pairs={{16,32},{32,16},{48,64},{64,48},{80,96},{96,80},{112,128},{128,112... | collective-permute-start | bytes 147464 | tf_op jit(solution)/shard_map/ppermute | solution.py:23
  91.9 5.4 %collective-permute-start.13 = (f32[16,24,128]{2,1,0:T(8,128)S(1)}, f32[16,24,128]{2,1,0:T(8,128)S(1)}, u32[]{:S(2)}, u32[]{:S(2)}) collective-permute-start(f32[16,24,128]{2,1,0:T(8,128)S(1)} %bitcast.81), channel_id=1, source_target_pairs={{1,2},{2,1},{3,4},{4,3},{5,6},{6,5},{7,8},{8,7},{9,10},{10,9},{11,... | collective-permute-start | bytes 589832 | tf_op jit(solution)/shard_map/ppermute | solution.py:23
  97.3 4.0 %collective-permute-start.14 = (f32[8,24,128]{2,1,0:T(8,128)S(1)}, f32[8,24,128]{2,1,0:T(8,128)S(1)}, u32[]{:S(2)}, u32[]{:S(2)}) collective-permute-start(f32[8,24,128]{2,1,0:T(8,128)S(1)} %get-tuple-element.60), channel_id=1, source_target_pairs={{0,2},{2,0},{1,3},{3,1},{4,6},{6,4},{5,7},{7,5},{8,10},{10,8},{9,1... | collective-permute-start | bytes 294920 | tf_op jit(solution)/shard_map/ppermute | solution.py:23
  106.0 4.3 %collective-permute-start.20 = (f32[28,24,128]{2,1,0:T(8,128)}, f32[28,24,128]{2,1,0:T(8,128)S(1)}, u32[]{:S(2)}, u32[]{:S(2)}) collective-permute-start(f32[28,24,128]{2,1,0:T(8,128)} %get-tuple-element.41), channel_id=1, source_target_pairs={{16,32},{32,16},{48,64},{64,48},{80,96},{96,80},{112,128},{128,112... | collective-permute-start | bytes 1032200 | tf_op jit(solution)/shard_map/ppermute | solution.py:23
  112.3 25.0 %all-gather = f32[512,128]{1,0:T(8,128)S(1)} all-gather(f32[32,128]{1,0:T(8,128)S(1)} %concatenate.66), channel_id=2, replica_groups=mesh['gx'=32,'gy'=16] {'gy'}, dimensions={0}, use_global_device_ids=true | all-gather | bytes 278528 | tf_op jit(solution)/shard_map/all_gather | solution.py:330
  143.0 3.1 %collective-permute-start.23 = (f32[52,24,128]{2,1,0:T(8,128)}, f32[52,24,128]{2,1,0:T(8,128)S(1)}, u32[]{:S(2)}, u32[]{:S(2)}) collective-permute-start(f32[52,24,128]{2,1,0:T(8,128)} %get-tuple-element.29), channel_id=1, source_target_pairs={{1,2},{2,1},{3,4},{4,3},{5,6},{6,5},{7,8},{8,7},{9,10},{10,9},{11,... | collective-permute-start | bytes 1916936 | tf_op jit(solution)/shard_map/ppermute | solution.py:23
  147.1 20.2 %all-gather.1 = f32[384,128]{1,0:T(8,128)S(1)} all-gather(f32[24,128]{1,0:T(8,128)S(1)} %fusion), channel_id=3, replica_groups=mesh['gx'=32,'gy'=16] {'gy'}, dimensions={0}, use_global_device_ids=true | all-gather | bytes 208896 | tf_op jit(solution)/shard_map/all_gather | solution.py:339
  168.3 3.6 %collective-permute-start.16 = (f32[5,24,128]{2,1,0:T(8,128)}, f32[5,24,128]{2,1,0:T(8,128)S(1)}, u32[]{:S(2)}, u32[]{:S(2)}) collective-permute-start(f32[5,24,128]{2,1,0:T(8,128)} %copy.13.coarse_rows), channel_id=1, source_target_pairs={{0,16},{16,0},{32,48},{48,32},{64,80},{80,64},{96,112},{112,96},{1... | collective-permute-start | bytes 184328 | tf_op jit(solution)/shard_map/ppermute | solution.py:23
  172.0 4.4 %collective-permute-start.17 = (f32[5,24,128]{2,1,0:T(8,128)}, f32[5,24,128]{2,1,0:T(8,128)}, u32[]{:S(2)}, u32[]{:S(2)}) collective-permute-start(f32[5,24,128]{2,1,0:T(8,128)} %copy.13.coarse_rows), channel_id=1, source_target_pairs={{16,32},{32,16},{48,64},{64,48},{80,96},{96,80},{112,128},{128,112... | collective-permute-start | bytes 184328 | tf_op jit(solution)/shard_map/ppermute | solution.py:23
  178.9 4.4 %collective-permute-start.19 = (f32[5,24,128]{2,1,0:T(8,128)}, f32[5,24,128]{2,1,0:T(8,128)}, u32[]{:S(2)}, u32[]{:S(2)}) collective-permute-start(f32[5,24,128]{2,1,0:T(8,128)} %copy.13.coarse_rows), channel_id=1, source_target_pairs={{32,64},{64,32},{48,80},{80,48},{96,128},{128,96},{112,144},{144,1... | collective-permute-start | bytes 184328 | tf_op jit(solution)/shard_map/ppermute | solution.py:23
  183.5 4.3 %collective-permute-done.19.refs_3_ = f32[5,24,128]{2,1,0:T(8,128)} collective-permute-done((f32[5,24,128]{2,1,0:T(8,128)}, f32[5,24,128]{2,1,0:T(8,128)}, u32[]{:S(2)}, u32[]{:S(2)}) %collective-permute-start.19) | collective-permute-done | bytes 61472 | tf_op jit(solution)/shard_map/ppermute | solution.py:23
  191.1 2.3 up_2.1
  193.4 4.2 %collective-permute-start.24 = (f32[2,2,24,128]{3,2,1,0:T(8,128)S(1)}, f32[2,2,24,128]{3,2,1,0:T(8,128)S(1)}, u32[]{:S(2)}, u32[]{:S(2)}) collective-permute-start(f32[2,2,24,128]{3,2,1,0:T(8,128)S(1)} %up_2.1), channel_id=1, source_target_pairs={{16,32},{32,16},{48,64},{64,48},{80,96},{96,80},{112,128},{128,112... | collective-permute-start | bytes 147464 | tf_op jit(solution)/shard_map/ppermute | solution.py:23
  203.4 4.9 %collective-permute-start.26 = (f32[12,24,128]{2,1,0:T(8,128)}, f32[12,24,128]{2,1,0:T(8,128)}, u32[]{:S(2)}, u32[]{:S(2)}) collective-permute-start(f32[12,24,128]{2,1,0:T(8,128)} %bitcast.57), channel_id=1, source_target_pairs={{0,1},{1,0},{2,3},{3,2},{4,5},{5,4},{6,7},{7,6},{8,9},{9,8},{10,11... | collective-permute-start | bytes 442376 | tf_op jit(solution)/shard_map/ppermute | solution.py:23
  210.3 4.8 %collective-permute-done.27.refs_1_ = f32[12,24,128]{2,1,0:T(8,128)} collective-permute-done((f32[12,24,128]{2,1,0:T(8,128)}, f32[12,24,128]{2,1,0:T(8,128)}, u32[]{:S(2)}, u32[]{:S(2)}) %collective-permute-start.27) | collective-permute-done | bytes 147488 | tf_op jit(solution)/shard_map/ppermute | solution.py:23
  217.0 3.3 %up_4.1 = f32[4,4,24,128]{3,2,1,0:T(8,128)S(1)} custom-call(s32[7]{0:T(128)S(1)} %stack.39.where, f32[6,2,24,128]{3,2,1,0:T(8,128)} %pad_maximum_fusion.15.coarse_rows, f32[12,24,128]{2,1,0:T(8,128)} %collective-permute-done.26.refs_0_, f32[12,24,128]{2,1,0:T(8,128)} %collective-permute-done.27.refs_1_, f32[8,8,128]{2,1,0:T(8,128)S(1)} %slice.185.refs_2_, ...), custom_call_target="tpu_custom_call" | custom-call | tf_op jit(solution)/shard_map/up_4/pallas_call | solution.py:190
  220.4 4.5 %collective-permute-start.28 = (f32[2,4,24,128]{3,2,1,0:T(8,128)S(1)}, f32[2,4,24,128]{3,2,1,0:T(8,128)S(1)}, u32[]{:S(2)}, u32[]{:S(2)}) collective-permute-start(f32[2,4,24,128]{3,2,1,0:T(8,128)S(1)} %get-tuple-element.55), channel_id=1, source_target_pairs={{16,32},{32,16},{48,64},{64,48},{80,96},{96,80},{112,128},{128,112... | collective-permute-start | bytes 294920 | tf_op jit(solution)/shard_map/ppermute | solution.py:23
  226.8 2.3 collective-permute-done.28
  232.3 3.4 %collective-permute-start.31 = (f32[16,24,128]{2,1,0:T(8,128)S(1)}, f32[16,24,128]{2,1,0:T(8,128)S(1)}, u32[]{:S(2)}, u32[]{:S(2)}) collective-permute-start(f32[16,24,128]{2,1,0:T(8,128)S(1)} %bitcast.114), channel_id=1, source_target_pairs={{1,2},{2,1},{3,4},{4,3},{5,6},{6,5},{7,8},{8,7},{9,10},{10,9},{11,... | collective-permute-start | bytes 589832 | tf_op jit(solution)/shard_map/ppermute | solution.py:23
  235.7 3.6 %collective-permute-done.31.refs_1_ = f32[16,24,128]{2,1,0:T(8,128)S(1)} collective-permute-done((f32[16,24,128]{2,1,0:T(8,128)S(1)}, f32[16,24,128]{2,1,0:T(8,128)S(1)}, u32[]{:S(2)}, u32[]{:S(2)}) %collective-permute-start.31) | collective-permute-done | bytes 196640 | tf_op jit(solution)/shard_map/ppermute | solution.py:23
  239.3 5.0 %up_8.1 = f32[8,8,24,128]{3,2,1,0:T(8,128)S(1)} custom-call(s32[7]{0:T(128)S(1)} %stack.36.where, f32[8,4,24,128]{3,2,1,0:T(8,128)S(1)} %pad_maximum_fusion.12.coarse_rows, f32[16,24,128]{2,1,0:T(8,128)S(1)} %collective-permute-done.30.refs_0_, f32[16,24,128]{2,1,0:T(8,128)S(1)} %collective-permute-done.31.refs_1_, f32[12,12,128]{2,1,0:T(8,128)S(1)} %copy-done.6, ...), custom_call_target="tpu_custom_call" | custom-call | tf_op jit(solution)/shard_map/up_8/pallas_call | solution.py:190
  (161 shorter events, 66.8 us)
Async XLA Ops:
  1.8 13.9 %collective-permute-start = (f32[27,24,128]{2,1,0:T(8,128)S(1)}, f32[27,24,128]{2,1,0:T(8,128)S(1)}, u32[]{:S(2)}, u32[]{:S(2)}) collective-permute-start(f32[27,24,128]{2,1,0:T(8,128)S(1)} %get-tuple-element.43), channel_id=1, source_target_pairs={{16,32},{32,16},{48,64},{64,48},{80,96},{96,80},{112,128},{128,112... | collective-permute-start | bytes 995336 | tf_op jit(solution)/shard_map/ppermute | solution.py:23
  6.2 10.3 %collective-permute-start.1 = (f32[27,24,128]{2,1,0:T(8,128)S(1)}, f32[27,24,128]{2,1,0:T(8,128)}, u32[]{:S(2)}, u32[]{:S(2)}) collective-permute-start(f32[27,24,128]{2,1,0:T(8,128)S(1)} %get-tuple-element.44), channel_id=1, source_target_pairs={{0,16},{16,0},{32,48},{48,32},{64,80},{80,64},{96,112},{112,96},{1... | collective-permute-start | bytes 995336 | tf_op jit(solution)/shard_map/ppermute | solution.py:23
  19.6 7.8 %collective-permute-start.2 = (f32[50,24,128]{2,1,0:T(8,128)}, f32[50,24,128]{2,1,0:T(8,128)S(1)}, u32[]{:S(2)}, u32[]{:S(2)}) collective-permute-start(f32[50,24,128]{2,1,0:T(8,128)} %get-tuple-element.32), channel_id=1, source_target_pairs={{0,1},{1,0},{2,3},{3,2},{4,5},{5,4},{6,7},{7,6},{8,9},{9,8},{10,11... | collective-permute-start | bytes 1843208 | tf_op jit(solution)/shard_map/ppermute | solution.py:23
  23.4 12.0 %collective-permute-start.3 = (f32[50,24,128]{2,1,0:T(8,128)}, f32[50,24,128]{2,1,0:T(8,128)}, u32[]{:S(2)}, u32[]{:S(2)}) collective-permute-start(f32[50,24,128]{2,1,0:T(8,128)} %get-tuple-element.31), channel_id=1, source_target_pairs={{1,2},{2,1},{3,4},{4,3},{5,6},{6,5},{7,8},{8,7},{9,10},{10,9},{11,... | collective-permute-start | bytes 1843208 | tf_op jit(solution)/shard_map/ppermute | solution.py:23
  45.6 9.2 %collective-permute-start.4 = (f32[3,4,24,128]{3,2,1,0:T(8,128)S(1)}, f32[3,4,24,128]{3,2,1,0:T(8,128)S(1)}, u32[]{:S(2)}, u32[]{:S(2)}) collective-permute-start(f32[3,4,24,128]{3,2,1,0:T(8,128)S(1)} %get-tuple-element.61), channel_id=1, source_target_pairs={{16,32},{32,16},{48,64},{64,48},{80,96},{96,80},{112,128},{128,112... | collective-permute-start | bytes 442376 | tf_op jit(solution)/shard_map/ppermute | solution.py:23
  49.8 5.9 %collective-permute-start.5 = (f32[3,4,24,128]{3,2,1,0:T(8,128)S(1)}, f32[3,4,24,128]{3,2,1,0:T(8,128)S(1)}, u32[]{:S(2)}, u32[]{:S(2)}) collective-permute-start(f32[3,4,24,128]{3,2,1,0:T(8,128)S(1)} %get-tuple-element.62), channel_id=1, source_target_pairs={{0,16},{16,0},{32,48},{48,32},{64,80},{80,64},{96,112},{112,96},{1... | collective-permute-start | bytes 442376 | tf_op jit(solution)/shard_map/ppermute | solution.py:23
  56.8 8.3 %collective-permute-start.6 = (f32[30,24,128]{2,1,0:T(8,128)}, f32[30,24,128]{2,1,0:T(8,128)S(1)}, u32[]{:S(2)}, u32[]{:S(2)}) collective-permute-start(f32[30,24,128]{2,1,0:T(8,128)} %bitcast.26), channel_id=1, source_target_pairs={{0,1},{1,0},{2,3},{3,2},{4,5},{5,4},{6,7},{7,6},{8,9},{9,8},{10,11... | collective-permute-start | bytes 1105928 | tf_op jit(solution)/shard_map/ppermute | solution.py:23
  58.7 11.6 %collective-permute-start.7 = (f32[30,24,128]{2,1,0:T(8,128)}, f32[30,24,128]{2,1,0:T(8,128)S(1)}, u32[]{:S(2)}, u32[]{:S(2)}) collective-permute-start(f32[30,24,128]{2,1,0:T(8,128)} %bitcast.27), channel_id=1, source_target_pairs={{1,2},{2,1},{3,4},{4,3},{5,6},{6,5},{7,8},{8,7},{9,10},{10,9},{11,... | collective-permute-start | bytes 1105928 | tf_op jit(solution)/shard_map/ppermute | solution.py:23
  74.8 12.5 %collective-permute-start.8 = (f32[1,2,24,128]{3,2,1,0:T(8,128)S(1)}, f32[1,2,24,128]{3,2,1,0:T(8,128)S(1)}, u32[]{:S(2)}, u32[]{:S(2)}) collective-permute-start(f32[1,2,24,128]{3,2,1,0:T(8,128)S(1)} %get-tuple-element.66), channel_id=1, source_target_pairs={{32,64},{64,32},{48,80},{80,48},{96,128},{128,96},{112,144},{144,1... | collective-permute-start | bytes 73736 | tf_op jit(solution)/shard_map/ppermute | solution.py:23
  78.8 8.4 %collective-permute-start.9 = (f32[1,2,24,128]{3,2,1,0:T(8,128)S(1)}, f32[1,2,24,128]{3,2,1,0:T(8,128)S(1)}, u32[]{:S(2)}, u32[]{:S(2)}) collective-permute-start(f32[1,2,24,128]{3,2,1,0:T(8,128)S(1)} %get-tuple-element.65), channel_id=1, source_target_pairs={{0,32},{32,0},{16,48},{48,16},{64,96},{96,64},{80,112},{112,80},{1... | collective-permute-start | bytes 73736 | tf_op jit(solution)/shard_map/ppermute | solution.py:23
  80.8 8.2 %collective-permute-start.10 = (f32[2,2,24,128]{3,2,1,0:T(8,128)S(1)}, f32[2,2,24,128]{3,2,1,0:T(8,128)S(1)}, u32[]{:S(2)}, u32[]{:S(2)}) collective-permute-start(f32[2,2,24,128]{3,2,1,0:T(8,128)S(1)} %get-tuple-element.15), channel_id=1, source_target_pairs={{16,32},{32,16},{48,64},{64,48},{80,96},{96,80},{112,128},{128,112... | collective-permute-start | bytes 147464 | tf_op jit(solution)/shard_map/ppermute | solution.py:23
  85.1 4.8 %collective-permute-start.11 = (f32[2,2,24,128]{3,2,1,0:T(8,128)S(1)}, f32[2,2,24,128]{3,2,1,0:T(8,128)S(1)}, u32[]{:S(2)}, u32[]{:S(2)}) collective-permute-start(f32[2,2,24,128]{3,2,1,0:T(8,128)S(1)} %get-tuple-element.15), channel_id=1, source_target_pairs={{0,16},{16,0},{32,48},{48,32},{64,80},{80,64},{96,112},{112,96},{1... | collective-permute-start | bytes 147464 | tf_op jit(solution)/shard_map/ppermute | solution.py:23
  90.0 13.4 %collective-permute-start.12 = (f32[16,24,128]{2,1,0:T(8,128)S(1)}, f32[16,24,128]{2,1,0:T(8,128)S(1)}, u32[]{:S(2)}, u32[]{:S(2)}) collective-permute-start(f32[16,24,128]{2,1,0:T(8,128)S(1)} %bitcast.80), channel_id=1, source_target_pairs={{0,1},{1,0},{2,3},{3,2},{4,5},{5,4},{6,7},{7,6},{8,9},{9,8},{10,11... | collective-permute-start | bytes 589832 | tf_op jit(solution)/shard_map/ppermute | solution.py:23
  91.9 11.4 %collective-permute-start.13 = (f32[16,24,128]{2,1,0:T(8,128)S(1)}, f32[16,24,128]{2,1,0:T(8,128)S(1)}, u32[]{:S(2)}, u32[]{:S(2)}) collective-permute-start(f32[16,24,128]{2,1,0:T(8,128)S(1)} %bitcast.81), channel_id=1, source_target_pairs={{1,2},{2,1},{3,4},{4,3},{5,6},{6,5},{7,8},{8,7},{9,10},{10,9},{11,... | collective-permute-start | bytes 589832 | tf_op jit(solution)/shard_map/ppermute | solution.py:23
  97.3 6.0 %collective-permute-start.14 = (f32[8,24,128]{2,1,0:T(8,128)S(1)}, f32[8,24,128]{2,1,0:T(8,128)S(1)}, u32[]{:S(2)}, u32[]{:S(2)}) collective-permute-start(f32[8,24,128]{2,1,0:T(8,128)S(1)} %get-tuple-element.60), channel_id=1, source_target_pairs={{0,2},{2,0},{1,3},{3,1},{4,6},{6,4},{5,7},{7,5},{8,10},{10,8},{9,1... | collective-permute-start | bytes 294920 | tf_op jit(solution)/shard_map/ppermute | solution.py:23
  101.3 2.0 collective-permute-start.15
  106.0 31.6 %collective-permute-start.20 = (f32[28,24,128]{2,1,0:T(8,128)}, f32[28,24,128]{2,1,0:T(8,128)S(1)}, u32[]{:S(2)}, u32[]{:S(2)}) collective-permute-start(f32[28,24,128]{2,1,0:T(8,128)} %get-tuple-element.41), channel_id=1, source_target_pairs={{16,32},{32,16},{48,64},{64,48},{80,96},{96,80},{112,128},{128,112... | collective-permute-start | bytes 1032200 | tf_op jit(solution)/shard_map/ppermute | solution.py:23
  110.3 27.3 %collective-permute-start.21 = (f32[28,24,128]{2,1,0:T(8,128)S(1)}, f32[28,24,128]{2,1,0:T(8,128)}, u32[]{:S(2)}, u32[]{:S(2)}) collective-permute-start(f32[28,24,128]{2,1,0:T(8,128)S(1)} %get-tuple-element.42), channel_id=1, source_target_pairs={{0,16},{16,0},{32,48},{48,32},{64,80},{80,64},{96,112},{112,96},{1... | collective-permute-start | bytes 1032200 | tf_op jit(solution)/shard_map/ppermute | solution.py:23
  141.0 46.9 %collective-permute-start.22 = (f32[52,24,128]{2,1,0:T(8,128)}, f32[52,24,128]{2,1,0:T(8,128)S(1)}, u32[]{:S(2)}, u32[]{:S(2)}) collective-permute-start(f32[52,24,128]{2,1,0:T(8,128)} %get-tuple-element.30), channel_id=1, source_target_pairs={{0,1},{1,0},{2,3},{3,2},{4,5},{5,4},{6,7},{7,6},{8,9},{9,8},{10,11... | collective-permute-start | bytes 1916936 | tf_op jit(solution)/shard_map/ppermute | solution.py:23
  143.0 44.8 %collective-permute-start.23 = (f32[52,24,128]{2,1,0:T(8,128)}, f32[52,24,128]{2,1,0:T(8,128)S(1)}, u32[]{:S(2)}, u32[]{:S(2)}) collective-permute-start(f32[52,24,128]{2,1,0:T(8,128)} %get-tuple-element.29), channel_id=1, source_target_pairs={{1,2},{2,1},{3,4},{4,3},{5,6},{6,5},{7,8},{8,7},{9,10},{10,9},{11,... | collective-permute-start | bytes 1916936 | tf_op jit(solution)/shard_map/ppermute | solution.py:23
  168.3 10.0 %collective-permute-start.16 = (f32[5,24,128]{2,1,0:T(8,128)}, f32[5,24,128]{2,1,0:T(8,128)S(1)}, u32[]{:S(2)}, u32[]{:S(2)}) collective-permute-start(f32[5,24,128]{2,1,0:T(8,128)} %copy.13.coarse_rows), channel_id=1, source_target_pairs={{0,16},{16,0},{32,48},{48,32},{64,80},{80,64},{96,112},{112,96},{1... | collective-permute-start | bytes 184328 | tf_op jit(solution)/shard_map/ppermute | solution.py:23
  172.0 11.5 %collective-permute-start.17 = (f32[5,24,128]{2,1,0:T(8,128)}, f32[5,24,128]{2,1,0:T(8,128)}, u32[]{:S(2)}, u32[]{:S(2)}) collective-permute-start(f32[5,24,128]{2,1,0:T(8,128)} %copy.13.coarse_rows), channel_id=1, source_target_pairs={{16,32},{32,16},{48,64},{64,48},{80,96},{96,80},{112,128},{128,112... | collective-permute-start | bytes 184328 | tf_op jit(solution)/shard_map/ppermute | solution.py:23
  176.4 7.1 %collective-permute-start.18 = (f32[5,24,128]{2,1,0:T(8,128)}, f32[5,24,128]{2,1,0:T(8,128)}, u32[]{:S(2)}, u32[]{:S(2)}) collective-permute-start(f32[5,24,128]{2,1,0:T(8,128)} %copy.13.coarse_rows), channel_id=1, source_target_pairs={{0,32},{32,0},{16,48},{48,16},{64,96},{96,64},{80,112},{112,80},{1... | collective-permute-start | bytes 184328 | tf_op jit(solution)/shard_map/ppermute | solution.py:23
  178.9 8.9 %collective-permute-start.19 = (f32[5,24,128]{2,1,0:T(8,128)}, f32[5,24,128]{2,1,0:T(8,128)}, u32[]{:S(2)}, u32[]{:S(2)}) collective-permute-start(f32[5,24,128]{2,1,0:T(8,128)} %copy.13.coarse_rows), channel_id=1, source_target_pairs={{32,64},{64,32},{48,80},{80,48},{96,128},{128,96},{112,144},{144,1... | collective-permute-start | bytes 184328 | tf_op jit(solution)/shard_map/ppermute | solution.py:23
  193.4 8.2 %collective-permute-start.24 = (f32[2,2,24,128]{3,2,1,0:T(8,128)S(1)}, f32[2,2,24,128]{3,2,1,0:T(8,128)S(1)}, u32[]{:S(2)}, u32[]{:S(2)}) collective-permute-start(f32[2,2,24,128]{3,2,1,0:T(8,128)S(1)} %up_2.1), channel_id=1, source_target_pairs={{16,32},{32,16},{48,64},{64,48},{80,96},{96,80},{112,128},{128,112... | collective-permute-start | bytes 147464 | tf_op jit(solution)/shard_map/ppermute | solution.py:23
  197.6 5.1 %collective-permute-start.25 = (f32[2,2,24,128]{3,2,1,0:T(8,128)S(1)}, f32[2,2,24,128]{3,2,1,0:T(8,128)S(1)}, u32[]{:S(2)}, u32[]{:S(2)}) collective-permute-start(f32[2,2,24,128]{3,2,1,0:T(8,128)S(1)} %up_2.1), channel_id=1, source_target_pairs={{0,16},{16,0},{32,48},{48,32},{64,80},{80,64},{96,112},{112,96},{1... | collective-permute-start | bytes 147464 | tf_op jit(solution)/shard_map/ppermute | solution.py:23
  203.4 6.9 %collective-permute-start.26 = (f32[12,24,128]{2,1,0:T(8,128)}, f32[12,24,128]{2,1,0:T(8,128)}, u32[]{:S(2)}, u32[]{:S(2)}) collective-permute-start(f32[12,24,128]{2,1,0:T(8,128)} %bitcast.57), channel_id=1, source_target_pairs={{0,1},{1,0},{2,3},{3,2},{4,5},{5,4},{6,7},{7,6},{8,9},{9,8},{10,11... | collective-permute-start | bytes 442376 | tf_op jit(solution)/shard_map/ppermute | solution.py:23
  208.3 6.8 %collective-permute-start.27 = (f32[12,24,128]{2,1,0:T(8,128)}, f32[12,24,128]{2,1,0:T(8,128)}, u32[]{:S(2)}, u32[]{:S(2)}) collective-permute-start(f32[12,24,128]{2,1,0:T(8,128)} %bitcast.57), channel_id=1, source_target_pairs={{1,2},{2,1},{3,4},{4,3},{5,6},{6,5},{7,8},{8,7},{9,10},{10,9},{11,... | collective-permute-start | bytes 442376 | tf_op jit(solution)/shard_map/ppermute | solution.py:23
  220.4 8.8 %collective-permute-start.28 = (f32[2,4,24,128]{3,2,1,0:T(8,128)S(1)}, f32[2,4,24,128]{3,2,1,0:T(8,128)S(1)}, u32[]{:S(2)}, u32[]{:S(2)}) collective-permute-start(f32[2,4,24,128]{3,2,1,0:T(8,128)S(1)} %get-tuple-element.55), channel_id=1, source_target_pairs={{16,32},{32,16},{48,64},{64,48},{80,96},{96,80},{112,128},{128,112... | collective-permute-start | bytes 294920 | tf_op jit(solution)/shard_map/ppermute | solution.py:23
  224.9 5.4 %collective-permute-start.29 = (f32[2,4,24,128]{3,2,1,0:T(8,128)S(1)}, f32[2,4,24,128]{3,2,1,0:T(8,128)S(1)}, u32[]{:S(2)}, u32[]{:S(2)}) collective-permute-start(f32[2,4,24,128]{3,2,1,0:T(8,128)S(1)} %get-tuple-element.56), channel_id=1, source_target_pairs={{0,16},{16,0},{32,48},{48,32},{64,80},{80,64},{96,112},{112,96},{1... | collective-permute-start | bytes 294920 | tf_op jit(solution)/shard_map/ppermute | solution.py:23
  230.4 5.3 %collective-permute-start.30 = (f32[16,24,128]{2,1,0:T(8,128)S(1)}, f32[16,24,128]{2,1,0:T(8,128)S(1)}, u32[]{:S(2)}, u32[]{:S(2)}) collective-permute-start(f32[16,24,128]{2,1,0:T(8,128)S(1)} %bitcast.115), channel_id=1, source_target_pairs={{0,1},{1,0},{2,3},{3,2},{4,5},{5,4},{6,7},{7,6},{8,9},{9,8},{10,11... | collective-permute-start | bytes 589832 | tf_op jit(solution)/shard_map/ppermute | solution.py:23
  232.3 7.0 %collective-permute-start.31 = (f32[16,24,128]{2,1,0:T(8,128)S(1)}, f32[16,24,128]{2,1,0:T(8,128)S(1)}, u32[]{:S(2)}, u32[]{:S(2)}) collective-permute-start(f32[16,24,128]{2,1,0:T(8,128)S(1)} %bitcast.114), channel_id=1, source_target_pairs={{1,2},{2,1},{3,4},{4,3},{5,6},{6,5},{7,8},{8,7},{9,10},{10,9},{11,... | collective-permute-start | bytes 589832 | tf_op jit(solution)/shard_map/ppermute | solution.py:23
  (24 other events, 319.4 us)

commit v2 on v1

v2 whole, which is shorter than its diff:
```python
import functools
import math

import jax
import jax.numpy as jnp
from jax import lax
from jax.experimental import pallas as pl
from jax.experimental.pallas import tpu as pltpu
from jax.sharding import PartitionSpec as P

THETA = 8.0
DELTA = 6.5
ROOTS = tuple(THETA + DELTA * math.cos(math.pi * (2 * k + 1) / 6) for k in range(3))
HALO = 3


def swap(x, axis, dist, odd):
    count = lax.axis_size(axis)
    pairs = []
    for i in range(count - dist):
        if (i // dist) % 2 == odd:
            pairs += [(i, i + dist), (i + dist, i)]
    return lax.ppermute(x, axis, pairs)


def parity(axis, dist):
    return lax.rem(lax.div(lax.axis_index(axis), dist), 2)


def swap_ends(at, low, high, axis, dist):
    even = at[axis]
    first = swap(jnp.where(even, high, low), axis, dist, 0)
    second = swap(jnp.where(even, low, high), axis, dist, 1)
    return first, second


def in_order(at, first, second, axis):
    even = at[axis]
    return jnp.where(even, second, first), jnp.where(even, first, second)


def cells(x):
    return x.reshape((-1,) + x.shape[-2:])


def z_neighbours(v):
    lane = lax.broadcasted_iota(jnp.int32, v.shape, 1)
    below = jnp.where(lane == 0, 0.0, pltpu.roll(v, 1, 1))
    above = jnp.where(lane == v.shape[1] - 1, 0.0, pltpu.roll(v, v.shape[1] - 1, 1))
    return below + above


def inside(at, size):
    return jnp.where((at >= 0) & (at < size), 1.0, 0.0).astype(jnp.float32)


def beside(src, x, y):
    centre = src[x, y]
    total = (src[x - 1, y] + src[x + 1, y]) + (src[x, y - 1] + src[x, y + 1])
    return total + z_neighbours(centre), centre


def factor_cell(src, x, y, shift_row, root, mask):
    total, centre = beside(src, x, y)
    scale = mask * (1.0 / root)
    return (scale * ((root - 6.0) - shift_row)) * centre + scale * total


def factor(src, dst, shift, shift_at, size, root, masks):
    def row(x, carry):
        row_mask = masks(x, None)
        for y in range(size[1]):
            shift_row = shift[x + shift_at[0], pl.ds(y + shift_at[1], 1), :]
            mask = row_mask * masks(None, y)
            dst[x, y] = factor_cell(src, x + 1, y + 1, shift_row, root, mask)
        return carry

    lax.fori_loop(0, size[0], row, 0)


def masks_of(first, reach, grid):
    def masks(x, y):
        if x is not None:
            return inside(first[0] + x - reach, grid[0])
        return inside(first[1] + y - reach, grid[1])

    return masks


def put_frame(dst, own, pieces, where, n, width):
    x_even, x_odd, y_even, y_odd, c_even, c_odd = pieces
    high = n + width
    rows = [jnp.where(where[3] == odd, high, 0) for odd in (0, 1)]
    columns = [jnp.where(where[2] == odd, high, 0) for odd in (0, 1)]

    def middle(x, carry):
        for y in range(n):
            dst[x + width, y + width] = own[x, y]
        for ref, at in ((y_even, columns[0]), (y_odd, columns[1])):
            for k in range(width):
                dst[x + width, at + k] = ref[x * width + k]
        return carry

    lax.fori_loop(0, n, middle, 0)

    def outer(x, carry):
        for ref, at in ((x_even, rows[0]), (x_odd, rows[1])):
            for y in range(n):
                dst[at + x, width + y] = ref[x * n + y]
        for ref, at in ((c_even, columns[0]), (c_odd, columns[1])):
            for k in range(width):
                dst[x, at + k] = ref[x * width + k]
                dst[high + x, at + k] = ref[(width + x) * width + k]
        return carry

    lax.fori_loop(0, width, outer, 0)


def put_columns(dst, centre, pieces, where, rows, width, reach):
    def row(x, carry):
        for y in range(width):
            dst[x, reach + y] = centre[x, y]
        for ref, base, odd in pieces:
            at = jnp.where(where[2] == odd, reach + width, 0)
            for k in range(reach):
                dst[x, at + k] = ref[base + x * reach + k]
        return carry

    lax.fori_loop(0, rows, row, 0)


def put_shift(wide, one, one_wide, two, own, pieces, where, n):
    x_even, x_odd, y_even, y_odd, c_even, c_odd = pieces
    chans = x_even.shape[1]
    strip, corner = HALO * n, 2 * HALO * HALO

    def line(ref, first, x):
        at = x * n
        return ref[first + at // chans, at % chans : at % chans + n, :]

    for odd, x_ref, y_ref, c_ref in ((0, x_even, y_even, c_even), (1, x_odd, y_odd, c_odd)):
        row = jnp.where(where[3] == odd, 2 * n, 0)
        column = pl.ds(pl.multiple_of(jnp.where(where[2] == odd, 2 * n, 0), n), n)
        for x in range(n):
            wide[row + x, n : 2 * n, :] = line(x_ref, strip, x)
            wide[n + x, column, :] = line(y_ref, strip, x)
            wide[x, column, :] = line(c_ref, corner, x)
            wide[2 * n + x, column, :] = line(c_ref, corner, n + x)
    for x in range(n):
        wide[n + x, n : 2 * n, :] = own[x]

    def halve(src, x, count):
        total = 0.0
        for k in range(4):
            total = total + src[2 * x + k // 2, pl.ds(k % 2, count, 2), :]
        return 0.25 * total

    half = n // 2
    for x in range(3 * half):
        row = halve(wide, x, 3 * half)
        one_wide[x, 0 : 3 * half, :] = row
        if half - 2 <= x < 2 * half + 2:
            one[x - half + 2] = row[half - 2 : 2 * half + 2]
    for x in range(3 * half // 2):
        two[x] = halve(one_wide, x, 3 * half // 2)


def down_body(size, grid, first, pad, shift, shift_at, iterate, leftover, coarser, one, two):
    nx, ny = size
    sx, sy = shift_at
    factor(pad, one, shift, (sx, sy), (nx + 4, ny + 4), ROOTS[0], masks_of(first, 2, grid))
    factor(one, two, shift, (sx + 1, sy + 1), (nx + 2, ny + 2), ROOTS[1], masks_of(first, 1, grid))

    def row(x, carry):
        for y in range(ny):
            shift_row = shift[x + 2 + sx, pl.ds(y + 2 + sy, 1), :]
            leftover[x, y] = factor_cell(two, x + 1, y + 1, shift_row, ROOTS[2], 1.0)
            iterate[x, y] = (
                pad[x + 3, y + 3] * (1.0 / ROOTS[0])
                + one[x + 2, y + 2] * (1.0 / ROOTS[1])
                + two[x + 1, y + 1] * (1.0 / ROOTS[2])
            )
        return carry

    lax.fori_loop(0, nx, row, 0)

    def coarse_row(x, carry):
        for y in range(ny // 2):
            near = leftover[2 * x, 2 * y] + leftover[2 * x, 2 * y + 1]
            far = leftover[2 * x + 1, 2 * y] + leftover[2 * x + 1, 2 * y + 1]
            coarser[x, y] = 0.25 * (near + far)
        return carry

    lax.fori_loop(0, nx // 2, coarse_row, 0)


def down_fine_kernel(n, grid, where, own, *refs):
    pieces, own_shift = refs[:6], refs[6]
    iterate, leftover, coarser, shift, shift_one, shift_two, one_wide, pad, one, two = refs[7:]
    put_frame(pad, own, pieces, where, n, HALO)
    put_shift(shift, shift_one, one_wide, shift_two, own_shift, pieces, where, n)
    first = (where[0] * n, where[1] * n)
    down_body((n, n), grid, first, pad, shift, (n - 2, n - 2), iterate, leftover, coarser, one, two)


def down_kernel(n, grid, where, own, *refs):
    pieces, shift = refs[:6], refs[6]
    iterate, leftover, coarser, pad, one, two = refs[7:]
    put_frame(pad, own, pieces, where, n, HALO)
    first = (where[0] * n, where[1] * n)
    down_body((n, n), grid, first, pad, shift, (0, 0), iterate, leftover, coarser, one, two)


def down_chip_kernel(size, grid, where, pad, shift, iterate, leftover, coarser, one, two):
    first = (where[0] * size[0], (where[1] - where[2]) * size[0])
    down_body(size, grid, first, pad, shift, (0, 0), iterate, leftover, coarser, one, two)


def solve_kernel(where, shares, inverse, solved, ordered):
    count, rows, depth = shares.shape
    chans = solved.shape[0]
    for m in range(count):
        block = jnp.zeros((chans, depth), jnp.float32)
        for j in range(count):
            block = jnp.where(shares[j, chans : chans + 1, :] == float(m), shares[j, 0:chans, :], block)
        ordered[:, m * depth : (m + 1) * depth] = block
    solved[...] = lax.dot_general(
        ordered[...],
        inverse[...],
        (((1,), (1,)), ((), ())),
        precision=lax.Precision.HIGHEST,
        preferred_element_type=jnp.float32,
    )


def pick_kernel(where, shares, back, picked):
    count, chans, depth = back.shape
    for k in range(picked.shape[0]):
        j = where[1] - where[2] + k - 2
        slot = shares[jnp.clip(j, 0, count - 1), pl.ds(chans, 1), :]
        slot = jnp.where((j >= 0) & (j < count), slot, -1.0)
        block = jnp.zeros((chans, depth), jnp.float32)
        for m in range(count):
            block = jnp.where(slot == float(m), back[m], block)
        picked[k] = block


def up_kernel(n, grid, shift_at, offset, pieces_count, where, coarse_own, *refs):
    half = n // 2
    sx, sy = shift_at
    pieces = refs[:pieces_count]
    shift, iterate, leftover_rows, left_even, left_odd, result, coarse, start, one = refs[pieces_count:]
    if pieces_count == 2:
        mine, others = pieces
        core, line, far = where[2], where[4], where[5]
        for k in range(5):
            coarse[2, k] = coarse_own[core + k]
            coarse[3 - 2 * line, k] = mine[core + k]
            coarse[1 + 2 * line, k] = others[core + k]
            coarse[4 * far, k] = mine[6 + core + k]
            coarse[4 - 4 * far, k] = others[6 + core + k]
    else:
        put_frame(coarse, coarse_own, pieces, where, half, 2)
    put_columns(start, leftover_rows, [(left_even, offset, 0), (left_odd, offset, 1)], where, n + 4, n, 2)
    first = (where[0] * n, where[1] * n)
    outer = masks_of(first, 2, grid)

    def first_row(x, carry):
        row_mask = outer(x, None)
        here, before, after = (x + 2) // 2, (x + 1) // 2, (x + 3) // 2
        for y in range(n + 4):
            at, left, right = (y + 2) // 2, (y + 1) // 2, (y + 3) // 2
            centre = coarse[here, at]
            total = (coarse[before, at] + coarse[after, at]) + (coarse[here, left] + coarse[here, right])
            total = total + z_neighbours(centre)
            shift_row = shift[x + sx, pl.ds(y + sy, 1), :]
            mask = row_mask * outer(None, y)
            start[x, y] = mask * ((start[x, y] - (6.0 + shift_row) * centre) + total)
        return carry

    lax.fori_loop(0, n + 4, first_row, 0)
    factor(start, one, shift, (sx + 1, sy + 1), (n + 2, n + 2), ROOTS[0], masks_of(first, 1, grid))

    def row(x, carry):
        for y in range(n):
            shift_row = shift[x + 2 + sx, pl.ds(y + 2 + sy, 1), :]
            two = factor_cell(one, x + 1, y + 1, shift_row, ROOTS[1], 1.0)
            step = (
                start[x + 2, y + 2] * (1.0 / ROOTS[0]) + one[x + 1, y + 1] * (1.0 / ROOTS[1]) + two * (1.0 / ROOTS[2])
            )
            result[x, y] = (iterate[x, y] + coarse[x // 2 + 2, y // 2 + 2]) + step
        return carry

    lax.fori_loop(0, n, row, 0)


VMEM = pl.BlockSpec(memory_space=pltpu.VMEM)
SMEM = pl.BlockSpec(memory_space=pltpu.SMEM)


def call(kernel, where, operands, outs, scratch, name):
    return pl.pallas_call(
        kernel,
        out_shape=[jax.ShapeDtypeStruct(out, jnp.float32) for out in outs],
        in_specs=[SMEM] + [VMEM] * len(operands),
        out_specs=[VMEM] * len(outs),
        scratch_shapes=[pltpu.VMEM(own, jnp.float32) for own in scratch],
        compiler_params=pltpu.CompilerParams(vmem_limit_bytes=12 * 1024 * 1024),
        name=name,
    )(where, *operands)


def place():
    core = parity("gy", 1)
    line, far = parity("gx", 1), parity("gx", 2)
    numbers = [lax.axis_index("gx"), lax.axis_index("gy"), core, line, line ^ core, far ^ core]
    where = jnp.stack(numbers + [jnp.zeros_like(core)] * 2).astype(jnp.int32)
    sides = {
        "gx": line == 0,
        "gy": core == 0,
        "line": line == core,
        "far": far != core,
        "chip": parity("gy", 2) == core,
    }
    return where, sides


def grid_of(n):
    return (lax.axis_size("gx") * n, lax.axis_size("gy") * n)


def up(n, where, coarse_own, pieces, shift, shift_at, iterate, leftover_rows, left, offset):
    tail = iterate.shape[-2:]
    return call(
        functools.partial(up_kernel, n, grid_of(n), shift_at, offset, len(pieces)),
        where,
        [coarse_own, *pieces, shift, iterate, leftover_rows, *left],
        [(n, n) + tail],
        [(n // 2 + 4, n // 2 + 4) + tail, (n + 4, n + 4) + tail, (n + 2, n + 2) + tail],
        "up_%d" % n,
    )[0]


def frame(at, v, width, blocks=None):
    n = v.shape[0]
    tail = v.shape[-2:]

    def message(strip, rows):
        flat = cells(strip)
        if rows is None:
            return flat
        rows = rows.reshape(-1, tail[1])
        rows = jnp.pad(rows, ((0, -rows.shape[0] % tail[0]), (0, 0)))
        return jnp.concatenate([flat, rows.reshape((-1,) + tail)], axis=0)

    def rows_of(piece):
        flat = piece[width * n :].reshape(-1, tail[1])[: blocks.shape[0] * blocks.shape[1]]
        return flat.reshape(blocks.shape)

    x_pieces = swap_ends(at, message(v[:width], blocks), message(v[n - width :], blocks), "gx", 1)
    y_pieces = swap_ends(at, message(v[:, :width], blocks), message(v[:, n - width :], blocks), "gy", 1)
    x_pieces, y_pieces = lax.optimization_barrier((x_pieces, y_pieces))
    sides = in_order(at, *x_pieces, "gx")
    strips = [side[: width * n].reshape((width, n) + tail) for side in sides]
    beyond = None if blocks is None else jnp.concatenate([rows_of(side) for side in sides], axis=0)
    low = jnp.concatenate([strip[:, :width] for strip in strips], axis=0)
    high = jnp.concatenate([strip[:, n - width :] for strip in strips], axis=0)
    corners = swap_ends(at, message(low, beyond), message(high, beyond), "gy", 1)
    return [*x_pieces, *y_pieces, *corners]


def by_core(x, swaps):
    lines, blocks = lax.axis_size("gx"), lax.axis_size("gy")
    pairs = []
    for j in range(blocks):
        dist, odd = swaps[j % 2]
        for i in range(lines - dist):
            if (i // dist) % 2 == odd:
                pairs += [(i * blocks + j, (i + dist) * blocks + j), ((i + dist) * blocks + j, i * blocks + j)]
    return lax.ppermute(x, ("gx", "gy"), pairs)


def to_core(x):
    return swap(x, "gy", 1, 0)


def lines_around(at, near, low, high):
    first = by_core(near, [(1, 0), (1, 1)])
    second = by_core(jnp.where(at["far"], high, low), [(2, 1), (2, 0)])
    mine = jnp.concatenate([cells(first), cells(second)], axis=0)
    return mine, to_core(mine)


def body(rhs, shift, slots, coarse_inverse):
    where, at = place()
    where, at, rhs = lax.optimization_barrier((where, at, rhs))
    right = jnp.transpose(rhs, (1, 2, 0, 3))
    n = right.shape[0]
    tail = chans, depth = right.shape[2:]
    half, size = n // 2, n // 4

    x0, q0, b1, shift_wide, shift_one, shift_two = call(
        functools.partial(down_fine_kernel, n, grid_of(n)),
        where,
        [right, *frame(at, right, HALO, shift), shift],
        [
            (n, n) + tail,
            (n, n) + tail,
            (half, half) + tail,
            (3 * n, 3 * n, depth),
            (half + 4, half + 4, depth),
            (3 * size, 3 * size, depth),
        ],
        [(3 * half, 2 * n, depth), (n + 6, n + 6) + tail, (n + 4, n + 4) + tail, (n + 2, n + 2) + tail],
        "down_fine",
    )
    x1, q1, b2 = call(
        functools.partial(down_kernel, half, grid_of(half)),
        where,
        [b1, *frame(at, b1, HALO), shift_one],
        [(half, half) + tail, (half, half) + tail, (size, size) + tail],
        [(half + 6, half + 6) + tail, (half + 4, half + 4) + tail, (half + 2, half + 2) + tail],
        "down_middle",
    )

    first_core = at["gy"]
    edge = jnp.where(first_core, shift_two[:, : 2 * size], shift_two[:, size:])
    edge_rows = edge.shape[0] * edge.shape[1]
    spare = -edge_rows % chans
    message = jnp.concatenate(
        [cells(b2), jnp.pad(edge.reshape(-1, depth), ((0, spare), (0, 0))).reshape(-1, chans, depth)], axis=0
    )
    other = to_core(message)
    edge = other[size * size :].reshape(-1, depth)[:edge_rows].reshape(edge.shape)
    other = other[: size * size].reshape(b2.shape)
    chip = jnp.concatenate([jnp.where(first_core, b2, other), jnp.where(first_core, other, b2)], axis=1)
    mine, others = lines_around(at, chip, chip[:1], chip[1:])
    near, wide = 2 * size * size, (1, 2 * size, chans, depth)
    mine_first, other_first = mine[:near].reshape(chip.shape), others[:near].reshape(chip.shape)
    mine_far, other_far = mine[near:].reshape(wide), others[near:].reshape(wide)
    rows = jnp.concatenate(
        [
            jnp.where(at["far"], other_far, mine_far),
            jnp.where(at["line"], other_first, mine_first),
            chip,
            jnp.where(at["line"], mine_first, other_first),
            jnp.where(at["far"], mine_far, other_far),
        ],
        axis=0,
    )
    blocks = lax.axis_size("gy")
    pairs = []
    for j in range(blocks - 2):
        if (j // 2) % 2 == j % 2:
            pairs += [(j, j + 2), (j + 2, j)]
    mine = lax.ppermute(jnp.where(at["chip"], rows[1:-1, 1:], rows[1:-1, :-1]), "gy", pairs)
    others = to_core(mine)
    ends = [jnp.where(at["chip"], others, mine), jnp.where(at["chip"], mine, others)]
    ends = [jnp.pad(end, ((1, 1), (0, 0), (0, 0), (0, 0))) for end in ends]
    pad = jnp.concatenate([ends[0], rows, ends[1]], axis=1)
    chip_shift = jnp.where(
        first_core,
        jnp.concatenate([shift_two[:, : 2 * size], edge], axis=1),
        jnp.concatenate([edge, shift_two[:, size:]], axis=1),
    )
    x2, q2, b3 = call(
        functools.partial(down_chip_kernel, (size, 2 * size), grid_of(size)),
        where,
        [pad, chip_shift],
        [(size, 2 * size) + tail, (size, 2 * size) + tail, (1, 2) + tail],
        [(size + 4, 2 * size + 4) + tail, (size + 2, 2 * size + 2) + tail],
        "down_chip",
    )
    x2, q2 = [jnp.where(first_core, v[:, :size], v[:, size:]) for v in (x2, q2)]
    b3 = jnp.where(first_core, b3[0, 0], b3[0, 1])

    lefts = [q0, q1, q2]
    low = jnp.concatenate([cells(q[:2]) for q in lefts], axis=0)
    high = jnp.concatenate([cells(q[-2:]) for q in lefts], axis=0)
    left_ends = swap_ends(at, low, high, "gx", 1)

    slot = jnp.broadcast_to(slots.astype(jnp.float32), (8, depth))
    shares = lax.all_gather(jnp.concatenate([b3, slot], axis=0)[None], "gy", axis=0, tiled=True)
    left_ends, shares = lax.optimization_barrier((left_ends, shares))
    before, after = in_order(at, *left_ends, "gx")
    left_rows, done = [], 0
    for q in lefts:
        strip = 2 * q.shape[1]
        shape = (2,) + q.shape[1:]
        ends = [side[done : done + strip].reshape(shape) for side in (before, after)]
        left_rows.append(jnp.concatenate([ends[0], q, ends[1]], axis=0))
        done += strip
    low = jnp.concatenate([cells(q[:, :2]) for q in left_rows], axis=0)
    high = jnp.concatenate([cells(q[:, -2:]) for q in left_rows], axis=0)
    left_sides = swap_ends(at, low, high, "gy", 1)
    offsets = [0, 2 * (n + 4), 2 * (n + 4) + 2 * (half + 4)]

    solved = call(
        solve_kernel, where, [shares, coarse_inverse[0, 0]], [tail], [(chans, blocks * depth)], "solve"
    )[0]
    back = lax.all_gather(solved[None], "gy", axis=0, tiled=True)
    fix = call(pick_kernel, where, [shares, back], [(6,) + tail], [], "pick")[0]
    lines = lines_around(at, fix, fix, fix)

    x2 = up(size, where, fix, lines, shift_two, (0, 0), x2, left_rows[2], left_sides, offsets[2])
    x1 = up(half, where, x2, frame(at, x2, 2), shift_one, (0, 0), x1, left_rows[1], left_sides, offsets[1])
    x0 = up(n, where, x1, frame(at, x1, 2), shift_wide, (n - 2, n - 2), x0, left_rows[0], left_sides, offsets[0])
    return jnp.transpose(x0, (2, 0, 1, 3))


def solution(mesh):
    return jax.shard_map(
        body,
        mesh=mesh,
        in_specs=(
            P(None, "gx", "gy", None),
            P("gx", "gy", None),
            P("gx", "gy"),
            P("gx", "gy", None, None),
        ),
        out_specs=P(None, "gx", "gy", None),
        check_vma=False,
    )
```

time: 247 us -> 232 us (0.939)
  the two profiles are of different devices: /device:TPU:31 before, /device:TPU:223 now
where the time goes in v2:
time: 232 us; the launch traced here: 231 us
  starting transfers between devices  123 us (53%)
  waiting for transfers between devices  44.9 us (19%)
  blocking collectives  34.4 us (15%)
  Pallas kernels  21.7 us (9%)
  local copies, waits for them, and re-layouts  3.81 us (2%)
    ppermute x32, starting transfers between devices, swap(): return lax.ppermute(x, axis, pairs)  106 us
    ppermute x32, waiting for transfers between devices, swap(): return lax.ppermute(x, axis, pairs)  31.8 us
    pallas_call x8, Pallas kernels, call(): pl.pallas_call(kernel, out_shape=[jax.ShapeDtypeStruct(out, jnp.float32)...  21.7 us
    all_gather x1, blocking collectives, body(): lax.all_gather(jnp.concatenate([b3, slot], axis=0)[None], 'gy', axis=0, t...  17.3 us
    all_gather x1, blocking collectives, body(): back = lax.all_gather(solved[None], 'gy', axis=0, tiled=True)  17.1 us
    ppermute x4, starting transfers between devices, by_core(): return lax.ppermute(x, ('gx', 'gy'), pairs)  12.4 us
    ppermute x4, waiting for transfers between devices, by_core(): return lax.ppermute(x, ('gx', 'gy'), pairs)  9.9 us
    ppermute x1, starting transfers between devices, body(): lax.ppermute(jnp.where(at['chip'], rows[1:-1, 1:], rows[1:-1, :-1]), 'gy'...  4.71 us
  transfers between devices with their start and end apart: 37, of which 17 were waited for; matrix products, arithmetic and copies ran while one was open for 0% of the time, Pallas kernels for 1%

profile of v2, /device:TPU:223, one launch (start us, length us, event | category | flops | bytes accessed | tf_op | source)
XLA Modules:
  0.0 230.7 jit_solution(15759829942583779889)
XLA Ops:
  5.0 5.0 %collective-permute-start.1 = (f32[27,24,128]{2,1,0:T(8,128)S(1)}, f32[27,24,128]{2,1,0:T(8,128)S(1)}, u32[]{:S(2)}, u32[]{:S(2)}) collective-permute-start(f32[27,24,128]{2,1,0:T(8,128)S(1)} %get-tuple-element.146), channel_id=1, source_target_pairs={{16,32},{32,16},{48,64},{64,48},{80,96},{96,80},{112,128},{128,112... | collective-permute-start | bytes 995336 | tf_op jit(solution)/shard_map/ppermute | solution.py:23
  10.0 3.1 %collective-permute-start.2 = (f32[27,24,128]{2,1,0:T(8,128)S(1)}, f32[27,24,128]{2,1,0:T(8,128)S(1)}, u32[]{:S(2)}, u32[]{:S(2)}) collective-permute-start(f32[27,24,128]{2,1,0:T(8,128)S(1)} %get-tuple-element.102), channel_id=1, source_target_pairs={{0,1},{1,0},{2,3},{3,2},{4,5},{5,4},{6,7},{7,6},{8,9},{9,8},{10,11... | collective-permute-start | bytes 995336 | tf_op jit(solution)/shard_map/ppermute | solution.py:23
  13.2 5.1 %collective-permute-start.3 = (f32[27,24,128]{2,1,0:T(8,128)S(1)}, f32[27,24,128]{2,1,0:T(8,128)S(1)}, u32[]{:S(2)}, u32[]{:S(2)}) collective-permute-start(f32[27,24,128]{2,1,0:T(8,128)S(1)} %get-tuple-element.101), channel_id=1, source_target_pairs={{1,2},{2,1},{3,4},{4,3},{5,6},{6,5},{7,8},{8,7},{9,10},{10,9},{11,... | collective-permute-start | bytes 995336 | tf_op jit(solution)/shard_map/ppermute | solution.py:23
  18.6 4.5 %collective-permute-done.3.refs_3_ = f32[27,24,128]{2,1,0:T(8,128)S(1)} collective-permute-done((f32[27,24,128]{2,1,0:T(8,128)S(1)}, f32[27,24,128]{2,1,0:T(8,128)S(1)}, u32[]{:S(2)}, u32[]{:S(2)}) %collective-permute-start.3) | collective-permute-done | bytes 331808 | tf_op jit(solution)/shard_map/ppermute | solution.py:23
  25.3 4.9 %collective-permute-start.5 = (f32[24,24,128]{2,1,0:T(8,128)S(1)}, f32[24,24,128]{2,1,0:T(8,128)S(1)}, u32[]{:S(2)}, u32[]{:S(2)}) collective-permute-start(f32[24,24,128]{2,1,0:T(8,128)S(1)} %get-tuple-element.105), channel_id=1, source_target_pairs={{1,2},{2,1},{3,4},{4,3},{5,6},{6,5},{7,8},{8,7},{9,10},{10,9},{11,... | collective-permute-start | bytes 884744 | tf_op jit(solution)/shard_map/ppermute | solution.py:23
  30.2 4.4 %collective-permute-done.5.refs_5_ = f32[24,24,128]{2,1,0:T(8,128)S(1)} collective-permute-done((f32[24,24,128]{2,1,0:T(8,128)S(1)}, f32[24,24,128]{2,1,0:T(8,128)S(1)}, u32[]{:S(2)}, u32[]{:S(2)}) %collective-permute-start.5) | collective-permute-done | bytes 294944 | tf_op jit(solution)/shard_map/ppermute | solution.py:23
  34.6 5.0 %down_fine.1 = (f32[8,8,24,128]{3,2,1,0:T(8,128)S(1)}, f32[8,8,24,128]{3,2,1,0:T(8,128)S(1)}, f32[4,4,24,128]{3,2,1,0:T(8,128)S(1)}, f32[24,24,128]{2,1,0:T(8,12...) custom-call(s32[8]{0:T(128)S(1)} %stack.27.where, f32[8,8,24,128]{3,2,1,0:T(8,128)S(1)} %bitcast.86, ...), custom_call_target="tpu_custom_call" | custom-call | tf_op jit(solution)/shard_map/down_fine/pallas_call | solution.py:302
  41.6 4.0 %collective-permute-start.7 = (f32[12,24,128]{2,1,0:T(8,128)S(1)}, f32[12,24,128]{2,1,0:T(8,128)S(1)}, u32[]{:S(2)}, u32[]{:S(2)}) collective-permute-start(f32[12,24,128]{2,1,0:T(8,128)S(1)} %bitcast.138), channel_id=1, source_target_pairs={{16,32},{32,16},{48,64},{64,48},{80,96},{96,80},{112,128},{128,112... | collective-permute-start | bytes 442376 | tf_op jit(solution)/shard_map/ppermute | solution.py:23
  47.6 5.4 %collective-permute-start.9 = (f32[12,24,128]{2,1,0:T(8,128)S(1)}, f32[12,24,128]{2,1,0:T(8,128)S(1)}, u32[]{:S(2)}, u32[]{:S(2)}) collective-permute-start(f32[12,24,128]{2,1,0:T(8,128)S(1)} %bitcast.136), channel_id=1, source_target_pairs={{1,2},{2,1},{3,4},{4,3},{5,6},{6,5},{7,8},{8,7},{9,10},{10,9},{11,... | collective-permute-start | bytes 442376 | tf_op jit(solution)/shard_map/ppermute | solution.py:23
  57.9 4.9 %collective-permute-start.11 = (f32[18,24,128]{2,1,0:T(8,128)S(1)}, f32[18,24,128]{2,1,0:T(8,128)S(1)}, u32[]{:S(2)}, u32[]{:S(2)}) collective-permute-start(f32[18,24,128]{2,1,0:T(8,128)S(1)} %bitcast.129), channel_id=1, source_target_pairs={{1,2},{2,1},{3,4},{4,3},{5,6},{6,5},{7,8},{8,7},{9,10},{10,9},{11,... | collective-permute-start | bytes 663560 | tf_op jit(solution)/shard_map/ppermute | solution.py:23
  62.7 3.6 %collective-permute-done.11.refs_5_ = f32[18,24,128]{2,1,0:T(8,128)S(1)} collective-permute-done((f32[18,24,128]{2,1,0:T(8,128)S(1)}, f32[18,24,128]{2,1,0:T(8,128)S(1)}, u32[]{:S(2)}, u32[]{:S(2)}) %collective-permute-start.11) | collective-permute-done | bytes 221216 | tf_op jit(solution)/shard_map/ppermute | solution.py:23
  72.2 4.3 %collective-permute-start.13 = (f32[2,4,24,128]{3,2,1,0:T(8,128)S(1)}, f32[2,4,24,128]{3,2,1,0:T(8,128)S(1)}, u32[]{:S(2)}, u32[]{:S(2)}) collective-permute-start(f32[2,4,24,128]{3,2,1,0:T(8,128)S(1)} %pad_maximum_fusion.19), channel_id=1, source_target_pairs={{0,16},{16,0},{32,48},{48,32},{64,80},{80,64},{96,112},{112,96},{1... | collective-permute-start | bytes 294920 | tf_op jit(solution)/shard_map/ppermute | solution.py:380
  79.1 4.4 %collective-permute-done.14 = f32[1,4,24,128]{3,2,1,0:T(8,128)S(1)} collective-permute-done((f32[1,4,24,128]{3,2,1,0:T(8,128)S(1)}, f32[1,4,24,128]{3,2,1,0:T(8,128)S(1)}, u32[]{:S(2)}, u32[]{:S(2)}) %collective-permute-start.14) | collective-permute-done | bytes 49184 | tf_op jit(solution)/shard_map/ppermute | solution.py:380
  87.1 4.7 %collective-permute-start.16 = (f32[6,3,24,128]{3,2,1,0:T(8,128)S(1)}, f32[6,3,24,128]{3,2,1,0:T(8,128)S(1)}, u32[]{:S(2)}, u32[]{:S(2)}) collective-permute-start(f32[6,3,24,128]{3,2,1,0:T(8,128)S(1)} %slice_select_fusion), channel_id=1, source_target_pairs={{0,2},{2,0},{3,5},{5,3},{4,6},{6,4},{7,9},{9,7},{8,10},{10,8},{11,... | collective-permute-start | bytes 663560 | tf_op jit(solution)/shard_map/ppermute | solution.py:456
  91.9 3.2 %collective-permute-done.16 = f32[6,3,24,128]{3,2,1,0:T(8,128)S(1)} collective-permute-done((f32[6,3,24,128]{3,2,1,0:T(8,128)S(1)}, f32[6,3,24,128]{3,2,1,0:T(8,128)S(1)}, u32[]{:S(2)}, u32[]{:S(2)}) %collective-permute-start.16) | collective-permute-done | bytes 221216 | tf_op jit(solution)/shard_map/ppermute | solution.py:456
  100.6 3.6 %collective-permute-start.18 = (f32[28,24,128]{2,1,0:T(8,128)S(1)}, f32[28,24,128]{2,1,0:T(8,128)S(1)}, u32[]{:S(2)}, u32[]{:S(2)}) collective-permute-start(f32[28,24,128]{2,1,0:T(8,128)S(1)} %get-tuple-element.100), channel_id=1, source_target_pairs={{0,16},{16,0},{32,48},{48,32},{64,80},{80,64},{96,112},{112,96},{1... | collective-permute-start | bytes 1032200 | tf_op jit(solution)/shard_map/ppermute | solution.py:23
  104.3 4.3 %collective-permute-start.19 = (f32[28,24,128]{2,1,0:T(8,128)S(1)}, f32[28,24,128]{2,1,0:T(8,128)S(1)}, u32[]{:S(2)}, u32[]{:S(2)}) collective-permute-start(f32[28,24,128]{2,1,0:T(8,128)S(1)} %get-tuple-element.99), channel_id=1, source_target_pairs={{16,32},{32,16},{48,64},{64,48},{80,96},{96,80},{112,128},{128,112... | collective-permute-start | bytes 1032200 | tf_op jit(solution)/shard_map/ppermute | solution.py:23
  108.6 17.3 %all-gather = f32[512,128]{1,0:T(8,128)S(1)} all-gather(f32[32,128]{1,0:T(8,128)S(1)} %concatenate.116), channel_id=2, replica_groups=mesh['gx'=32,'gy'=16] {'gy'}, dimensions={0}, use_global_device_ids=true | all-gather | bytes 278528 | tf_op jit(solution)/shard_map/all_gather | solution.py:483
  128.6 3.2 %collective-permute-start.24 = (f32[52,24,128]{2,1,0:T(8,128)S(1)}, f32[52,24,128]{2,1,0:T(8,128)S(1)}, u32[]{:S(2)}, u32[]{:S(2)}) collective-permute-start(f32[52,24,128]{2,1,0:T(8,128)S(1)} %get-tuple-element.87), channel_id=1, source_target_pairs={{1,2},{2,1},{3,4},{4,3},{5,6},{6,5},{7,8},{8,7},{9,10},{10,9},{11,... | collective-permute-start | bytes 1916936 | tf_op jit(solution)/shard_map/ppermute | solution.py:23
  133.5 17.1 %all-gather.1 = f32[384,128]{1,0:T(8,128)S(1)} all-gather(f32[24,128]{1,0:T(8,128)S(1)} %solve.1), channel_id=3, replica_groups=mesh['gx'=32,'gy'=16] {'gy'}, dimensions={0}, use_global_device_ids=true | all-gather | bytes 208896 | tf_op jit(solution)/shard_map/all_gather | solution.py:501
  151.2 4.3 %collective-permute-start.20 = (f32[6,24,128]{2,1,0:T(8,128)S(1)}, f32[6,24,128]{2,1,0:T(8,128)S(1)}, u32[]{:S(2)}, u32[]{:S(2)}) collective-permute-start(f32[6,24,128]{2,1,0:T(8,128)S(1)} %pick.1.coarse_own), channel_id=1, source_target_pairs={{0,16},{16,0},{32,48},{48,32},{64,80},{80,64},{96,112},{112,96},{1... | collective-permute-start | bytes 221192 | tf_op jit(solution)/shard_map/ppermute | solution.py:380
  159.7 3.3 %collective-permute-done.21 = f32[6,24,128]{2,1,0:T(8,128)S(1)} collective-permute-done((f32[6,24,128]{2,1,0:T(8,128)S(1)}, f32[6,24,128]{2,1,0:T(8,128)S(1)}, u32[]{:S(2)}, u32[]{:S(2)}) %collective-permute-start.21) | collective-permute-done | bytes 73760 | tf_op jit(solution)/shard_map/ppermute | solution.py:380
  168.3 3.5 %collective-permute-start.25 = (f32[4,24,128]{2,1,0:T(8,128)S(1)}, f32[4,24,128]{2,1,0:T(8,128)S(1)}, u32[]{:S(2)}, u32[]{:S(2)}) collective-permute-start(f32[4,24,128]{2,1,0:T(8,128)S(1)} %bitcast.94), channel_id=1, source_target_pairs={{0,16},{16,0},{32,48},{48,32},{64,80},{80,64},{96,112},{112,96},{1... | collective-permute-start | bytes 147464 | tf_op jit(solution)/shard_map/ppermute | solution.py:23
  171.8 4.3 %collective-permute-start.26 = (f32[4,24,128]{2,1,0:T(8,128)S(1)}, f32[4,24,128]{2,1,0:T(8,128)S(1)}, u32[]{:S(2)}, u32[]{:S(2)}) collective-permute-start(f32[4,24,128]{2,1,0:T(8,128)S(1)} %bitcast.95), channel_id=1, source_target_pairs={{16,32},{32,16},{48,64},{64,48},{80,96},{96,80},{112,128},{128,112... | collective-permute-start | bytes 147464 | tf_op jit(solution)/shard_map/ppermute | solution.py:23
  179.0 5.4 %collective-permute-start.28 = (f32[4,24,128]{2,1,0:T(8,128)S(1)}, f32[4,24,128]{2,1,0:T(8,128)S(1)}, u32[]{:S(2)}, u32[]{:S(2)}) collective-permute-start(f32[4,24,128]{2,1,0:T(8,128)S(1)} %bitcast.97), channel_id=1, source_target_pairs={{1,2},{2,1},{3,4},{4,3},{5,6},{6,5},{7,8},{8,7},{9,10},{10,9},{11,... | collective-permute-start | bytes 147464 | tf_op jit(solution)/shard_map/ppermute | solution.py:23
  188.1 4.9 %collective-permute-start.30 = (f32[8,24,128]{2,1,0:T(8,128)S(1)}, f32[8,24,128]{2,1,0:T(8,128)S(1)}, u32[]{:S(2)}, u32[]{:S(2)}) collective-permute-start(f32[8,24,128]{2,1,0:T(8,128)S(1)} %bitcast.144), channel_id=1, source_target_pairs={{1,2},{2,1},{3,4},{4,3},{5,6},{6,5},{7,8},{8,7},{9,10},{10,9},{11,... | collective-permute-start | bytes 294920 | tf_op jit(solution)/shard_map/ppermute | solution.py:23
  200.0 4.9 %collective-permute-start.34 = (f32[8,24,128]{2,1,0:T(8,128)S(1)}, f32[8,24,128]{2,1,0:T(8,128)S(1)}, u32[]{:S(2)}, u32[]{:S(2)}) collective-permute-start(f32[8,24,128]{2,1,0:T(8,128)S(1)} %bitcast.147), channel_id=1, source_target_pairs={{1,2},{2,1},{3,4},{4,3},{5,6},{6,5},{7,8},{8,7},{9,10},{10,9},{11,... | collective-permute-start | bytes 294920 | tf_op jit(solution)/shard_map/ppermute | solution.py:23
  206.8 4.3 %collective-permute-start.32 = (f32[8,24,128]{2,1,0:T(8,128)S(1)}, f32[8,24,128]{2,1,0:T(8,128)S(1)}, u32[]{:S(2)}, u32[]{:S(2)}) collective-permute-start(f32[8,24,128]{2,1,0:T(8,128)S(1)} %bitcast.145), channel_id=1, source_target_pairs={{16,32},{32,16},{48,64},{64,48},{80,96},{96,80},{112,128},{128,112... | collective-permute-start | bytes 294920 | tf_op jit(solution)/shard_map/ppermute | solution.py:23
  211.1 4.3 %collective-permute-done.32.refs_1_ = f32[8,24,128]{2,1,0:T(8,128)S(1)} collective-permute-done((f32[8,24,128]{2,1,0:T(8,128)S(1)}, f32[8,24,128]{2,1,0:T(8,128)S(1)}, u32[]{:S(2)}, u32[]{:S(2)}) %collective-permute-start.32) | collective-permute-done | bytes 98336 | tf_op jit(solution)/shard_map/ppermute | solution.py:23
  217.5 3.7 %collective-permute-start.36 = (f32[8,24,128]{2,1,0:T(8,128)S(1)}, f32[8,24,128]{2,1,0:T(8,128)S(1)}, u32[]{:S(2)}, u32[]{:S(2)}) collective-permute-start(f32[8,24,128]{2,1,0:T(8,128)S(1)} %bitcast.149), channel_id=1, source_target_pairs={{1,2},{2,1},{3,4},{4,3},{5,6},{6,5},{7,8},{8,7},{9,10},{10,9},{11,... | collective-permute-start | bytes 294920 | tf_op jit(solution)/shard_map/ppermute | solution.py:23
  221.1 3.5 %collective-permute-done.36.refs_5_ = f32[8,24,128]{2,1,0:T(8,128)S(1)} collective-permute-done((f32[8,24,128]{2,1,0:T(8,128)S(1)}, f32[8,24,128]{2,1,0:T(8,128)S(1)}, u32[]{:S(2)}, u32[]{:S(2)}) %collective-permute-start.36) | collective-permute-done | bytes 98336 | tf_op jit(solution)/shard_map/ppermute | solution.py:23
  224.6 5.0 %up_8.1 = f32[8,8,24,128]{3,2,1,0:T(8,128)S(1)} custom-call(s32[8]{0:T(128)S(1)} %stack.27.where, f32[4,4,24,128]{3,2,1,0:T(8,128)S(1)} %up_4.1.coarse_own, f32[8,24,128]{2,1,0:T(8,128)S(1)} %collective-permute-done.31.refs_0_, f32[8,24,128]{2,1,0:T(8,128)S(1)} %collective-permute-done.32.refs_1_, f32[8,24,128]{2,1,0:T(8,128)S(1)} %collective-permute-done.33.refs_2_, ...), custom_call_target="tpu_custom_call" | custom-call | tf_op jit(solution)/shard_map/up_8/pallas_call | solution.py:302
  (131 shorter events, 65.7 us)
Async XLA Ops:
  2.6 15.7 %collective-permute-start = (f32[27,24,128]{2,1,0:T(8,128)S(1)}, f32[27,24,128]{2,1,0:T(8,128)S(1)}, u32[]{:S(2)}, u32[]{:S(2)}) collective-permute-start(f32[27,24,128]{2,1,0:T(8,128)S(1)} %get-tuple-element.145), channel_id=1, source_target_pairs={{0,16},{16,0},{32,48},{48,32},{64,80},{80,64},{96,112},{112,96},{1... | collective-permute-start | bytes 995336 | tf_op jit(solution)/shard_map/ppermute | solution.py:23
  5.0 13.6 %collective-permute-start.1 = (f32[27,24,128]{2,1,0:T(8,128)S(1)}, f32[27,24,128]{2,1,0:T(8,128)S(1)}, u32[]{:S(2)}, u32[]{:S(2)}) collective-permute-start(f32[27,24,128]{2,1,0:T(8,128)S(1)} %get-tuple-element.146), channel_id=1, source_target_pairs={{16,32},{32,16},{48,64},{64,48},{80,96},{96,80},{112,128},{128,112... | collective-permute-start | bytes 995336 | tf_op jit(solution)/shard_map/ppermute | solution.py:23
  10.0 8.6 %collective-permute-start.2 = (f32[27,24,128]{2,1,0:T(8,128)S(1)}, f32[27,24,128]{2,1,0:T(8,128)S(1)}, u32[]{:S(2)}, u32[]{:S(2)}) collective-permute-start(f32[27,24,128]{2,1,0:T(8,128)S(1)} %get-tuple-element.102), channel_id=1, source_target_pairs={{0,1},{1,0},{2,3},{3,2},{4,5},{5,4},{6,7},{7,6},{8,9},{9,8},{10,11... | collective-permute-start | bytes 995336 | tf_op jit(solution)/shard_map/ppermute | solution.py:23
  13.2 9.9 %collective-permute-start.3 = (f32[27,24,128]{2,1,0:T(8,128)S(1)}, f32[27,24,128]{2,1,0:T(8,128)S(1)}, u32[]{:S(2)}, u32[]{:S(2)}) collective-permute-start(f32[27,24,128]{2,1,0:T(8,128)S(1)} %get-tuple-element.101), channel_id=1, source_target_pairs={{1,2},{2,1},{3,4},{4,3},{5,6},{6,5},{7,8},{8,7},{9,10},{10,9},{11,... | collective-permute-start | bytes 995336 | tf_op jit(solution)/shard_map/ppermute | solution.py:23
  23.4 6.8 %collective-permute-start.4 = (f32[24,24,128]{2,1,0:T(8,128)S(1)}, f32[24,24,128]{2,1,0:T(8,128)S(1)}, u32[]{:S(2)}, u32[]{:S(2)}) collective-permute-start(f32[24,24,128]{2,1,0:T(8,128)S(1)} %get-tuple-element.106), channel_id=1, source_target_pairs={{0,1},{1,0},{2,3},{3,2},{4,5},{5,4},{6,7},{7,6},{8,9},{9,8},{10,11... | collective-permute-start | bytes 884744 | tf_op jit(solution)/shard_map/ppermute | solution.py:23
  25.3 9.3 %collective-permute-start.5 = (f32[24,24,128]{2,1,0:T(8,128)S(1)}, f32[24,24,128]{2,1,0:T(8,128)S(1)}, u32[]{:S(2)}, u32[]{:S(2)}) collective-permute-start(f32[24,24,128]{2,1,0:T(8,128)S(1)} %get-tuple-element.105), channel_id=1, source_target_pairs={{1,2},{2,1},{3,4},{4,3},{5,6},{6,5},{7,8},{8,7},{9,10},{10,9},{11,... | collective-permute-start | bytes 884744 | tf_op jit(solution)/shard_map/ppermute | solution.py:23
  39.7 13.3 %collective-permute-start.6 = (f32[12,24,128]{2,1,0:T(8,128)S(1)}, f32[12,24,128]{2,1,0:T(8,128)S(1)}, u32[]{:S(2)}, u32[]{:S(2)}) collective-permute-start(f32[12,24,128]{2,1,0:T(8,128)S(1)} %bitcast.139), channel_id=1, source_target_pairs={{0,16},{16,0},{32,48},{48,32},{64,80},{80,64},{96,112},{112,96},{1... | collective-permute-start | bytes 442376 | tf_op jit(solution)/shard_map/ppermute | solution.py:23
  41.6 11.4 %collective-permute-start.7 = (f32[12,24,128]{2,1,0:T(8,128)S(1)}, f32[12,24,128]{2,1,0:T(8,128)S(1)}, u32[]{:S(2)}, u32[]{:S(2)}) collective-permute-start(f32[12,24,128]{2,1,0:T(8,128)S(1)} %bitcast.138), channel_id=1, source_target_pairs={{16,32},{32,16},{48,64},{64,48},{80,96},{96,80},{112,128},{128,112... | collective-permute-start | bytes 442376 | tf_op jit(solution)/shard_map/ppermute | solution.py:23
  45.6 7.4 %collective-permute-start.8 = (f32[12,24,128]{2,1,0:T(8,128)S(1)}, f32[12,24,128]{2,1,0:T(8,128)S(1)}, u32[]{:S(2)}, u32[]{:S(2)}) collective-permute-start(f32[12,24,128]{2,1,0:T(8,128)S(1)} %bitcast.137), channel_id=1, source_target_pairs={{0,1},{1,0},{2,3},{3,2},{4,5},{5,4},{6,7},{7,6},{8,9},{9,8},{10,11... | collective-permute-start | bytes 442376 | tf_op jit(solution)/shard_map/ppermute | solution.py:23
  47.6 8.2 %collective-permute-start.9 = (f32[12,24,128]{2,1,0:T(8,128)S(1)}, f32[12,24,128]{2,1,0:T(8,128)S(1)}, u32[]{:S(2)}, u32[]{:S(2)}) collective-permute-start(f32[12,24,128]{2,1,0:T(8,128)S(1)} %bitcast.136), channel_id=1, source_target_pairs={{1,2},{2,1},{3,4},{4,3},{5,6},{6,5},{7,8},{8,7},{9,10},{10,9},{11,... | collective-permute-start | bytes 442376 | tf_op jit(solution)/shard_map/ppermute | solution.py:23
  55.9 6.8 %collective-permute-start.10 = (f32[18,24,128]{2,1,0:T(8,128)S(1)}, f32[18,24,128]{2,1,0:T(8,128)S(1)}, u32[]{:S(2)}, u32[]{:S(2)}) collective-permute-start(f32[18,24,128]{2,1,0:T(8,128)S(1)} %bitcast.130), channel_id=1, source_target_pairs={{0,1},{1,0},{2,3},{3,2},{4,5},{5,4},{6,7},{7,6},{8,9},{9,8},{10,11... | collective-permute-start | bytes 663560 | tf_op jit(solution)/shard_map/ppermute | solution.py:23
  57.9 8.5 %collective-permute-start.11 = (f32[18,24,128]{2,1,0:T(8,128)S(1)}, f32[18,24,128]{2,1,0:T(8,128)S(1)}, u32[]{:S(2)}, u32[]{:S(2)}) collective-permute-start(f32[18,24,128]{2,1,0:T(8,128)S(1)} %bitcast.129), channel_id=1, source_target_pairs={{1,2},{2,1},{3,4},{4,3},{5,6},{6,5},{7,8},{8,7},{9,10},{10,9},{11,... | collective-permute-start | bytes 663560 | tf_op jit(solution)/shard_map/ppermute | solution.py:23
  72.2 11.3 %collective-permute-start.13 = (f32[2,4,24,128]{3,2,1,0:T(8,128)S(1)}, f32[2,4,24,128]{3,2,1,0:T(8,128)S(1)}, u32[]{:S(2)}, u32[]{:S(2)}) collective-permute-start(f32[2,4,24,128]{3,2,1,0:T(8,128)S(1)} %pad_maximum_fusion.19), channel_id=1, source_target_pairs={{0,16},{16,0},{32,48},{48,32},{64,80},{80,64},{96,112},{112,96},{1... | collective-permute-start | bytes 294920 | tf_op jit(solution)/shard_map/ppermute | solution.py:380
  76.6 7.0 %collective-permute-start.14 = (f32[1,4,24,128]{3,2,1,0:T(8,128)S(1)}, f32[1,4,24,128]{3,2,1,0:T(8,128)S(1)}, u32[]{:S(2)}, u32[]{:S(2)}) collective-permute-start(f32[1,4,24,128]{3,2,1,0:T(8,128)S(1)} %fusion.15), channel_id=1, source_target_pairs={{32,64},{64,32},{48,80},{80,48},{96,128},{128,96},{112,144},{144,1... | collective-permute-start | bytes 147464 | tf_op jit(solution)/shard_map/ppermute | solution.py:380
  87.1 8.0 %collective-permute-start.16 = (f32[6,3,24,128]{3,2,1,0:T(8,128)S(1)}, f32[6,3,24,128]{3,2,1,0:T(8,128)S(1)}, u32[]{:S(2)}, u32[]{:S(2)}) collective-permute-start(f32[6,3,24,128]{3,2,1,0:T(8,128)S(1)} %slice_select_fusion), channel_id=1, source_target_pairs={{0,2},{2,0},{3,5},{5,3},{4,6},{6,4},{7,9},{9,7},{8,10},{10,8},{11,... | collective-permute-start | bytes 663560 | tf_op jit(solution)/shard_map/ppermute | solution.py:456
  100.6 25.3 %collective-permute-start.18 = (f32[28,24,128]{2,1,0:T(8,128)S(1)}, f32[28,24,128]{2,1,0:T(8,128)S(1)}, u32[]{:S(2)}, u32[]{:S(2)}) collective-permute-start(f32[28,24,128]{2,1,0:T(8,128)S(1)} %get-tuple-element.100), channel_id=1, source_target_pairs={{0,16},{16,0},{32,48},{48,32},{64,80},{80,64},{96,112},{112,96},{1... | collective-permute-start | bytes 1032200 | tf_op jit(solution)/shard_map/ppermute | solution.py:23
  104.3 21.6 %collective-permute-start.19 = (f32[28,24,128]{2,1,0:T(8,128)S(1)}, f32[28,24,128]{2,1,0:T(8,128)S(1)}, u32[]{:S(2)}, u32[]{:S(2)}) collective-permute-start(f32[28,24,128]{2,1,0:T(8,128)S(1)} %get-tuple-element.99), channel_id=1, source_target_pairs={{16,32},{32,16},{48,64},{64,48},{80,96},{96,80},{112,128},{128,112... | collective-permute-start | bytes 1032200 | tf_op jit(solution)/shard_map/ppermute | solution.py:23
  126.4 40.0 %collective-permute-start.23 = (f32[52,24,128]{2,1,0:T(8,128)S(1)}, f32[52,24,128]{2,1,0:T(8,128)S(1)}, u32[]{:S(2)}, u32[]{:S(2)}) collective-permute-start(f32[52,24,128]{2,1,0:T(8,128)S(1)} %get-tuple-element.88), channel_id=1, source_target_pairs={{0,1},{1,0},{2,3},{3,2},{4,5},{5,4},{6,7},{7,6},{8,9},{9,8},{10,11... | collective-permute-start | bytes 1916936 | tf_op jit(solution)/shard_map/ppermute | solution.py:23
  128.6 37.8 %collective-permute-start.24 = (f32[52,24,128]{2,1,0:T(8,128)S(1)}, f32[52,24,128]{2,1,0:T(8,128)S(1)}, u32[]{:S(2)}, u32[]{:S(2)}) collective-permute-start(f32[52,24,128]{2,1,0:T(8,128)S(1)} %get-tuple-element.87), channel_id=1, source_target_pairs={{1,2},{2,1},{3,4},{4,3},{5,6},{6,5},{7,8},{8,7},{9,10},{10,9},{11,... | collective-permute-start | bytes 1916936 | tf_op jit(solution)/shard_map/ppermute | solution.py:23
  151.2 8.4 %collective-permute-start.20 = (f32[6,24,128]{2,1,0:T(8,128)S(1)}, f32[6,24,128]{2,1,0:T(8,128)S(1)}, u32[]{:S(2)}, u32[]{:S(2)}) collective-permute-start(f32[6,24,128]{2,1,0:T(8,128)S(1)} %pick.1.coarse_own), channel_id=1, source_target_pairs={{0,16},{16,0},{32,48},{48,32},{64,80},{80,64},{96,112},{112,96},{1... | collective-permute-start | bytes 221192 | tf_op jit(solution)/shard_map/ppermute | solution.py:380
  155.5 7.4 %collective-permute-start.21 = (f32[6,24,128]{2,1,0:T(8,128)S(1)}, f32[6,24,128]{2,1,0:T(8,128)S(1)}, u32[]{:S(2)}, u32[]{:S(2)}) collective-permute-start(f32[6,24,128]{2,1,0:T(8,128)S(1)} %pick.1.coarse_own), channel_id=1, source_target_pairs={{32,64},{64,32},{48,80},{80,48},{96,128},{128,96},{112,144},{144,1... | collective-permute-start | bytes 221192 | tf_op jit(solution)/shard_map/ppermute | solution.py:380
  168.3 16.1 %collective-permute-start.25 = (f32[4,24,128]{2,1,0:T(8,128)S(1)}, f32[4,24,128]{2,1,0:T(8,128)S(1)}, u32[]{:S(2)}, u32[]{:S(2)}) collective-permute-start(f32[4,24,128]{2,1,0:T(8,128)S(1)} %bitcast.94), channel_id=1, source_target_pairs={{0,16},{16,0},{32,48},{48,32},{64,80},{80,64},{96,112},{112,96},{1... | collective-permute-start | bytes 147464 | tf_op jit(solution)/shard_map/ppermute | solution.py:23
  171.8 12.6 %collective-permute-start.26 = (f32[4,24,128]{2,1,0:T(8,128)S(1)}, f32[4,24,128]{2,1,0:T(8,128)S(1)}, u32[]{:S(2)}, u32[]{:S(2)}) collective-permute-start(f32[4,24,128]{2,1,0:T(8,128)S(1)} %bitcast.95), channel_id=1, source_target_pairs={{16,32},{32,16},{48,64},{64,48},{80,96},{96,80},{112,128},{128,112... | collective-permute-start | bytes 147464 | tf_op jit(solution)/shard_map/ppermute | solution.py:23
  176.1 8.3 %collective-permute-start.27 = (f32[4,24,128]{2,1,0:T(8,128)S(1)}, f32[4,24,128]{2,1,0:T(8,128)S(1)}, u32[]{:S(2)}, u32[]{:S(2)}) collective-permute-start(f32[4,24,128]{2,1,0:T(8,128)S(1)} %bitcast.96), channel_id=1, source_target_pairs={{0,1},{1,0},{2,3},{3,2},{4,5},{5,4},{6,7},{7,6},{8,9},{9,8},{10,11... | collective-permute-start | bytes 147464 | tf_op jit(solution)/shard_map/ppermute | solution.py:23
  179.0 7.2 %collective-permute-start.28 = (f32[4,24,128]{2,1,0:T(8,128)S(1)}, f32[4,24,128]{2,1,0:T(8,128)S(1)}, u32[]{:S(2)}, u32[]{:S(2)}) collective-permute-start(f32[4,24,128]{2,1,0:T(8,128)S(1)} %bitcast.97), channel_id=1, source_target_pairs={{1,2},{2,1},{3,4},{4,3},{5,6},{6,5},{7,8},{8,7},{9,10},{10,9},{11,... | collective-permute-start | bytes 147464 | tf_op jit(solution)/shard_map/ppermute | solution.py:23
  186.2 6.8 %collective-permute-start.29 = (f32[8,24,128]{2,1,0:T(8,128)S(1)}, f32[8,24,128]{2,1,0:T(8,128)S(1)}, u32[]{:S(2)}, u32[]{:S(2)}) collective-permute-start(f32[8,24,128]{2,1,0:T(8,128)S(1)} %bitcast.143), channel_id=1, source_target_pairs={{0,1},{1,0},{2,3},{3,2},{4,5},{5,4},{6,7},{7,6},{8,9},{9,8},{10,11... | collective-permute-start | bytes 294920 | tf_op jit(solution)/shard_map/ppermute | solution.py:23
  188.1 7.1 %collective-permute-start.30 = (f32[8,24,128]{2,1,0:T(8,128)S(1)}, f32[8,24,128]{2,1,0:T(8,128)S(1)}, u32[]{:S(2)}, u32[]{:S(2)}) collective-permute-start(f32[8,24,128]{2,1,0:T(8,128)S(1)} %bitcast.144), channel_id=1, source_target_pairs={{1,2},{2,1},{3,4},{4,3},{5,6},{6,5},{7,8},{8,7},{9,10},{10,9},{11,... | collective-permute-start | bytes 294920 | tf_op jit(solution)/shard_map/ppermute | solution.py:23
  198.1 13.0 %collective-permute-start.33 = (f32[8,24,128]{2,1,0:T(8,128)S(1)}, f32[8,24,128]{2,1,0:T(8,128)S(1)}, u32[]{:S(2)}, u32[]{:S(2)}) collective-permute-start(f32[8,24,128]{2,1,0:T(8,128)S(1)} %bitcast.148), channel_id=1, source_target_pairs={{0,1},{1,0},{2,3},{3,2},{4,5},{5,4},{6,7},{7,6},{8,9},{9,8},{10,11... | collective-permute-start | bytes 294920 | tf_op jit(solution)/shard_map/ppermute | solution.py:23
  200.0 11.1 %collective-permute-start.34 = (f32[8,24,128]{2,1,0:T(8,128)S(1)}, f32[8,24,128]{2,1,0:T(8,128)S(1)}, u32[]{:S(2)}, u32[]{:S(2)}) collective-permute-start(f32[8,24,128]{2,1,0:T(8,128)S(1)} %bitcast.147), channel_id=1, source_target_pairs={{1,2},{2,1},{3,4},{4,3},{5,6},{6,5},{7,8},{8,7},{9,10},{10,9},{11,... | collective-permute-start | bytes 294920 | tf_op jit(solution)/shard_map/ppermute | solution.py:23
  204.9 6.3 %collective-permute-start.31 = (f32[8,24,128]{2,1,0:T(8,128)S(1)}, f32[8,24,128]{2,1,0:T(8,128)S(1)}, u32[]{:S(2)}, u32[]{:S(2)}) collective-permute-start(f32[8,24,128]{2,1,0:T(8,128)S(1)} %bitcast.146), channel_id=1, source_target_pairs={{0,16},{16,0},{32,48},{48,32},{64,80},{80,64},{96,112},{112,96},{1... | collective-permute-start | bytes 294920 | tf_op jit(solution)/shard_map/ppermute | solution.py:23
  206.8 8.7 %collective-permute-start.32 = (f32[8,24,128]{2,1,0:T(8,128)S(1)}, f32[8,24,128]{2,1,0:T(8,128)S(1)}, u32[]{:S(2)}, u32[]{:S(2)}) collective-permute-start(f32[8,24,128]{2,1,0:T(8,128)S(1)} %bitcast.145), channel_id=1, source_target_pairs={{16,32},{32,16},{48,64},{64,48},{80,96},{96,80},{112,128},{128,112... | collective-permute-start | bytes 294920 | tf_op jit(solution)/shard_map/ppermute | solution.py:23
  217.5 7.1 %collective-permute-start.36 = (f32[8,24,128]{2,1,0:T(8,128)S(1)}, f32[8,24,128]{2,1,0:T(8,128)S(1)}, u32[]{:S(2)}, u32[]{:S(2)}) collective-permute-start(f32[8,24,128]{2,1,0:T(8,128)S(1)} %bitcast.149), channel_id=1, source_target_pairs={{1,2},{2,1},{3,4},{4,3},{5,6},{6,5},{7,8},{8,7},{9,10},{10,9},{11,... | collective-permute-start | bytes 294920 | tf_op jit(solution)/shard_map/ppermute | solution.py:23
  (7 other events, 25.2 us)

commit v3 on v2

--- a/solution.py
+++ b/solution.py
@@ -66,16 +66,29 @@
     return (scale * ((root - 6.0) - shift_row)) * centre + scale * total
 
 
+def each_row(count, row):
+    if count <= 4:
+        for x in range(count):
+            row(x)
+        return
+
+    def pair(step, carry):
+        row(2 * step)
+        row(2 * step + 1)
+        return carry
+
+    lax.fori_loop(0, count // 2, pair, 0)
+
+
 def factor(src, dst, shift, shift_at, size, root, masks):
-    def row(x, carry):
+    def row(x):
         row_mask = masks(x, None)
         for y in range(size[1]):
             shift_row = shift[x + shift_at[0], pl.ds(y + shift_at[1], 1), :]
             mask = row_mask * masks(None, y)
             dst[x, y] = factor_cell(src, x + 1, y + 1, shift_row, root, mask)
-        return carry
-
-    lax.fori_loop(0, size[0], row, 0)
+
+    each_row(size[0], row)
 
 
 def masks_of(first, reach, grid):
@@ -88,64 +101,59 @@
 
 
 def put_frame(dst, own, pieces, where, n, width):
-    x_even, x_odd, y_even, y_odd, c_even, c_odd = pieces
+    x_even, x_odd, y_even, y_odd = pieces
     high = n + width
     rows = [jnp.where(where[3] == odd, high, 0) for odd in (0, 1)]
     columns = [jnp.where(where[2] == odd, high, 0) for odd in (0, 1)]
 
-    def middle(x, carry):
+    def middle(x):
         for y in range(n):
             dst[x + width, y + width] = own[x, y]
-        for ref, at in ((y_even, columns[0]), (y_odd, columns[1])):
-            for k in range(width):
-                dst[x + width, at + k] = ref[x * width + k]
-        return carry
-
-    lax.fori_loop(0, n, middle, 0)
-
-    def outer(x, carry):
+
+    def outer(x):
         for ref, at in ((x_even, rows[0]), (x_odd, rows[1])):
             for y in range(n):
                 dst[at + x, width + y] = ref[x * n + y]
-        for ref, at in ((c_even, columns[0]), (c_odd, columns[1])):
+
+    def beside(x):
+        for ref, at in ((y_even, columns[0]), (y_odd, columns[1])):
             for k in range(width):
                 dst[x, at + k] = ref[x * width + k]
-                dst[high + x, at + k] = ref[(width + x) * width + k]
-        return carry
-
-    lax.fori_loop(0, width, outer, 0)
+
+    each_row(n, middle)
+    for x in range(width):
+        outer(x)
+    each_row(n + 2 * width, beside)
 
 
 def put_columns(dst, centre, pieces, where, rows, width, reach):
-    def row(x, carry):
+    def row(x):
         for y in range(width):
             dst[x, reach + y] = centre[x, y]
         for ref, base, odd in pieces:
             at = jnp.where(where[2] == odd, reach + width, 0)
             for k in range(reach):
                 dst[x, at + k] = ref[base + x * reach + k]
-        return carry
-
-    lax.fori_loop(0, rows, row, 0)
+
+    each_row(rows, row)
 
 
 def put_shift(wide, one, one_wide, two, own, pieces, where, n):
-    x_even, x_odd, y_even, y_odd, c_even, c_odd = pieces
+    x_even, x_odd, y_even, y_odd = pieces
     chans = x_even.shape[1]
-    strip, corner = HALO * n, 2 * HALO * HALO
+    strip, side = HALO * n, HALO * (n + 2 * HALO)
 
     def line(ref, first, x):
         at = x * n
         return ref[first + at // chans, at % chans : at % chans + n, :]
 
-    for odd, x_ref, y_ref, c_ref in ((0, x_even, y_even, c_even), (1, x_odd, y_odd, c_odd)):
+    for odd, x_ref, y_ref in ((0, x_even, y_even), (1, x_odd, y_odd)):
         row = jnp.where(where[3] == odd, 2 * n, 0)
         column = pl.ds(pl.multiple_of(jnp.where(where[2] == odd, 2 * n, 0), n), n)
         for x in range(n):
             wide[row + x, n : 2 * n, :] = line(x_ref, strip, x)
-            wide[n + x, column, :] = line(y_ref, strip, x)
-            wide[x, column, :] = line(c_ref, corner, x)
-            wide[2 * n + x, column, :] = line(c_ref, corner, n + x)
+        for x in range(3 * n):
+            wide[x, column, :] = line(y_ref, side, x)
     for x in range(n):
         wide[n + x, n : 2 * n, :] = own[x]
 
@@ -171,7 +179,7 @@
     factor(pad, one, shift, (sx, sy), (nx + 4, ny + 4), ROOTS[0], masks_of(first, 2, grid))
     factor(one, two, shift, (sx + 1, sy + 1), (nx + 2, ny + 2), ROOTS[1], masks_of(first, 1, grid))
 
-    def row(x, carry):
+    def row(x):
         for y in range(ny):
             shift_row = shift[x + 2 + sx, pl.ds(y + 2 + sy, 1), :]
             leftover[x, y] = factor_cell(two, x + 1, y + 1, shift_row, ROOTS[2], 1.0)
@@ -180,23 +188,21 @@
                 + one[x + 2, y + 2] * (1.0 / ROOTS[1])
                 + two[x + 1, y + 1] * (1.0 / ROOTS[2])
             )
-        return carry
-
-    lax.fori_loop(0, nx, row, 0)
-
-    def coarse_row(x, carry):
+
+    each_row(nx, row)
+
+    def coarse_row(x):
         for y in range(ny // 2):
             near = leftover[2 * x, 2 * y] + leftover[2 * x, 2 * y + 1]
             far = leftover[2 * x + 1, 2 * y] + leftover[2 * x + 1, 2 * y + 1]
             coarser[x, y] = 0.25 * (near + far)
-        return carry
-
-    lax.fori_loop(0, nx // 2, coarse_row, 0)
+
+    each_row(nx // 2, coarse_row)
 
 
 def down_fine_kernel(n, grid, where, own, *refs):
-    pieces, own_shift = refs[:6], refs[6]
-    iterate, leftover, coarser, shift, shift_one, shift_two, one_wide, pad, one, two = refs[7:]
+    pieces, own_shift = refs[:4], refs[4]
+    iterate, leftover, coarser, shift, shift_one, shift_two, one_wide, pad, one, two = refs[5:]
     put_frame(pad, own, pieces, where, n, HALO)
     put_shift(shift, shift_one, one_wide, shift_two, own_shift, pieces, where, n)
     first = (where[0] * n, where[1] * n)
@@ -204,8 +210,8 @@
 
 
 def down_kernel(n, grid, where, own, *refs):
-    pieces, shift = refs[:6], refs[6]
-    iterate, leftover, coarser, pad, one, two = refs[7:]
+    pieces, shift = refs[:4], refs[4]
+    iterate, leftover, coarser, pad, one, two = refs[5:]
     put_frame(pad, own, pieces, where, n, HALO)
     first = (where[0] * n, where[1] * n)
     down_body((n, n), grid, first, pad, shift, (0, 0), iterate, leftover, coarser, one, two)
@@ -217,12 +223,14 @@
 
 
 def solve_kernel(where, shares, inverse, solved, ordered):
-    count, rows, depth = shares.shape
+    chips, _, depth = shares.shape
     chans = solved.shape[0]
+    count = 2 * chips
     for m in range(count):
         block = jnp.zeros((chans, depth), jnp.float32)
         for j in range(count):
-            block = jnp.where(shares[j, chans : chans + 1, :] == float(m), shares[j, 0:chans, :], block)
+            slot = shares[j // 2, 2 * chans + 8 * (j % 2) : 2 * chans + 8 * (j % 2) + 1, :]
+            block = jnp.where(slot == float(m), shares[j // 2, j % 2 * chans : (j % 2 + 1) * chans, :], block)
         ordered[:, m * depth : (m + 1) * depth] = block
     solved[...] = lax.dot_general(
         ordered[...],
@@ -234,14 +242,16 @@
 
 
 def pick_kernel(where, shares, back, picked):
-    count, chans, depth = back.shape
+    chips, rows, depth = back.shape
+    chans = rows // 2
     for k in range(picked.shape[0]):
         j = where[1] - where[2] + k - 2
-        slot = shares[jnp.clip(j, 0, count - 1), pl.ds(chans, 1), :]
-        slot = jnp.where((j >= 0) & (j < count), slot, -1.0)
+        chip = jnp.clip(where[6] + k // 2 - 1, 0, chips - 1)
+        slot = shares[chip, pl.ds(2 * chans + 8 * (k % 2), 1), :]
+        slot = jnp.where((j >= 0) & (j < 2 * chips), slot, -1.0)
         block = jnp.zeros((chans, depth), jnp.float32)
-        for m in range(count):
-            block = jnp.where(slot == float(m), back[m], block)
+        for m in range(2 * chips):
+            block = jnp.where(slot == float(m), back[m // 2, m % 2 * chans : (m % 2 + 1) * chans, :], block)
         picked[k] = block
 
 
@@ -265,7 +275,7 @@
     first = (where[0] * n, where[1] * n)
     outer = masks_of(first, 2, grid)
 
-    def first_row(x, carry):
+    def first_row(x):
         row_mask = outer(x, None)
         here, before, after = (x + 2) // 2, (x + 1) // 2, (x + 3) // 2
         for y in range(n + 4):
@@ -276,12 +286,11 @@
             shift_row = shift[x + sx, pl.ds(y + sy, 1), :]
             mask = row_mask * outer(None, y)
             start[x, y] = mask * ((start[x, y] - (6.0 + shift_row) * centre) + total)
-        return carry
-
-    lax.fori_loop(0, n + 4, first_row, 0)
+
+    each_row(n + 4, first_row)
     factor(start, one, shift, (sx + 1, sy + 1), (n + 2, n + 2), ROOTS[0], masks_of(first, 1, grid))
 
-    def row(x, carry):
+    def row(x):
         for y in range(n):
             shift_row = shift[x + 2 + sx, pl.ds(y + 2 + sy, 1), :]
             two = factor_cell(one, x + 1, y + 1, shift_row, ROOTS[1], 1.0)
@@ -289,9 +298,8 @@
                 start[x + 2, y + 2] * (1.0 / ROOTS[0]) + one[x + 1, y + 1] * (1.0 / ROOTS[1]) + two * (1.0 / ROOTS[2])
             )
             result[x, y] = (iterate[x, y] + coarse[x // 2 + 2, y // 2 + 2]) + step
-        return carry
-
-    lax.fori_loop(0, n, row, 0)
+
+    each_row(n, row)
 
 
 VMEM = pl.BlockSpec(memory_space=pltpu.VMEM)
@@ -314,7 +322,8 @@
     core = parity("gy", 1)
     line, far = parity("gx", 1), parity("gx", 2)
     numbers = [lax.axis_index("gx"), lax.axis_index("gy"), core, line, line ^ core, far ^ core]
-    where = jnp.stack(numbers + [jnp.zeros_like(core)] * 2).astype(jnp.int32)
+    numbers += [lax.div(lax.axis_index("gy"), 2), jnp.zeros_like(core)]
+    where = jnp.stack(numbers).astype(jnp.int32)
     sides = {
         "gx": line == 0,
         "gy": core == 0,
@@ -358,15 +367,14 @@
         return flat.reshape(blocks.shape)
 
     x_pieces = swap_ends(at, message(v[:width], blocks), message(v[n - width :], blocks), "gx", 1)
-    y_pieces = swap_ends(at, message(v[:, :width], blocks), message(v[:, n - width :], blocks), "gy", 1)
-    x_pieces, y_pieces = lax.optimization_barrier((x_pieces, y_pieces))
     sides = in_order(at, *x_pieces, "gx")
     strips = [side[: width * n].reshape((width, n) + tail) for side in sides]
-    beyond = None if blocks is None else jnp.concatenate([rows_of(side) for side in sides], axis=0)
-    low = jnp.concatenate([strip[:, :width] for strip in strips], axis=0)
-    high = jnp.concatenate([strip[:, n - width :] for strip in strips], axis=0)
-    corners = swap_ends(at, message(low, beyond), message(high, beyond), "gy", 1)
-    return [*x_pieces, *y_pieces, *corners]
+    rows = None
+    if blocks is not None:
+        rows = jnp.concatenate([rows_of(sides[0]), blocks, rows_of(sides[1])], axis=0)
+    low = jnp.concatenate([strips[0][:, :width], v[:, :width], strips[1][:, :width]], axis=0)
+    high = jnp.concatenate([strips[0][:, n - width :], v[:, n - width :], strips[1][:, n - width :]], axis=0)
+    return [*x_pieces, *swap_ends(at, message(low, rows), message(high, rows), "gy", 1)]
 
 
 def by_core(x, swaps):
@@ -427,10 +435,11 @@
     edge = jnp.where(first_core, shift_two[:, : 2 * size], shift_two[:, size:])
     edge_rows = edge.shape[0] * edge.shape[1]
     spare = -edge_rows % chans
-    message = jnp.concatenate(
-        [cells(b2), jnp.pad(edge.reshape(-1, depth), ((0, spare), (0, 0))).reshape(-1, chans, depth)], axis=0
-    )
-    other = to_core(message)
+    slot = jnp.broadcast_to(slots.astype(jnp.float32), (chans, depth))
+    message = [cells(b2), jnp.pad(edge.reshape(-1, depth), ((0, spare), (0, 0))).reshape(-1, chans, depth), slot[None]]
+    other = to_core(jnp.concatenate(message, axis=0))
+    other_slot = other[-1]
+    slot_rows = [jnp.where(first_core, slot, other_slot)[:8], jnp.where(first_core, other_slot, slot)[:8]]
     edge = other[size * size :].reshape(-1, depth)[:edge_rows].reshape(edge.shape)
     other = other[: size * size].reshape(b2.shape)
     chip = jnp.concatenate([jnp.where(first_core, b2, other), jnp.where(first_core, other, b2)], axis=1)
@@ -472,15 +481,16 @@
         "down_chip",
     )
     x2, q2 = [jnp.where(first_core, v[:, :size], v[:, size:]) for v in (x2, q2)]
-    b3 = jnp.where(first_core, b3[0, 0], b3[0, 1])
 
     lefts = [q0, q1, q2]
     low = jnp.concatenate([cells(q[:2]) for q in lefts], axis=0)
     high = jnp.concatenate([cells(q[-2:]) for q in lefts], axis=0)
     left_ends = swap_ends(at, low, high, "gx", 1)
 
-    slot = jnp.broadcast_to(slots.astype(jnp.float32), (8, depth))
-    shares = lax.all_gather(jnp.concatenate([b3, slot], axis=0)[None], "gy", axis=0, tiled=True)
+    line = [list(range(first, blocks, 2)) for first in range(2)]
+    shares = lax.all_gather(
+        jnp.concatenate([b3[0, 0], b3[0, 1], *slot_rows], axis=0)[None], "gy", axis_index_groups=line, axis=0, tiled=True
+    )
     left_ends, shares = lax.optimization_barrier((left_ends, shares))
     before, after = in_order(at, *left_ends, "gx")
     left_rows, done = [], 0
@@ -498,7 +508,9 @@
     solved = call(
         solve_kernel, where, [shares, coarse_inverse[0, 0]], [tail], [(chans, blocks * depth)], "solve"
     )[0]
-    back = lax.all_gather(solved[None], "gy", axis=0, tiled=True)
+    other = to_core(solved)
+    solved = jnp.concatenate([jnp.where(first_core, solved, other), jnp.where(first_core, other, solved)], axis=0)
+    back = lax.all_gather(solved[None], "gy", axis_index_groups=line, axis=0, tiled=True)
     fix = call(pick_kernel, where, [shares, back], [(6,) + tail], [], "pick")[0]
     lines = lines_around(at, fix, fix, fix)
 

time: 232 us -> 241 us (1.039)
  the two profiles are of different devices: /device:TPU:223 before, /device:TPU:31 now
where the time goes in v3:
time: 241 us; the launch traced here: 240 us
  starting transfers between devices  111 us (46%)
  waiting for transfers between devices  55.6 us (23%)
  blocking collectives  49.6 us (21%)
  Pallas kernels  16.6 us (7%)
  local copies, waits for them, and re-layouts  4.29 us (2%)
    ppermute x25, starting transfers between devices, swap(): return lax.ppermute(x, axis, pairs)  98.2 us
    ppermute x25, waiting for transfers between devices, swap(): return lax.ppermute(x, axis, pairs)  46.3 us
    all_gather x1, blocking collectives, body(): lax.all_gather(jnp.concatenate([b3[0, 0], b3[0, 1], *slot_rows], axis=0)[...  24.9 us
    all_gather x1, blocking collectives, body(): lax.all_gather(solved[None], 'gy', axis_index_groups=line, axis=0, tiled=...  24.7 us
    pallas_call x8, Pallas kernels, call(): pl.pallas_call(kernel, out_shape=[jax.ShapeDtypeStruct(out, jnp.float32)...  16.6 us
    ppermute x4, starting transfers between devices, by_core(): return lax.ppermute(x, ('gx', 'gy'), pairs)  12.3 us
    ppermute x4, waiting for transfers between devices, by_core(): return lax.ppermute(x, ('gx', 'gy'), pairs)  9.24 us
  transfers between devices with their start and end apart: 30, of which 16 were waited for; matrix products, arithmetic and copies ran while one was open for 0% of the time, Pallas kernels for 0%

profile of v3, /device:TPU:31, one launch (start us, length us, event | category | flops | bytes accessed | tf_op | source)
XLA Modules:
  0.0 240.0 jit_solution(6527617762108062301)
XLA Ops:
  4.3 5.0 %collective-permute-start.1 = (f32[27,24,128]{2,1,0:T(8,128)S(1)}, f32[27,24,128]{2,1,0:T(8,128)S(1)}, u32[]{:S(2)}, u32[]{:S(2)}) collective-permute-start(f32[27,24,128]{2,1,0:T(8,128)S(1)} %get-tuple-element.73), channel_id=1, source_target_pairs={{16,32},{32,16},{48,64},{64,48},{80,96},{96,80},{112,128},{128,112... | collective-permute-start | bytes 995336 | tf_op jit(solution)/shard_map/ppermute | solution.py:23
  9.3 3.0 %collective-permute-done.refs_0_ = f32[27,24,128]{2,1,0:T(8,128)S(1)} collective-permute-done((f32[27,24,128]{2,1,0:T(8,128)S(1)}, f32[27,24,128]{2,1,0:T(8,128)S(1)}, u32[]{:S(2)}, u32[]{:S(2)}) %collective-permute-start) | collective-permute-done | bytes 331808 | tf_op jit(solution)/shard_map/ppermute | solution.py:23
  12.4 5.5 %collective-permute-done.1.refs_1_ = f32[27,24,128]{2,1,0:T(8,128)S(1)} collective-permute-done((f32[27,24,128]{2,1,0:T(8,128)S(1)}, f32[27,24,128]{2,1,0:T(8,128)S(1)}, u32[]{:S(2)}, u32[]{:S(2)}) %collective-permute-start.1) | collective-permute-done | bytes 331808 | tf_op jit(solution)/shard_map/ppermute | solution.py:23
  18.3 3.8 %collective-permute-start.2 = (f32[50,24,128]{2,1,0:T(8,128)S(1)}, f32[50,24,128]{2,1,0:T(8,128)S(1)}, u32[]{:S(2)}, u32[]{:S(2)}) collective-permute-start(f32[50,24,128]{2,1,0:T(8,128)S(1)} %get-tuple-element.58), channel_id=1, source_target_pairs={{0,1},{1,0},{2,3},{3,2},{4,5},{5,4},{6,7},{7,6},{8,9},{9,8},{10,11... | collective-permute-start | bytes 1843208 | tf_op jit(solution)/shard_map/ppermute | solution.py:23
  22.1 3.9 %collective-permute-start.3 = (f32[50,24,128]{2,1,0:T(8,128)S(1)}, f32[50,24,128]{2,1,0:T(8,128)S(1)}, u32[]{:S(2)}, u32[]{:S(2)}) collective-permute-start(f32[50,24,128]{2,1,0:T(8,128)S(1)} %get-tuple-element.57), channel_id=1, source_target_pairs={{1,2},{2,1},{3,4},{4,3},{5,6},{6,5},{7,8},{8,7},{9,10},{10,9},{11,... | collective-permute-start | bytes 1843208 | tf_op jit(solution)/shard_map/ppermute | solution.py:23
  26.0 8.1 %collective-permute-done.3.refs_3_ = f32[50,24,128]{2,1,0:T(8,128)S(1)} collective-permute-done((f32[50,24,128]{2,1,0:T(8,128)S(1)}, f32[50,24,128]{2,1,0:T(8,128)S(1)}, u32[]{:S(2)}, u32[]{:S(2)}) %collective-permute-start.3) | collective-permute-done | bytes 614432 | tf_op jit(solution)/shard_map/ppermute | solution.py:23
  34.1 3.9 %down_fine.1 = (f32[8,8,24,128]{3,2,1,0:T(8,128)S(1)}, f32[8,8,24,128]{3,2,1,0:T(8,128)S(1)}, f32[4,4,24,128]{3,2,1,0:T(8,128)S(1)}, f32[24,24,128]{2,1,0:T(8,12...) custom-call(s32[8]{0:T(128)S(1)} %stack.31.where, f32[8,8,24,128]{3,2,1,0:T(8,128)S(1)} %bitcast.85, ...), custom_call_target="tpu_custom_call" | custom-call | tf_op jit(solution)/shard_map/down_fine/pallas_call | solution.py:310
  40.0 5.0 %collective-permute-start.5 = (f32[12,24,128]{2,1,0:T(8,128)S(1)}, f32[12,24,128]{2,1,0:T(8,128)S(1)}, u32[]{:S(2)}, u32[]{:S(2)}) collective-permute-start(f32[12,24,128]{2,1,0:T(8,128)S(1)} %bitcast.136), channel_id=1, source_target_pairs={{16,32},{32,16},{48,64},{64,48},{80,96},{96,80},{112,128},{128,112... | collective-permute-start | bytes 442376 | tf_op jit(solution)/shard_map/ppermute | solution.py:23
  45.0 4.2 %collective-permute-done.5.refs_1_ = f32[12,24,128]{2,1,0:T(8,128)S(1)} collective-permute-done((f32[12,24,128]{2,1,0:T(8,128)S(1)}, f32[12,24,128]{2,1,0:T(8,128)S(1)}, u32[]{:S(2)}, u32[]{:S(2)}) %collective-permute-start.5) | collective-permute-done | bytes 147488 | tf_op jit(solution)/shard_map/ppermute | solution.py:23
  51.3 5.9 %collective-permute-start.7 = (f32[30,24,128]{2,1,0:T(8,128)S(1)}, f32[30,24,128]{2,1,0:T(8,128)S(1)}, u32[]{:S(2)}, u32[]{:S(2)}) collective-permute-start(f32[30,24,128]{2,1,0:T(8,128)S(1)} %bitcast.124), channel_id=1, source_target_pairs={{1,2},{2,1},{3,4},{4,3},{5,6},{6,5},{7,8},{8,7},{9,10},{10,9},{11,... | collective-permute-start | bytes 1105928 | tf_op jit(solution)/shard_map/ppermute | solution.py:23
  57.8 4.5 %collective-permute-done.7.refs_3_ = f32[30,24,128]{2,1,0:T(8,128)S(1)} collective-permute-done((f32[30,24,128]{2,1,0:T(8,128)S(1)}, f32[30,24,128]{2,1,0:T(8,128)S(1)}, u32[]{:S(2)}, u32[]{:S(2)}) %collective-permute-start.7) | collective-permute-done | bytes 368672 | tf_op jit(solution)/shard_map/ppermute | solution.py:23
  67.5 5.0 %collective-permute-start.9 = (f32[2,4,24,128]{3,2,1,0:T(8,128)S(1)}, f32[2,4,24,128]{3,2,1,0:T(8,128)S(1)}, u32[]{:S(2)}, u32[]{:S(2)}) collective-permute-start(f32[2,4,24,128]{3,2,1,0:T(8,128)S(1)} %pad_maximum_fusion.20), channel_id=1, source_target_pairs={{0,16},{16,0},{32,48},{48,32},{64,80},{80,64},{96,112},{112,96},{1... | collective-permute-start | bytes 294920 | tf_op jit(solution)/shard_map/ppermute | solution.py:388
  74.5 4.6 %collective-permute-done.10 = f32[1,4,24,128]{3,2,1,0:T(8,128)S(1)} collective-permute-done((f32[1,4,24,128]{3,2,1,0:T(8,128)S(1)}, f32[1,4,24,128]{3,2,1,0:T(8,128)S(1)}, u32[]{:S(2)}, u32[]{:S(2)}) %collective-permute-start.10) | collective-permute-done | bytes 49184 | tf_op jit(solution)/shard_map/ppermute | solution.py:388
  83.2 9.6 %collective-permute-start.13 = (f32[6,3,24,128]{3,2,1,0:T(8,128)S(1)}, f32[6,3,24,128]{3,2,1,0:T(8,128)S(1)}, u32[]{:S(2)}, u32[]{:S(2)}) collective-permute-start(f32[6,3,24,128]{3,2,1,0:T(8,128)S(1)} %collective-permute-done.12), channel_id=1, source_target_pairs={{0,1},{1,0},{2,3},{3,2},{4,5},{5,4},{6,7},{7,6},{8,9},{9,8},{10,11... | collective-permute-start | bytes 663560 | tf_op jit(solution)/shard_map/ppermute | solution.py:23
  95.4 3.6 %collective-permute-start.14 = (f32[28,24,128]{2,1,0:T(8,128)S(1)}, f32[28,24,128]{2,1,0:T(8,128)S(1)}, u32[]{:S(2)}, u32[]{:S(2)}) collective-permute-start(f32[28,24,128]{2,1,0:T(8,128)S(1)} %get-tuple-element.72), channel_id=1, source_target_pairs={{0,16},{16,0},{32,48},{48,32},{64,80},{80,64},{96,112},{112,96},{1... | collective-permute-start | bytes 1032200 | tf_op jit(solution)/shard_map/ppermute | solution.py:23
  99.0 5.0 %collective-permute-start.15 = (f32[28,24,128]{2,1,0:T(8,128)S(1)}, f32[28,24,128]{2,1,0:T(8,128)S(1)}, u32[]{:S(2)}, u32[]{:S(2)}) collective-permute-start(f32[28,24,128]{2,1,0:T(8,128)S(1)} %get-tuple-element.71), channel_id=1, source_target_pairs={{16,32},{32,16},{48,64},{64,48},{80,96},{96,80},{112,128},{128,112... | collective-permute-start | bytes 1032200 | tf_op jit(solution)/shard_map/ppermute | solution.py:23
  104.0 24.9 %all-gather = f32[512,128]{1,0:T(8,128)S(1)} all-gather(f32[64,128]{1,0:T(8,128)S(1)} %pad_maximum_fusion.23), channel_id=2, replica_groups={{0,2,4,6,8,10,12,14},{1,3,5,7,9,11,13,15},{16,18,20,22,24,26,28,30},{17..., dimensions={0}, use_global_device_ids=true | all-gather | bytes 294912 | tf_op jit(solution)/shard_map/all_gather | solution.py:491
  132.1 8.2 %collective-permute-start.16 = (f32[24,128]{1,0:T(8,128)S(1)}, f32[24,128]{1,0:T(8,128)S(1)}, u32[]{:S(2)}, u32[]{:S(2)}) collective-permute-start(f32[24,128]{1,0:T(8,128)S(1)} %solve.1), channel_id=1, source_target_pairs={{0,1},{1,0},{2,3},{3,2},{4,5},{5,4},{6,7},{7,6},{8,9},{9,8},{10,11... | collective-permute-start | bytes 36872 | tf_op jit(solution)/shard_map/ppermute | solution.py:23
  144.8 24.7 %all-gather.1 = f32[384,128]{1,0:T(8,128)S(1)} all-gather(f32[48,128]{1,0:T(8,128)S(1)} %pad_maximum_fusion.24), channel_id=3, replica_groups={{0,2,4,6,8,10,12,14},{1,3,5,7,9,11,13,15},{16,18,20,22,24,26,28,30},{17..., dimensions={0}, use_global_device_ids=true | all-gather | bytes 221184 | tf_op jit(solution)/shard_map/all_gather | solution.py:513
  170.1 3.5 %collective-permute-start.17 = (f32[6,24,128]{2,1,0:T(8,128)S(1)}, f32[6,24,128]{2,1,0:T(8,128)S(1)}, u32[]{:S(2)}, u32[]{:S(2)}) collective-permute-start(f32[6,24,128]{2,1,0:T(8,128)S(1)} %pick.1.coarse_own), channel_id=1, source_target_pairs={{0,16},{16,0},{32,48},{48,32},{64,80},{80,64},{96,112},{112,96},{1... | collective-permute-start | bytes 221192 | tf_op jit(solution)/shard_map/ppermute | solution.py:388
  175.5 3.0 %collective-permute-done.17 = f32[6,24,128]{2,1,0:T(8,128)S(1)} collective-permute-done((f32[6,24,128]{2,1,0:T(8,128)S(1)}, f32[6,24,128]{2,1,0:T(8,128)S(1)}, u32[]{:S(2)}, u32[]{:S(2)}) %collective-permute-start.17) | collective-permute-done | bytes 73760 | tf_op jit(solution)/shard_map/ppermute | solution.py:388
  180.2 8.3 %collective-permute-start.19 = (f32[12,24,128]{2,1,0:T(8,128)S(1)}, f32[12,24,128]{2,1,0:T(8,128)S(1)}, u32[]{:S(2)}, u32[]{:S(2)}) collective-permute-start(f32[12,24,128]{2,1,0:T(8,128)S(1)} %constant_dynamic-update-slice_fusion.3.refs_0_), channel_id=1, source_target_pairs={{0,1},{1,0},{2,3},{3,2},{4,5},{5,4},{6,7},{7,6},{8,9},{9,8},{10,11... | collective-permute-start | bytes 442376 | tf_op jit(solution)/shard_map/ppermute | solution.py:23
  190.8 3.6 %collective-permute-start.22 = (f32[4,24,128]{2,1,0:T(8,128)S(1)}, f32[4,24,128]{2,1,0:T(8,128)S(1)}, u32[]{:S(2)}, u32[]{:S(2)}) collective-permute-start(f32[4,24,128]{2,1,0:T(8,128)S(1)} %bitcast.92), channel_id=1, source_target_pairs={{0,16},{16,0},{32,48},{48,32},{64,80},{80,64},{96,112},{112,96},{1... | collective-permute-start | bytes 147464 | tf_op jit(solution)/shard_map/ppermute | solution.py:23
  194.4 3.7 %collective-permute-start.23 = (f32[4,24,128]{2,1,0:T(8,128)S(1)}, f32[4,24,128]{2,1,0:T(8,128)S(1)}, u32[]{:S(2)}, u32[]{:S(2)}) collective-permute-start(f32[4,24,128]{2,1,0:T(8,128)S(1)} %bitcast.93), channel_id=1, source_target_pairs={{16,32},{32,16},{48,64},{64,48},{80,96},{96,80},{112,128},{128,112... | collective-permute-start | bytes 147464 | tf_op jit(solution)/shard_map/ppermute | solution.py:23
  198.2 4.4 %collective-permute-done.23.refs_1_ = f32[4,24,128]{2,1,0:T(8,128)S(1)} collective-permute-done((f32[4,24,128]{2,1,0:T(8,128)S(1)}, f32[4,24,128]{2,1,0:T(8,128)S(1)}, u32[]{:S(2)}, u32[]{:S(2)}) %collective-permute-start.23) | collective-permute-done | bytes 49184 | tf_op jit(solution)/shard_map/ppermute | solution.py:23
  202.6 3.7 %collective-permute-start.24 = (f32[12,24,128]{2,1,0:T(8,128)S(1)}, f32[12,24,128]{2,1,0:T(8,128)S(1)}, u32[]{:S(2)}, u32[]{:S(2)}) collective-permute-start(f32[12,24,128]{2,1,0:T(8,128)S(1)} %bitcast.134), channel_id=1, source_target_pairs={{0,1},{1,0},{2,3},{3,2},{4,5},{5,4},{6,7},{7,6},{8,9},{9,8},{10,11... | collective-permute-start | bytes 442376 | tf_op jit(solution)/shard_map/ppermute | solution.py:23
  208.9 3.9 %collective-permute-done.25.refs_3_ = f32[12,24,128]{2,1,0:T(8,128)S(1)} collective-permute-done((f32[12,24,128]{2,1,0:T(8,128)S(1)}, f32[12,24,128]{2,1,0:T(8,128)S(1)}, u32[]{:S(2)}, u32[]{:S(2)}) %collective-permute-start.25) | collective-permute-done | bytes 147488 | tf_op jit(solution)/shard_map/ppermute | solution.py:23
  216.8 3.7 %collective-permute-start.27 = (f32[8,24,128]{2,1,0:T(8,128)S(1)}, f32[8,24,128]{2,1,0:T(8,128)S(1)}, u32[]{:S(2)}, u32[]{:S(2)}) collective-permute-start(f32[8,24,128]{2,1,0:T(8,128)S(1)} %bitcast.140), channel_id=1, source_target_pairs={{16,32},{32,16},{48,64},{64,48},{80,96},{96,80},{112,128},{128,112... | collective-permute-start | bytes 294920 | tf_op jit(solution)/shard_map/ppermute | solution.py:23
  220.5 4.9 %collective-permute-done.27.refs_1_ = f32[8,24,128]{2,1,0:T(8,128)S(1)} collective-permute-done((f32[8,24,128]{2,1,0:T(8,128)S(1)}, f32[8,24,128]{2,1,0:T(8,128)S(1)}, u32[]{:S(2)}, u32[]{:S(2)}) %collective-permute-start.27) | collective-permute-done | bytes 98336 | tf_op jit(solution)/shard_map/ppermute | solution.py:23
  227.5 4.2 %collective-permute-start.29 = (f32[16,24,128]{2,1,0:T(8,128)S(1)}, f32[16,24,128]{2,1,0:T(8,128)S(1)}, u32[]{:S(2)}, u32[]{:S(2)}) collective-permute-start(f32[16,24,128]{2,1,0:T(8,128)S(1)} %bitcast.131), channel_id=1, source_target_pairs={{1,2},{2,1},{3,4},{4,3},{5,6},{6,5},{7,8},{8,7},{9,10},{10,9},{11,... | collective-permute-start | bytes 589832 | tf_op jit(solution)/shard_map/ppermute | solution.py:23
  231.7 3.3 %collective-permute-done.29.refs_3_ = f32[16,24,128]{2,1,0:T(8,128)S(1)} collective-permute-done((f32[16,24,128]{2,1,0:T(8,128)S(1)}, f32[16,24,128]{2,1,0:T(8,128)S(1)}, u32[]{:S(2)}, u32[]{:S(2)}) %collective-permute-start.29) | collective-permute-done | bytes 196640 | tf_op jit(solution)/shard_map/ppermute | solution.py:23
  235.1 3.9 %up_8.1 = f32[8,8,24,128]{3,2,1,0:T(8,128)S(1)} custom-call(s32[8]{0:T(128)S(1)} %stack.31.where, f32[4,4,24,128]{3,2,1,0:T(8,128)S(1)} %up_4.1.coarse_own, f32[8,24,128]{2,1,0:T(8,128)S(1)} %collective-permute-done.26.refs_0_, f32[8,24,128]{2,1,0:T(8,128)S(1)} %collective-permute-done.27.refs_1_, f32[16,24,128]{2,1,0:T(8,128)S(1)} %collective-permute-done.28.refs_2_, ...), custom_call_target="tpu_custom_call" | custom-call | tf_op jit(solution)/shard_map/up_8/pallas_call | solution.py:310
  (119 shorter events, 45.9 us)
Async XLA Ops:
  0.1 1.7 copy-start.1
  1.8 10.6 %collective-permute-start = (f32[27,24,128]{2,1,0:T(8,128)S(1)}, f32[27,24,128]{2,1,0:T(8,128)S(1)}, u32[]{:S(2)}, u32[]{:S(2)}) collective-permute-start(f32[27,24,128]{2,1,0:T(8,128)S(1)} %get-tuple-element.74), channel_id=1, source_target_pairs={{0,16},{16,0},{32,48},{48,32},{64,80},{80,64},{96,112},{112,96},{1... | collective-permute-start | bytes 995336 | tf_op jit(solution)/shard_map/ppermute | solution.py:23
  4.3 13.6 %collective-permute-start.1 = (f32[27,24,128]{2,1,0:T(8,128)S(1)}, f32[27,24,128]{2,1,0:T(8,128)S(1)}, u32[]{:S(2)}, u32[]{:S(2)}) collective-permute-start(f32[27,24,128]{2,1,0:T(8,128)S(1)} %get-tuple-element.73), channel_id=1, source_target_pairs={{16,32},{32,16},{48,64},{64,48},{80,96},{96,80},{112,128},{128,112... | collective-permute-start | bytes 995336 | tf_op jit(solution)/shard_map/ppermute | solution.py:23
  18.3 7.7 %collective-permute-start.2 = (f32[50,24,128]{2,1,0:T(8,128)S(1)}, f32[50,24,128]{2,1,0:T(8,128)S(1)}, u32[]{:S(2)}, u32[]{:S(2)}) collective-permute-start(f32[50,24,128]{2,1,0:T(8,128)S(1)} %get-tuple-element.58), channel_id=1, source_target_pairs={{0,1},{1,0},{2,3},{3,2},{4,5},{5,4},{6,7},{7,6},{8,9},{9,8},{10,11... | collective-permute-start | bytes 1843208 | tf_op jit(solution)/shard_map/ppermute | solution.py:23
  22.1 12.0 %collective-permute-start.3 = (f32[50,24,128]{2,1,0:T(8,128)S(1)}, f32[50,24,128]{2,1,0:T(8,128)S(1)}, u32[]{:S(2)}, u32[]{:S(2)}) collective-permute-start(f32[50,24,128]{2,1,0:T(8,128)S(1)} %get-tuple-element.57), channel_id=1, source_target_pairs={{1,2},{2,1},{3,4},{4,3},{5,6},{6,5},{7,8},{8,7},{9,10},{10,9},{11,... | collective-permute-start | bytes 1843208 | tf_op jit(solution)/shard_map/ppermute | solution.py:23
  38.1 7.0 %collective-permute-start.4 = (f32[12,24,128]{2,1,0:T(8,128)S(1)}, f32[12,24,128]{2,1,0:T(8,128)S(1)}, u32[]{:S(2)}, u32[]{:S(2)}) collective-permute-start(f32[12,24,128]{2,1,0:T(8,128)S(1)} %bitcast.137), channel_id=1, source_target_pairs={{0,16},{16,0},{32,48},{48,32},{64,80},{80,64},{96,112},{112,96},{1... | collective-permute-start | bytes 442376 | tf_op jit(solution)/shard_map/ppermute | solution.py:23
  40.0 9.2 %collective-permute-start.5 = (f32[12,24,128]{2,1,0:T(8,128)S(1)}, f32[12,24,128]{2,1,0:T(8,128)S(1)}, u32[]{:S(2)}, u32[]{:S(2)}) collective-permute-start(f32[12,24,128]{2,1,0:T(8,128)S(1)} %bitcast.136), channel_id=1, source_target_pairs={{16,32},{32,16},{48,64},{64,48},{80,96},{96,80},{112,128},{128,112... | collective-permute-start | bytes 442376 | tf_op jit(solution)/shard_map/ppermute | solution.py:23
  49.3 8.5 %collective-permute-start.6 = (f32[30,24,128]{2,1,0:T(8,128)S(1)}, f32[30,24,128]{2,1,0:T(8,128)S(1)}, u32[]{:S(2)}, u32[]{:S(2)}) collective-permute-start(f32[30,24,128]{2,1,0:T(8,128)S(1)} %bitcast.125), channel_id=1, source_target_pairs={{0,1},{1,0},{2,3},{3,2},{4,5},{5,4},{6,7},{7,6},{8,9},{9,8},{10,11... | collective-permute-start | bytes 1105928 | tf_op jit(solution)/shard_map/ppermute | solution.py:23
  51.3 11.1 %collective-permute-start.7 = (f32[30,24,128]{2,1,0:T(8,128)S(1)}, f32[30,24,128]{2,1,0:T(8,128)S(1)}, u32[]{:S(2)}, u32[]{:S(2)}) collective-permute-start(f32[30,24,128]{2,1,0:T(8,128)S(1)} %bitcast.124), channel_id=1, source_target_pairs={{1,2},{2,1},{3,4},{4,3},{5,6},{6,5},{7,8},{8,7},{9,10},{10,9},{11,... | collective-permute-start | bytes 1105928 | tf_op jit(solution)/shard_map/ppermute | solution.py:23
  64.3 3.2 %collective-permute-start.8 = (f32[6,24,128]{2,1,0:T(8,128)S(1)}, f32[6,24,128]{2,1,0:T(8,128)S(1)}, u32[]{:S(2)}, u32[]{:S(2)}) collective-permute-start(f32[6,24,128]{2,1,0:T(8,128)S(1)} %pad_maximum_fusion.22), channel_id=1, source_target_pairs={{0,1},{1,0},{2,3},{3,2},{4,5},{5,4},{6,7},{7,6},{8,9},{9,8},{10,11... | collective-permute-start | bytes 221192 | tf_op jit(solution)/shard_map/ppermute | solution.py:23
  67.5 11.5 %collective-permute-start.9 = (f32[2,4,24,128]{3,2,1,0:T(8,128)S(1)}, f32[2,4,24,128]{3,2,1,0:T(8,128)S(1)}, u32[]{:S(2)}, u32[]{:S(2)}) collective-permute-start(f32[2,4,24,128]{3,2,1,0:T(8,128)S(1)} %pad_maximum_fusion.20), channel_id=1, source_target_pairs={{0,16},{16,0},{32,48},{48,32},{64,80},{80,64},{96,112},{112,96},{1... | collective-permute-start | bytes 294920 | tf_op jit(solution)/shard_map/ppermute | solution.py:388
  72.5 6.5 %collective-permute-start.10 = (f32[1,4,24,128]{3,2,1,0:T(8,128)S(1)}, f32[1,4,24,128]{3,2,1,0:T(8,128)S(1)}, u32[]{:S(2)}, u32[]{:S(2)}) collective-permute-start(f32[1,4,24,128]{3,2,1,0:T(8,128)S(1)} %fusion.13), channel_id=1, source_target_pairs={{32,64},{64,32},{48,80},{80,48},{96,128},{128,96},{112,144},{144,1... | collective-permute-start | bytes 147464 | tf_op jit(solution)/shard_map/ppermute | solution.py:388
  79.1 3.3 %collective-permute-start.11 = (f32[12,24,128]{2,1,0:T(8,128)S(1)}, f32[12,24,128]{2,1,0:T(8,128)S(1)}, u32[]{:S(2)}, u32[]{:S(2)}) collective-permute-start(f32[12,24,128]{2,1,0:T(8,128)S(1)} %pad_maximum_fusion.17), channel_id=1, source_target_pairs={{0,1},{1,0},{2,3},{3,2},{4,5},{5,4},{6,7},{7,6},{8,9},{9,8},{10,11... | collective-permute-start | bytes 442376 | tf_op jit(solution)/shard_map/ppermute | solution.py:23
  82.5 0.7 collective-permute-start.12
  83.2 10.6 %collective-permute-start.13 = (f32[6,3,24,128]{3,2,1,0:T(8,128)S(1)}, f32[6,3,24,128]{3,2,1,0:T(8,128)S(1)}, u32[]{:S(2)}, u32[]{:S(2)}) collective-permute-start(f32[6,3,24,128]{3,2,1,0:T(8,128)S(1)} %collective-permute-done.12), channel_id=1, source_target_pairs={{0,1},{1,0},{2,3},{3,2},{4,5},{5,4},{6,7},{7,6},{8,9},{9,8},{10,11... | collective-permute-start | bytes 663560 | tf_op jit(solution)/shard_map/ppermute | solution.py:23
  95.4 33.6 %collective-permute-start.14 = (f32[28,24,128]{2,1,0:T(8,128)S(1)}, f32[28,24,128]{2,1,0:T(8,128)S(1)}, u32[]{:S(2)}, u32[]{:S(2)}) collective-permute-start(f32[28,24,128]{2,1,0:T(8,128)S(1)} %get-tuple-element.72), channel_id=1, source_target_pairs={{0,16},{16,0},{32,48},{48,32},{64,80},{80,64},{96,112},{112,96},{1... | collective-permute-start | bytes 1032200 | tf_op jit(solution)/shard_map/ppermute | solution.py:23
  99.0 29.9 %collective-permute-start.15 = (f32[28,24,128]{2,1,0:T(8,128)S(1)}, f32[28,24,128]{2,1,0:T(8,128)S(1)}, u32[]{:S(2)}, u32[]{:S(2)}) collective-permute-start(f32[28,24,128]{2,1,0:T(8,128)S(1)} %get-tuple-element.71), channel_id=1, source_target_pairs={{16,32},{32,16},{48,64},{64,48},{80,96},{96,80},{112,128},{128,112... | collective-permute-start | bytes 1032200 | tf_op jit(solution)/shard_map/ppermute | solution.py:23
  129.2 1.2 copy-start
  132.1 12.7 %collective-permute-start.16 = (f32[24,128]{1,0:T(8,128)S(1)}, f32[24,128]{1,0:T(8,128)S(1)}, u32[]{:S(2)}, u32[]{:S(2)}) collective-permute-start(f32[24,128]{1,0:T(8,128)S(1)} %solve.1), channel_id=1, source_target_pairs={{0,1},{1,0},{2,3},{3,2},{4,5},{5,4},{6,7},{7,6},{8,9},{9,8},{10,11... | collective-permute-start | bytes 36872 | tf_op jit(solution)/shard_map/ppermute | solution.py:23
  140.4 49.1 %collective-permute-start.20 = (f32[52,24,128]{2,1,0:T(8,128)S(1)}, f32[52,24,128]{2,1,0:T(8,128)S(1)}, u32[]{:S(2)}, u32[]{:S(2)}) collective-permute-start(f32[52,24,128]{2,1,0:T(8,128)S(1)} %get-tuple-element.56), channel_id=1, source_target_pairs={{0,1},{1,0},{2,3},{3,2},{4,5},{5,4},{6,7},{7,6},{8,9},{9,8},{10,11... | collective-permute-start | bytes 1916936 | tf_op jit(solution)/shard_map/ppermute | solution.py:23
  142.4 47.2 %collective-permute-start.21 = (f32[52,24,128]{2,1,0:T(8,128)S(1)}, f32[52,24,128]{2,1,0:T(8,128)S(1)}, u32[]{:S(2)}, u32[]{:S(2)}) collective-permute-start(f32[52,24,128]{2,1,0:T(8,128)S(1)} %get-tuple-element.55), channel_id=1, source_target_pairs={{1,2},{2,1},{3,4},{4,3},{5,6},{6,5},{7,8},{8,7},{9,10},{10,9},{11,... | collective-permute-start | bytes 1916936 | tf_op jit(solution)/shard_map/ppermute | solution.py:23
  170.1 8.4 %collective-permute-start.17 = (f32[6,24,128]{2,1,0:T(8,128)S(1)}, f32[6,24,128]{2,1,0:T(8,128)S(1)}, u32[]{:S(2)}, u32[]{:S(2)}) collective-permute-start(f32[6,24,128]{2,1,0:T(8,128)S(1)} %pick.1.coarse_own), channel_id=1, source_target_pairs={{0,16},{16,0},{32,48},{48,32},{64,80},{80,64},{96,112},{112,96},{1... | collective-permute-start | bytes 221192 | tf_op jit(solution)/shard_map/ppermute | solution.py:388
  173.6 6.6 %collective-permute-start.18 = (f32[6,24,128]{2,1,0:T(8,128)S(1)}, f32[6,24,128]{2,1,0:T(8,128)S(1)}, u32[]{:S(2)}, u32[]{:S(2)}) collective-permute-start(f32[6,24,128]{2,1,0:T(8,128)S(1)} %pick.1.coarse_own), channel_id=1, source_target_pairs={{32,64},{64,32},{48,80},{80,48},{96,128},{128,96},{112,144},{144,1... | collective-permute-start | bytes 221192 | tf_op jit(solution)/shard_map/ppermute | solution.py:388
  180.2 9.3 %collective-permute-start.19 = (f32[12,24,128]{2,1,0:T(8,128)S(1)}, f32[12,24,128]{2,1,0:T(8,128)S(1)}, u32[]{:S(2)}, u32[]{:S(2)}) collective-permute-start(f32[12,24,128]{2,1,0:T(8,128)S(1)} %constant_dynamic-update-slice_fusion.3.refs_0_), channel_id=1, source_target_pairs={{0,1},{1,0},{2,3},{3,2},{4,5},{5,4},{6,7},{7,6},{8,9},{9,8},{10,11... | collective-permute-start | bytes 442376 | tf_op jit(solution)/shard_map/ppermute | solution.py:23
  190.8 7.4 %collective-permute-start.22 = (f32[4,24,128]{2,1,0:T(8,128)S(1)}, f32[4,24,128]{2,1,0:T(8,128)S(1)}, u32[]{:S(2)}, u32[]{:S(2)}) collective-permute-start(f32[4,24,128]{2,1,0:T(8,128)S(1)} %bitcast.92), channel_id=1, source_target_pairs={{0,16},{16,0},{32,48},{48,32},{64,80},{80,64},{96,112},{112,96},{1... | collective-permute-start | bytes 147464 | tf_op jit(solution)/shard_map/ppermute | solution.py:23
  194.4 8.2 %collective-permute-start.23 = (f32[4,24,128]{2,1,0:T(8,128)S(1)}, f32[4,24,128]{2,1,0:T(8,128)S(1)}, u32[]{:S(2)}, u32[]{:S(2)}) collective-permute-start(f32[4,24,128]{2,1,0:T(8,128)S(1)} %bitcast.93), channel_id=1, source_target_pairs={{16,32},{32,16},{48,64},{64,48},{80,96},{96,80},{112,128},{128,112... | collective-permute-start | bytes 147464 | tf_op jit(solution)/shard_map/ppermute | solution.py:23
  202.6 6.2 %collective-permute-start.24 = (f32[12,24,128]{2,1,0:T(8,128)S(1)}, f32[12,24,128]{2,1,0:T(8,128)S(1)}, u32[]{:S(2)}, u32[]{:S(2)}) collective-permute-start(f32[12,24,128]{2,1,0:T(8,128)S(1)} %bitcast.134), channel_id=1, source_target_pairs={{0,1},{1,0},{2,3},{3,2},{4,5},{5,4},{6,7},{7,6},{8,9},{9,8},{10,11... | collective-permute-start | bytes 442376 | tf_op jit(solution)/shard_map/ppermute | solution.py:23
  206.3 6.5 %collective-permute-start.25 = (f32[12,24,128]{2,1,0:T(8,128)S(1)}, f32[12,24,128]{2,1,0:T(8,128)S(1)}, u32[]{:S(2)}, u32[]{:S(2)}) collective-permute-start(f32[12,24,128]{2,1,0:T(8,128)S(1)} %bitcast.135), channel_id=1, source_target_pairs={{1,2},{2,1},{3,4},{4,3},{5,6},{6,5},{7,8},{8,7},{9,10},{10,9},{11,... | collective-permute-start | bytes 442376 | tf_op jit(solution)/shard_map/ppermute | solution.py:23
  214.8 5.7 %collective-permute-start.26 = (f32[8,24,128]{2,1,0:T(8,128)S(1)}, f32[8,24,128]{2,1,0:T(8,128)S(1)}, u32[]{:S(2)}, u32[]{:S(2)}) collective-permute-start(f32[8,24,128]{2,1,0:T(8,128)S(1)} %bitcast.141), channel_id=1, source_target_pairs={{0,16},{16,0},{32,48},{48,32},{64,80},{80,64},{96,112},{112,96},{1... | collective-permute-start | bytes 294920 | tf_op jit(solution)/shard_map/ppermute | solution.py:23
  216.8 8.7 %collective-permute-start.27 = (f32[8,24,128]{2,1,0:T(8,128)S(1)}, f32[8,24,128]{2,1,0:T(8,128)S(1)}, u32[]{:S(2)}, u32[]{:S(2)}) collective-permute-start(f32[8,24,128]{2,1,0:T(8,128)S(1)} %bitcast.140), channel_id=1, source_target_pairs={{16,32},{32,16},{48,64},{64,48},{80,96},{96,80},{112,128},{128,112... | collective-permute-start | bytes 294920 | tf_op jit(solution)/shard_map/ppermute | solution.py:23
  225.5 6.2 %collective-permute-start.28 = (f32[16,24,128]{2,1,0:T(8,128)S(1)}, f32[16,24,128]{2,1,0:T(8,128)S(1)}, u32[]{:S(2)}, u32[]{:S(2)}) collective-permute-start(f32[16,24,128]{2,1,0:T(8,128)S(1)} %bitcast.132), channel_id=1, source_target_pairs={{0,1},{1,0},{2,3},{3,2},{4,5},{5,4},{6,7},{7,6},{8,9},{9,8},{10,11... | collective-permute-start | bytes 589832 | tf_op jit(solution)/shard_map/ppermute | solution.py:23
  227.5 7.6 %collective-permute-start.29 = (f32[16,24,128]{2,1,0:T(8,128)S(1)}, f32[16,24,128]{2,1,0:T(8,128)S(1)}, u32[]{:S(2)}, u32[]{:S(2)}) collective-permute-start(f32[16,24,128]{2,1,0:T(8,128)S(1)} %bitcast.131), channel_id=1, source_target_pairs={{1,2},{2,1},{3,4},{4,3},{5,6},{6,5},{7,8},{8,7},{9,10},{10,9},{11,... | collective-permute-start | bytes 589832 | tf_op jit(solution)/shard_map/ppermute | solution.py:23

commit v4 on v3

--- a/solution.py
+++ b/solution.py
@@ -223,14 +223,12 @@
 
 
 def solve_kernel(where, shares, inverse, solved, ordered):
-    chips, _, depth = shares.shape
+    count, rows, depth = shares.shape
     chans = solved.shape[0]
-    count = 2 * chips
     for m in range(count):
         block = jnp.zeros((chans, depth), jnp.float32)
         for j in range(count):
-            slot = shares[j // 2, 2 * chans + 8 * (j % 2) : 2 * chans + 8 * (j % 2) + 1, :]
-            block = jnp.where(slot == float(m), shares[j // 2, j % 2 * chans : (j % 2 + 1) * chans, :], block)
+            block = jnp.where(shares[j, chans : chans + 1, :] == float(m), shares[j, 0:chans, :], block)
         ordered[:, m * depth : (m + 1) * depth] = block
     solved[...] = lax.dot_general(
         ordered[...],
@@ -242,16 +240,14 @@
 
 
 def pick_kernel(where, shares, back, picked):
-    chips, rows, depth = back.shape
-    chans = rows // 2
+    count, chans, depth = back.shape
     for k in range(picked.shape[0]):
         j = where[1] - where[2] + k - 2
-        chip = jnp.clip(where[6] + k // 2 - 1, 0, chips - 1)
-        slot = shares[chip, pl.ds(2 * chans + 8 * (k % 2), 1), :]
-        slot = jnp.where((j >= 0) & (j < 2 * chips), slot, -1.0)
+        slot = shares[jnp.clip(j, 0, count - 1), pl.ds(chans, 1), :]
+        slot = jnp.where((j >= 0) & (j < count), slot, -1.0)
         block = jnp.zeros((chans, depth), jnp.float32)
-        for m in range(2 * chips):
-            block = jnp.where(slot == float(m), back[m // 2, m % 2 * chans : (m % 2 + 1) * chans, :], block)
+        for m in range(count):
+            block = jnp.where(slot == float(m), back[m], block)
         picked[k] = block
 
 
@@ -322,8 +318,7 @@
     core = parity("gy", 1)
     line, far = parity("gx", 1), parity("gx", 2)
     numbers = [lax.axis_index("gx"), lax.axis_index("gy"), core, line, line ^ core, far ^ core]
-    numbers += [lax.div(lax.axis_index("gy"), 2), jnp.zeros_like(core)]
-    where = jnp.stack(numbers).astype(jnp.int32)
+    where = jnp.stack(numbers + [jnp.zeros_like(core)] * 2).astype(jnp.int32)
     sides = {
         "gx": line == 0,
         "gy": core == 0,
@@ -435,11 +430,10 @@
     edge = jnp.where(first_core, shift_two[:, : 2 * size], shift_two[:, size:])
     edge_rows = edge.shape[0] * edge.shape[1]
     spare = -edge_rows % chans
-    slot = jnp.broadcast_to(slots.astype(jnp.float32), (chans, depth))
-    message = [cells(b2), jnp.pad(edge.reshape(-1, depth), ((0, spare), (0, 0))).reshape(-1, chans, depth), slot[None]]
-    other = to_core(jnp.concatenate(message, axis=0))
-    other_slot = other[-1]
-    slot_rows = [jnp.where(first_core, slot, other_slot)[:8], jnp.where(first_core, other_slot, slot)[:8]]
+    message = jnp.concatenate(
+        [cells(b2), jnp.pad(edge.reshape(-1, depth), ((0, spare), (0, 0))).reshape(-1, chans, depth)], axis=0
+    )
+    other = to_core(message)
     edge = other[size * size :].reshape(-1, depth)[:edge_rows].reshape(edge.shape)
     other = other[: size * size].reshape(b2.shape)
     chip = jnp.concatenate([jnp.where(first_core, b2, other), jnp.where(first_core, other, b2)], axis=1)
@@ -481,16 +475,15 @@
         "down_chip",
     )
     x2, q2 = [jnp.where(first_core, v[:, :size], v[:, size:]) for v in (x2, q2)]
+    b3 = jnp.where(first_core, b3[0, 0], b3[0, 1])
 
     lefts = [q0, q1, q2]
     low = jnp.concatenate([cells(q[:2]) for q in lefts], axis=0)
     high = jnp.concatenate([cells(q[-2:]) for q in lefts], axis=0)
     left_ends = swap_ends(at, low, high, "gx", 1)
 
-    line = [list(range(first, blocks, 2)) for first in range(2)]
-    shares = lax.all_gather(
-        jnp.concatenate([b3[0, 0], b3[0, 1], *slot_rows], axis=0)[None], "gy", axis_index_groups=line, axis=0, tiled=True
-    )
+    slot = jnp.broadcast_to(slots.astype(jnp.float32), (8, depth))
+    shares = lax.all_gather(jnp.concatenate([b3, slot], axis=0)[None], "gy", axis=0, tiled=True)
     left_ends, shares = lax.optimization_barrier((left_ends, shares))
     before, after = in_order(at, *left_ends, "gx")
     left_rows, done = [], 0
@@ -508,9 +501,7 @@
     solved = call(
         solve_kernel, where, [shares, coarse_inverse[0, 0]], [tail], [(chans, blocks * depth)], "solve"
     )[0]
-    other = to_core(solved)
-    solved = jnp.concatenate([jnp.where(first_core, solved, other), jnp.where(first_core, other, solved)], axis=0)
-    back = lax.all_gather(solved[None], "gy", axis_index_groups=line, axis=0, tiled=True)
+    back = lax.all_gather(solved[None], "gy", axis=0, tiled=True)
     fix = call(pick_kernel, where, [shares, back], [(6,) + tail], [], "pick")[0]
     lines = lines_around(at, fix, fix, fix)
 

time: 241 us -> 219 us (0.909)
  starting transfers between devices: 111 us -> 98.3 us
  blocking collectives: 49.6 us -> 41 us
    ppermute x25 -> x24, starting transfers between devices: 98.2 us -> 85.1 us  [swap(): return lax.ppermute(x, axis, pairs)]
    all_gather x2, blocking collectives: 49.6 us -> 41 us  [the longest x1 22.5 us: body(): lax.all_gather(jnp.concatenate([b3, slot], axis=0)[None], 'gy', axis=0, t...]
    ppermute x25 -> x24, waiting for transfers between devices: 46.3 us -> 47.1 us  [swap(): return lax.ppermute(x, axis, pairs)]
  transfers between devices with their start and end apart: 30 -> 29, of which waited for: 16 -> 17; matrix products, arithmetic and copies ran while one was open for 0% -> 0% of each run, Pallas kernels for 0% -> 1%
where the time goes in v4:
time: 219 us; the launch traced here: 218 us
  starting transfers between devices  98.3 us (45%)
  waiting for transfers between devices  56 us (26%)
  blocking collectives  41 us (19%)
  Pallas kernels  16.6 us (8%)
  local copies, waits for them, and re-layouts  3.19 us (1%)
    ppermute x24, starting transfers between devices, swap(): return lax.ppermute(x, axis, pairs)  85.1 us
    ppermute x24, waiting for transfers between devices, swap(): return lax.ppermute(x, axis, pairs)  47.1 us
    all_gather x1, blocking collectives, body(): lax.all_gather(jnp.concatenate([b3, slot], axis=0)[None], 'gy', axis=0, t...  22.5 us
    all_gather x1, blocking collectives, body(): back = lax.all_gather(solved[None], 'gy', axis=0, tiled=True)  18.5 us
    pallas_call x8, Pallas kernels, call(): pl.pallas_call(kernel, out_shape=[jax.ShapeDtypeStruct(out, jnp.float32)...  16.6 us
    ppermute x4, starting transfers between devices, by_core(): return lax.ppermute(x, ('gx', 'gy'), pairs)  12.4 us
    ppermute x4, waiting for transfers between devices, by_core(): return lax.ppermute(x, ('gx', 'gy'), pairs)  8.91 us
  transfers between devices with their start and end apart: 29, of which 17 were waited for; matrix products, arithmetic and copies ran while one was open for 0% of the time, Pallas kernels for 1%

profile of v4, /device:TPU:31, one launch (start us, length us, event | category | flops | bytes accessed | tf_op | source)
XLA Modules:
  0.0 217.8 jit_solution(1137905299192594452)
XLA Ops:
  4.3 5.0 %collective-permute-start.1 = (f32[27,24,128]{2,1,0:T(8,128)S(1)}, f32[27,24,128]{2,1,0:T(8,128)S(1)}, u32[]{:S(2)}, u32[]{:S(2)}) collective-permute-start(f32[27,24,128]{2,1,0:T(8,128)S(1)} %get-tuple-element.73), channel_id=1, source_target_pairs={{16,32},{32,16},{48,64},{64,48},{80,96},{96,80},{112,128},{128,112... | collective-permute-start | bytes 995336 | tf_op jit(solution)/shard_map/ppermute | solution.py:23
  9.3 3.0 %collective-permute-done.refs_0_ = f32[27,24,128]{2,1,0:T(8,128)S(1)} collective-permute-done((f32[27,24,128]{2,1,0:T(8,128)S(1)}, f32[27,24,128]{2,1,0:T(8,128)S(1)}, u32[]{:S(2)}, u32[]{:S(2)}) %collective-permute-start) | collective-permute-done | bytes 331808 | tf_op jit(solution)/shard_map/ppermute | solution.py:23
  12.4 5.5 %collective-permute-done.1.refs_1_ = f32[27,24,128]{2,1,0:T(8,128)S(1)} collective-permute-done((f32[27,24,128]{2,1,0:T(8,128)S(1)}, f32[27,24,128]{2,1,0:T(8,128)S(1)}, u32[]{:S(2)}, u32[]{:S(2)}) %collective-permute-start.1) | collective-permute-done | bytes 331808 | tf_op jit(solution)/shard_map/ppermute | solution.py:23
  18.3 3.8 %collective-permute-start.2 = (f32[50,24,128]{2,1,0:T(8,128)S(1)}, f32[50,24,128]{2,1,0:T(8,128)S(1)}, u32[]{:S(2)}, u32[]{:S(2)}) collective-permute-start(f32[50,24,128]{2,1,0:T(8,128)S(1)} %get-tuple-element.58), channel_id=1, source_target_pairs={{0,1},{1,0},{2,3},{3,2},{4,5},{5,4},{6,7},{7,6},{8,9},{9,8},{10,11... | collective-permute-start | bytes 1843208 | tf_op jit(solution)/shard_map/ppermute | solution.py:23
  22.1 3.9 %collective-permute-start.3 = (f32[50,24,128]{2,1,0:T(8,128)S(1)}, f32[50,24,128]{2,1,0:T(8,128)S(1)}, u32[]{:S(2)}, u32[]{:S(2)}) collective-permute-start(f32[50,24,128]{2,1,0:T(8,128)S(1)} %get-tuple-element.57), channel_id=1, source_target_pairs={{1,2},{2,1},{3,4},{4,3},{5,6},{6,5},{7,8},{8,7},{9,10},{10,9},{11,... | collective-permute-start | bytes 1843208 | tf_op jit(solution)/shard_map/ppermute | solution.py:23
  26.0 8.1 %collective-permute-done.3.refs_3_ = f32[50,24,128]{2,1,0:T(8,128)S(1)} collective-permute-done((f32[50,24,128]{2,1,0:T(8,128)S(1)}, f32[50,24,128]{2,1,0:T(8,128)S(1)}, u32[]{:S(2)}, u32[]{:S(2)}) %collective-permute-start.3) | collective-permute-done | bytes 614432 | tf_op jit(solution)/shard_map/ppermute | solution.py:23
  34.1 3.9 %down_fine.1 = (f32[8,8,24,128]{3,2,1,0:T(8,128)S(1)}, f32[8,8,24,128]{3,2,1,0:T(8,128)S(1)}, f32[4,4,24,128]{3,2,1,0:T(8,128)S(1)}, f32[24,24,128]{2,1,0:T(8,12...) custom-call(s32[8]{0:T(128)S(1)} %stack.27.where, f32[8,8,24,128]{3,2,1,0:T(8,128)S(1)} %bitcast.78, ...), custom_call_target="tpu_custom_call" | custom-call | tf_op jit(solution)/shard_map/down_fine/pallas_call | solution.py:306
  40.0 5.0 %collective-permute-start.5 = (f32[12,24,128]{2,1,0:T(8,128)S(1)}, f32[12,24,128]{2,1,0:T(8,128)S(1)}, u32[]{:S(2)}, u32[]{:S(2)}) collective-permute-start(f32[12,24,128]{2,1,0:T(8,128)S(1)} %bitcast.129), channel_id=1, source_target_pairs={{16,32},{32,16},{48,64},{64,48},{80,96},{96,80},{112,128},{128,112... | collective-permute-start | bytes 442376 | tf_op jit(solution)/shard_map/ppermute | solution.py:23
  45.0 4.2 %collective-permute-done.5.refs_1_ = f32[12,24,128]{2,1,0:T(8,128)S(1)} collective-permute-done((f32[12,24,128]{2,1,0:T(8,128)S(1)}, f32[12,24,128]{2,1,0:T(8,128)S(1)}, u32[]{:S(2)}, u32[]{:S(2)}) %collective-permute-start.5) | collective-permute-done | bytes 147488 | tf_op jit(solution)/shard_map/ppermute | solution.py:23
  51.3 5.9 %collective-permute-start.7 = (f32[30,24,128]{2,1,0:T(8,128)S(1)}, f32[30,24,128]{2,1,0:T(8,128)S(1)}, u32[]{:S(2)}, u32[]{:S(2)}) collective-permute-start(f32[30,24,128]{2,1,0:T(8,128)S(1)} %bitcast.117), channel_id=1, source_target_pairs={{1,2},{2,1},{3,4},{4,3},{5,6},{6,5},{7,8},{8,7},{9,10},{10,9},{11,... | collective-permute-start | bytes 1105928 | tf_op jit(solution)/shard_map/ppermute | solution.py:23
  57.1 5.2 %collective-permute-done.7.refs_3_ = f32[30,24,128]{2,1,0:T(8,128)S(1)} collective-permute-done((f32[30,24,128]{2,1,0:T(8,128)S(1)}, f32[30,24,128]{2,1,0:T(8,128)S(1)}, u32[]{:S(2)}, u32[]{:S(2)}) %collective-permute-start.7) | collective-permute-done | bytes 368672 | tf_op jit(solution)/shard_map/ppermute | solution.py:23
  67.5 5.0 %collective-permute-start.9 = (f32[2,4,24,128]{3,2,1,0:T(8,128)S(1)}, f32[2,4,24,128]{3,2,1,0:T(8,128)S(1)}, u32[]{:S(2)}, u32[]{:S(2)}) collective-permute-start(f32[2,4,24,128]{3,2,1,0:T(8,128)S(1)} %pad_maximum_fusion.20), channel_id=1, source_target_pairs={{0,16},{16,0},{32,48},{48,32},{64,80},{80,64},{96,112},{112,96},{1... | collective-permute-start | bytes 294920 | tf_op jit(solution)/shard_map/ppermute | solution.py:383
  75.1 3.9 %collective-permute-done.10 = f32[1,4,24,128]{3,2,1,0:T(8,128)S(1)} collective-permute-done((f32[1,4,24,128]{3,2,1,0:T(8,128)S(1)}, f32[1,4,24,128]{3,2,1,0:T(8,128)S(1)}, u32[]{:S(2)}, u32[]{:S(2)}) %collective-permute-start.10) | collective-permute-done | bytes 49184 | tf_op jit(solution)/shard_map/ppermute | solution.py:383
  83.2 9.5 %collective-permute-start.13 = (f32[6,3,24,128]{3,2,1,0:T(8,128)S(1)}, f32[6,3,24,128]{3,2,1,0:T(8,128)S(1)}, u32[]{:S(2)}, u32[]{:S(2)}) collective-permute-start(f32[6,3,24,128]{3,2,1,0:T(8,128)S(1)} %collective-permute-done.12), channel_id=1, source_target_pairs={{0,1},{1,0},{2,3},{3,2},{4,5},{5,4},{6,7},{7,6},{8,9},{9,8},{10,11... | collective-permute-start | bytes 663560 | tf_op jit(solution)/shard_map/ppermute | solution.py:23
  95.3 3.6 %collective-permute-start.14 = (f32[28,24,128]{2,1,0:T(8,128)S(1)}, f32[28,24,128]{2,1,0:T(8,128)S(1)}, u32[]{:S(2)}, u32[]{:S(2)}) collective-permute-start(f32[28,24,128]{2,1,0:T(8,128)S(1)} %get-tuple-element.72), channel_id=1, source_target_pairs={{0,16},{16,0},{32,48},{48,32},{64,80},{80,64},{96,112},{112,96},{1... | collective-permute-start | bytes 1032200 | tf_op jit(solution)/shard_map/ppermute | solution.py:23
  98.9 5.0 %collective-permute-start.15 = (f32[28,24,128]{2,1,0:T(8,128)S(1)}, f32[28,24,128]{2,1,0:T(8,128)S(1)}, u32[]{:S(2)}, u32[]{:S(2)}) collective-permute-start(f32[28,24,128]{2,1,0:T(8,128)S(1)} %get-tuple-element.71), channel_id=1, source_target_pairs={{16,32},{32,16},{48,64},{64,48},{80,96},{96,80},{112,128},{128,112... | collective-permute-start | bytes 1032200 | tf_op jit(solution)/shard_map/ppermute | solution.py:23
  104.0 22.5 %all-gather = f32[512,128]{1,0:T(8,128)S(1)} all-gather(f32[32,128]{1,0:T(8,128)S(1)} %concatenate.108), channel_id=2, replica_groups=mesh['gx'=32,'gy'=16] {'gy'}, dimensions={0}, use_global_device_ids=true | all-gather | bytes 278528 | tf_op jit(solution)/shard_map/all_gather | solution.py:486
  133.3 18.5 %all-gather.1 = f32[384,128]{1,0:T(8,128)S(1)} all-gather(f32[24,128]{1,0:T(8,128)S(1)} %solve.1), channel_id=3, replica_groups=mesh['gx'=32,'gy'=16] {'gy'}, dimensions={0}, use_global_device_ids=true | all-gather | bytes 208896 | tf_op jit(solution)/shard_map/all_gather | solution.py:504
  152.5 3.6 %collective-permute-start.16 = (f32[6,24,128]{2,1,0:T(8,128)S(1)}, f32[6,24,128]{2,1,0:T(8,128)S(1)}, u32[]{:S(2)}, u32[]{:S(2)}) collective-permute-start(f32[6,24,128]{2,1,0:T(8,128)S(1)} %pick.1.coarse_own), channel_id=1, source_target_pairs={{0,16},{16,0},{32,48},{48,32},{64,80},{80,64},{96,112},{112,96},{1... | collective-permute-start | bytes 221192 | tf_op jit(solution)/shard_map/ppermute | solution.py:383
  158.0 2.9 %collective-permute-done.16 = f32[6,24,128]{2,1,0:T(8,128)S(1)} collective-permute-done((f32[6,24,128]{2,1,0:T(8,128)S(1)}, f32[6,24,128]{2,1,0:T(8,128)S(1)}, u32[]{:S(2)}, u32[]{:S(2)}) %collective-permute-start.16) | collective-permute-done | bytes 73760 | tf_op jit(solution)/shard_map/ppermute | solution.py:383
  163.0 3.3 %collective-permute-start.18 = (f32[12,24,128]{2,1,0:T(8,128)S(1)}, f32[12,24,128]{2,1,0:T(8,128)S(1)}, u32[]{:S(2)}, u32[]{:S(2)}) collective-permute-start(f32[12,24,128]{2,1,0:T(8,128)S(1)} %constant_dynamic-update-slice_fusion.3.refs_0_), channel_id=1, source_target_pairs={{0,1},{1,0},{2,3},{3,2},{4,5},{5,4},{6,7},{7,6},{8,9},{9,8},{10,11... | collective-permute-start | bytes 442376 | tf_op jit(solution)/shard_map/ppermute | solution.py:23
  168.6 3.6 %collective-permute-start.21 = (f32[4,24,128]{2,1,0:T(8,128)S(1)}, f32[4,24,128]{2,1,0:T(8,128)S(1)}, u32[]{:S(2)}, u32[]{:S(2)}) collective-permute-start(f32[4,24,128]{2,1,0:T(8,128)S(1)} %bitcast.85), channel_id=1, source_target_pairs={{0,16},{16,0},{32,48},{48,32},{64,80},{80,64},{96,112},{112,96},{1... | collective-permute-start | bytes 147464 | tf_op jit(solution)/shard_map/ppermute | solution.py:23
  172.3 3.6 %collective-permute-start.22 = (f32[4,24,128]{2,1,0:T(8,128)S(1)}, f32[4,24,128]{2,1,0:T(8,128)S(1)}, u32[]{:S(2)}, u32[]{:S(2)}) collective-permute-start(f32[4,24,128]{2,1,0:T(8,128)S(1)} %bitcast.86), channel_id=1, source_target_pairs={{16,32},{32,16},{48,64},{64,48},{80,96},{96,80},{112,128},{128,112... | collective-permute-start | bytes 147464 | tf_op jit(solution)/shard_map/ppermute | solution.py:23
  175.9 4.5 %collective-permute-done.22.refs_1_ = f32[4,24,128]{2,1,0:T(8,128)S(1)} collective-permute-done((f32[4,24,128]{2,1,0:T(8,128)S(1)}, f32[4,24,128]{2,1,0:T(8,128)S(1)}, u32[]{:S(2)}, u32[]{:S(2)}) %collective-permute-start.22) | collective-permute-done | bytes 49184 | tf_op jit(solution)/shard_map/ppermute | solution.py:23
  180.5 3.7 %collective-permute-start.23 = (f32[12,24,128]{2,1,0:T(8,128)S(1)}, f32[12,24,128]{2,1,0:T(8,128)S(1)}, u32[]{:S(2)}, u32[]{:S(2)}) collective-permute-start(f32[12,24,128]{2,1,0:T(8,128)S(1)} %bitcast.127), channel_id=1, source_target_pairs={{0,1},{1,0},{2,3},{3,2},{4,5},{5,4},{6,7},{7,6},{8,9},{9,8},{10,11... | collective-permute-start | bytes 442376 | tf_op jit(solution)/shard_map/ppermute | solution.py:23
  184.2 2.5 %collective-permute-start.24 = (f32[12,24,128]{2,1,0:T(8,128)S(1)}, f32[12,24,128]{2,1,0:T(8,128)S(1)}, u32[]{:S(2)}, u32[]{:S(2)}) collective-permute-start(f32[12,24,128]{2,1,0:T(8,128)S(1)} %bitcast.128), channel_id=1, source_target_pairs={{1,2},{2,1},{3,4},{4,3},{5,6},{6,5},{7,8},{8,7},{9,10},{10,9},{11,... | collective-permute-start | bytes 442376 | tf_op jit(solution)/shard_map/ppermute | solution.py:23
  186.7 3.9 %collective-permute-done.24.refs_3_ = f32[12,24,128]{2,1,0:T(8,128)S(1)} collective-permute-done((f32[12,24,128]{2,1,0:T(8,128)S(1)}, f32[12,24,128]{2,1,0:T(8,128)S(1)}, u32[]{:S(2)}, u32[]{:S(2)}) %collective-permute-start.24) | collective-permute-done | bytes 147488 | tf_op jit(solution)/shard_map/ppermute | solution.py:23
  194.6 3.6 %collective-permute-start.26 = (f32[8,24,128]{2,1,0:T(8,128)S(1)}, f32[8,24,128]{2,1,0:T(8,128)S(1)}, u32[]{:S(2)}, u32[]{:S(2)}) collective-permute-start(f32[8,24,128]{2,1,0:T(8,128)S(1)} %bitcast.133), channel_id=1, source_target_pairs={{16,32},{32,16},{48,64},{64,48},{80,96},{96,80},{112,128},{128,112... | collective-permute-start | bytes 294920 | tf_op jit(solution)/shard_map/ppermute | solution.py:23
  198.3 5.0 %collective-permute-done.26.refs_1_ = f32[8,24,128]{2,1,0:T(8,128)S(1)} collective-permute-done((f32[8,24,128]{2,1,0:T(8,128)S(1)}, f32[8,24,128]{2,1,0:T(8,128)S(1)}, u32[]{:S(2)}, u32[]{:S(2)}) %collective-permute-start.26) | collective-permute-done | bytes 98336 | tf_op jit(solution)/shard_map/ppermute | solution.py:23
  205.3 4.3 %collective-permute-start.28 = (f32[16,24,128]{2,1,0:T(8,128)S(1)}, f32[16,24,128]{2,1,0:T(8,128)S(1)}, u32[]{:S(2)}, u32[]{:S(2)}) collective-permute-start(f32[16,24,128]{2,1,0:T(8,128)S(1)} %bitcast.124), channel_id=1, source_target_pairs={{1,2},{2,1},{3,4},{4,3},{5,6},{6,5},{7,8},{8,7},{9,10},{10,9},{11,... | collective-permute-start | bytes 589832 | tf_op jit(solution)/shard_map/ppermute | solution.py:23
  209.6 3.3 %collective-permute-done.28.refs_3_ = f32[16,24,128]{2,1,0:T(8,128)S(1)} collective-permute-done((f32[16,24,128]{2,1,0:T(8,128)S(1)}, f32[16,24,128]{2,1,0:T(8,128)S(1)}, u32[]{:S(2)}, u32[]{:S(2)}) %collective-permute-start.28) | collective-permute-done | bytes 196640 | tf_op jit(solution)/shard_map/ppermute | solution.py:23
  212.9 3.9 %up_8.1 = f32[8,8,24,128]{3,2,1,0:T(8,128)S(1)} custom-call(s32[8]{0:T(128)S(1)} %stack.27.where, f32[4,4,24,128]{3,2,1,0:T(8,128)S(1)} %up_4.1.coarse_own, f32[8,24,128]{2,1,0:T(8,128)S(1)} %collective-permute-done.25.refs_0_, f32[8,24,128]{2,1,0:T(8,128)S(1)} %collective-permute-done.26.refs_1_, f32[16,24,128]{2,1,0:T(8,128)S(1)} %collective-permute-done.27.refs_2_, ...), custom_call_target="tpu_custom_call" | custom-call | tf_op jit(solution)/shard_map/up_8/pallas_call | solution.py:306
  (114 shorter events, 43.1 us)
Async XLA Ops:
  0.1 1.7 copy-start.1
  1.8 10.6 %collective-permute-start = (f32[27,24,128]{2,1,0:T(8,128)S(1)}, f32[27,24,128]{2,1,0:T(8,128)S(1)}, u32[]{:S(2)}, u32[]{:S(2)}) collective-permute-start(f32[27,24,128]{2,1,0:T(8,128)S(1)} %get-tuple-element.74), channel_id=1, source_target_pairs={{0,16},{16,0},{32,48},{48,32},{64,80},{80,64},{96,112},{112,96},{1... | collective-permute-start | bytes 995336 | tf_op jit(solution)/shard_map/ppermute | solution.py:23
  4.3 13.6 %collective-permute-start.1 = (f32[27,24,128]{2,1,0:T(8,128)S(1)}, f32[27,24,128]{2,1,0:T(8,128)S(1)}, u32[]{:S(2)}, u32[]{:S(2)}) collective-permute-start(f32[27,24,128]{2,1,0:T(8,128)S(1)} %get-tuple-element.73), channel_id=1, source_target_pairs={{16,32},{32,16},{48,64},{64,48},{80,96},{96,80},{112,128},{128,112... | collective-permute-start | bytes 995336 | tf_op jit(solution)/shard_map/ppermute | solution.py:23
  18.3 7.7 %collective-permute-start.2 = (f32[50,24,128]{2,1,0:T(8,128)S(1)}, f32[50,24,128]{2,1,0:T(8,128)S(1)}, u32[]{:S(2)}, u32[]{:S(2)}) collective-permute-start(f32[50,24,128]{2,1,0:T(8,128)S(1)} %get-tuple-element.58), channel_id=1, source_target_pairs={{0,1},{1,0},{2,3},{3,2},{4,5},{5,4},{6,7},{7,6},{8,9},{9,8},{10,11... | collective-permute-start | bytes 1843208 | tf_op jit(solution)/shard_map/ppermute | solution.py:23
  22.1 12.0 %collective-permute-start.3 = (f32[50,24,128]{2,1,0:T(8,128)S(1)}, f32[50,24,128]{2,1,0:T(8,128)S(1)}, u32[]{:S(2)}, u32[]{:S(2)}) collective-permute-start(f32[50,24,128]{2,1,0:T(8,128)S(1)} %get-tuple-element.57), channel_id=1, source_target_pairs={{1,2},{2,1},{3,4},{4,3},{5,6},{6,5},{7,8},{8,7},{9,10},{10,9},{11,... | collective-permute-start | bytes 1843208 | tf_op jit(solution)/shard_map/ppermute | solution.py:23
  38.0 7.0 %collective-permute-start.4 = (f32[12,24,128]{2,1,0:T(8,128)S(1)}, f32[12,24,128]{2,1,0:T(8,128)S(1)}, u32[]{:S(2)}, u32[]{:S(2)}) collective-permute-start(f32[12,24,128]{2,1,0:T(8,128)S(1)} %bitcast.130), channel_id=1, source_target_pairs={{0,16},{16,0},{32,48},{48,32},{64,80},{80,64},{96,112},{112,96},{1... | collective-permute-start | bytes 442376 | tf_op jit(solution)/shard_map/ppermute | solution.py:23
  40.0 9.2 %collective-permute-start.5 = (f32[12,24,128]{2,1,0:T(8,128)S(1)}, f32[12,24,128]{2,1,0:T(8,128)S(1)}, u32[]{:S(2)}, u32[]{:S(2)}) collective-permute-start(f32[12,24,128]{2,1,0:T(8,128)S(1)} %bitcast.129), channel_id=1, source_target_pairs={{16,32},{32,16},{48,64},{64,48},{80,96},{96,80},{112,128},{128,112... | collective-permute-start | bytes 442376 | tf_op jit(solution)/shard_map/ppermute | solution.py:23
  49.3 7.8 %collective-permute-start.6 = (f32[30,24,128]{2,1,0:T(8,128)S(1)}, f32[30,24,128]{2,1,0:T(8,128)S(1)}, u32[]{:S(2)}, u32[]{:S(2)}) collective-permute-start(f32[30,24,128]{2,1,0:T(8,128)S(1)} %bitcast.118), channel_id=1, source_target_pairs={{0,1},{1,0},{2,3},{3,2},{4,5},{5,4},{6,7},{7,6},{8,9},{9,8},{10,11... | collective-permute-start | bytes 1105928 | tf_op jit(solution)/shard_map/ppermute | solution.py:23
  51.3 11.1 %collective-permute-start.7 = (f32[30,24,128]{2,1,0:T(8,128)S(1)}, f32[30,24,128]{2,1,0:T(8,128)S(1)}, u32[]{:S(2)}, u32[]{:S(2)}) collective-permute-start(f32[30,24,128]{2,1,0:T(8,128)S(1)} %bitcast.117), channel_id=1, source_target_pairs={{1,2},{2,1},{3,4},{4,3},{5,6},{6,5},{7,8},{8,7},{9,10},{10,9},{11,... | collective-permute-start | bytes 1105928 | tf_op jit(solution)/shard_map/ppermute | solution.py:23
  64.3 3.1 %collective-permute-start.8 = (f32[5,24,128]{2,1,0:T(8,128)S(1)}, f32[5,24,128]{2,1,0:T(8,128)S(1)}, u32[]{:S(2)}, u32[]{:S(2)}) collective-permute-start(f32[5,24,128]{2,1,0:T(8,128)S(1)} %pad_maximum_fusion.22), channel_id=1, source_target_pairs={{0,1},{1,0},{2,3},{3,2},{4,5},{5,4},{6,7},{7,6},{8,9},{9,8},{10,11... | collective-permute-start | bytes 184328 | tf_op jit(solution)/shard_map/ppermute | solution.py:23
  67.5 11.5 %collective-permute-start.9 = (f32[2,4,24,128]{3,2,1,0:T(8,128)S(1)}, f32[2,4,24,128]{3,2,1,0:T(8,128)S(1)}, u32[]{:S(2)}, u32[]{:S(2)}) collective-permute-start(f32[2,4,24,128]{3,2,1,0:T(8,128)S(1)} %pad_maximum_fusion.20), channel_id=1, source_target_pairs={{0,16},{16,0},{32,48},{48,32},{64,80},{80,64},{96,112},{112,96},{1... | collective-permute-start | bytes 294920 | tf_op jit(solution)/shard_map/ppermute | solution.py:383
  72.5 6.5 %collective-permute-start.10 = (f32[1,4,24,128]{3,2,1,0:T(8,128)S(1)}, f32[1,4,24,128]{3,2,1,0:T(8,128)S(1)}, u32[]{:S(2)}, u32[]{:S(2)}) collective-permute-start(f32[1,4,24,128]{3,2,1,0:T(8,128)S(1)} %fusion.13), channel_id=1, source_target_pairs={{32,64},{64,32},{48,80},{80,48},{96,128},{128,96},{112,144},{144,1... | collective-permute-start | bytes 147464 | tf_op jit(solution)/shard_map/ppermute | solution.py:383
  79.0 3.3 %collective-permute-start.11 = (f32[12,24,128]{2,1,0:T(8,128)S(1)}, f32[12,24,128]{2,1,0:T(8,128)S(1)}, u32[]{:S(2)}, u32[]{:S(2)}) collective-permute-start(f32[12,24,128]{2,1,0:T(8,128)S(1)} %pad_maximum_fusion.17), channel_id=1, source_target_pairs={{0,1},{1,0},{2,3},{3,2},{4,5},{5,4},{6,7},{7,6},{8,9},{9,8},{10,11... | collective-permute-start | bytes 442376 | tf_op jit(solution)/shard_map/ppermute | solution.py:23
  82.4 0.7 collective-permute-start.12
  83.2 10.6 %collective-permute-start.13 = (f32[6,3,24,128]{3,2,1,0:T(8,128)S(1)}, f32[6,3,24,128]{3,2,1,0:T(8,128)S(1)}, u32[]{:S(2)}, u32[]{:S(2)}) collective-permute-start(f32[6,3,24,128]{3,2,1,0:T(8,128)S(1)} %collective-permute-done.12), channel_id=1, source_target_pairs={{0,1},{1,0},{2,3},{3,2},{4,5},{5,4},{6,7},{7,6},{8,9},{9,8},{10,11... | collective-permute-start | bytes 663560 | tf_op jit(solution)/shard_map/ppermute | solution.py:23
  95.3 31.2 %collective-permute-start.14 = (f32[28,24,128]{2,1,0:T(8,128)S(1)}, f32[28,24,128]{2,1,0:T(8,128)S(1)}, u32[]{:S(2)}, u32[]{:S(2)}) collective-permute-start(f32[28,24,128]{2,1,0:T(8,128)S(1)} %get-tuple-element.72), channel_id=1, source_target_pairs={{0,16},{16,0},{32,48},{48,32},{64,80},{80,64},{96,112},{112,96},{1... | collective-permute-start | bytes 1032200 | tf_op jit(solution)/shard_map/ppermute | solution.py:23
  98.9 27.6 %collective-permute-start.15 = (f32[28,24,128]{2,1,0:T(8,128)S(1)}, f32[28,24,128]{2,1,0:T(8,128)S(1)}, u32[]{:S(2)}, u32[]{:S(2)}) collective-permute-start(f32[28,24,128]{2,1,0:T(8,128)S(1)} %get-tuple-element.71), channel_id=1, source_target_pairs={{16,32},{32,16},{48,64},{64,48},{80,96},{96,80},{112,128},{128,112... | collective-permute-start | bytes 1032200 | tf_op jit(solution)/shard_map/ppermute | solution.py:23
  126.9 4.8 %copy-start = (f32[1,1,128,2048]{3,2,1,0:T(8,128)S(1)}, f32[1,1,128,2048]{3,2,1,0:T(8,128)}, u32[]{:S(2)}) copy-start(f32[1,1,128,2048]{3,2,1,0:T(8,128)} %param.7) | copy-start | bytes 3145732
  127.0 40.3 %collective-permute-start.19 = (f32[52,24,128]{2,1,0:T(8,128)S(1)}, f32[52,24,128]{2,1,0:T(8,128)S(1)}, u32[]{:S(2)}, u32[]{:S(2)}) collective-permute-start(f32[52,24,128]{2,1,0:T(8,128)S(1)} %get-tuple-element.56), channel_id=1, source_target_pairs={{0,1},{1,0},{2,3},{3,2},{4,5},{5,4},{6,7},{7,6},{8,9},{9,8},{10,11... | collective-permute-start | bytes 1916936 | tf_op jit(solution)/shard_map/ppermute | solution.py:23
  129.2 38.1 %collective-permute-start.20 = (f32[52,24,128]{2,1,0:T(8,128)S(1)}, f32[52,24,128]{2,1,0:T(8,128)S(1)}, u32[]{:S(2)}, u32[]{:S(2)}) collective-permute-start(f32[52,24,128]{2,1,0:T(8,128)S(1)} %get-tuple-element.55), channel_id=1, source_target_pairs={{1,2},{2,1},{3,4},{4,3},{5,6},{6,5},{7,8},{8,7},{9,10},{10,9},{11,... | collective-permute-start | bytes 1916936 | tf_op jit(solution)/shard_map/ppermute | solution.py:23
  152.5 8.4 %collective-permute-start.16 = (f32[6,24,128]{2,1,0:T(8,128)S(1)}, f32[6,24,128]{2,1,0:T(8,128)S(1)}, u32[]{:S(2)}, u32[]{:S(2)}) collective-permute-start(f32[6,24,128]{2,1,0:T(8,128)S(1)} %pick.1.coarse_own), channel_id=1, source_target_pairs={{0,16},{16,0},{32,48},{48,32},{64,80},{80,64},{96,112},{112,96},{1... | collective-permute-start | bytes 221192 | tf_op jit(solution)/shard_map/ppermute | solution.py:383
  156.1 6.9 %collective-permute-start.17 = (f32[6,24,128]{2,1,0:T(8,128)S(1)}, f32[6,24,128]{2,1,0:T(8,128)S(1)}, u32[]{:S(2)}, u32[]{:S(2)}) collective-permute-start(f32[6,24,128]{2,1,0:T(8,128)S(1)} %pick.1.coarse_own), channel_id=1, source_target_pairs={{32,64},{64,32},{48,80},{80,48},{96,128},{128,96},{112,144},{144,1... | collective-permute-start | bytes 221192 | tf_op jit(solution)/shard_map/ppermute | solution.py:383
  163.0 4.3 %collective-permute-start.18 = (f32[12,24,128]{2,1,0:T(8,128)S(1)}, f32[12,24,128]{2,1,0:T(8,128)S(1)}, u32[]{:S(2)}, u32[]{:S(2)}) collective-permute-start(f32[12,24,128]{2,1,0:T(8,128)S(1)} %constant_dynamic-update-slice_fusion.3.refs_0_), channel_id=1, source_target_pairs={{0,1},{1,0},{2,3},{3,2},{4,5},{5,4},{6,7},{7,6},{8,9},{9,8},{10,11... | collective-permute-start | bytes 442376 | tf_op jit(solution)/shard_map/ppermute | solution.py:23
  168.6 7.3 %collective-permute-start.21 = (f32[4,24,128]{2,1,0:T(8,128)S(1)}, f32[4,24,128]{2,1,0:T(8,128)S(1)}, u32[]{:S(2)}, u32[]{:S(2)}) collective-permute-start(f32[4,24,128]{2,1,0:T(8,128)S(1)} %bitcast.85), channel_id=1, source_target_pairs={{0,16},{16,0},{32,48},{48,32},{64,80},{80,64},{96,112},{112,96},{1... | collective-permute-start | bytes 147464 | tf_op jit(solution)/shard_map/ppermute | solution.py:23
  172.3 8.2 %collective-permute-start.22 = (f32[4,24,128]{2,1,0:T(8,128)S(1)}, f32[4,24,128]{2,1,0:T(8,128)S(1)}, u32[]{:S(2)}, u32[]{:S(2)}) collective-permute-start(f32[4,24,128]{2,1,0:T(8,128)S(1)} %bitcast.86), channel_id=1, source_target_pairs={{16,32},{32,16},{48,64},{64,48},{80,96},{96,80},{112,128},{128,112... | collective-permute-start | bytes 147464 | tf_op jit(solution)/shard_map/ppermute | solution.py:23
  180.5 6.3 %collective-permute-start.23 = (f32[12,24,128]{2,1,0:T(8,128)S(1)}, f32[12,24,128]{2,1,0:T(8,128)S(1)}, u32[]{:S(2)}, u32[]{:S(2)}) collective-permute-start(f32[12,24,128]{2,1,0:T(8,128)S(1)} %bitcast.127), channel_id=1, source_target_pairs={{0,1},{1,0},{2,3},{3,2},{4,5},{5,4},{6,7},{7,6},{8,9},{9,8},{10,11... | collective-permute-start | bytes 442376 | tf_op jit(solution)/shard_map/ppermute | solution.py:23
  184.2 6.5 %collective-permute-start.24 = (f32[12,24,128]{2,1,0:T(8,128)S(1)}, f32[12,24,128]{2,1,0:T(8,128)S(1)}, u32[]{:S(2)}, u32[]{:S(2)}) collective-permute-start(f32[12,24,128]{2,1,0:T(8,128)S(1)} %bitcast.128), channel_id=1, source_target_pairs={{1,2},{2,1},{3,4},{4,3},{5,6},{6,5},{7,8},{8,7},{9,10},{10,9},{11,... | collective-permute-start | bytes 442376 | tf_op jit(solution)/shard_map/ppermute | solution.py:23
  192.7 5.7 %collective-permute-start.25 = (f32[8,24,128]{2,1,0:T(8,128)S(1)}, f32[8,24,128]{2,1,0:T(8,128)S(1)}, u32[]{:S(2)}, u32[]{:S(2)}) collective-permute-start(f32[8,24,128]{2,1,0:T(8,128)S(1)} %bitcast.134), channel_id=1, source_target_pairs={{0,16},{16,0},{32,48},{48,32},{64,80},{80,64},{96,112},{112,96},{1... | collective-permute-start | bytes 294920 | tf_op jit(solution)/shard_map/ppermute | solution.py:23
  194.6 8.7 %collective-permute-start.26 = (f32[8,24,128]{2,1,0:T(8,128)S(1)}, f32[8,24,128]{2,1,0:T(8,128)S(1)}, u32[]{:S(2)}, u32[]{:S(2)}) collective-permute-start(f32[8,24,128]{2,1,0:T(8,128)S(1)} %bitcast.133), channel_id=1, source_target_pairs={{16,32},{32,16},{48,64},{64,48},{80,96},{96,80},{112,128},{128,112... | collective-permute-start | bytes 294920 | tf_op jit(solution)/shard_map/ppermute | solution.py:23
  203.4 6.2 %collective-permute-start.27 = (f32[16,24,128]{2,1,0:T(8,128)S(1)}, f32[16,24,128]{2,1,0:T(8,128)S(1)}, u32[]{:S(2)}, u32[]{:S(2)}) collective-permute-start(f32[16,24,128]{2,1,0:T(8,128)S(1)} %bitcast.125), channel_id=1, source_target_pairs={{0,1},{1,0},{2,3},{3,2},{4,5},{5,4},{6,7},{7,6},{8,9},{9,8},{10,11... | collective-permute-start | bytes 589832 | tf_op jit(solution)/shard_map/ppermute | solution.py:23
  205.3 7.6 %collective-permute-start.28 = (f32[16,24,128]{2,1,0:T(8,128)S(1)}, f32[16,24,128]{2,1,0:T(8,128)S(1)}, u32[]{:S(2)}, u32[]{:S(2)}) collective-permute-start(f32[16,24,128]{2,1,0:T(8,128)S(1)} %bitcast.124), channel_id=1, source_target_pairs={{1,2},{2,1},{3,4},{4,3},{5,6},{6,5},{7,8},{8,7},{9,10},{10,9},{11,... | collective-permute-start | bytes 589832 | tf_op jit(solution)/shard_map/ppermute | solution.py:23

commit v5 on v4

v5 whole, which is shorter than its diff:
```python
import functools
import math

import jax
import jax.numpy as jnp
from jax import lax
from jax.experimental import pallas as pl
from jax.experimental.pallas import tpu as pltpu
from jax.sharding import PartitionSpec as P

THETA = 8.0
DELTA = 6.5
ROOTS = tuple(THETA + DELTA * math.cos(math.pi * (2 * k + 1) / 6) for k in range(3))
HALO = 3


def swap(x, axis, dist, odd):
    count = lax.axis_size(axis)
    pairs = []
    for i in range(count - dist):
        if (i // dist) % 2 == odd:
            pairs += [(i, i + dist), (i + dist, i)]
    return lax.ppermute(x, axis, pairs)


def parity(axis, dist):
    return lax.rem(lax.div(lax.axis_index(axis), dist), 2)


def swap_ends(at, low, high, axis, dist):
    even = at[axis]
    first = swap(jnp.where(even, high, low), axis, dist, 0)
    second = swap(jnp.where(even, low, high), axis, dist, 1)
    return first, second


def in_order(at, first, second, axis):
    even = at[axis]
    return jnp.where(even, second, first), jnp.where(even, first, second)


def cells(x):
    return x.reshape((-1,) + x.shape[-2:])


def z_neighbours(v):
    lane = lax.broadcasted_iota(jnp.int32, v.shape, 1)
    below = jnp.where(lane == 0, 0.0, pltpu.roll(v, 1, 1))
    above = jnp.where(lane == v.shape[1] - 1, 0.0, pltpu.roll(v, v.shape[1] - 1, 1))
    return below + above


def inside(at, size):
    return jnp.where((at >= 0) & (at < size), 1.0, 0.0).astype(jnp.float32)


def beside(src, x, y):
    centre = src[x, y]
    total = (src[x - 1, y] + src[x + 1, y]) + (src[x, y - 1] + src[x, y + 1])
    return total + z_neighbours(centre), centre


def factor_cell(src, x, y, shift_row, root, mask):
    total, centre = beside(src, x, y)
    scale = mask * (1.0 / root)
    return (scale * ((root - 6.0) - shift_row)) * centre + scale * total


def each_row(count, row):
    if count <= 4:
        for x in range(count):
            row(x)
        return

    def pair(step, carry):
        row(2 * step)
        row(2 * step + 1)
        return carry

    lax.fori_loop(0, count // 2, pair, 0)


def factor(src, dst, shift, shift_at, size, root, masks):
    def row(x):
        row_mask = masks(x, None)
        for y in range(size[1]):
            shift_row = shift[x + shift_at[0], pl.ds(y + shift_at[1], 1), :]
            mask = row_mask * masks(None, y)
            dst[x, y] = factor_cell(src, x + 1, y + 1, shift_row, root, mask)

    each_row(size[0], row)


def masks_of(first, reach, grid):
    def masks(x, y):
        if x is not None:
            return inside(first[0] + x - reach, grid[0])
        return inside(first[1] + y - reach, grid[1])

    return masks


def triangle_cells(n, reach):
    return sum(n + 2 * (reach - d) for d in range(1, reach + 1))


def put_triangles(dst, pieces, where, n, width, reach):
    for odd, (ref, at) in enumerate(pieces):
        for d in range(1, reach + 1):
            column = jnp.where(where[2] == odd, reach + width - 1 + d, reach - d)
            for x in range(d, n + 2 * reach - d):
                dst[x, column] = ref[at]
                at += 1


def put_frame(dst, own, pieces, where, n, reach, own_at=0):
    x_even, x_odd, y_even, y_odd = pieces

    def middle(x):
        for y in range(n):
            dst[x + reach, y + reach] = own[x + own_at, y + own_at]

    each_row(n, middle)
    for odd, ref in enumerate((x_even, x_odd)):
        at = jnp.where(where[3] == odd, n + reach, 0)
        for x in range(reach):
            for y in range(n):
                dst[at + x, reach + y] = ref[x * n + y]
    put_triangles(dst, [(y_even, 0), (y_odd, 0)], where, n, n, reach)


def put_rows(dst, rows, pieces, where, n, width, reach):
    def row(x):
        for y in range(width):
            dst[x, reach + y] = rows[x, y]

    each_row(n + 2 * reach, row)
    put_triangles(dst, pieces, where, n, width, reach)


def put_shift(wide, one, two, own, pieces, where, n):
    x_even, x_odd, y_even, y_odd = pieces
    chans = x_even.shape[1]
    strip, side = HALO * n, triangle_cells(n, HALO)

    def line(ref, first, x):
        at = x * n
        return ref[first + at // chans, at % chans : at % chans + n, :]

    for odd, x_ref, y_ref in ((0, x_even, y_even), (1, x_odd, y_odd)):
        row = jnp.where(where[3] == odd, 2 * n, 0)
        column = pl.ds(pl.multiple_of(jnp.where(where[2] == odd, 2 * n, 0), n), n)
        for x in range(n):
            wide[row + x, n : 2 * n, :] = line(x_ref, strip, x)
        for x in range(3 * n):
            wide[x, column, :] = line(y_ref, side, x)
    for x in range(n):
        wide[n + x, n : 2 * n, :] = own[x]

    def halve(src, x, count):
        total = 0.0
        for k in range(4):
            total = total + src[2 * x + k // 2, pl.ds(k % 2, count, 2), :]
        return 0.25 * total

    half = n // 2
    for x in range(3 * half):
        one[x] = halve(wide, x, 3 * half)
    for x in range(3 * half // 2):
        two[x] = halve(one, x, 3 * half // 2)


def put_coarse_shift(dst, own, pieces, where, n):
    x_even, x_odd, y_even, y_odd = pieces
    strip, side = HALO * n, triangle_cells(n, HALO)
    wide = own.shape[0]
    for x in range(wide):
        dst[x + 2, 2 : wide + 2, :] = own[x]
    for odd, x_ref, y_ref in ((0, x_even, y_even), (1, x_odd, y_odd)):
        row = jnp.where(where[3] == odd, wide + 2, 0)
        for x in range(2):
            dst[row + x, 2 : wide + 2, :] = x_ref[strip, wide * x : wide * (x + 1), :]

        def aside(after, y_ref=y_ref):
            at = wide + 2 if after else 0
            for x in range(wide + 4):
                dst[x, at : at + 2, :] = y_ref[side, 2 * x : 2 * x + 2, :]

        for value in (0, 1):
            pl.when(where[2] == value)(functools.partial(aside, value == odd))


def down_body(size, beyond, grid, first, pad, shift, shift_at, iterate, leftover, coarser, one, two):
    nx, ny = size[0] + 2 * beyond, size[1] + 2 * beyond
    sx, sy = shift_at
    factor(pad, one, shift, (sx, sy), (nx + 4, ny + 4), ROOTS[0], masks_of(first, beyond + 2, grid))
    factor(one, two, shift, (sx + 1, sy + 1), (nx + 2, ny + 2), ROOTS[1], masks_of(first, beyond + 1, grid))
    masks = masks_of(first, beyond, grid)

    def row(x):
        row_mask = masks(x, None) if beyond else 1.0
        for y in range(ny):
            shift_row = shift[x + 2 + sx, pl.ds(y + 2 + sy, 1), :]
            mask = row_mask * masks(None, y) if beyond else 1.0
            leftover[x, y] = factor_cell(two, x + 1, y + 1, shift_row, ROOTS[2], mask)
            iterate[x, y] = (
                pad[x + 3, y + 3] * (1.0 / ROOTS[0])
                + one[x + 2, y + 2] * (1.0 / ROOTS[1])
                + two[x + 1, y + 1] * (1.0 / ROOTS[2])
            )

    each_row(nx, row)

    def coarse_row(x):
        for y in range(size[1] // 2):
            i, j = 2 * x + beyond, 2 * y + beyond
            near = leftover[i, j] + leftover[i, j + 1]
            far = leftover[i + 1, j] + leftover[i + 1, j + 1]
            coarser[x, y] = 0.25 * (near + far)

    each_row(size[0] // 2, coarse_row)


def down_fine_kernel(n, grid, where, own, *refs):
    pieces, own_shift = refs[:4], refs[4]
    iterate, leftover, coarser, shift, shift_one, shift_two, pad, one, two = refs[5:]
    put_frame(pad, own, pieces, where, n, HALO)
    put_shift(shift, shift_one, shift_two, own_shift, pieces, where, n)
    first = (where[0] * n, where[1] * n)
    down_body((n, n), 0, grid, first, pad, shift, (n - 2, n - 2), iterate, leftover, coarser, one, two)


def down_kernel(n, grid, where, own, *refs):
    pieces, shift, shift_near = refs[:4], refs[4], refs[5]
    iterate, leftover, coarser, shift_wide, pad, one, two = refs[6:]
    put_frame(pad, own, pieces, where, n, HALO)
    put_coarse_shift(shift_wide, shift_near, pieces, where, n)
    first = (where[0] * n, where[1] * n)
    down_body((n, n), 0, grid, first, pad, shift, (2, 2), iterate, leftover, coarser, one, two)


def down_chip_kernel(size, grid, where, rows, left, right, shift, iterate, leftover, coarser, pad, one, two):
    def row(x):
        for y in range(size[1]):
            pad[x, y + 4] = rows[x, y]

    each_row(size[0] + 8, row)
    for ref, base in ((left, 0), (right, 4 + size[1])):
        for y in range(4):
            near = y >= 2 if base == 0 else y < 2
            for x in range(8 if near else 4):
                cell = 2 * x + y % 2 + (0 if near else 16)
                pad[x + (1 if near else 3), base + y] = ref[cell]
    first = (where[0] * size[0], (where[1] - where[2]) * size[0])
    down_body(size, 1, grid, first, pad, shift, (1, 1), iterate, leftover, coarser, one, two)


def solve_kernel(where, shares, inverse, solved, ordered):
    count, rows, depth = shares.shape
    chans = solved.shape[0]
    for m in range(count):
        block = jnp.zeros((chans, depth), jnp.float32)
        for j in range(count):
            block = jnp.where(shares[j, chans : chans + 1, :] == float(m), shares[j, 0:chans, :], block)
        ordered[:, m * depth : (m + 1) * depth] = block
    solved[...] = lax.dot_general(
        ordered[...],
        inverse[...],
        (((1,), (1,)), ((), ())),
        precision=lax.Precision.HIGHEST,
        preferred_element_type=jnp.float32,
    )


def pick_kernel(where, shares, back, picked):
    count, chans, depth = back.shape
    for k in range(picked.shape[0]):
        j = where[1] - where[2] + k - 2
        slot = shares[jnp.clip(j, 0, count - 1), pl.ds(chans, 1), :]
        slot = jnp.where((j >= 0) & (j < count), slot, -1.0)
        block = jnp.zeros((chans, depth), jnp.float32)
        for m in range(count):
            block = jnp.where(slot == float(m), back[m], block)
        picked[k] = block


def up_body(n, beyond, grid, where, coarse, reach, shift, shift_at, iterate, result, start, one):
    sx, sy = shift_at
    first = (where[0] * n, where[1] * n)
    wide = n + 2 * beyond
    outer, masks = masks_of(first, beyond + 2, grid), masks_of(first, beyond, grid)
    offset = 2 * reach - beyond - 2

    def first_row(x):
        row_mask = outer(x, None)
        here, before, after = (x + offset) // 2, (x + offset - 1) // 2, (x + offset + 1) // 2
        for y in range(wide + 4):
            at, left, right = (y + offset) // 2, (y + offset - 1) // 2, (y + offset + 1) // 2
            centre = coarse[here, at]
            total = (coarse[before, at] + coarse[after, at]) + (coarse[here, left] + coarse[here, right])
            total = total + z_neighbours(centre)
            shift_row = shift[x + sx, pl.ds(y + sy, 1), :]
            mask = row_mask * outer(None, y)
            start[x, y] = mask * ((start[x, y] - (6.0 + shift_row) * centre) + total)

    each_row(wide + 4, first_row)
    factor(start, one, shift, (sx + 1, sy + 1), (wide + 2, wide + 2), ROOTS[0], masks_of(first, beyond + 1, grid))

    def row(x):
        row_mask = masks(x, None) if beyond else 1.0
        for y in range(wide):
            shift_row = shift[x + 2 + sx, pl.ds(y + 2 + sy, 1), :]
            mask = row_mask * masks(None, y) if beyond else 1.0
            two = factor_cell(one, x + 1, y + 1, shift_row, ROOTS[1], mask)
            step = (
                start[x + 2, y + 2] * (1.0 / ROOTS[0]) + one[x + 1, y + 1] * (1.0 / ROOTS[1]) + two * (1.0 / ROOTS[2])
            )
            below = coarse[(x - beyond + 2 * reach) // 2, (y - beyond + 2 * reach) // 2]
            result[x, y] = (iterate[x, y] + below) + step

    each_row(wide, row)


def up_block_kernel(n, grid, offset, where, fix, mine, others, shift, iterate, rows, even, odd, result, coarse, start, one):
    core, line, far = where[2], where[4], where[5]
    for k in range(5):
        coarse[2, k] = fix[core + k]
        coarse[3 - 2 * line, k] = mine[core + k]
        coarse[1 + 2 * line, k] = others[core + k]
        coarse[4 * far, k] = mine[6 + core + k]
        coarse[4 - 4 * far, k] = others[6 + core + k]
    put_rows(start, rows, [(even, offset), (odd, offset)], where, n, n, 3)
    up_body(n, 1, grid, where, coarse, 2, shift, (1, 1), iterate, result, start, one)


def up_middle_kernel(
    n, grid, offset, iterate_offset, where, coarse_own, x_even, x_odd, y_even, y_odd, shift, iterate_rows, rows, even, odd,
    result, coarse, iterate, start, one,
):
    put_frame(coarse, coarse_own, [x_even, x_odd, y_even, y_odd], where, n // 2, 3, 1)
    put_rows(start, rows, [(even, offset), (odd, offset)], where, n, n, 4)
    put_rows(iterate, iterate_rows, [(even, iterate_offset), (odd, iterate_offset)], where, n, n, 2)
    up_body(n, 2, grid, where, coarse, 3, shift, (0, 0), iterate, result, start, one)


def up_fine_kernel(n, grid, offset, where, coarse, shift, iterate, rows, even, odd, result, start, one):
    put_rows(start, rows, [(even, offset), (odd, offset)], where, n, n, 2)
    up_body(n, 0, grid, where, coarse, 2, shift, (n - 2, n - 2), iterate, result, start, one)


VMEM = pl.BlockSpec(memory_space=pltpu.VMEM)
SMEM = pl.BlockSpec(memory_space=pltpu.SMEM)


def call(kernel, where, operands, outs, scratch, name):
    return pl.pallas_call(
        kernel,
        out_shape=[jax.ShapeDtypeStruct(out, jnp.float32) for out in outs],
        in_specs=[SMEM] + [VMEM] * len(operands),
        out_specs=[VMEM] * len(outs),
        scratch_shapes=[pltpu.VMEM(own, jnp.float32) for own in scratch],
        compiler_params=pltpu.CompilerParams(vmem_limit_bytes=12 * 1024 * 1024),
        name=name,
    )(where, *operands)


def place():
    core = parity("gy", 1)
    line, far = parity("gx", 1), parity("gx", 2)
    numbers = [lax.axis_index("gx"), lax.axis_index("gy"), core, line, line ^ core, far ^ core]
    where = jnp.stack(numbers + [jnp.zeros_like(core)] * 2).astype(jnp.int32)
    sides = {
        "gx": line == 0,
        "gy": core == 0,
        "line": line == core,
        "far": far != core,
        "chip": parity("gy", 2) == core,
    }
    return where, sides


def grid_of(n):
    return (lax.axis_size("gx") * n, lax.axis_size("gy") * n)


def triangle(columns, n, reach):
    parts = []
    for d, column in enumerate(columns, 1):
        over = (column.shape[0] - n) // 2 - (reach - d)
        parts.append(column[over : column.shape[0] - over])
    return jnp.concatenate(parts, axis=0)


def columns_of(rows, reach):
    width = rows.shape[1]
    return [rows[:, d] for d in range(reach)], [rows[:, width - 1 - d] for d in range(reach)]


def with_rows(strip, rows, tail):
    if rows is None:
        return strip
    rows = rows.reshape(-1, tail[1])
    rows = jnp.pad(rows, ((0, -rows.shape[0] % tail[0]), (0, 0)))
    return jnp.concatenate([strip, rows.reshape((-1,) + tail)], axis=0)


def frame(at, v, reach, beyond=0, blocks=None, rims=None):
    n = v.shape[0] - 2 * beyond
    tail = v.shape[-2:]
    own = v[beyond : beyond + n, beyond : beyond + n]
    extra = [blocks, blocks] if rims is None else [rims[-2:], rims[:2]]
    low = v[beyond : beyond + reach, beyond : beyond + n]
    high = v[beyond + n - reach : beyond + n, beyond : beyond + n]
    x_pieces = swap_ends(at, with_rows(cells(low), extra[0], tail), with_rows(cells(high), extra[1], tail), "gx", 1)
    sides = in_order(at, *x_pieces, "gx")
    strips = [side[: reach * n].reshape((reach, n) + tail) for side in sides]
    rows = jnp.concatenate([strips[0], own, strips[1]], axis=0)
    known = min(reach, n)
    low, high = columns_of(rows, known)
    for d in range(known, reach):
        low.append(v[beyond : beyond + n, beyond + d])
        high.append(v[beyond : beyond + n, beyond + n - 1 - d])
    if blocks is not None or rims is not None:
        sent = extra[0].shape

        def rows_of(side):
            return side[reach * n :].reshape(-1, tail[1])[: sent[0] * sent[1]].reshape(sent)

        extra = jnp.concatenate([rows_of(sides[0]), blocks if rims is None else rims, rows_of(sides[1])], axis=0)
        extra = [extra, extra] if rims is None else [extra[:, -2:], extra[:, :2]]
    low, high = triangle(low, n, reach), triangle(high, n, reach)
    y_pieces = swap_ends(at, with_rows(low, extra[0], tail), with_rows(high, extra[1], tail), "gy", 1)
    return [*x_pieces, *y_pieces]


def by_core(x, swaps):
    lines, blocks = lax.axis_size("gx"), lax.axis_size("gy")
    pairs = []
    for j in range(blocks):
        dist, odd = swaps[j % 2]
        for i in range(lines - dist):
            if (i // dist) % 2 == odd:
                pairs += [(i * blocks + j, (i + dist) * blocks + j), ((i + dist) * blocks + j, i * blocks + j)]
    return lax.ppermute(x, ("gx", "gy"), pairs)


def to_core(x):
    return swap(x, "gy", 1, 0)


def lines_around(near):
    first = by_core(near, [(1, 0), (1, 1)])
    second = by_core(near, [(2, 1), (2, 0)])
    mine = jnp.concatenate([cells(first), cells(second)], axis=0)
    return mine, to_core(mine)


def body(rhs, shift, slots, coarse_inverse):
    where, at = place()
    where, at, rhs = lax.optimization_barrier((where, at, rhs))
    right = jnp.transpose(rhs, (1, 2, 0, 3))
    n = right.shape[0]
    tail = chans, depth = right.shape[2:]
    half, size = n // 2, n // 4

    def fields(*shapes):
        return [shape + tail for shape in shapes]

    x0, q0, b1, shift_wide, shift_one, shift_two = call(
        functools.partial(down_fine_kernel, n, grid_of(n)),
        where,
        [right, *frame(at, right, HALO, 0, shift), shift],
        fields((n, n), (n, n), (half, half))
        + [(3 * n, 3 * n, depth), (3 * half, 3 * half, depth), (3 * size, 3 * size, depth)],
        fields((n + 6, n + 6), (n + 4, n + 4), (n + 2, n + 2)),
        "down_fine",
    )
    x1, q1, b2, shift_two = call(
        functools.partial(down_kernel, half, grid_of(half)),
        where,
        [b1, *frame(at, b1, HALO, 0, None, shift_two), shift_one, shift_two],
        fields((half, half), (half, half), (size, size)) + [(3 * size + 4, 3 * size + 4, depth)],
        fields((half + 6, half + 6), (half + 4, half + 4), (half + 2, half + 2)),
        "down_middle",
    )

    first_core = at["gy"]
    edge = jnp.where(first_core, shift_two[:, :2], shift_two[:, -2:])
    other = to_core(with_rows(cells(b2), edge, tail))
    edge = other[size * size :].reshape(-1, depth)[: edge.shape[0] * 2].reshape(edge.shape)
    other = other[: size * size].reshape(b2.shape)
    chip = jnp.concatenate([jnp.where(first_core, b2, other), jnp.where(first_core, other, b2)], axis=1)
    chip_shift = jnp.where(
        first_core, jnp.concatenate([shift_two, edge], axis=1), jnp.concatenate([edge, shift_two], axis=1)
    )
    mine, others = lines_around(chip)
    near = 2 * size * size
    (mine_near, other_near), (mine_far, other_far) = [
        [v[part].reshape(chip.shape) for v in (mine, others)] for part in (slice(0, near), slice(near, 2 * near))
    ]
    rows = jnp.concatenate(
        [
            jnp.where(at["far"], other_far, mine_far),
            jnp.where(at["line"], other_near, mine_near),
            chip,
            jnp.where(at["line"], mine_near, other_near),
            jnp.where(at["far"], mine_far, other_far),
        ],
        axis=0,
    )
    blocks = lax.axis_size("gy")
    pairs = []
    for j in range(blocks - 2):
        if (j // 2) % 2 == j % 2:
            pairs += [(j, j + 2), (j + 2, j)]
    high = jnp.concatenate([cells(rows[1:-1, -2:]), cells(rows[3:-3, :2])], axis=0)
    low = jnp.concatenate([cells(rows[1:-1, :2]), cells(rows[3:-3, -2:])], axis=0)
    mine = lax.ppermute(jnp.where(at["chip"], high, low), "gy", pairs)
    others = to_core(mine)
    x2, q2, b3 = call(
        functools.partial(down_chip_kernel, (size, 2 * size), grid_of(size)),
        where,
        [rows, jnp.where(at["chip"], others, mine), jnp.where(at["chip"], mine, others), chip_shift],
        fields((size + 2, 2 * size + 2), (size + 2, 2 * size + 2), (1, 2)),
        fields((size + 8, 2 * size + 8), (size + 6, 2 * size + 6), (size + 4, 2 * size + 4)),
        "down_chip",
    )
    x2, q2 = [jnp.where(first_core, v[:, : size + 2], v[:, size:]) for v in (x2, q2)]
    b3 = jnp.where(first_core, b3[0, 0], b3[0, 1])

    own = [q0, q1, x1, q2[1:-1, 1:-1]]
    reaches = [2, 4, 2, 3]
    low = jnp.concatenate([cells(q0[:2]), cells(q1), cells(x1[:2]), cells(q2[1:, 1:-1])], axis=0)
    high = jnp.concatenate([cells(q0[-2:]), cells(q1), cells(x1[-2:]), cells(q2[:-1, 1:-1])], axis=0)
    ends = swap_ends(at, low, high, "gx", 1)

    slot = jnp.broadcast_to(slots.astype(jnp.float32), (8, depth))
    shares = lax.all_gather(jnp.concatenate([b3, slot], axis=0)[None], "gy", axis=0, tiled=True)
    ends, shares = lax.optimization_barrier((ends, shares))
    before, after = in_order(at, *ends, "gx")
    around, lows, highs, offsets, done = [], [], [], [0], 0
    for v, reach in zip(own, reaches):
        strip = reach * v.shape[1]
        parts = [side[done : done + strip].reshape((reach,) + v.shape[1:]) for side in (before, after)]
        around.append(jnp.concatenate([parts[0], v, parts[1]], axis=0))
        low, high = columns_of(around[-1], min(reach, v.shape[1]))
        if reach > v.shape[1]:
            low, high = low + [q2[1:-1, -1]], high + [q2[1:-1, 0]]
        lows.append(triangle(low, v.shape[0], reach))
        highs.append(triangle(high, v.shape[0], reach))
        offsets.append(offsets[-1] + lows[-1].shape[0])
        done += strip
    sides = swap_ends(at, jnp.concatenate(lows, axis=0), jnp.concatenate(highs, axis=0), "gy", 1)
    solved = call(
        solve_kernel, where, [shares, coarse_inverse[0, 0]], [tail], [(chans, blocks * depth)], "solve"
    )[0]
    back = lax.all_gather(solved[None], "gy", axis=0, tiled=True)
    fix = call(pick_kernel, where, [shares, back], [(6,) + tail], [], "pick")[0]

    x2 = call(
        functools.partial(up_block_kernel, size, grid_of(size), offsets[3]),
        where,
        [fix, *lines_around(fix), shift_two, x2, around[3], *sides],
        fields((size + 2, size + 2)),
        fields((5, 5), (size + 6, size + 6), (size + 4, size + 4)),
        "up_block",
    )[0]
    x1 = call(
        functools.partial(up_middle_kernel, half, grid_of(half), offsets[1], offsets[2]),
        where,
        [x2, *frame(at, x2, 3, 1), shift_one, around[2], around[1], *sides],
        fields((half + 4, half + 4)),
        fields((size + 6, size + 6), (half + 4, half + 4), (half + 8, half + 8), (half + 6, half + 6)),
        "up_middle",
    )[0]
    x0 = call(
        functools.partial(up_fine_kernel, n, grid_of(n), offsets[0]),
        where,
        [x1, shift_wide, x0, around[0], *sides],
        fields((n, n)),
        fields((n + 4, n + 4), (n + 2, n + 2)),
        "up_fine",
    )[0]
    return jnp.transpose(x0, (2, 0, 1, 3))


def solution(mesh):
    return jax.shard_map(
        body,
        mesh=mesh,
        in_specs=(
            P(None, "gx", "gy", None),
            P("gx", "gy", None),
            P("gx", "gy"),
            P("gx", "gy", None, None),
        ),
        out_specs=P(None, "gx", "gy", None),
        check_vma=False,
    )
```

time: 219 us -> 192 us (0.88)
  waiting for transfers between devices: 56 us -> 35.3 us
  starting transfers between devices: 98.3 us -> 86.4 us
  Pallas kernels: 16.6 us -> 19.8 us
    ppermute x24 -> x20, waiting for transfers between devices: 47.1 us -> 28.6 us  [swap(): return lax.ppermute(x, axis, pairs)]
    ppermute x24 -> x20, starting transfers between devices: 85.1 us -> 70.4 us  [swap(): return lax.ppermute(x, axis, pairs)]
    pallas_call x8, Pallas kernels: 16.6 us -> 19.8 us  [call(): pl.pallas_call(kernel, out_shape=[jax.ShapeDtypeStruct(out, jnp.float32)...]
    ppermute x4, waiting for transfers between devices: 8.91 us -> 6.64 us  [by_core(): return lax.ppermute(x, ('gx', 'gy'), pairs)]
  transfers between devices with their start and end apart: 29 -> 25, of which waited for: 17 -> 16; matrix products, arithmetic and copies ran while one was open for 0% -> 0% of each run, Pallas kernels for 1% -> 1%
where the time goes in v5:
time: 192 us; the launch traced here: 191 us
  starting transfers between devices  86.4 us (45%)
  blocking collectives  41 us (21%)
  waiting for transfers between devices  35.3 us (18%)
  Pallas kernels  19.8 us (10%)
  local copies, waits for them, and re-layouts  4.59 us (2%)
  other arithmetic  2.21 us (1%)
    ppermute x20, starting transfers between devices, swap(): return lax.ppermute(x, axis, pairs)  70.4 us
    ppermute x20, waiting for transfers between devices, swap(): return lax.ppermute(x, axis, pairs)  28.6 us
    all_gather x1, blocking collectives, body(): lax.all_gather(jnp.concatenate([b3, slot], axis=0)[None], 'gy', axis=0, t...  21.9 us
    pallas_call x8, Pallas kernels, call(): pl.pallas_call(kernel, out_shape=[jax.ShapeDtypeStruct(out, jnp.float32)...  19.8 us
    all_gather x1, blocking collectives, body(): back = lax.all_gather(solved[None], 'gy', axis=0, tiled=True)  19.1 us
    ppermute x4, starting transfers between devices, by_core(): return lax.ppermute(x, ('gx', 'gy'), pairs)  14.6 us
    ppermute x4, waiting for transfers between devices, by_core(): return lax.ppermute(x, ('gx', 'gy'), pairs)  6.64 us
  transfers between devices with their start and end apart: 25, of which 16 were waited for; matrix products, arithmetic and copies ran while one was open for 0% of the time, Pallas kernels for 1%

profile of v5, /device:TPU:31, one launch (start us, length us, event | category | flops | bytes accessed | tf_op | source)
XLA Modules:
  0.0 191.0 jit_solution(18421362182987728742)
XLA Ops:
  2.5 4.3 %collective-permute-start.1 = (f32[27,24,128]{2,1,0:T(8,128)S(1)}, f32[27,24,128]{2,1,0:T(8,128)S(1)}, u32[]{:S(2)}, u32[]{:S(2)}) collective-permute-start(f32[27,24,128]{2,1,0:T(8,128)S(1)} %get-tuple-element.79), channel_id=1, source_target_pairs={{16,32},{32,16},{48,64},{64,48},{80,96},{96,80},{112,128},{128,112... | collective-permute-start | bytes 995336 | tf_op jit(solution)/shard_map/ppermute | solution.py:23
  6.8 1.9 %collective-permute-start = (f32[27,24,128]{2,1,0:T(8,128)S(1)}, f32[27,24,128]{2,1,0:T(8,128)S(1)}, u32[]{:S(2)}, u32[]{:S(2)}) collective-permute-start(f32[27,24,128]{2,1,0:T(8,128)S(1)} %get-tuple-element.80), channel_id=1, source_target_pairs={{0,16},{16,0},{32,48},{48,32},{64,80},{80,64},{96,112},{112,96},{1... | collective-permute-start | bytes 995336 | tf_op jit(solution)/shard_map/ppermute | solution.py:23
  8.8 7.6 %collective-permute-done.1.refs_1_ = f32[27,24,128]{2,1,0:T(8,128)S(1)} collective-permute-done((f32[27,24,128]{2,1,0:T(8,128)S(1)}, f32[27,24,128]{2,1,0:T(8,128)S(1)}, u32[]{:S(2)}, u32[]{:S(2)}) %collective-permute-start.1) | collective-permute-done | bytes 331808 | tf_op jit(solution)/shard_map/ppermute | solution.py:23
  17.4 5.9 %collective-permute-start.3 = (f32[38,24,128]{2,1,0:T(8,128)S(1)}, f32[38,24,128]{2,1,0:T(8,128)S(1)}, u32[]{:S(2)}, u32[]{:S(2)}) collective-permute-start(f32[38,24,128]{2,1,0:T(8,128)S(1)} %get-tuple-element.67), channel_id=1, source_target_pairs={{1,2},{2,1},{3,4},{4,3},{5,6},{6,5},{7,8},{8,7},{9,10},{10,9},{11,... | collective-permute-start | bytes 1400840 | tf_op jit(solution)/shard_map/ppermute | solution.py:23
  23.3 1.9 %collective-permute-start.2 = (f32[38,24,128]{2,1,0:T(8,128)S(1)}, f32[38,24,128]{2,1,0:T(8,128)S(1)}, u32[]{:S(2)}, u32[]{:S(2)}) collective-permute-start(f32[38,24,128]{2,1,0:T(8,128)S(1)} %get-tuple-element.68), channel_id=1, source_target_pairs={{0,1},{1,0},{2,3},{3,2},{4,5},{5,4},{6,7},{7,6},{8,9},{9,8},{10,11... | collective-permute-start | bytes 1400840 | tf_op jit(solution)/shard_map/ppermute | solution.py:23
  25.7 3.8 %collective-permute-done.3.refs_3_ = f32[38,24,128]{2,1,0:T(8,128)S(1)} collective-permute-done((f32[38,24,128]{2,1,0:T(8,128)S(1)}, f32[38,24,128]{2,1,0:T(8,128)S(1)}, u32[]{:S(2)}, u32[]{:S(2)}) %collective-permute-start.3) | collective-permute-done | bytes 466976 | tf_op jit(solution)/shard_map/ppermute | solution.py:23
  29.5 3.8 %down_fine.1 = (f32[8,8,24,128]{3,2,1,0:T(8,128)S(1)}, f32[8,8,24,128]{3,2,1,0:T(8,128)S(1)}, f32[4,4,24,128]{3,2,1,0:T(8,128)S(1)}, f32[24,24,128]{2,1,0:T(8,12...) custom-call(s32[8]{0:T(128)S(1)} %stack.27.where, f32[8,8,24,128]{3,2,1,0:T(8,128)S(1)} %copy.37.own, ...), custom_call_target="tpu_custom_call" | custom-call | tf_op jit(solution)/shard_map/down_fine/pallas_call | solution.py:356
  33.5 4.3 %collective-permute-start.5 = (f32[13,24,128]{2,1,0:T(8,128)S(1)}, f32[13,24,128]{2,1,0:T(8,128)S(1)}, u32[]{:S(2)}, u32[]{:S(2)}) collective-permute-start(f32[13,24,128]{2,1,0:T(8,128)S(1)} %get-tuple-element.105), channel_id=1, source_target_pairs={{16,32},{32,16},{48,64},{64,48},{80,96},{96,80},{112,128},{128,112... | collective-permute-start | bytes 479240 | tf_op jit(solution)/shard_map/ppermute | solution.py:23
  39.7 3.1 %collective-permute-done.5.refs_1_ = f32[13,24,128]{2,1,0:T(8,128)S(1)} collective-permute-done((f32[13,24,128]{2,1,0:T(8,128)S(1)}, f32[13,24,128]{2,1,0:T(8,128)S(1)}, u32[]{:S(2)}, u32[]{:S(2)}) %collective-permute-start.5) | collective-permute-done | bytes 159776 | tf_op jit(solution)/shard_map/ppermute | solution.py:23
  44.2 6.2 %collective-permute-start.7 = (f32[19,24,128]{2,1,0:T(8,128)S(1)}, f32[19,24,128]{2,1,0:T(8,128)S(1)}, u32[]{:S(2)}, u32[]{:S(2)}) collective-permute-start(f32[19,24,128]{2,1,0:T(8,128)S(1)} %get-tuple-element.99), channel_id=1, source_target_pairs={{1,2},{2,1},{3,4},{4,3},{5,6},{6,5},{7,8},{8,7},{9,10},{10,9},{11,... | collective-permute-start | bytes 700424 | tf_op jit(solution)/shard_map/ppermute | solution.py:23
  50.4 1.9 %collective-permute-start.6 = (f32[19,24,128]{2,1,0:T(8,128)S(1)}, f32[19,24,128]{2,1,0:T(8,128)S(1)}, u32[]{:S(2)}, u32[]{:S(2)}) collective-permute-start(f32[19,24,128]{2,1,0:T(8,128)S(1)} %get-tuple-element.100), channel_id=1, source_target_pairs={{0,1},{1,0},{2,3},{3,2},{4,5},{5,4},{6,7},{7,6},{8,9},{9,8},{10,11... | collective-permute-start | bytes 700424 | tf_op jit(solution)/shard_map/ppermute | solution.py:23
  54.1 1.9 %down_middle.1 = (f32[4,4,24,128]{3,2,1,0:T(8,128)S(1)}, f32[4,4,24,128]{3,2,1,0:T(8,128)S(1)}, f32[2,2,24,128]{3,2,1,0:T(8,128)S(1)}, f32[10,10,128]{2,1,0:T(8,128)S(1)}) custom-call(s32[8]{0:T(128)S(1)} %stack.27.where, f32[4,4,24,128]{3,2,1,0:T(8,128)S(1)} %get-tuple-element.33.own, f32[13,24,128]{2,1,0:T(8,128)S(1)} %collective-permute-done.4.refs_0_, ...), custom_call_target="tpu_custom_call" | custom-call | tf_op jit(solution)/shard_map/down_middle/pallas_call | solution.py:356
  56.1 1.9 %collective-permute-start.8 = (f32[5,24,128]{2,1,0:T(8,128)S(1)}, f32[5,24,128]{2,1,0:T(8,128)S(1)}, u32[]{:S(2)}, u32[]{:S(2)}) collective-permute-start(f32[5,24,128]{2,1,0:T(8,128)S(1)} %pad_maximum_fusion.28), channel_id=1, source_target_pairs={{0,1},{1,0},{2,3},{3,2},{4,5},{5,4},{6,7},{7,6},{8,9},{9,8},{10,11... | collective-permute-start | bytes 184328 | tf_op jit(solution)/shard_map/ppermute | solution.py:23
  61.2 5.3 %collective-permute-start.9 = (f32[2,4,24,128]{3,2,1,0:T(8,128)S(1)}, f32[2,4,24,128]{3,2,1,0:T(8,128)S(1)}, u32[]{:S(2)}, u32[]{:S(2)}) collective-permute-start(f32[2,4,24,128]{3,2,1,0:T(8,128)S(1)} %pad_maximum_fusion.25), channel_id=1, source_target_pairs={{0,16},{16,0},{32,48},{48,32},{64,80},{80,64},{96,112},{112,96},{1... | collective-permute-start | bytes 294920 | tf_op jit(solution)/shard_map/ppermute | solution.py:444
  66.6 3.5 %collective-permute-done.9 = f32[2,4,24,128]{3,2,1,0:T(8,128)S(1)} collective-permute-done((f32[2,4,24,128]{3,2,1,0:T(8,128)S(1)}, f32[2,4,24,128]{3,2,1,0:T(8,128)S(1)}, u32[]{:S(2)}, u32[]{:S(2)}) %collective-permute-start.9) | collective-permute-done | bytes 98336 | tf_op jit(solution)/shard_map/ppermute | solution.py:444
  70.1 2.2 %collective-permute-start.11 = (f32[16,24,128]{2,1,0:T(8,128)S(1)}, f32[16,24,128]{2,1,0:T(8,128)S(1)}, u32[]{:S(2)}, u32[]{:S(2)}) collective-permute-start(f32[16,24,128]{2,1,0:T(8,128)S(1)} %pad_maximum_fusion.11), channel_id=1, source_target_pairs={{0,1},{1,0},{2,3},{3,2},{4,5},{5,4},{6,7},{7,6},{8,9},{9,8},{10,11... | collective-permute-start | bytes 589832 | tf_op jit(solution)/shard_map/ppermute | solution.py:23
  75.1 9.8 %collective-permute-start.13 = (f32[24,24,128]{2,1,0:T(8,128)}, f32[24,24,128]{2,1,0:T(8,128)}, u32[]{:S(2)}, u32[]{:S(2)}) collective-permute-start(f32[24,24,128]{2,1,0:T(8,128)} %collective-permute-done.12), channel_id=1, source_target_pairs={{0,1},{1,0},{2,3},{3,2},{4,5},{5,4},{6,7},{7,6},{8,9},{9,8},{10,11... | collective-permute-start | bytes 884744 | tf_op jit(solution)/shard_map/ppermute | solution.py:23
  87.5 2.2 %down_chip.1 = (f32[4,6,24,128]{3,2,1,0:T(8,128)S(1)}, f32[4,6,24,128]{3,2,1,0:T(8,128)S(1)}, f32[1,2,24,128]{3,2,1,0:T(8,128)S(1)}) custom-call(s32[8]{0:T(128)S(1)} %stack.27.where, f32[10,4,24,128]{3,2,1,0:T(8,128)S(1)} %select_dynamic-update-slice_fusion.rows, f32[24,24,128]{2,1,0:T(8,128)S(1)} %get-tuple-element.88.left, ...), custom_call_target="tpu_custom_call" | custom-call | tf_op jit(solution)/shard_map/down_chip/pallas_call | solution.py:356
  89.9 5.0 %collective-permute-start.15 = (f32[46,24,128]{2,1,0:T(8,128)S(1)}, f32[46,24,128]{2,1,0:T(8,128)S(1)}, u32[]{:S(2)}, u32[]{:S(2)}) collective-permute-start(f32[46,24,128]{2,1,0:T(8,128)S(1)} %get-tuple-element.65), channel_id=1, source_target_pairs={{16,32},{32,16},{48,64},{64,48},{80,96},{96,80},{112,128},{128,112... | collective-permute-start | bytes 1695752 | tf_op jit(solution)/shard_map/ppermute | solution.py:23
  97.6 21.9 %all-gather = f32[512,128]{1,0:T(8,128)S(1)} all-gather(f32[32,128]{1,0:T(8,128)S(1)} %concatenate.126), channel_id=2, replica_groups=mesh['gx'=32,'gy'=16] {'gy'}, dimensions={0}, use_global_device_ids=true | all-gather | bytes 278528 | tf_op jit(solution)/shard_map/all_gather | solution.py:538
  120.3 2.1 %collective-permute-start.20 = (f32[68,24,128]{2,1,0:T(8,128)S(1)}, f32[68,24,128]{2,1,0:T(8,128)S(1)}, u32[]{:S(2)}, u32[]{:S(2)}) collective-permute-start(f32[68,24,128]{2,1,0:T(8,128)S(1)} %get-tuple-element.55), channel_id=1, source_target_pairs={{1,2},{2,1},{3,4},{4,3},{5,6},{6,5},{7,8},{8,7},{9,10},{10,9},{11,... | collective-permute-start | bytes 2506760 | tf_op jit(solution)/shard_map/ppermute | solution.py:23
  125.9 19.1 %all-gather.1 = f32[384,128]{1,0:T(8,128)S(1)} all-gather(f32[24,128]{1,0:T(8,128)S(1)} %solve.1), channel_id=3, replica_groups=mesh['gx'=32,'gy'=16] {'gy'}, dimensions={0}, use_global_device_ids=true | all-gather | bytes 208896 | tf_op jit(solution)/shard_map/all_gather | solution.py:557
  145.7 3.9 %collective-permute-start.16 = (f32[6,24,128]{2,1,0:T(8,128)S(1)}, f32[6,24,128]{2,1,0:T(8,128)S(1)}, u32[]{:S(2)}, u32[]{:S(2)}) collective-permute-start(f32[6,24,128]{2,1,0:T(8,128)S(1)} %pick.1.fix), channel_id=1, source_target_pairs={{0,16},{16,0},{32,48},{48,32},{64,80},{80,64},{96,112},{112,96},{1... | collective-permute-start | bytes 221192 | tf_op jit(solution)/shard_map/ppermute | solution.py:444
  149.6 3.4 %collective-permute-start.17 = (f32[6,24,128]{2,1,0:T(8,128)S(1)}, f32[6,24,128]{2,1,0:T(8,128)S(1)}, u32[]{:S(2)}, u32[]{:S(2)}) collective-permute-start(f32[6,24,128]{2,1,0:T(8,128)S(1)} %pick.1.fix), channel_id=1, source_target_pairs={{32,64},{64,32},{48,80},{80,48},{96,128},{128,96},{112,144},{144,1... | collective-permute-start | bytes 221192 | tf_op jit(solution)/shard_map/ppermute | solution.py:444
  154.1 2.1 %collective-permute-done.17 = f32[6,24,128]{2,1,0:T(8,128)S(1)} collective-permute-done((f32[6,24,128]{2,1,0:T(8,128)S(1)}, f32[6,24,128]{2,1,0:T(8,128)S(1)}, u32[]{:S(2)}, u32[]{:S(2)}) %collective-permute-start.17) | collective-permute-done | bytes 73760 | tf_op jit(solution)/shard_map/ppermute | solution.py:444
  156.2 5.3 %collective-permute-start.18 = (f32[12,24,128]{2,1,0:T(8,128)S(1)}, f32[12,24,128]{2,1,0:T(8,128)S(1)}, u32[]{:S(2)}, u32[]{:S(2)}) collective-permute-start(f32[12,24,128]{2,1,0:T(8,128)S(1)} %constant_dynamic-update-slice_fusion.6.mine), channel_id=1, source_target_pairs={{0,1},{1,0},{2,3},{3,2},{4,5},{5,4},{6,7},{7,6},{8,9},{9,8},{10,11... | collective-permute-start | bytes 442376 | tf_op jit(solution)/shard_map/ppermute | solution.py:23
  162.5 2.0 %up_block.1.coarse_own = f32[4,4,24,128]{3,2,1,0:T(8,128)S(1)} custom-call(s32[8]{0:T(128)S(1)} %stack.27.where, f32[6,24,128]{2,1,0:T(8,128)S(1)} %pick.1.fix, f32[12,24,128]{2,1,0:T(8,128)S(1)} %constant_dynamic-update-slice_fusion.6.mine, f32[12,24,128]{2,1,0:T(8,128)S(1)} %collective-permute-done.18.others, f32[10,10,128]{2,1,0:T(8,128)S(1)} %get-tuple-element.40.shift, ...), custom_call_target="tpu_custom_call" | custom-call | tf_op jit(solution)/shard_map/up_block/pallas_call | solution.py:356
  166.5 3.9 %collective-permute-start.22 = (f32[6,24,128]{2,1,0:T(8,128)S(1)}, f32[6,24,128]{2,1,0:T(8,128)S(1)}, u32[]{:S(2)}, u32[]{:S(2)}) collective-permute-start(f32[6,24,128]{2,1,0:T(8,128)S(1)} %bitcast.293), channel_id=1, source_target_pairs={{16,32},{32,16},{48,64},{64,48},{80,96},{96,80},{112,128},{128,112... | collective-permute-start | bytes 221192 | tf_op jit(solution)/shard_map/ppermute | solution.py:23
  170.4 4.5 %collective-permute-done.22.x_odd = f32[6,24,128]{2,1,0:T(8,128)S(1)} collective-permute-done((f32[6,24,128]{2,1,0:T(8,128)S(1)}, f32[6,24,128]{2,1,0:T(8,128)S(1)}, u32[]{:S(2)}, u32[]{:S(2)}) %collective-permute-start.22) | collective-permute-done | bytes 73760 | tf_op jit(solution)/shard_map/ppermute | solution.py:23
  175.0 4.1 %collective-permute-start.24 = (f32[12,24,128]{2,1,0:T(8,128)S(1)}, f32[12,24,128]{2,1,0:T(8,128)S(1)}, u32[]{:S(2)}, u32[]{:S(2)}) collective-permute-start(f32[12,24,128]{2,1,0:T(8,128)S(1)} %get-tuple-element.107), channel_id=1, source_target_pairs={{1,2},{2,1},{3,4},{4,3},{5,6},{6,5},{7,8},{8,7},{9,10},{10,9},{11,... | collective-permute-start | bytes 442376 | tf_op jit(solution)/shard_map/ppermute | solution.py:23
  182.4 3.8 %up_middle.1.coarse = f32[8,8,24,128]{3,2,1,0:T(8,128)S(1)} custom-call(s32[8]{0:T(128)S(1)} %stack.27.where, f32[4,4,24,128]{3,2,1,0:T(8,128)S(1)} %up_block.1.coarse_own, f32[6,24,128]{2,1,0:T(8,128)S(1)} %collective-permute-done.21.x_even, f32[6,24,128]{2,1,0:T(8,128)S(1)} %collective-permute-done.22.x_odd, ...), custom_call_target="tpu_custom_call" | custom-call | tf_op jit(solution)/shard_map/up_middle/pallas_call | solution.py:356
  186.2 3.8 %up_fine.1 = f32[8,8,24,128]{3,2,1,0:T(8,128)S(1)} custom-call(s32[8]{0:T(128)S(1)} %stack.27.where, f32[8,8,24,128]{3,2,1,0:T(8,128)S(1)} %up_middle.1.coarse, f32[24,24,128]{2,1,0:T(8,128)S(1)} %get-tuple-element.49.shift, f32[8,8,24,128]{3,2,1,0:T(8,128)S(1)} %get-tuple-element.50.iterate, f32[12,8,24,128]{3,2,1,0:T(8,128)S(1)} %pad_maximum_fusion.rows, ...), custom_call_target="tpu_custom_call" | custom-call | tf_op jit(solution)/shard_map/up_fine/pallas_call | solution.py:356
  (148 shorter events, 32.7 us)
Async XLA Ops:
  1.7 0.8 copy-start.1
  2.5 13.9 %collective-permute-start.1 = (f32[27,24,128]{2,1,0:T(8,128)S(1)}, f32[27,24,128]{2,1,0:T(8,128)S(1)}, u32[]{:S(2)}, u32[]{:S(2)}) collective-permute-start(f32[27,24,128]{2,1,0:T(8,128)S(1)} %get-tuple-element.79), channel_id=1, source_target_pairs={{16,32},{32,16},{48,64},{64,48},{80,96},{96,80},{112,128},{128,112... | collective-permute-start | bytes 995336 | tf_op jit(solution)/shard_map/ppermute | solution.py:23
  6.8 10.2 %collective-permute-start = (f32[27,24,128]{2,1,0:T(8,128)S(1)}, f32[27,24,128]{2,1,0:T(8,128)S(1)}, u32[]{:S(2)}, u32[]{:S(2)}) collective-permute-start(f32[27,24,128]{2,1,0:T(8,128)S(1)} %get-tuple-element.80), channel_id=1, source_target_pairs={{0,16},{16,0},{32,48},{48,32},{64,80},{80,64},{96,112},{112,96},{1... | collective-permute-start | bytes 995336 | tf_op jit(solution)/shard_map/ppermute | solution.py:23
  17.3 7.9 %copy-start.2 = (f32[24,8,8,128]{3,2,1,0:T(8,128)S(1)}, f32[24,8,8,128]{3,2,1,0:T(8,128)}, u32[]{:S(2)}) copy-start(f32[24,8,8,128]{3,2,1,0:T(8,128)} %param.4) | copy-start | bytes 2359300
  17.4 12.1 %collective-permute-start.3 = (f32[38,24,128]{2,1,0:T(8,128)S(1)}, f32[38,24,128]{2,1,0:T(8,128)S(1)}, u32[]{:S(2)}, u32[]{:S(2)}) collective-permute-start(f32[38,24,128]{2,1,0:T(8,128)S(1)} %get-tuple-element.67), channel_id=1, source_target_pairs={{1,2},{2,1},{3,4},{4,3},{5,6},{6,5},{7,8},{8,7},{9,10},{10,9},{11,... | collective-permute-start | bytes 1400840 | tf_op jit(solution)/shard_map/ppermute | solution.py:23
  23.3 6.2 %collective-permute-start.2 = (f32[38,24,128]{2,1,0:T(8,128)S(1)}, f32[38,24,128]{2,1,0:T(8,128)S(1)}, u32[]{:S(2)}, u32[]{:S(2)}) collective-permute-start(f32[38,24,128]{2,1,0:T(8,128)S(1)} %get-tuple-element.68), channel_id=1, source_target_pairs={{0,1},{1,0},{2,3},{3,2},{4,5},{5,4},{6,7},{7,6},{8,9},{9,8},{10,11... | collective-permute-start | bytes 1400840 | tf_op jit(solution)/shard_map/ppermute | solution.py:23
  33.5 9.3 %collective-permute-start.5 = (f32[13,24,128]{2,1,0:T(8,128)S(1)}, f32[13,24,128]{2,1,0:T(8,128)S(1)}, u32[]{:S(2)}, u32[]{:S(2)}) collective-permute-start(f32[13,24,128]{2,1,0:T(8,128)S(1)} %get-tuple-element.105), channel_id=1, source_target_pairs={{16,32},{32,16},{48,64},{64,48},{80,96},{96,80},{112,128},{128,112... | collective-permute-start | bytes 479240 | tf_op jit(solution)/shard_map/ppermute | solution.py:23
  37.8 6.1 %collective-permute-start.4 = (f32[13,24,128]{2,1,0:T(8,128)S(1)}, f32[13,24,128]{2,1,0:T(8,128)S(1)}, u32[]{:S(2)}, u32[]{:S(2)}) collective-permute-start(f32[13,24,128]{2,1,0:T(8,128)S(1)} %get-tuple-element.106), channel_id=1, source_target_pairs={{0,16},{16,0},{32,48},{48,32},{64,80},{80,64},{96,112},{112,96},{1... | collective-permute-start | bytes 479240 | tf_op jit(solution)/shard_map/ppermute | solution.py:23
  44.2 10.0 %collective-permute-start.7 = (f32[19,24,128]{2,1,0:T(8,128)S(1)}, f32[19,24,128]{2,1,0:T(8,128)S(1)}, u32[]{:S(2)}, u32[]{:S(2)}) collective-permute-start(f32[19,24,128]{2,1,0:T(8,128)S(1)} %get-tuple-element.99), channel_id=1, source_target_pairs={{1,2},{2,1},{3,4},{4,3},{5,6},{6,5},{7,8},{8,7},{9,10},{10,9},{11,... | collective-permute-start | bytes 700424 | tf_op jit(solution)/shard_map/ppermute | solution.py:23
  50.4 3.7 %collective-permute-start.6 = (f32[19,24,128]{2,1,0:T(8,128)S(1)}, f32[19,24,128]{2,1,0:T(8,128)S(1)}, u32[]{:S(2)}, u32[]{:S(2)}) collective-permute-start(f32[19,24,128]{2,1,0:T(8,128)S(1)} %get-tuple-element.100), channel_id=1, source_target_pairs={{0,1},{1,0},{2,3},{3,2},{4,5},{5,4},{6,7},{7,6},{8,9},{9,8},{10,11... | collective-permute-start | bytes 700424 | tf_op jit(solution)/shard_map/ppermute | solution.py:23
  56.1 3.1 %collective-permute-start.8 = (f32[5,24,128]{2,1,0:T(8,128)S(1)}, f32[5,24,128]{2,1,0:T(8,128)S(1)}, u32[]{:S(2)}, u32[]{:S(2)}) collective-permute-start(f32[5,24,128]{2,1,0:T(8,128)S(1)} %pad_maximum_fusion.28), channel_id=1, source_target_pairs={{0,1},{1,0},{2,3},{3,2},{4,5},{5,4},{6,7},{7,6},{8,9},{9,8},{10,11... | collective-permute-start | bytes 184328 | tf_op jit(solution)/shard_map/ppermute | solution.py:23
  59.3 7.3 %collective-permute-start.10 = (f32[2,4,24,128]{3,2,1,0:T(8,128)S(1)}, f32[2,4,24,128]{3,2,1,0:T(8,128)S(1)}, u32[]{:S(2)}, u32[]{:S(2)}) collective-permute-start(f32[2,4,24,128]{3,2,1,0:T(8,128)S(1)} %pad_maximum_fusion.25), channel_id=1, source_target_pairs={{32,64},{64,32},{48,80},{80,48},{96,128},{128,96},{112,144},{144,1... | collective-permute-start | bytes 294920 | tf_op jit(solution)/shard_map/ppermute | solution.py:444
  61.2 8.8 %collective-permute-start.9 = (f32[2,4,24,128]{3,2,1,0:T(8,128)S(1)}, f32[2,4,24,128]{3,2,1,0:T(8,128)S(1)}, u32[]{:S(2)}, u32[]{:S(2)}) collective-permute-start(f32[2,4,24,128]{3,2,1,0:T(8,128)S(1)} %pad_maximum_fusion.25), channel_id=1, source_target_pairs={{0,16},{16,0},{32,48},{48,32},{64,80},{80,64},{96,112},{112,96},{1... | collective-permute-start | bytes 294920 | tf_op jit(solution)/shard_map/ppermute | solution.py:444
  70.1 3.3 %collective-permute-start.11 = (f32[16,24,128]{2,1,0:T(8,128)S(1)}, f32[16,24,128]{2,1,0:T(8,128)S(1)}, u32[]{:S(2)}, u32[]{:S(2)}) collective-permute-start(f32[16,24,128]{2,1,0:T(8,128)S(1)} %pad_maximum_fusion.11), channel_id=1, source_target_pairs={{0,1},{1,0},{2,3},{3,2},{4,5},{5,4},{6,7},{7,6},{8,9},{9,8},{10,11... | collective-permute-start | bytes 589832 | tf_op jit(solution)/shard_map/ppermute | solution.py:23
  73.6 1.4 collective-permute-start.12
  75.1 11.3 %collective-permute-start.13 = (f32[24,24,128]{2,1,0:T(8,128)}, f32[24,24,128]{2,1,0:T(8,128)}, u32[]{:S(2)}, u32[]{:S(2)}) collective-permute-start(f32[24,24,128]{2,1,0:T(8,128)} %collective-permute-done.12), channel_id=1, source_target_pairs={{0,1},{1,0},{2,3},{3,2},{4,5},{5,4},{6,7},{7,6},{8,9},{9,8},{10,11... | collective-permute-start | bytes 884744 | tf_op jit(solution)/shard_map/ppermute | solution.py:23
  89.9 29.6 %collective-permute-start.15 = (f32[46,24,128]{2,1,0:T(8,128)S(1)}, f32[46,24,128]{2,1,0:T(8,128)S(1)}, u32[]{:S(2)}, u32[]{:S(2)}) collective-permute-start(f32[46,24,128]{2,1,0:T(8,128)S(1)} %get-tuple-element.65), channel_id=1, source_target_pairs={{16,32},{32,16},{48,64},{64,48},{80,96},{96,80},{112,128},{128,112... | collective-permute-start | bytes 1695752 | tf_op jit(solution)/shard_map/ppermute | solution.py:23
  94.9 24.5 %collective-permute-start.14 = (f32[46,24,128]{2,1,0:T(8,128)S(1)}, f32[46,24,128]{2,1,0:T(8,128)S(1)}, u32[]{:S(2)}, u32[]{:S(2)}) collective-permute-start(f32[46,24,128]{2,1,0:T(8,128)S(1)} %get-tuple-element.66), channel_id=1, source_target_pairs={{0,16},{16,0},{32,48},{48,32},{64,80},{80,64},{96,112},{112,96},{1... | collective-permute-start | bytes 1695752 | tf_op jit(solution)/shard_map/ppermute | solution.py:23
  120.1 4.1 %copy-start = (f32[1,1,128,2048]{3,2,1,0:T(8,128)S(1)}, f32[1,1,128,2048]{3,2,1,0:T(8,128)}, u32[]{:S(2)}) copy-start(f32[1,1,128,2048]{3,2,1,0:T(8,128)} %param.7) | copy-start | bytes 3145732
  120.3 42.3 %collective-permute-start.20 = (f32[68,24,128]{2,1,0:T(8,128)S(1)}, f32[68,24,128]{2,1,0:T(8,128)S(1)}, u32[]{:S(2)}, u32[]{:S(2)}) collective-permute-start(f32[68,24,128]{2,1,0:T(8,128)S(1)} %get-tuple-element.55), channel_id=1, source_target_pairs={{1,2},{2,1},{3,4},{4,3},{5,6},{6,5},{7,8},{8,7},{9,10},{10,9},{11,... | collective-permute-start | bytes 2506760 | tf_op jit(solution)/shard_map/ppermute | solution.py:23
  122.3 40.2 %collective-permute-start.19 = (f32[68,24,128]{2,1,0:T(8,128)S(1)}, f32[68,24,128]{2,1,0:T(8,128)S(1)}, u32[]{:S(2)}, u32[]{:S(2)}) collective-permute-start(f32[68,24,128]{2,1,0:T(8,128)S(1)} %get-tuple-element.56), channel_id=1, source_target_pairs={{0,1},{1,0},{2,3},{3,2},{4,5},{5,4},{6,7},{7,6},{8,9},{9,8},{10,11... | collective-permute-start | bytes 2506760 | tf_op jit(solution)/shard_map/ppermute | solution.py:23
  145.7 8.4 %collective-permute-start.16 = (f32[6,24,128]{2,1,0:T(8,128)S(1)}, f32[6,24,128]{2,1,0:T(8,128)S(1)}, u32[]{:S(2)}, u32[]{:S(2)}) collective-permute-start(f32[6,24,128]{2,1,0:T(8,128)S(1)} %pick.1.fix), channel_id=1, source_target_pairs={{0,16},{16,0},{32,48},{48,32},{64,80},{80,64},{96,112},{112,96},{1... | collective-permute-start | bytes 221192 | tf_op jit(solution)/shard_map/ppermute | solution.py:444
  149.6 6.6 %collective-permute-start.17 = (f32[6,24,128]{2,1,0:T(8,128)S(1)}, f32[6,24,128]{2,1,0:T(8,128)S(1)}, u32[]{:S(2)}, u32[]{:S(2)}) collective-permute-start(f32[6,24,128]{2,1,0:T(8,128)S(1)} %pick.1.fix), channel_id=1, source_target_pairs={{32,64},{64,32},{48,80},{80,48},{96,128},{128,96},{112,144},{144,1... | collective-permute-start | bytes 221192 | tf_op jit(solution)/shard_map/ppermute | solution.py:444
  156.2 6.3 %collective-permute-start.18 = (f32[12,24,128]{2,1,0:T(8,128)S(1)}, f32[12,24,128]{2,1,0:T(8,128)S(1)}, u32[]{:S(2)}, u32[]{:S(2)}) collective-permute-start(f32[12,24,128]{2,1,0:T(8,128)S(1)} %constant_dynamic-update-slice_fusion.6.mine), channel_id=1, source_target_pairs={{0,1},{1,0},{2,3},{3,2},{4,5},{5,4},{6,7},{7,6},{8,9},{9,8},{10,11... | collective-permute-start | bytes 442376 | tf_op jit(solution)/shard_map/ppermute | solution.py:23
  164.5 5.9 %collective-permute-start.21 = (f32[6,24,128]{2,1,0:T(8,128)S(1)}, f32[6,24,128]{2,1,0:T(8,128)S(1)}, u32[]{:S(2)}, u32[]{:S(2)}) collective-permute-start(f32[6,24,128]{2,1,0:T(8,128)S(1)} %bitcast.294), channel_id=1, source_target_pairs={{0,16},{16,0},{32,48},{48,32},{64,80},{80,64},{96,112},{112,96},{1... | collective-permute-start | bytes 221192 | tf_op jit(solution)/shard_map/ppermute | solution.py:23
  166.5 8.4 %collective-permute-start.22 = (f32[6,24,128]{2,1,0:T(8,128)S(1)}, f32[6,24,128]{2,1,0:T(8,128)S(1)}, u32[]{:S(2)}, u32[]{:S(2)}) collective-permute-start(f32[6,24,128]{2,1,0:T(8,128)S(1)} %bitcast.293), channel_id=1, source_target_pairs={{16,32},{32,16},{48,64},{64,48},{80,96},{96,80},{112,128},{128,112... | collective-permute-start | bytes 221192 | tf_op jit(solution)/shard_map/ppermute | solution.py:23
  175.0 7.0 %collective-permute-start.24 = (f32[12,24,128]{2,1,0:T(8,128)S(1)}, f32[12,24,128]{2,1,0:T(8,128)S(1)}, u32[]{:S(2)}, u32[]{:S(2)}) collective-permute-start(f32[12,24,128]{2,1,0:T(8,128)S(1)} %get-tuple-element.107), channel_id=1, source_target_pairs={{1,2},{2,1},{3,4},{4,3},{5,6},{6,5},{7,8},{8,7},{9,10},{10,9},{11,... | collective-permute-start | bytes 442376 | tf_op jit(solution)/shard_map/ppermute | solution.py:23
  179.1 3.3 %collective-permute-start.23 = (f32[12,24,128]{2,1,0:T(8,128)S(1)}, f32[12,24,128]{2,1,0:T(8,128)S(1)}, u32[]{:S(2)}, u32[]{:S(2)}) collective-permute-start(f32[12,24,128]{2,1,0:T(8,128)S(1)} %get-tuple-element.108), channel_id=1, source_target_pairs={{0,1},{1,0},{2,3},{3,2},{4,5},{5,4},{6,7},{7,6},{8,9},{9,8},{10,11... | collective-permute-start | bytes 442376 | tf_op jit(solution)/shard_map/ppermute | solution.py:23

commit v6 on v5

--- a/solution.py
+++ b/solution.py
@@ -54,16 +54,16 @@
     return jnp.where((at >= 0) & (at < size), 1.0, 0.0).astype(jnp.float32)
 
 
-def beside(src, x, y):
-    centre = src[x, y]
-    total = (src[x - 1, y] + src[x + 1, y]) + (src[x, y - 1] + src[x, y + 1])
-    return total + z_neighbours(centre), centre
-
-
-def factor_cell(src, x, y, shift_row, root, mask):
-    total, centre = beside(src, x, y)
-    scale = mask * (1.0 / root)
-    return (scale * ((root - 6.0) - shift_row)) * centre + scale * total
+def factor_row(src, x, count, coefficients):
+    left, centre = src[x, 0], src[x, 1]
+    for y in range(count):
+        right = src[x, y + 2]
+        shift_row, root, mask = coefficients(y)
+        total = (src[x - 1, y + 1] + src[x + 1, y + 1]) + (left + right)
+        total = total + z_neighbours(centre)
+        scale = mask * (1.0 / root)
+        yield (scale * ((root - 6.0) - shift_row)) * centre + scale * total
+        left, centre = centre, right
 
 
 def each_row(count, row):
@@ -83,10 +83,12 @@
 def factor(src, dst, shift, shift_at, size, root, masks):
     def row(x):
         row_mask = masks(x, None)
-        for y in range(size[1]):
-            shift_row = shift[x + shift_at[0], pl.ds(y + shift_at[1], 1), :]
-            mask = row_mask * masks(None, y)
-            dst[x, y] = factor_cell(src, x + 1, y + 1, shift_row, root, mask)
+
+        def coefficients(y):
+            return shift[x + shift_at[0], pl.ds(y + shift_at[1], 1), :], root, row_mask * masks(None, y)
+
+        for y, value in enumerate(factor_row(src, x + 1, size[1], coefficients)):
+            dst[x, y] = value
 
     each_row(size[0], row)
 
@@ -199,10 +201,13 @@
 
     def row(x):
         row_mask = masks(x, None) if beyond else 1.0
-        for y in range(ny):
-            shift_row = shift[x + 2 + sx, pl.ds(y + 2 + sy, 1), :]
+
+        def coefficients(y):
             mask = row_mask * masks(None, y) if beyond else 1.0
-            leftover[x, y] = factor_cell(two, x + 1, y + 1, shift_row, ROOTS[2], mask)
+            return shift[x + 2 + sx, pl.ds(y + 2 + sy, 1), :], ROOTS[2], mask
+
+        for y, value in enumerate(factor_row(two, x + 1, ny, coefficients)):
+            leftover[x, y] = value
             iterate[x, y] = (
                 pad[x + 3, y + 3] * (1.0 / ROOTS[0])
                 + one[x + 2, y + 2] * (1.0 / ROOTS[1])
@@ -239,20 +244,22 @@
     down_body((n, n), 0, grid, first, pad, shift, (2, 2), iterate, leftover, coarser, one, two)
 
 
-def down_chip_kernel(size, grid, where, rows, left, right, shift, iterate, leftover, coarser, pad, one, two):
+def down_block_kernel(n, grid, where, rows, near, far, shift, iterate, leftover, coarser, pad, one, two):
+    core = where[2]
+
     def row(x):
-        for y in range(size[1]):
-            pad[x, y + 4] = rows[x, y]
-
-    each_row(size[0] + 8, row)
-    for ref, base in ((left, 0), (right, 4 + size[1])):
-        for y in range(4):
-            near = y >= 2 if base == 0 else y < 2
-            for x in range(8 if near else 4):
-                cell = 2 * x + y % 2 + (0 if near else 16)
-                pad[x + (1 if near else 3), base + y] = ref[cell]
-    first = (where[0] * size[0], (where[1] - where[2]) * size[0])
-    down_body(size, 1, grid, first, pad, shift, (1, 1), iterate, leftover, coarser, one, two)
+        for y in range(2 * n):
+            pad[x, 2 * n - n * core + y] = rows[x, y]
+
+    each_row(n + 8, row)
+    for ref, at, first, side in ((near, 0, 1, core), (far, 0, n + 1, 1 - core)):
+        for d in range(first, 5):
+            column = jnp.where(side == 1, n + 3 + d, 4 - d)
+            for x in range(d, n + 8 - d):
+                pad[x, column] = ref[at]
+                at += 1
+    first = (where[0] * n, where[1] * n)
+    down_body((n, n), 1, grid, first, pad, shift, (1, 1), iterate, leftover, coarser, one, two)
 
 
 def solve_kernel(where, shares, inverse, solved, ordered):
@@ -294,11 +301,15 @@
     def first_row(x):
         row_mask = outer(x, None)
         here, before, after = (x + offset) // 2, (x + offset - 1) // 2, (x + offset + 1) // 2
+        shared = {}
         for y in range(wide + 4):
             at, left, right = (y + offset) // 2, (y + offset - 1) // 2, (y + offset + 1) // 2
-            centre = coarse[here, at]
-            total = (coarse[before, at] + coarse[after, at]) + (coarse[here, left] + coarse[here, right])
-            total = total + z_neighbours(centre)
+            if at not in shared:
+                centre = coarse[here, at]
+                shared = {at: (centre, (coarse[before, at] + coarse[after, at]) + z_neighbours(centre))}
+            centre, total = shared[at]
+            other = coarse[here, left if left != at else right]
+            total = total + (centre + other)
             shift_row = shift[x + sx, pl.ds(y + sy, 1), :]
             mask = row_mask * outer(None, y)
             start[x, y] = mask * ((start[x, y] - (6.0 + shift_row) * centre) + total)
@@ -308,10 +319,12 @@
 
     def row(x):
         row_mask = masks(x, None) if beyond else 1.0
-        for y in range(wide):
-            shift_row = shift[x + 2 + sx, pl.ds(y + 2 + sy, 1), :]
+
+        def coefficients(y):
             mask = row_mask * masks(None, y) if beyond else 1.0
-            two = factor_cell(one, x + 1, y + 1, shift_row, ROOTS[1], mask)
+            return shift[x + 2 + sx, pl.ds(y + 2 + sy, 1), :], ROOTS[1], mask
+
+        for y, two in enumerate(factor_row(one, x + 1, wide, coefficients)):
             step = (
                 start[x + 2, y + 2] * (1.0 / ROOTS[0]) + one[x + 1, y + 1] * (1.0 / ROOTS[1]) + two * (1.0 / ROOTS[2])
             )
@@ -333,19 +346,17 @@
     up_body(n, 1, grid, where, coarse, 2, shift, (1, 1), iterate, result, start, one)
 
 
-def up_middle_kernel(
-    n, grid, offset, iterate_offset, where, coarse_own, x_even, x_odd, y_even, y_odd, shift, iterate_rows, rows, even, odd,
-    result, coarse, iterate, start, one,
-):
+def up_last_kernel(n, grids, offsets, where, *refs):
+    coarse_own, x_even, x_odd, y_even, y_odd, even, odd = refs[:7]
+    shift, iterate_rows, rows, fine_shift, fine_iterate, fine_rows = refs[7:13]
+    result, coarse, iterate, start, one, middle, fine_start, fine_one = refs[13:]
     put_frame(coarse, coarse_own, [x_even, x_odd, y_even, y_odd], where, n // 2, 3, 1)
-    put_rows(start, rows, [(even, offset), (odd, offset)], where, n, n, 4)
-    put_rows(iterate, iterate_rows, [(even, iterate_offset), (odd, iterate_offset)], where, n, n, 2)
-    up_body(n, 2, grid, where, coarse, 3, shift, (0, 0), iterate, result, start, one)
-
-
-def up_fine_kernel(n, grid, offset, where, coarse, shift, iterate, rows, even, odd, result, start, one):
-    put_rows(start, rows, [(even, offset), (odd, offset)], where, n, n, 2)
-    up_body(n, 0, grid, where, coarse, 2, shift, (n - 2, n - 2), iterate, result, start, one)
+    put_rows(start, rows, [(even, offsets[1]), (odd, offsets[1])], where, n, n, 4)
+    put_rows(iterate, iterate_rows, [(even, offsets[2]), (odd, offsets[2])], where, n, n, 2)
+    put_rows(fine_start, fine_rows, [(even, offsets[0]), (odd, offsets[0])], where, 2 * n, 2 * n, 2)
+    up_body(n, 2, grids[0], where, coarse, 3, shift, (0, 0), iterate, middle, start, one)
+    fine_at = (2 * n - 2, 2 * n - 2)
+    up_body(2 * n, 0, grids[1], where, middle, 2, fine_shift, fine_at, fine_iterate, result, fine_start, fine_one)
 
 
 VMEM = pl.BlockSpec(memory_space=pltpu.VMEM)
@@ -374,7 +385,6 @@
         "gy": core == 0,
         "line": line == core,
         "far": far != core,
-        "chip": parity("gy", 2) == core,
     }
     return where, sides
 
@@ -485,14 +495,8 @@
     )
 
     first_core = at["gy"]
-    edge = jnp.where(first_core, shift_two[:, :2], shift_two[:, -2:])
-    other = to_core(with_rows(cells(b2), edge, tail))
-    edge = other[size * size :].reshape(-1, depth)[: edge.shape[0] * 2].reshape(edge.shape)
-    other = other[: size * size].reshape(b2.shape)
+    other = to_core(b2)
     chip = jnp.concatenate([jnp.where(first_core, b2, other), jnp.where(first_core, other, b2)], axis=1)
-    chip_shift = jnp.where(
-        first_core, jnp.concatenate([shift_two, edge], axis=1), jnp.concatenate([edge, shift_two], axis=1)
-    )
     mine, others = lines_around(chip)
     near = 2 * size * size
     (mine_near, other_near), (mine_far, other_far) = [
@@ -509,24 +513,22 @@
         axis=0,
     )
     blocks = lax.axis_size("gy")
+    columns = [rows[:, y] for y in range(2 * size)]
+    near = jnp.where(first_core, triangle(columns, size, 4), triangle(columns[::-1], size, 4))
+    far = [[column[3 + d : -3 - d] for d, column in enumerate(side[:2])] for side in (columns[::-1], columns)]
+    far = jnp.where(first_core, *[jnp.concatenate(side, axis=0) for side in far])
     pairs = []
-    for j in range(blocks - 2):
-        if (j // 2) % 2 == j % 2:
-            pairs += [(j, j + 2), (j + 2, j)]
-    high = jnp.concatenate([cells(rows[1:-1, -2:]), cells(rows[3:-3, :2])], axis=0)
-    low = jnp.concatenate([cells(rows[1:-1, :2]), cells(rows[3:-3, -2:])], axis=0)
-    mine = lax.ppermute(jnp.where(at["chip"], high, low), "gy", pairs)
-    others = to_core(mine)
+    for j in range(0, blocks - 3, 2):
+        pairs += [(j, j + 3), (j + 3, j)]
     x2, q2, b3 = call(
-        functools.partial(down_chip_kernel, (size, 2 * size), grid_of(size)),
+        functools.partial(down_block_kernel, size, grid_of(size)),
         where,
-        [rows, jnp.where(at["chip"], others, mine), jnp.where(at["chip"], mine, others), chip_shift],
-        fields((size + 2, 2 * size + 2), (size + 2, 2 * size + 2), (1, 2)),
-        fields((size + 8, 2 * size + 8), (size + 6, 2 * size + 6), (size + 4, 2 * size + 4)),
-        "down_chip",
+        [rows, swap(near, "gy", 1, 1), lax.ppermute(far, "gy", pairs), shift_two],
+        fields((size + 2, size + 2), (size + 2, size + 2), (1, 1)),
+        fields((size + 8, size + 8), (size + 6, size + 6), (size + 4, size + 4)),
+        "down_block",
     )
-    x2, q2 = [jnp.where(first_core, v[:, : size + 2], v[:, size:]) for v in (x2, q2)]
-    b3 = jnp.where(first_core, b3[0, 0], b3[0, 1])
+    b3 = b3[0, 0]
 
     own = [q0, q1, x1, q2[1:-1, 1:-1]]
     reaches = [2, 4, 2, 3]
@@ -565,21 +567,16 @@
         fields((5, 5), (size + 6, size + 6), (size + 4, size + 4)),
         "up_block",
     )[0]
-    x1 = call(
-        functools.partial(up_middle_kernel, half, grid_of(half), offsets[1], offsets[2]),
+    x0 = call(
+        functools.partial(up_last_kernel, half, (grid_of(half), grid_of(n)), offsets),
         where,
-        [x2, *frame(at, x2, 3, 1), shift_one, around[2], around[1], *sides],
-        fields((half + 4, half + 4)),
-        fields((size + 6, size + 6), (half + 4, half + 4), (half + 8, half + 8), (half + 6, half + 6)),
-        "up_middle",
-    )[0]
-    x0 = call(
-        functools.partial(up_fine_kernel, n, grid_of(n), offsets[0]),
-        where,
-        [x1, shift_wide, x0, around[0], *sides],
+        [x2, *frame(at, x2, 3, 1), *sides, shift_one, around[2], around[1], shift_wide, x0, around[0]],
         fields((n, n)),
-        fields((n + 4, n + 4), (n + 2, n + 2)),
-        "up_fine",
+        fields(
+            (size + 6, size + 6), (half + 4, half + 4), (half + 8, half + 8), (half + 6, half + 6), (half + 4, half + 4),
+            (n + 4, n + 4), (n + 2, n + 2),
+        ),
+        "up_last",
     )[0]
     return jnp.transpose(x0, (2, 0, 1, 3))
 

time: 192 us -> 185 us (0.964)
  starting transfers between devices: 86.4 us -> 80.1 us
    ppermute x20, starting transfers between devices: 70.4 us -> 64.9 us  [swap(): return lax.ppermute(x, axis, pairs)]
    pallas_call x8 -> x7, Pallas kernels: 19.8 us -> 18 us  [call(): pl.pallas_call(kernel, out_shape=[jax.ShapeDtypeStruct(out, jnp.float32)...]
where the time goes in v6:
time: 185 us; the launch traced here: 184 us
  starting transfers between devices  80.1 us (43%)
  blocking collectives  41.6 us (22%)
  waiting for transfers between devices  36.9 us (20%)
  Pallas kernels  18 us (10%)
  local copies, waits for them, and re-layouts  4.63 us (3%)
    ppermute x20, starting transfers between devices, swap(): return lax.ppermute(x, axis, pairs)  64.9 us
    ppermute x20, waiting for transfers between devices, swap(): return lax.ppermute(x, axis, pairs)  30.3 us
    all_gather x1, blocking collectives, body(): lax.all_gather(jnp.concatenate([b3, slot], axis=0)[None], 'gy', axis=0, t...  22.6 us
    all_gather x1, blocking collectives, body(): back = lax.all_gather(solved[None], 'gy', axis=0, tiled=True)  19 us
    pallas_call x7, Pallas kernels, call(): pl.pallas_call(kernel, out_shape=[jax.ShapeDtypeStruct(out, jnp.float32)...  18 us
    ppermute x4, starting transfers between devices, by_core(): return lax.ppermute(x, ('gx', 'gy'), pairs)  14.6 us
    ppermute x4, waiting for transfers between devices, by_core(): return lax.ppermute(x, ('gx', 'gy'), pairs)  6.61 us
  transfers between devices with their start and end apart: 25, of which 16 were waited for; matrix products, arithmetic and copies ran while one was open for 0% of the time, Pallas kernels for 1%

profile of v6, /device:TPU:31, one launch (start us, length us, event | category | flops | bytes accessed | tf_op | source)
XLA Modules:
  0.0 184.0 jit_solution(15548118721835124342)
XLA Ops:
  2.5 4.3 %collective-permute-start.1 = (f32[27,24,128]{2,1,0:T(8,128)S(1)}, f32[27,24,128]{2,1,0:T(8,128)S(1)}, u32[]{:S(2)}, u32[]{:S(2)}) collective-permute-start(f32[27,24,128]{2,1,0:T(8,128)S(1)} %get-tuple-element.77), channel_id=1, source_target_pairs={{16,32},{32,16},{48,64},{64,48},{80,96},{96,80},{112,128},{128,112... | collective-permute-start | bytes 995336 | tf_op jit(solution)/shard_map/ppermute | solution.py:23
  6.8 1.9 %collective-permute-start = (f32[27,24,128]{2,1,0:T(8,128)S(1)}, f32[27,24,128]{2,1,0:T(8,128)S(1)}, u32[]{:S(2)}, u32[]{:S(2)}) collective-permute-start(f32[27,24,128]{2,1,0:T(8,128)S(1)} %get-tuple-element.78), channel_id=1, source_target_pairs={{0,16},{16,0},{32,48},{48,32},{64,80},{80,64},{96,112},{112,96},{1... | collective-permute-start | bytes 995336 | tf_op jit(solution)/shard_map/ppermute | solution.py:23
  8.8 7.6 %collective-permute-done.1.refs_1_ = f32[27,24,128]{2,1,0:T(8,128)S(1)} collective-permute-done((f32[27,24,128]{2,1,0:T(8,128)S(1)}, f32[27,24,128]{2,1,0:T(8,128)S(1)}, u32[]{:S(2)}, u32[]{:S(2)}) %collective-permute-start.1) | collective-permute-done | bytes 331808 | tf_op jit(solution)/shard_map/ppermute | solution.py:23
  17.4 5.9 %collective-permute-start.3 = (f32[38,24,128]{2,1,0:T(8,128)S(1)}, f32[38,24,128]{2,1,0:T(8,128)S(1)}, u32[]{:S(2)}, u32[]{:S(2)}) collective-permute-start(f32[38,24,128]{2,1,0:T(8,128)S(1)} %get-tuple-element.65), channel_id=1, source_target_pairs={{1,2},{2,1},{3,4},{4,3},{5,6},{6,5},{7,8},{8,7},{9,10},{10,9},{11,... | collective-permute-start | bytes 1400840 | tf_op jit(solution)/shard_map/ppermute | solution.py:23
  23.3 1.9 %collective-permute-start.2 = (f32[38,24,128]{2,1,0:T(8,128)S(1)}, f32[38,24,128]{2,1,0:T(8,128)S(1)}, u32[]{:S(2)}, u32[]{:S(2)}) collective-permute-start(f32[38,24,128]{2,1,0:T(8,128)S(1)} %get-tuple-element.66), channel_id=1, source_target_pairs={{0,1},{1,0},{2,3},{3,2},{4,5},{5,4},{6,7},{7,6},{8,9},{9,8},{10,11... | collective-permute-start | bytes 1400840 | tf_op jit(solution)/shard_map/ppermute | solution.py:23
  25.7 3.8 %collective-permute-done.3.refs_3_ = f32[38,24,128]{2,1,0:T(8,128)S(1)} collective-permute-done((f32[38,24,128]{2,1,0:T(8,128)S(1)}, f32[38,24,128]{2,1,0:T(8,128)S(1)}, u32[]{:S(2)}, u32[]{:S(2)}) %collective-permute-start.3) | collective-permute-done | bytes 466976 | tf_op jit(solution)/shard_map/ppermute | solution.py:23
  29.5 3.8 %down_fine.1 = (f32[8,8,24,128]{3,2,1,0:T(8,128)S(1)}, f32[8,8,24,128]{3,2,1,0:T(8,128)S(1)}, f32[4,4,24,128]{3,2,1,0:T(8,128)S(1)}, f32[24,24,128]{2,1,0:T(8,12...) custom-call(s32[8]{0:T(128)S(1)} %stack.27.where, f32[8,8,24,128]{3,2,1,0:T(8,128)S(1)} %copy.38.own, ...), custom_call_target="tpu_custom_call" | custom-call | tf_op jit(solution)/shard_map/down_fine/pallas_call | solution.py:367
  33.5 4.3 %collective-permute-start.5 = (f32[13,24,128]{2,1,0:T(8,128)S(1)}, f32[13,24,128]{2,1,0:T(8,128)S(1)}, u32[]{:S(2)}, u32[]{:S(2)}) collective-permute-start(f32[13,24,128]{2,1,0:T(8,128)S(1)} %get-tuple-element.101), channel_id=1, source_target_pairs={{16,32},{32,16},{48,64},{64,48},{80,96},{96,80},{112,128},{128,112... | collective-permute-start | bytes 479240 | tf_op jit(solution)/shard_map/ppermute | solution.py:23
  37.8 1.9 %collective-permute-start.4 = (f32[13,24,128]{2,1,0:T(8,128)S(1)}, f32[13,24,128]{2,1,0:T(8,128)S(1)}, u32[]{:S(2)}, u32[]{:S(2)}) collective-permute-start(f32[13,24,128]{2,1,0:T(8,128)S(1)} %get-tuple-element.102), channel_id=1, source_target_pairs={{0,16},{16,0},{32,48},{48,32},{64,80},{80,64},{96,112},{112,96},{1... | collective-permute-start | bytes 479240 | tf_op jit(solution)/shard_map/ppermute | solution.py:23
  39.7 3.1 %collective-permute-done.5.refs_1_ = f32[13,24,128]{2,1,0:T(8,128)S(1)} collective-permute-done((f32[13,24,128]{2,1,0:T(8,128)S(1)}, f32[13,24,128]{2,1,0:T(8,128)S(1)}, u32[]{:S(2)}, u32[]{:S(2)}) %collective-permute-start.5) | collective-permute-done | bytes 159776 | tf_op jit(solution)/shard_map/ppermute | solution.py:23
  44.2 6.2 %collective-permute-start.7 = (f32[19,24,128]{2,1,0:T(8,128)S(1)}, f32[19,24,128]{2,1,0:T(8,128)S(1)}, u32[]{:S(2)}, u32[]{:S(2)}) collective-permute-start(f32[19,24,128]{2,1,0:T(8,128)S(1)} %get-tuple-element.95), channel_id=1, source_target_pairs={{1,2},{2,1},{3,4},{4,3},{5,6},{6,5},{7,8},{8,7},{9,10},{10,9},{11,... | collective-permute-start | bytes 700424 | tf_op jit(solution)/shard_map/ppermute | solution.py:23
  54.1 2.0 %down_middle.1 = (f32[4,4,24,128]{3,2,1,0:T(8,128)S(1)}, f32[4,4,24,128]{3,2,1,0:T(8,128)S(1)}, f32[2,2,24,128]{3,2,1,0:T(8,128)S(1)}, f32[10,10,128]{2,1,0:T(8,128)S(1)}) custom-call(s32[8]{0:T(128)S(1)} %stack.27.where, f32[4,4,24,128]{3,2,1,0:T(8,128)S(1)} %get-tuple-element.32.own, f32[13,24,128]{2,1,0:T(8,128)S(1)} %collective-permute-done.4.refs_0_, ...), custom_call_target="tpu_custom_call" | custom-call | tf_op jit(solution)/shard_map/down_middle/pallas_call | solution.py:367
  56.1 1.9 %collective-permute-start.8 = (f32[2,2,24,128]{3,2,0,1:T(8,128)S(1)}, f32[2,2,24,128]{3,2,0,1:T(8,128)S(1)}, u32[]{:S(2)}, u32[]{:S(2)}) collective-permute-start(f32[2,2,24,128]{3,2,0,1:T(8,128)S(1)} %copy.45), channel_id=1, source_target_pairs={{0,1},{1,0},{2,3},{3,2},{4,5},{5,4},{6,7},{7,6},{8,9},{9,8},{10,11... | collective-permute-start | bytes 147464 | tf_op jit(solution)/shard_map/ppermute | solution.py:23
  61.2 5.3 %collective-permute-start.9 = (f32[2,4,24,128]{3,2,0,1:T(8,128)S(1)}, f32[2,4,24,128]{3,2,0,1:T(8,128)S(1)}, u32[]{:S(2)}, u32[]{:S(2)}) collective-permute-start(f32[2,4,24,128]{3,2,0,1:T(8,128)S(1)} %pad_maximum_fusion.22), channel_id=1, source_target_pairs={{0,16},{16,0},{32,48},{48,32},{64,80},{80,64},{96,112},{112,96},{1... | collective-permute-start | bytes 294920 | tf_op jit(solution)/shard_map/ppermute | solution.py:454
  66.5 3.5 %collective-permute-done.9 = f32[2,4,24,128]{3,2,0,1:T(8,128)S(1)} collective-permute-done((f32[2,4,24,128]{3,2,0,1:T(8,128)S(1)}, f32[2,4,24,128]{3,2,0,1:T(8,128)S(1)}, u32[]{:S(2)}, u32[]{:S(2)}) %collective-permute-start.9) | collective-permute-done | bytes 98336 | tf_op jit(solution)/shard_map/ppermute | solution.py:454
  70.0 2.2 %collective-permute-start.11 = (f32[16,24,128]{2,1,0:T(8,128)S(1)}, f32[16,24,128]{2,1,0:T(8,128)S(1)}, u32[]{:S(2)}, u32[]{:S(2)}) collective-permute-start(f32[16,24,128]{2,1,0:T(8,128)S(1)} %pad_maximum_fusion.12), channel_id=1, source_target_pairs={{0,1},{1,0},{2,3},{3,2},{4,5},{5,4},{6,7},{7,6},{8,9},{9,8},{10,11... | collective-permute-start | bytes 589832 | tf_op jit(solution)/shard_map/ppermute | solution.py:23
  73.6 4.2 %collective-permute-start.12 = (f32[20,24,128]{2,1,0:T(8,128)S(1)}, f32[20,24,128]{2,1,0:T(8,128)S(1)}, u32[]{:S(2)}, u32[]{:S(2)}) collective-permute-start(f32[20,24,128]{2,1,0:T(8,128)S(1)} %maximum_select_fusion), channel_id=1, source_target_pairs={{1,2},{2,1},{3,4},{4,3},{5,6},{6,5},{7,8},{8,7},{9,10},{10,9},{11,... | collective-permute-start | bytes 737288 | tf_op jit(solution)/shard_map/ppermute | solution.py:23
  78.6 3.1 %collective-permute-done.12.near = f32[20,24,128]{2,1,0:T(8,128)S(1)} collective-permute-done((f32[20,24,128]{2,1,0:T(8,128)S(1)}, f32[20,24,128]{2,1,0:T(8,128)S(1)}, u32[]{:S(2)}, u32[]{:S(2)}) %collective-permute-start.12) | collective-permute-done | bytes 245792 | tf_op jit(solution)/shard_map/ppermute | solution.py:23
  81.7 1.9 %down_block.1 = (f32[4,4,24,128]{3,2,1,0:T(8,128)S(1)}, f32[4,4,24,128]{3,2,1,0:T(8,128)S(1)}, f32[1,1,24,128]{3,2,1,0:T(8,128)S(1)}) custom-call(s32[8]{0:T(128)S(1)} %stack.27.where, f32[10,4,24,128]{3,2,1,0:T(8,128)S(1)} %copy.53.rows, f32[20,24,128]{2,1,0:T(8,128)S(1)} %collective-permute-done.12.near, f32[6,24,128]{2,1,0:T(8,128)S(1)} %collective-permute-done.13.far, ...), custom_call_target="tpu_custom_call" | custom-call | tf_op jit(solution)/shard_map/down_block/pallas_call | solution.py:367
  83.7 5.0 %collective-permute-start.15 = (f32[46,24,128]{2,1,0:T(8,128)S(1)}, f32[46,24,128]{2,1,0:T(8,128)S(1)}, u32[]{:S(2)}, u32[]{:S(2)}) collective-permute-start(f32[46,24,128]{2,1,0:T(8,128)S(1)} %get-tuple-element.63), channel_id=1, source_target_pairs={{16,32},{32,16},{48,64},{64,48},{80,96},{96,80},{112,128},{128,112... | collective-permute-start | bytes 1695752 | tf_op jit(solution)/shard_map/ppermute | solution.py:23
  91.4 22.6 %all-gather = f32[512,128]{1,0:T(8,128)S(1)} all-gather(f32[32,128]{1,0:T(8,128)S(1)} %concatenate.126), channel_id=2, replica_groups=mesh['gx'=32,'gy'=16] {'gy'}, dimensions={0}, use_global_device_ids=true | all-gather | bytes 278528 | tf_op jit(solution)/shard_map/all_gather | solution.py:540
  114.8 2.4 %collective-permute-start.20 = (f32[68,24,128]{2,1,0:T(8,128)S(1)}, f32[68,24,128]{2,1,0:T(8,128)S(1)}, u32[]{:S(2)}, u32[]{:S(2)}) collective-permute-start(f32[68,24,128]{2,1,0:T(8,128)S(1)} %get-tuple-element.53), channel_id=1, source_target_pairs={{1,2},{2,1},{3,4},{4,3},{5,6},{6,5},{7,8},{8,7},{9,10},{10,9},{11,... | collective-permute-start | bytes 2506760 | tf_op jit(solution)/shard_map/ppermute | solution.py:23
  120.8 19.0 %all-gather.1 = f32[384,128]{1,0:T(8,128)S(1)} all-gather(f32[24,128]{1,0:T(8,128)S(1)} %solve.1), channel_id=3, replica_groups=mesh['gx'=32,'gy'=16] {'gy'}, dimensions={0}, use_global_device_ids=true | all-gather | bytes 208896 | tf_op jit(solution)/shard_map/all_gather | solution.py:559
  140.5 3.9 %collective-permute-start.16 = (f32[6,24,128]{2,1,0:T(8,128)S(1)}, f32[6,24,128]{2,1,0:T(8,128)S(1)}, u32[]{:S(2)}, u32[]{:S(2)}) collective-permute-start(f32[6,24,128]{2,1,0:T(8,128)S(1)} %pick.1.fix), channel_id=1, source_target_pairs={{0,16},{16,0},{32,48},{48,32},{64,80},{80,64},{96,112},{112,96},{1... | collective-permute-start | bytes 221192 | tf_op jit(solution)/shard_map/ppermute | solution.py:454
  144.4 3.4 %collective-permute-start.17 = (f32[6,24,128]{2,1,0:T(8,128)S(1)}, f32[6,24,128]{2,1,0:T(8,128)S(1)}, u32[]{:S(2)}, u32[]{:S(2)}) collective-permute-start(f32[6,24,128]{2,1,0:T(8,128)S(1)} %pick.1.fix), channel_id=1, source_target_pairs={{32,64},{64,32},{48,80},{80,48},{96,128},{128,96},{112,144},{144,1... | collective-permute-start | bytes 221192 | tf_op jit(solution)/shard_map/ppermute | solution.py:454
  148.9 2.1 %collective-permute-done.17 = f32[6,24,128]{2,1,0:T(8,128)S(1)} collective-permute-done((f32[6,24,128]{2,1,0:T(8,128)S(1)}, f32[6,24,128]{2,1,0:T(8,128)S(1)}, u32[]{:S(2)}, u32[]{:S(2)}) %collective-permute-start.17) | collective-permute-done | bytes 73760 | tf_op jit(solution)/shard_map/ppermute | solution.py:454
  151.0 5.3 %collective-permute-start.18 = (f32[12,24,128]{2,1,0:T(8,128)S(1)}, f32[12,24,128]{2,1,0:T(8,128)S(1)}, u32[]{:S(2)}, u32[]{:S(2)}) collective-permute-start(f32[12,24,128]{2,1,0:T(8,128)S(1)} %constant_dynamic-update-slice_fusion.6.mine), channel_id=1, source_target_pairs={{0,1},{1,0},{2,3},{3,2},{4,5},{5,4},{6,7},{7,6},{8,9},{9,8},{10,11... | collective-permute-start | bytes 442376 | tf_op jit(solution)/shard_map/ppermute | solution.py:23
  159.2 1.9 %collective-permute-start.21 = (f32[6,24,128]{2,1,0:T(8,128)S(1)}, f32[6,24,128]{2,1,0:T(8,128)S(1)}, u32[]{:S(2)}, u32[]{:S(2)}) collective-permute-start(f32[6,24,128]{2,1,0:T(8,128)S(1)} %bitcast.302), channel_id=1, source_target_pairs={{0,16},{16,0},{32,48},{48,32},{64,80},{80,64},{96,112},{112,96},{1... | collective-permute-start | bytes 221192 | tf_op jit(solution)/shard_map/ppermute | solution.py:23
  161.1 3.9 %collective-permute-start.22 = (f32[6,24,128]{2,1,0:T(8,128)S(1)}, f32[6,24,128]{2,1,0:T(8,128)S(1)}, u32[]{:S(2)}, u32[]{:S(2)}) collective-permute-start(f32[6,24,128]{2,1,0:T(8,128)S(1)} %bitcast.301), channel_id=1, source_target_pairs={{16,32},{32,16},{48,64},{64,48},{80,96},{96,80},{112,128},{128,112... | collective-permute-start | bytes 221192 | tf_op jit(solution)/shard_map/ppermute | solution.py:23
  165.1 4.5 %collective-permute-done.22.refs_2_ = f32[6,24,128]{2,1,0:T(8,128)S(1)} collective-permute-done((f32[6,24,128]{2,1,0:T(8,128)S(1)}, f32[6,24,128]{2,1,0:T(8,128)S(1)}, u32[]{:S(2)}, u32[]{:S(2)}) %collective-permute-start.22) | collective-permute-done | bytes 73760 | tf_op jit(solution)/shard_map/ppermute | solution.py:23
  169.6 3.8 %collective-permute-start.24 = (f32[12,24,128]{2,1,0:T(8,128)S(1)}, f32[12,24,128]{2,1,0:T(8,128)S(1)}, u32[]{:S(2)}, u32[]{:S(2)}) collective-permute-start(f32[12,24,128]{2,1,0:T(8,128)S(1)} %get-tuple-element.103), channel_id=1, source_target_pairs={{1,2},{2,1},{3,4},{4,3},{5,6},{6,5},{7,8},{8,7},{9,10},{10,9},{11,... | collective-permute-start | bytes 442376 | tf_op jit(solution)/shard_map/ppermute | solution.py:23
  176.8 6.2 %up_last.1 = f32[8,8,24,128]{3,2,1,0:T(8,128)S(1)} custom-call(s32[8]{0:T(128)S(1)} %stack.27.where, f32[4,4,24,128]{3,2,1,0:T(8,128)S(1)} %up_block.1.refs_0_, f32[6,24,128]{2,1,0:T(8,128)S(1)} %collective-permute-done.21.refs_1_, f32[6,24,128]{2,1,0:T(8,128)S(1)} %collective-permute-done.22.refs_2_, f32[12,24,128]{2,1,0:T(8,128)S(1)} %collective-permute-done.23.refs_3_, ...), custom_call_target="tpu_custom_call" | custom-call | tf_op jit(solution)/shard_map/up_last/pallas_call | solution.py:367
  (142 shorter events, 29.3 us)
Async XLA Ops:
  1.7 0.8 copy-start.1
  2.5 13.9 %collective-permute-start.1 = (f32[27,24,128]{2,1,0:T(8,128)S(1)}, f32[27,24,128]{2,1,0:T(8,128)S(1)}, u32[]{:S(2)}, u32[]{:S(2)}) collective-permute-start(f32[27,24,128]{2,1,0:T(8,128)S(1)} %get-tuple-element.77), channel_id=1, source_target_pairs={{16,32},{32,16},{48,64},{64,48},{80,96},{96,80},{112,128},{128,112... | collective-permute-start | bytes 995336 | tf_op jit(solution)/shard_map/ppermute | solution.py:23
  6.8 10.2 %collective-permute-start = (f32[27,24,128]{2,1,0:T(8,128)S(1)}, f32[27,24,128]{2,1,0:T(8,128)S(1)}, u32[]{:S(2)}, u32[]{:S(2)}) collective-permute-start(f32[27,24,128]{2,1,0:T(8,128)S(1)} %get-tuple-element.78), channel_id=1, source_target_pairs={{0,16},{16,0},{32,48},{48,32},{64,80},{80,64},{96,112},{112,96},{1... | collective-permute-start | bytes 995336 | tf_op jit(solution)/shard_map/ppermute | solution.py:23
  17.3 7.9 %copy-start.2 = (f32[24,8,8,128]{3,2,1,0:T(8,128)S(1)}, f32[24,8,8,128]{3,2,1,0:T(8,128)}, u32[]{:S(2)}) copy-start(f32[24,8,8,128]{3,2,1,0:T(8,128)} %param.4) | copy-start | bytes 2359300
  17.4 12.1 %collective-permute-start.3 = (f32[38,24,128]{2,1,0:T(8,128)S(1)}, f32[38,24,128]{2,1,0:T(8,128)S(1)}, u32[]{:S(2)}, u32[]{:S(2)}) collective-permute-start(f32[38,24,128]{2,1,0:T(8,128)S(1)} %get-tuple-element.65), channel_id=1, source_target_pairs={{1,2},{2,1},{3,4},{4,3},{5,6},{6,5},{7,8},{8,7},{9,10},{10,9},{11,... | collective-permute-start | bytes 1400840 | tf_op jit(solution)/shard_map/ppermute | solution.py:23
  23.3 6.2 %collective-permute-start.2 = (f32[38,24,128]{2,1,0:T(8,128)S(1)}, f32[38,24,128]{2,1,0:T(8,128)S(1)}, u32[]{:S(2)}, u32[]{:S(2)}) collective-permute-start(f32[38,24,128]{2,1,0:T(8,128)S(1)} %get-tuple-element.66), channel_id=1, source_target_pairs={{0,1},{1,0},{2,3},{3,2},{4,5},{5,4},{6,7},{7,6},{8,9},{9,8},{10,11... | collective-permute-start | bytes 1400840 | tf_op jit(solution)/shard_map/ppermute | solution.py:23
  33.5 9.3 %collective-permute-start.5 = (f32[13,24,128]{2,1,0:T(8,128)S(1)}, f32[13,24,128]{2,1,0:T(8,128)S(1)}, u32[]{:S(2)}, u32[]{:S(2)}) collective-permute-start(f32[13,24,128]{2,1,0:T(8,128)S(1)} %get-tuple-element.101), channel_id=1, source_target_pairs={{16,32},{32,16},{48,64},{64,48},{80,96},{96,80},{112,128},{128,112... | collective-permute-start | bytes 479240 | tf_op jit(solution)/shard_map/ppermute | solution.py:23
  37.8 6.1 %collective-permute-start.4 = (f32[13,24,128]{2,1,0:T(8,128)S(1)}, f32[13,24,128]{2,1,0:T(8,128)S(1)}, u32[]{:S(2)}, u32[]{:S(2)}) collective-permute-start(f32[13,24,128]{2,1,0:T(8,128)S(1)} %get-tuple-element.102), channel_id=1, source_target_pairs={{0,16},{16,0},{32,48},{48,32},{64,80},{80,64},{96,112},{112,96},{1... | collective-permute-start | bytes 479240 | tf_op jit(solution)/shard_map/ppermute | solution.py:23
  44.2 10.0 %collective-permute-start.7 = (f32[19,24,128]{2,1,0:T(8,128)S(1)}, f32[19,24,128]{2,1,0:T(8,128)S(1)}, u32[]{:S(2)}, u32[]{:S(2)}) collective-permute-start(f32[19,24,128]{2,1,0:T(8,128)S(1)} %get-tuple-element.95), channel_id=1, source_target_pairs={{1,2},{2,1},{3,4},{4,3},{5,6},{6,5},{7,8},{8,7},{9,10},{10,9},{11,... | collective-permute-start | bytes 700424 | tf_op jit(solution)/shard_map/ppermute | solution.py:23
  50.4 3.7 %collective-permute-start.6 = (f32[19,24,128]{2,1,0:T(8,128)S(1)}, f32[19,24,128]{2,1,0:T(8,128)S(1)}, u32[]{:S(2)}, u32[]{:S(2)}) collective-permute-start(f32[19,24,128]{2,1,0:T(8,128)S(1)} %get-tuple-element.96), channel_id=1, source_target_pairs={{0,1},{1,0},{2,3},{3,2},{4,5},{5,4},{6,7},{7,6},{8,9},{9,8},{10,11... | collective-permute-start | bytes 700424 | tf_op jit(solution)/shard_map/ppermute | solution.py:23
  56.1 3.1 %collective-permute-start.8 = (f32[2,2,24,128]{3,2,0,1:T(8,128)S(1)}, f32[2,2,24,128]{3,2,0,1:T(8,128)S(1)}, u32[]{:S(2)}, u32[]{:S(2)}) collective-permute-start(f32[2,2,24,128]{3,2,0,1:T(8,128)S(1)} %copy.45), channel_id=1, source_target_pairs={{0,1},{1,0},{2,3},{3,2},{4,5},{5,4},{6,7},{7,6},{8,9},{9,8},{10,11... | collective-permute-start | bytes 147464 | tf_op jit(solution)/shard_map/ppermute | solution.py:23
  59.2 7.3 %collective-permute-start.10 = (f32[2,4,24,128]{3,2,0,1:T(8,128)S(1)}, f32[2,4,24,128]{3,2,0,1:T(8,128)S(1)}, u32[]{:S(2)}, u32[]{:S(2)}) collective-permute-start(f32[2,4,24,128]{3,2,0,1:T(8,128)S(1)} %pad_maximum_fusion.22), channel_id=1, source_target_pairs={{32,64},{64,32},{48,80},{80,48},{96,128},{128,96},{112,144},{144,1... | collective-permute-start | bytes 294920 | tf_op jit(solution)/shard_map/ppermute | solution.py:454
  61.2 8.8 %collective-permute-start.9 = (f32[2,4,24,128]{3,2,0,1:T(8,128)S(1)}, f32[2,4,24,128]{3,2,0,1:T(8,128)S(1)}, u32[]{:S(2)}, u32[]{:S(2)}) collective-permute-start(f32[2,4,24,128]{3,2,0,1:T(8,128)S(1)} %pad_maximum_fusion.22), channel_id=1, source_target_pairs={{0,16},{16,0},{32,48},{48,32},{64,80},{80,64},{96,112},{112,96},{1... | collective-permute-start | bytes 294920 | tf_op jit(solution)/shard_map/ppermute | solution.py:454
  70.0 3.3 %collective-permute-start.11 = (f32[16,24,128]{2,1,0:T(8,128)S(1)}, f32[16,24,128]{2,1,0:T(8,128)S(1)}, u32[]{:S(2)}, u32[]{:S(2)}) collective-permute-start(f32[16,24,128]{2,1,0:T(8,128)S(1)} %pad_maximum_fusion.12), channel_id=1, source_target_pairs={{0,1},{1,0},{2,3},{3,2},{4,5},{5,4},{6,7},{7,6},{8,9},{9,8},{10,11... | collective-permute-start | bytes 589832 | tf_op jit(solution)/shard_map/ppermute | solution.py:23
  73.6 8.0 %collective-permute-start.12 = (f32[20,24,128]{2,1,0:T(8,128)S(1)}, f32[20,24,128]{2,1,0:T(8,128)S(1)}, u32[]{:S(2)}, u32[]{:S(2)}) collective-permute-start(f32[20,24,128]{2,1,0:T(8,128)S(1)} %maximum_select_fusion), channel_id=1, source_target_pairs={{1,2},{2,1},{3,4},{4,3},{5,6},{6,5},{7,8},{8,7},{9,10},{10,9},{11,... | collective-permute-start | bytes 737288 | tf_op jit(solution)/shard_map/ppermute | solution.py:23
  77.8 0.7 collective-permute-start.13
  83.7 30.3 %collective-permute-start.15 = (f32[46,24,128]{2,1,0:T(8,128)S(1)}, f32[46,24,128]{2,1,0:T(8,128)S(1)}, u32[]{:S(2)}, u32[]{:S(2)}) collective-permute-start(f32[46,24,128]{2,1,0:T(8,128)S(1)} %get-tuple-element.63), channel_id=1, source_target_pairs={{16,32},{32,16},{48,64},{64,48},{80,96},{96,80},{112,128},{128,112... | collective-permute-start | bytes 1695752 | tf_op jit(solution)/shard_map/ppermute | solution.py:23
  88.8 25.2 %collective-permute-start.14 = (f32[46,24,128]{2,1,0:T(8,128)S(1)}, f32[46,24,128]{2,1,0:T(8,128)S(1)}, u32[]{:S(2)}, u32[]{:S(2)}) collective-permute-start(f32[46,24,128]{2,1,0:T(8,128)S(1)} %get-tuple-element.64), channel_id=1, source_target_pairs={{0,16},{16,0},{32,48},{48,32},{64,80},{80,64},{96,112},{112,96},{1... | collective-permute-start | bytes 1695752 | tf_op jit(solution)/shard_map/ppermute | solution.py:23
  114.6 4.5 %copy-start = (f32[1,1,128,2048]{3,2,1,0:T(8,128)S(1)}, f32[1,1,128,2048]{3,2,1,0:T(8,128)}, u32[]{:S(2)}) copy-start(f32[1,1,128,2048]{3,2,1,0:T(8,128)} %param.7) | copy-start | bytes 3145732
  114.8 42.6 %collective-permute-start.20 = (f32[68,24,128]{2,1,0:T(8,128)S(1)}, f32[68,24,128]{2,1,0:T(8,128)S(1)}, u32[]{:S(2)}, u32[]{:S(2)}) collective-permute-start(f32[68,24,128]{2,1,0:T(8,128)S(1)} %get-tuple-element.53), channel_id=1, source_target_pairs={{1,2},{2,1},{3,4},{4,3},{5,6},{6,5},{7,8},{8,7},{9,10},{10,9},{11,... | collective-permute-start | bytes 2506760 | tf_op jit(solution)/shard_map/ppermute | solution.py:23
  117.2 40.1 %collective-permute-start.19 = (f32[68,24,128]{2,1,0:T(8,128)S(1)}, f32[68,24,128]{2,1,0:T(8,128)S(1)}, u32[]{:S(2)}, u32[]{:S(2)}) collective-permute-start(f32[68,24,128]{2,1,0:T(8,128)S(1)} %get-tuple-element.54), channel_id=1, source_target_pairs={{0,1},{1,0},{2,3},{3,2},{4,5},{5,4},{6,7},{7,6},{8,9},{9,8},{10,11... | collective-permute-start | bytes 2506760 | tf_op jit(solution)/shard_map/ppermute | solution.py:23
  140.5 8.4 %collective-permute-start.16 = (f32[6,24,128]{2,1,0:T(8,128)S(1)}, f32[6,24,128]{2,1,0:T(8,128)S(1)}, u32[]{:S(2)}, u32[]{:S(2)}) collective-permute-start(f32[6,24,128]{2,1,0:T(8,128)S(1)} %pick.1.fix), channel_id=1, source_target_pairs={{0,16},{16,0},{32,48},{48,32},{64,80},{80,64},{96,112},{112,96},{1... | collective-permute-start | bytes 221192 | tf_op jit(solution)/shard_map/ppermute | solution.py:454
  144.4 6.6 %collective-permute-start.17 = (f32[6,24,128]{2,1,0:T(8,128)S(1)}, f32[6,24,128]{2,1,0:T(8,128)S(1)}, u32[]{:S(2)}, u32[]{:S(2)}) collective-permute-start(f32[6,24,128]{2,1,0:T(8,128)S(1)} %pick.1.fix), channel_id=1, source_target_pairs={{32,64},{64,32},{48,80},{80,48},{96,128},{128,96},{112,144},{144,1... | collective-permute-start | bytes 221192 | tf_op jit(solution)/shard_map/ppermute | solution.py:454
  151.0 6.3 %collective-permute-start.18 = (f32[12,24,128]{2,1,0:T(8,128)S(1)}, f32[12,24,128]{2,1,0:T(8,128)S(1)}, u32[]{:S(2)}, u32[]{:S(2)}) collective-permute-start(f32[12,24,128]{2,1,0:T(8,128)S(1)} %constant_dynamic-update-slice_fusion.6.mine), channel_id=1, source_target_pairs={{0,1},{1,0},{2,3},{3,2},{4,5},{5,4},{6,7},{7,6},{8,9},{9,8},{10,11... | collective-permute-start | bytes 442376 | tf_op jit(solution)/shard_map/ppermute | solution.py:23
  159.2 5.9 %collective-permute-start.21 = (f32[6,24,128]{2,1,0:T(8,128)S(1)}, f32[6,24,128]{2,1,0:T(8,128)S(1)}, u32[]{:S(2)}, u32[]{:S(2)}) collective-permute-start(f32[6,24,128]{2,1,0:T(8,128)S(1)} %bitcast.302), channel_id=1, source_target_pairs={{0,16},{16,0},{32,48},{48,32},{64,80},{80,64},{96,112},{112,96},{1... | collective-permute-start | bytes 221192 | tf_op jit(solution)/shard_map/ppermute | solution.py:23
  161.1 8.4 %collective-permute-start.22 = (f32[6,24,128]{2,1,0:T(8,128)S(1)}, f32[6,24,128]{2,1,0:T(8,128)S(1)}, u32[]{:S(2)}, u32[]{:S(2)}) collective-permute-start(f32[6,24,128]{2,1,0:T(8,128)S(1)} %bitcast.301), channel_id=1, source_target_pairs={{16,32},{32,16},{48,64},{64,48},{80,96},{96,80},{112,128},{128,112... | collective-permute-start | bytes 221192 | tf_op jit(solution)/shard_map/ppermute | solution.py:23
  169.6 6.7 %collective-permute-start.24 = (f32[12,24,128]{2,1,0:T(8,128)S(1)}, f32[12,24,128]{2,1,0:T(8,128)S(1)}, u32[]{:S(2)}, u32[]{:S(2)}) collective-permute-start(f32[12,24,128]{2,1,0:T(8,128)S(1)} %get-tuple-element.103), channel_id=1, source_target_pairs={{1,2},{2,1},{3,4},{4,3},{5,6},{6,5},{7,8},{8,7},{9,10},{10,9},{11,... | collective-permute-start | bytes 442376 | tf_op jit(solution)/shard_map/ppermute | solution.py:23
  173.5 3.3 %collective-permute-start.23 = (f32[12,24,128]{2,1,0:T(8,128)S(1)}, f32[12,24,128]{2,1,0:T(8,128)S(1)}, u32[]{:S(2)}, u32[]{:S(2)}) collective-permute-start(f32[12,24,128]{2,1,0:T(8,128)S(1)} %get-tuple-element.104), channel_id=1, source_target_pairs={{0,1},{1,0},{2,3},{3,2},{4,5},{5,4},{6,7},{7,6},{8,9},{9,8},{10,11... | collective-permute-start | bytes 442376 | tf_op jit(solution)/shard_map/ppermute | solution.py:23

commit v7 on v6

--- a/solution.py
+++ b/solution.py
@@ -27,11 +27,13 @@
     return lax.rem(lax.div(lax.axis_index(axis), dist), 2)
 
 
-def swap_ends(at, low, high, axis, dist):
+def swap_ends(at, low, high, axis, dist, odd_first=False):
     even = at[axis]
+    if odd_first:
+        second = swap(jnp.where(even, low, high), axis, dist, 1)
+        return swap(jnp.where(even, high, low), axis, dist, 0), second
     first = swap(jnp.where(even, high, low), axis, dist, 0)
-    second = swap(jnp.where(even, low, high), axis, dist, 1)
-    return first, second
+    return first, swap(jnp.where(even, low, high), axis, dist, 1)
 
 
 def in_order(at, first, second, axis):
@@ -71,13 +73,14 @@
         for x in range(count):
             row(x)
         return
-
-    def pair(step, carry):
-        row(2 * step)
-        row(2 * step + 1)
+    many = 4 if count % 4 == 0 else 2
+
+    def rows(step, carry):
+        for k in range(many):
+            row(many * step + k)
         return carry
 
-    lax.fori_loop(0, count // 2, pair, 0)
+    lax.fori_loop(0, count // many, rows, 0)
 
 
 def factor(src, dst, shift, shift_at, size, root, masks):
@@ -360,33 +363,32 @@
 
 
 VMEM = pl.BlockSpec(memory_space=pltpu.VMEM)
-SMEM = pl.BlockSpec(memory_space=pltpu.SMEM)
-
-
-def call(kernel, where, operands, outs, scratch, name):
+
+
+def call(kernel, operands, outs, scratch, name):
+    def run(*refs):
+        kernel(spot(), *refs)
+
     return pl.pallas_call(
-        kernel,
+        run,
         out_shape=[jax.ShapeDtypeStruct(out, jnp.float32) for out in outs],
-        in_specs=[SMEM] + [VMEM] * len(operands),
+        in_specs=[VMEM] * len(operands),
         out_specs=[VMEM] * len(outs),
         scratch_shapes=[pltpu.VMEM(own, jnp.float32) for own in scratch],
         compiler_params=pltpu.CompilerParams(vmem_limit_bytes=12 * 1024 * 1024),
         name=name,
-    )(where, *operands)
+    )(*operands)
 
 
 def place():
-    core = parity("gy", 1)
-    line, far = parity("gx", 1), parity("gx", 2)
-    numbers = [lax.axis_index("gx"), lax.axis_index("gy"), core, line, line ^ core, far ^ core]
-    where = jnp.stack(numbers + [jnp.zeros_like(core)] * 2).astype(jnp.int32)
-    sides = {
-        "gx": line == 0,
-        "gy": core == 0,
-        "line": line == core,
-        "far": far != core,
-    }
-    return where, sides
+    core, line, far = parity("gy", 1), parity("gx", 1), parity("gx", 2)
+    return {"gx": line == 0, "gy": core == 0, "line": line == core, "far": far != core}
+
+
+def spot():
+    core, line, far = parity("gy", 1), parity("gx", 1), parity("gx", 2)
+    numbers = [lax.axis_index("gx"), lax.axis_index("gy"), core, line]
+    return numbers + [lax.rem(line + core, 2), lax.rem(far + core, 2)]
 
 
 def grid_of(n):
@@ -414,14 +416,15 @@
     return jnp.concatenate([strip, rows.reshape((-1,) + tail)], axis=0)
 
 
-def frame(at, v, reach, beyond=0, blocks=None, rims=None):
+def frame(at, v, reach, beyond=0, blocks=None, rims=None, odd_first=False):
     n = v.shape[0] - 2 * beyond
     tail = v.shape[-2:]
     own = v[beyond : beyond + n, beyond : beyond + n]
     extra = [blocks, blocks] if rims is None else [rims[-2:], rims[:2]]
     low = v[beyond : beyond + reach, beyond : beyond + n]
     high = v[beyond + n - reach : beyond + n, beyond : beyond + n]
-    x_pieces = swap_ends(at, with_rows(cells(low), extra[0], tail), with_rows(cells(high), extra[1], tail), "gx", 1)
+    low, high = with_rows(cells(low), extra[0], tail), with_rows(cells(high), extra[1], tail)
+    x_pieces = swap_ends(at, low, high, "gx", 1, odd_first)
     sides = in_order(at, *x_pieces, "gx")
     strips = [side[: reach * n].reshape((reach, n) + tail) for side in sides]
     rows = jnp.concatenate([strips[0], own, strips[1]], axis=0)
@@ -466,8 +469,7 @@
 
 
 def body(rhs, shift, slots, coarse_inverse):
-    where, at = place()
-    where, at, rhs = lax.optimization_barrier((where, at, rhs))
+    at, rhs = lax.optimization_barrier((place(), rhs))
     right = jnp.transpose(rhs, (1, 2, 0, 3))
     n = right.shape[0]
     tail = chans, depth = right.shape[2:]
@@ -478,7 +480,6 @@
 
     x0, q0, b1, shift_wide, shift_one, shift_two = call(
         functools.partial(down_fine_kernel, n, grid_of(n)),
-        where,
         [right, *frame(at, right, HALO, 0, shift), shift],
         fields((n, n), (n, n), (half, half))
         + [(3 * n, 3 * n, depth), (3 * half, 3 * half, depth), (3 * size, 3 * size, depth)],
@@ -487,7 +488,6 @@
     )
     x1, q1, b2, shift_two = call(
         functools.partial(down_kernel, half, grid_of(half)),
-        where,
         [b1, *frame(at, b1, HALO, 0, None, shift_two), shift_one, shift_two],
         fields((half, half), (half, half), (size, size)) + [(3 * size + 4, 3 * size + 4, depth)],
         fields((half + 6, half + 6), (half + 4, half + 4), (half + 2, half + 2)),
@@ -522,7 +522,6 @@
         pairs += [(j, j + 3), (j + 3, j)]
     x2, q2, b3 = call(
         functools.partial(down_block_kernel, size, grid_of(size)),
-        where,
         [rows, swap(near, "gy", 1, 1), lax.ppermute(far, "gy", pairs), shift_two],
         fields((size + 2, size + 2), (size + 2, size + 2), (1, 1)),
         fields((size + 8, size + 8), (size + 6, size + 6), (size + 4, size + 4)),
@@ -554,14 +553,13 @@
         done += strip
     sides = swap_ends(at, jnp.concatenate(lows, axis=0), jnp.concatenate(highs, axis=0), "gy", 1)
     solved = call(
-        solve_kernel, where, [shares, coarse_inverse[0, 0]], [tail], [(chans, blocks * depth)], "solve"
+        solve_kernel, [shares, coarse_inverse[0, 0]], [tail], [(chans, blocks * depth)], "solve"
     )[0]
     back = lax.all_gather(solved[None], "gy", axis=0, tiled=True)
-    fix = call(pick_kernel, where, [shares, back], [(6,) + tail], [], "pick")[0]
+    fix = call(pick_kernel, [shares, back], [(6,) + tail], [], "pick")[0]
 
     x2 = call(
         functools.partial(up_block_kernel, size, grid_of(size), offsets[3]),
-        where,
         [fix, *lines_around(fix), shift_two, x2, around[3], *sides],
         fields((size + 2, size + 2)),
         fields((5, 5), (size + 6, size + 6), (size + 4, size + 4)),
@@ -569,8 +567,7 @@
     )[0]
     x0 = call(
         functools.partial(up_last_kernel, half, (grid_of(half), grid_of(n)), offsets),
-        where,
-        [x2, *frame(at, x2, 3, 1), *sides, shift_one, around[2], around[1], shift_wide, x0, around[0]],
+        [x2, *frame(at, x2, 3, 1, odd_first=True), *sides, shift_one, around[2], around[1], shift_wide, x0, around[0]],
         fields((n, n)),
         fields(
             (size + 6, size + 6), (half + 4, half + 4), (half + 8, half + 8), (half + 6, half + 6), (half + 4, half + 4),

time: 185 us -> 180 us (0.973)
  Pallas kernels: 18 us -> 12.8 us
    pallas_call x7, Pallas kernels: 18 us -> 12.8 us  [call(): pl.pallas_call(run, out_shape=[jax.ShapeDtypeStruct(out, jnp.float32) for...]
where the time goes in v7:
time: 180 us; the launch traced here: 179 us
  starting transfers between devices  80.1 us (44%)
  blocking collectives  42.1 us (23%)
  waiting for transfers between devices  36.9 us (20%)
  Pallas kernels  12.8 us (7%)
  local copies, waits for them, and re-layouts  4.54 us (3%)
    ppermute x20, starting transfers between devices, swap(): return lax.ppermute(x, axis, pairs)  64.9 us
    ppermute x20, waiting for transfers between devices, swap(): return lax.ppermute(x, axis, pairs)  30.3 us
    all_gather x1, blocking collectives, body(): lax.all_gather(jnp.concatenate([b3, slot], axis=0)[None], 'gy', axis=0, t...  22.6 us
    all_gather x1, blocking collectives, body(): back = lax.all_gather(solved[None], 'gy', axis=0, tiled=True)  19.5 us
    ppermute x4, starting transfers between devices, by_core(): return lax.ppermute(x, ('gx', 'gy'), pairs)  14.6 us
    pallas_call x7, Pallas kernels, call(): pl.pallas_call(run, out_shape=[jax.ShapeDtypeStruct(out, jnp.float32) for...  12.8 us
    ppermute x4, waiting for transfers between devices, by_core(): return lax.ppermute(x, ('gx', 'gy'), pairs)  6.61 us
  transfers between devices with their start and end apart: 25, of which 16 were waited for; matrix products, arithmetic and copies ran while one was open for 0% of the time, Pallas kernels for 1%

profile of v7, /device:TPU:31, one launch (start us, length us, event | category | flops | bytes accessed | tf_op | source)
XLA Modules:
  0.0 179.1 jit_solution(123270268388643933)
XLA Ops:
  2.4 4.3 %collective-permute-start.1 = (f32[27,24,128]{2,1,0:T(8,128)S(1)}, f32[27,24,128]{2,1,0:T(8,128)S(1)}, u32[]{:S(2)}, u32[]{:S(2)}) collective-permute-start(f32[27,24,128]{2,1,0:T(8,128)S(1)} %get-tuple-element.75), channel_id=1, source_target_pairs={{16,32},{32,16},{48,64},{64,48},{80,96},{96,80},{112,128},{128,112... | collective-permute-start | bytes 995336 | tf_op jit(solution)/shard_map/ppermute | solution.py:23
  6.7 1.9 %collective-permute-start = (f32[27,24,128]{2,1,0:T(8,128)S(1)}, f32[27,24,128]{2,1,0:T(8,128)S(1)}, u32[]{:S(2)}, u32[]{:S(2)}) collective-permute-start(f32[27,24,128]{2,1,0:T(8,128)S(1)} %get-tuple-element.76), channel_id=1, source_target_pairs={{0,16},{16,0},{32,48},{48,32},{64,80},{80,64},{96,112},{112,96},{1... | collective-permute-start | bytes 995336 | tf_op jit(solution)/shard_map/ppermute | solution.py:23
  8.7 7.6 %collective-permute-done.1.refs_2_ = f32[27,24,128]{2,1,0:T(8,128)S(1)} collective-permute-done((f32[27,24,128]{2,1,0:T(8,128)S(1)}, f32[27,24,128]{2,1,0:T(8,128)S(1)}, u32[]{:S(2)}, u32[]{:S(2)}) %collective-permute-start.1) | collective-permute-done | bytes 331808 | tf_op jit(solution)/shard_map/ppermute | solution.py:23
  17.3 5.9 %collective-permute-start.3 = (f32[38,24,128]{2,1,0:T(8,128)S(1)}, f32[38,24,128]{2,1,0:T(8,128)S(1)}, u32[]{:S(2)}, u32[]{:S(2)}) collective-permute-start(f32[38,24,128]{2,1,0:T(8,128)S(1)} %get-tuple-element.63), channel_id=1, source_target_pairs={{1,2},{2,1},{3,4},{4,3},{5,6},{6,5},{7,8},{8,7},{9,10},{10,9},{11,... | collective-permute-start | bytes 1400840 | tf_op jit(solution)/shard_map/ppermute | solution.py:23
  23.2 1.9 %collective-permute-start.2 = (f32[38,24,128]{2,1,0:T(8,128)S(1)}, f32[38,24,128]{2,1,0:T(8,128)S(1)}, u32[]{:S(2)}, u32[]{:S(2)}) collective-permute-start(f32[38,24,128]{2,1,0:T(8,128)S(1)} %get-tuple-element.64), channel_id=1, source_target_pairs={{0,1},{1,0},{2,3},{3,2},{4,5},{5,4},{6,7},{7,6},{8,9},{9,8},{10,11... | collective-permute-start | bytes 1400840 | tf_op jit(solution)/shard_map/ppermute | solution.py:23
  25.6 3.8 %collective-permute-done.3.refs_4_ = f32[38,24,128]{2,1,0:T(8,128)S(1)} collective-permute-done((f32[38,24,128]{2,1,0:T(8,128)S(1)}, f32[38,24,128]{2,1,0:T(8,128)S(1)}, u32[]{:S(2)}, u32[]{:S(2)}) %collective-permute-start.3) | collective-permute-done | bytes 466976 | tf_op jit(solution)/shard_map/ppermute | solution.py:23
  29.4 3.0 %down_fine.1 = (f32[8,8,24,128]{3,2,1,0:T(8,128)S(1)}, f32[8,8,24,128]{3,2,1,0:T(8,128)S(1)}, f32[4,4,24,128]{3,2,1,0:T(8,128)S(1)}, f32[24,24,128]{2,1,0:T(8,12...) custom-call(f32[8,8,24,128]{3,2,1,0:T(8,128)S(1)} %copy.38.refs_0_, ...), custom_call_target="tpu_custom_call" | custom-call | tf_op jit(solution)/shard_map/down_fine/pallas_call | solution.py:372
  32.5 4.3 %collective-permute-start.5 = (f32[13,24,128]{2,1,0:T(8,128)S(1)}, f32[13,24,128]{2,1,0:T(8,128)S(1)}, u32[]{:S(2)}, u32[]{:S(2)}) collective-permute-start(f32[13,24,128]{2,1,0:T(8,128)S(1)} %get-tuple-element.99), channel_id=1, source_target_pairs={{16,32},{32,16},{48,64},{64,48},{80,96},{96,80},{112,128},{128,112... | collective-permute-start | bytes 479240 | tf_op jit(solution)/shard_map/ppermute | solution.py:23
  36.8 1.9 %collective-permute-start.4 = (f32[13,24,128]{2,1,0:T(8,128)S(1)}, f32[13,24,128]{2,1,0:T(8,128)S(1)}, u32[]{:S(2)}, u32[]{:S(2)}) collective-permute-start(f32[13,24,128]{2,1,0:T(8,128)S(1)} %get-tuple-element.100), channel_id=1, source_target_pairs={{0,16},{16,0},{32,48},{48,32},{64,80},{80,64},{96,112},{112,96},{1... | collective-permute-start | bytes 479240 | tf_op jit(solution)/shard_map/ppermute | solution.py:23
  38.7 3.1 %collective-permute-done.5.refs_2_ = f32[13,24,128]{2,1,0:T(8,128)S(1)} collective-permute-done((f32[13,24,128]{2,1,0:T(8,128)S(1)}, f32[13,24,128]{2,1,0:T(8,128)S(1)}, u32[]{:S(2)}, u32[]{:S(2)}) %collective-permute-start.5) | collective-permute-done | bytes 159776 | tf_op jit(solution)/shard_map/ppermute | solution.py:23
  43.2 6.2 %collective-permute-start.7 = (f32[19,24,128]{2,1,0:T(8,128)S(1)}, f32[19,24,128]{2,1,0:T(8,128)S(1)}, u32[]{:S(2)}, u32[]{:S(2)}) collective-permute-start(f32[19,24,128]{2,1,0:T(8,128)S(1)} %get-tuple-element.93), channel_id=1, source_target_pairs={{1,2},{2,1},{3,4},{4,3},{5,6},{6,5},{7,8},{8,7},{9,10},{10,9},{11,... | collective-permute-start | bytes 700424 | tf_op jit(solution)/shard_map/ppermute | solution.py:23
  49.4 1.9 %collective-permute-start.6 = (f32[19,24,128]{2,1,0:T(8,128)S(1)}, f32[19,24,128]{2,1,0:T(8,128)S(1)}, u32[]{:S(2)}, u32[]{:S(2)}) collective-permute-start(f32[19,24,128]{2,1,0:T(8,128)S(1)} %get-tuple-element.94), channel_id=1, source_target_pairs={{0,1},{1,0},{2,3},{3,2},{4,5},{5,4},{6,7},{7,6},{8,9},{9,8},{10,11... | collective-permute-start | bytes 700424 | tf_op jit(solution)/shard_map/ppermute | solution.py:23
  54.4 1.9 %collective-permute-start.8 = (f32[2,2,24,128]{3,2,0,1:T(8,128)S(1)}, f32[2,2,24,128]{3,2,0,1:T(8,128)S(1)}, u32[]{:S(2)}, u32[]{:S(2)}) collective-permute-start(f32[2,2,24,128]{3,2,0,1:T(8,128)S(1)} %copy.45), channel_id=1, source_target_pairs={{0,1},{1,0},{2,3},{3,2},{4,5},{5,4},{6,7},{7,6},{8,9},{9,8},{10,11... | collective-permute-start | bytes 147464 | tf_op jit(solution)/shard_map/ppermute | solution.py:23
  59.5 5.3 %collective-permute-start.9 = (f32[2,4,24,128]{3,2,0,1:T(8,128)S(1)}, f32[2,4,24,128]{3,2,0,1:T(8,128)S(1)}, u32[]{:S(2)}, u32[]{:S(2)}) collective-permute-start(f32[2,4,24,128]{3,2,0,1:T(8,128)S(1)} %pad_maximum_fusion.22), channel_id=1, source_target_pairs={{0,16},{16,0},{32,48},{48,32},{64,80},{80,64},{96,112},{112,96},{1... | collective-permute-start | bytes 294920 | tf_op jit(solution)/shard_map/ppermute | solution.py:457
  64.9 3.5 %collective-permute-done.9 = f32[2,4,24,128]{3,2,0,1:T(8,128)S(1)} collective-permute-done((f32[2,4,24,128]{3,2,0,1:T(8,128)S(1)}, f32[2,4,24,128]{3,2,0,1:T(8,128)S(1)}, u32[]{:S(2)}, u32[]{:S(2)}) %collective-permute-start.9) | collective-permute-done | bytes 98336 | tf_op jit(solution)/shard_map/ppermute | solution.py:457
  68.4 2.2 %collective-permute-start.11 = (f32[16,24,128]{2,1,0:T(8,128)S(1)}, f32[16,24,128]{2,1,0:T(8,128)S(1)}, u32[]{:S(2)}, u32[]{:S(2)}) collective-permute-start(f32[16,24,128]{2,1,0:T(8,128)S(1)} %pad_maximum_fusion.12), channel_id=1, source_target_pairs={{0,1},{1,0},{2,3},{3,2},{4,5},{5,4},{6,7},{7,6},{8,9},{9,8},{10,11... | collective-permute-start | bytes 589832 | tf_op jit(solution)/shard_map/ppermute | solution.py:23
  72.0 4.2 %collective-permute-start.12 = (f32[20,24,128]{2,1,0:T(8,128)S(1)}, f32[20,24,128]{2,1,0:T(8,128)S(1)}, u32[]{:S(2)}, u32[]{:S(2)}) collective-permute-start(f32[20,24,128]{2,1,0:T(8,128)S(1)} %maximum_select_fusion), channel_id=1, source_target_pairs={{1,2},{2,1},{3,4},{4,3},{5,6},{6,5},{7,8},{8,7},{9,10},{10,9},{11,... | collective-permute-start | bytes 737288 | tf_op jit(solution)/shard_map/ppermute | solution.py:23
  76.9 3.1 %collective-permute-done.12.refs_1_ = f32[20,24,128]{2,1,0:T(8,128)S(1)} collective-permute-done((f32[20,24,128]{2,1,0:T(8,128)S(1)}, f32[20,24,128]{2,1,0:T(8,128)S(1)}, u32[]{:S(2)}, u32[]{:S(2)}) %collective-permute-start.12) | collective-permute-done | bytes 245792 | tf_op jit(solution)/shard_map/ppermute | solution.py:23
  81.4 5.0 %collective-permute-start.15 = (f32[46,24,128]{2,1,0:T(8,128)S(1)}, f32[46,24,128]{2,1,0:T(8,128)S(1)}, u32[]{:S(2)}, u32[]{:S(2)}) collective-permute-start(f32[46,24,128]{2,1,0:T(8,128)S(1)} %get-tuple-element.61), channel_id=1, source_target_pairs={{16,32},{32,16},{48,64},{64,48},{80,96},{96,80},{112,128},{128,112... | collective-permute-start | bytes 1695752 | tf_op jit(solution)/shard_map/ppermute | solution.py:23
  89.0 22.6 %all-gather = f32[512,128]{1,0:T(8,128)S(1)} all-gather(f32[32,128]{1,0:T(8,128)S(1)} %concatenate.126), channel_id=2, replica_groups=mesh['gx'=32,'gy'=16] {'gy'}, dimensions={0}, use_global_device_ids=true | all-gather | bytes 278528 | tf_op jit(solution)/shard_map/all_gather | solution.py:539
  112.4 2.4 %collective-permute-start.20 = (f32[68,24,128]{2,1,0:T(8,128)S(1)}, f32[68,24,128]{2,1,0:T(8,128)S(1)}, u32[]{:S(2)}, u32[]{:S(2)}) collective-permute-start(f32[68,24,128]{2,1,0:T(8,128)S(1)} %get-tuple-element.51), channel_id=1, source_target_pairs={{1,2},{2,1},{3,4},{4,3},{5,6},{6,5},{7,8},{8,7},{9,10},{10,9},{11,... | collective-permute-start | bytes 2506760 | tf_op jit(solution)/shard_map/ppermute | solution.py:23
  114.8 1.9 %collective-permute-start.19 = (f32[68,24,128]{2,1,0:T(8,128)S(1)}, f32[68,24,128]{2,1,0:T(8,128)S(1)}, u32[]{:S(2)}, u32[]{:S(2)}) collective-permute-start(f32[68,24,128]{2,1,0:T(8,128)S(1)} %get-tuple-element.52), channel_id=1, source_target_pairs={{0,1},{1,0},{2,3},{3,2},{4,5},{5,4},{6,7},{7,6},{8,9},{9,8},{10,11... | collective-permute-start | bytes 2506760 | tf_op jit(solution)/shard_map/ppermute | solution.py:23
  117.9 19.5 %all-gather.1 = f32[384,128]{1,0:T(8,128)S(1)} all-gather(f32[24,128]{1,0:T(8,128)S(1)} %solve.1), channel_id=3, replica_groups=mesh['gx'=32,'gy'=16] {'gy'}, dimensions={0}, use_global_device_ids=true | all-gather | bytes 208896 | tf_op jit(solution)/shard_map/all_gather | solution.py:558
  137.6 3.9 %collective-permute-start.16 = (f32[6,24,128]{2,1,0:T(8,128)S(1)}, f32[6,24,128]{2,1,0:T(8,128)S(1)}, u32[]{:S(2)}, u32[]{:S(2)}) collective-permute-start(f32[6,24,128]{2,1,0:T(8,128)S(1)} %pick.1.refs_0_), channel_id=1, source_target_pairs={{0,16},{16,0},{32,48},{48,32},{64,80},{80,64},{96,112},{112,96},{1... | collective-permute-start | bytes 221192 | tf_op jit(solution)/shard_map/ppermute | solution.py:457
  141.5 3.4 %collective-permute-start.17 = (f32[6,24,128]{2,1,0:T(8,128)S(1)}, f32[6,24,128]{2,1,0:T(8,128)S(1)}, u32[]{:S(2)}, u32[]{:S(2)}) collective-permute-start(f32[6,24,128]{2,1,0:T(8,128)S(1)} %pick.1.refs_0_), channel_id=1, source_target_pairs={{32,64},{64,32},{48,80},{80,48},{96,128},{128,96},{112,144},{144,1... | collective-permute-start | bytes 221192 | tf_op jit(solution)/shard_map/ppermute | solution.py:457
  146.0 2.1 %collective-permute-done.17 = f32[6,24,128]{2,1,0:T(8,128)S(1)} collective-permute-done((f32[6,24,128]{2,1,0:T(8,128)S(1)}, f32[6,24,128]{2,1,0:T(8,128)S(1)}, u32[]{:S(2)}, u32[]{:S(2)}) %collective-permute-start.17) | collective-permute-done | bytes 73760 | tf_op jit(solution)/shard_map/ppermute | solution.py:457
  148.1 5.3 %collective-permute-start.18 = (f32[12,24,128]{2,1,0:T(8,128)S(1)}, f32[12,24,128]{2,1,0:T(8,128)S(1)}, u32[]{:S(2)}, u32[]{:S(2)}) collective-permute-start(f32[12,24,128]{2,1,0:T(8,128)S(1)} %constant_dynamic-update-slice_fusion.6.refs_1_), channel_id=1, source_target_pairs={{0,1},{1,0},{2,3},{3,2},{4,5},{5,4},{6,7},{7,6},{8,9},{9,8},{10,11... | collective-permute-start | bytes 442376 | tf_op jit(solution)/shard_map/ppermute | solution.py:23
  157.5 3.9 %collective-permute-start.22 = (f32[6,24,128]{2,1,0:T(8,128)S(1)}, f32[6,24,128]{2,1,0:T(8,128)S(1)}, u32[]{:S(2)}, u32[]{:S(2)}) collective-permute-start(f32[6,24,128]{2,1,0:T(8,128)S(1)} %bitcast.295), channel_id=1, source_target_pairs={{16,32},{32,16},{48,64},{64,48},{80,96},{96,80},{112,128},{128,112... | collective-permute-start | bytes 221192 | tf_op jit(solution)/shard_map/ppermute | solution.py:23
  161.5 4.5 %collective-permute-done.22.refs_2_ = f32[6,24,128]{2,1,0:T(8,128)S(1)} collective-permute-done((f32[6,24,128]{2,1,0:T(8,128)S(1)}, f32[6,24,128]{2,1,0:T(8,128)S(1)}, u32[]{:S(2)}, u32[]{:S(2)}) %collective-permute-start.22) | collective-permute-done | bytes 73760 | tf_op jit(solution)/shard_map/ppermute | solution.py:23
  166.0 3.8 %collective-permute-start.24 = (f32[12,24,128]{2,1,0:T(8,128)S(1)}, f32[12,24,128]{2,1,0:T(8,128)S(1)}, u32[]{:S(2)}, u32[]{:S(2)}) collective-permute-start(f32[12,24,128]{2,1,0:T(8,128)S(1)} %get-tuple-element.101), channel_id=1, source_target_pairs={{1,2},{2,1},{3,4},{4,3},{5,6},{6,5},{7,8},{8,7},{9,10},{10,9},{11,... | collective-permute-start | bytes 442376 | tf_op jit(solution)/shard_map/ppermute | solution.py:23
  169.9 1.9 %collective-permute-start.23 = (f32[12,24,128]{2,1,0:T(8,128)S(1)}, f32[12,24,128]{2,1,0:T(8,128)S(1)}, u32[]{:S(2)}, u32[]{:S(2)}) collective-permute-start(f32[12,24,128]{2,1,0:T(8,128)S(1)} %get-tuple-element.102), channel_id=1, source_target_pairs={{0,1},{1,0},{2,3},{3,2},{4,5},{5,4},{6,7},{7,6},{8,9},{9,8},{10,11... | collective-permute-start | bytes 442376 | tf_op jit(solution)/shard_map/ppermute | solution.py:23
  173.2 5.0 %up_last.1 = f32[8,8,24,128]{3,2,1,0:T(8,128)S(1)} custom-call(f32[4,4,24,128]{3,2,1,0:T(8,128)S(1)} %up_block.1.refs_0_, f32[6,24,128]{2,1,0:T(8,128)S(1)} %collective-permute-done.21.refs_1_, f32[6,24,128]{2,1,0:T(8,128)S(1)} %collective-permute-done.22.refs_2_, f32[12,24,128]{2,1,0:T(8,128)S(1)} %collective-permute-done.23.refs_3_, ...), custom_call_target="tpu_custom_call" | custom-call | tf_op jit(solution)/shard_map/up_last/pallas_call | solution.py:372
  (140 shorter events, 26.1 us)
Async XLA Ops:
  1.6 0.8 copy-start.1
  2.4 13.9 %collective-permute-start.1 = (f32[27,24,128]{2,1,0:T(8,128)S(1)}, f32[27,24,128]{2,1,0:T(8,128)S(1)}, u32[]{:S(2)}, u32[]{:S(2)}) collective-permute-start(f32[27,24,128]{2,1,0:T(8,128)S(1)} %get-tuple-element.75), channel_id=1, source_target_pairs={{16,32},{32,16},{48,64},{64,48},{80,96},{96,80},{112,128},{128,112... | collective-permute-start | bytes 995336 | tf_op jit(solution)/shard_map/ppermute | solution.py:23
  6.7 10.2 %collective-permute-start = (f32[27,24,128]{2,1,0:T(8,128)S(1)}, f32[27,24,128]{2,1,0:T(8,128)S(1)}, u32[]{:S(2)}, u32[]{:S(2)}) collective-permute-start(f32[27,24,128]{2,1,0:T(8,128)S(1)} %get-tuple-element.76), channel_id=1, source_target_pairs={{0,16},{16,0},{32,48},{48,32},{64,80},{80,64},{96,112},{112,96},{1... | collective-permute-start | bytes 995336 | tf_op jit(solution)/shard_map/ppermute | solution.py:23
  17.2 7.9 %copy-start.2 = (f32[24,8,8,128]{3,2,1,0:T(8,128)S(1)}, f32[24,8,8,128]{3,2,1,0:T(8,128)}, u32[]{:S(2)}) copy-start(f32[24,8,8,128]{3,2,1,0:T(8,128)} %param.4) | copy-start | bytes 2359300
  17.3 12.1 %collective-permute-start.3 = (f32[38,24,128]{2,1,0:T(8,128)S(1)}, f32[38,24,128]{2,1,0:T(8,128)S(1)}, u32[]{:S(2)}, u32[]{:S(2)}) collective-permute-start(f32[38,24,128]{2,1,0:T(8,128)S(1)} %get-tuple-element.63), channel_id=1, source_target_pairs={{1,2},{2,1},{3,4},{4,3},{5,6},{6,5},{7,8},{8,7},{9,10},{10,9},{11,... | collective-permute-start | bytes 1400840 | tf_op jit(solution)/shard_map/ppermute | solution.py:23
  23.2 6.2 %collective-permute-start.2 = (f32[38,24,128]{2,1,0:T(8,128)S(1)}, f32[38,24,128]{2,1,0:T(8,128)S(1)}, u32[]{:S(2)}, u32[]{:S(2)}) collective-permute-start(f32[38,24,128]{2,1,0:T(8,128)S(1)} %get-tuple-element.64), channel_id=1, source_target_pairs={{0,1},{1,0},{2,3},{3,2},{4,5},{5,4},{6,7},{7,6},{8,9},{9,8},{10,11... | collective-permute-start | bytes 1400840 | tf_op jit(solution)/shard_map/ppermute | solution.py:23
  32.5 9.3 %collective-permute-start.5 = (f32[13,24,128]{2,1,0:T(8,128)S(1)}, f32[13,24,128]{2,1,0:T(8,128)S(1)}, u32[]{:S(2)}, u32[]{:S(2)}) collective-permute-start(f32[13,24,128]{2,1,0:T(8,128)S(1)} %get-tuple-element.99), channel_id=1, source_target_pairs={{16,32},{32,16},{48,64},{64,48},{80,96},{96,80},{112,128},{128,112... | collective-permute-start | bytes 479240 | tf_op jit(solution)/shard_map/ppermute | solution.py:23
  36.8 6.1 %collective-permute-start.4 = (f32[13,24,128]{2,1,0:T(8,128)S(1)}, f32[13,24,128]{2,1,0:T(8,128)S(1)}, u32[]{:S(2)}, u32[]{:S(2)}) collective-permute-start(f32[13,24,128]{2,1,0:T(8,128)S(1)} %get-tuple-element.100), channel_id=1, source_target_pairs={{0,16},{16,0},{32,48},{48,32},{64,80},{80,64},{96,112},{112,96},{1... | collective-permute-start | bytes 479240 | tf_op jit(solution)/shard_map/ppermute | solution.py:23
  43.2 10.0 %collective-permute-start.7 = (f32[19,24,128]{2,1,0:T(8,128)S(1)}, f32[19,24,128]{2,1,0:T(8,128)S(1)}, u32[]{:S(2)}, u32[]{:S(2)}) collective-permute-start(f32[19,24,128]{2,1,0:T(8,128)S(1)} %get-tuple-element.93), channel_id=1, source_target_pairs={{1,2},{2,1},{3,4},{4,3},{5,6},{6,5},{7,8},{8,7},{9,10},{10,9},{11,... | collective-permute-start | bytes 700424 | tf_op jit(solution)/shard_map/ppermute | solution.py:23
  49.4 3.7 %collective-permute-start.6 = (f32[19,24,128]{2,1,0:T(8,128)S(1)}, f32[19,24,128]{2,1,0:T(8,128)S(1)}, u32[]{:S(2)}, u32[]{:S(2)}) collective-permute-start(f32[19,24,128]{2,1,0:T(8,128)S(1)} %get-tuple-element.94), channel_id=1, source_target_pairs={{0,1},{1,0},{2,3},{3,2},{4,5},{5,4},{6,7},{7,6},{8,9},{9,8},{10,11... | collective-permute-start | bytes 700424 | tf_op jit(solution)/shard_map/ppermute | solution.py:23
  54.4 3.1 %collective-permute-start.8 = (f32[2,2,24,128]{3,2,0,1:T(8,128)S(1)}, f32[2,2,24,128]{3,2,0,1:T(8,128)S(1)}, u32[]{:S(2)}, u32[]{:S(2)}) collective-permute-start(f32[2,2,24,128]{3,2,0,1:T(8,128)S(1)} %copy.45), channel_id=1, source_target_pairs={{0,1},{1,0},{2,3},{3,2},{4,5},{5,4},{6,7},{7,6},{8,9},{9,8},{10,11... | collective-permute-start | bytes 147464 | tf_op jit(solution)/shard_map/ppermute | solution.py:23
  57.6 7.3 %collective-permute-start.10 = (f32[2,4,24,128]{3,2,0,1:T(8,128)S(1)}, f32[2,4,24,128]{3,2,0,1:T(8,128)S(1)}, u32[]{:S(2)}, u32[]{:S(2)}) collective-permute-start(f32[2,4,24,128]{3,2,0,1:T(8,128)S(1)} %pad_maximum_fusion.22), channel_id=1, source_target_pairs={{32,64},{64,32},{48,80},{80,48},{96,128},{128,96},{112,144},{144,1... | collective-permute-start | bytes 294920 | tf_op jit(solution)/shard_map/ppermute | solution.py:457
  59.5 8.8 %collective-permute-start.9 = (f32[2,4,24,128]{3,2,0,1:T(8,128)S(1)}, f32[2,4,24,128]{3,2,0,1:T(8,128)S(1)}, u32[]{:S(2)}, u32[]{:S(2)}) collective-permute-start(f32[2,4,24,128]{3,2,0,1:T(8,128)S(1)} %pad_maximum_fusion.22), channel_id=1, source_target_pairs={{0,16},{16,0},{32,48},{48,32},{64,80},{80,64},{96,112},{112,96},{1... | collective-permute-start | bytes 294920 | tf_op jit(solution)/shard_map/ppermute | solution.py:457
  68.4 3.3 %collective-permute-start.11 = (f32[16,24,128]{2,1,0:T(8,128)S(1)}, f32[16,24,128]{2,1,0:T(8,128)S(1)}, u32[]{:S(2)}, u32[]{:S(2)}) collective-permute-start(f32[16,24,128]{2,1,0:T(8,128)S(1)} %pad_maximum_fusion.12), channel_id=1, source_target_pairs={{0,1},{1,0},{2,3},{3,2},{4,5},{5,4},{6,7},{7,6},{8,9},{9,8},{10,11... | collective-permute-start | bytes 589832 | tf_op jit(solution)/shard_map/ppermute | solution.py:23
  72.0 8.0 %collective-permute-start.12 = (f32[20,24,128]{2,1,0:T(8,128)S(1)}, f32[20,24,128]{2,1,0:T(8,128)S(1)}, u32[]{:S(2)}, u32[]{:S(2)}) collective-permute-start(f32[20,24,128]{2,1,0:T(8,128)S(1)} %maximum_select_fusion), channel_id=1, source_target_pairs={{1,2},{2,1},{3,4},{4,3},{5,6},{6,5},{7,8},{8,7},{9,10},{10,9},{11,... | collective-permute-start | bytes 737288 | tf_op jit(solution)/shard_map/ppermute | solution.py:23
  76.2 0.7 collective-permute-start.13
  81.4 30.3 %collective-permute-start.15 = (f32[46,24,128]{2,1,0:T(8,128)S(1)}, f32[46,24,128]{2,1,0:T(8,128)S(1)}, u32[]{:S(2)}, u32[]{:S(2)}) collective-permute-start(f32[46,24,128]{2,1,0:T(8,128)S(1)} %get-tuple-element.61), channel_id=1, source_target_pairs={{16,32},{32,16},{48,64},{64,48},{80,96},{96,80},{112,128},{128,112... | collective-permute-start | bytes 1695752 | tf_op jit(solution)/shard_map/ppermute | solution.py:23
  86.4 25.2 %collective-permute-start.14 = (f32[46,24,128]{2,1,0:T(8,128)S(1)}, f32[46,24,128]{2,1,0:T(8,128)S(1)}, u32[]{:S(2)}, u32[]{:S(2)}) collective-permute-start(f32[46,24,128]{2,1,0:T(8,128)S(1)} %get-tuple-element.62), channel_id=1, source_target_pairs={{0,16},{16,0},{32,48},{48,32},{64,80},{80,64},{96,112},{112,96},{1... | collective-permute-start | bytes 1695752 | tf_op jit(solution)/shard_map/ppermute | solution.py:23
  112.3 4.5 %copy-start = (f32[1,1,128,2048]{3,2,1,0:T(8,128)S(1)}, f32[1,1,128,2048]{3,2,1,0:T(8,128)}, u32[]{:S(2)}) copy-start(f32[1,1,128,2048]{3,2,1,0:T(8,128)} %param.7) | copy-start | bytes 3145732
  112.4 42.0 %collective-permute-start.20 = (f32[68,24,128]{2,1,0:T(8,128)S(1)}, f32[68,24,128]{2,1,0:T(8,128)S(1)}, u32[]{:S(2)}, u32[]{:S(2)}) collective-permute-start(f32[68,24,128]{2,1,0:T(8,128)S(1)} %get-tuple-element.51), channel_id=1, source_target_pairs={{1,2},{2,1},{3,4},{4,3},{5,6},{6,5},{7,8},{8,7},{9,10},{10,9},{11,... | collective-permute-start | bytes 2506760 | tf_op jit(solution)/shard_map/ppermute | solution.py:23
  114.8 39.6 %collective-permute-start.19 = (f32[68,24,128]{2,1,0:T(8,128)S(1)}, f32[68,24,128]{2,1,0:T(8,128)S(1)}, u32[]{:S(2)}, u32[]{:S(2)}) collective-permute-start(f32[68,24,128]{2,1,0:T(8,128)S(1)} %get-tuple-element.52), channel_id=1, source_target_pairs={{0,1},{1,0},{2,3},{3,2},{4,5},{5,4},{6,7},{7,6},{8,9},{9,8},{10,11... | collective-permute-start | bytes 2506760 | tf_op jit(solution)/shard_map/ppermute | solution.py:23
  137.6 8.4 %collective-permute-start.16 = (f32[6,24,128]{2,1,0:T(8,128)S(1)}, f32[6,24,128]{2,1,0:T(8,128)S(1)}, u32[]{:S(2)}, u32[]{:S(2)}) collective-permute-start(f32[6,24,128]{2,1,0:T(8,128)S(1)} %pick.1.refs_0_), channel_id=1, source_target_pairs={{0,16},{16,0},{32,48},{48,32},{64,80},{80,64},{96,112},{112,96},{1... | collective-permute-start | bytes 221192 | tf_op jit(solution)/shard_map/ppermute | solution.py:457
  141.5 6.6 %collective-permute-start.17 = (f32[6,24,128]{2,1,0:T(8,128)S(1)}, f32[6,24,128]{2,1,0:T(8,128)S(1)}, u32[]{:S(2)}, u32[]{:S(2)}) collective-permute-start(f32[6,24,128]{2,1,0:T(8,128)S(1)} %pick.1.refs_0_), channel_id=1, source_target_pairs={{32,64},{64,32},{48,80},{80,48},{96,128},{128,96},{112,144},{144,1... | collective-permute-start | bytes 221192 | tf_op jit(solution)/shard_map/ppermute | solution.py:457
  148.1 6.3 %collective-permute-start.18 = (f32[12,24,128]{2,1,0:T(8,128)S(1)}, f32[12,24,128]{2,1,0:T(8,128)S(1)}, u32[]{:S(2)}, u32[]{:S(2)}) collective-permute-start(f32[12,24,128]{2,1,0:T(8,128)S(1)} %constant_dynamic-update-slice_fusion.6.refs_1_), channel_id=1, source_target_pairs={{0,1},{1,0},{2,3},{3,2},{4,5},{5,4},{6,7},{7,6},{8,9},{9,8},{10,11... | collective-permute-start | bytes 442376 | tf_op jit(solution)/shard_map/ppermute | solution.py:23
  155.6 5.9 %collective-permute-start.21 = (f32[6,24,128]{2,1,0:T(8,128)S(1)}, f32[6,24,128]{2,1,0:T(8,128)S(1)}, u32[]{:S(2)}, u32[]{:S(2)}) collective-permute-start(f32[6,24,128]{2,1,0:T(8,128)S(1)} %bitcast.296), channel_id=1, source_target_pairs={{0,16},{16,0},{32,48},{48,32},{64,80},{80,64},{96,112},{112,96},{1... | collective-permute-start | bytes 221192 | tf_op jit(solution)/shard_map/ppermute | solution.py:23
  157.5 8.4 %collective-permute-start.22 = (f32[6,24,128]{2,1,0:T(8,128)S(1)}, f32[6,24,128]{2,1,0:T(8,128)S(1)}, u32[]{:S(2)}, u32[]{:S(2)}) collective-permute-start(f32[6,24,128]{2,1,0:T(8,128)S(1)} %bitcast.295), channel_id=1, source_target_pairs={{16,32},{32,16},{48,64},{64,48},{80,96},{96,80},{112,128},{128,112... | collective-permute-start | bytes 221192 | tf_op jit(solution)/shard_map/ppermute | solution.py:23
  166.0 6.7 %collective-permute-start.24 = (f32[12,24,128]{2,1,0:T(8,128)S(1)}, f32[12,24,128]{2,1,0:T(8,128)S(1)}, u32[]{:S(2)}, u32[]{:S(2)}) collective-permute-start(f32[12,24,128]{2,1,0:T(8,128)S(1)} %get-tuple-element.101), channel_id=1, source_target_pairs={{1,2},{2,1},{3,4},{4,3},{5,6},{6,5},{7,8},{8,7},{9,10},{10,9},{11,... | collective-permute-start | bytes 442376 | tf_op jit(solution)/shard_map/ppermute | solution.py:23
  169.9 3.3 %collective-permute-start.23 = (f32[12,24,128]{2,1,0:T(8,128)S(1)}, f32[12,24,128]{2,1,0:T(8,128)S(1)}, u32[]{:S(2)}, u32[]{:S(2)}) collective-permute-start(f32[12,24,128]{2,1,0:T(8,128)S(1)} %get-tuple-element.102), channel_id=1, source_target_pairs={{0,1},{1,0},{2,3},{3,2},{4,5},{5,4},{6,7},{7,6},{8,9},{9,8},{10,11... | collective-permute-start | bytes 442376 | tf_op jit(solution)/shard_map/ppermute | solution.py:23

commit v8 on v7

--- a/solution.py
+++ b/solution.py
@@ -27,11 +27,8 @@
     return lax.rem(lax.div(lax.axis_index(axis), dist), 2)
 
 
-def swap_ends(at, low, high, axis, dist, odd_first=False):
+def swap_ends(at, low, high, axis, dist):
     even = at[axis]
-    if odd_first:
-        second = swap(jnp.where(even, low, high), axis, dist, 1)
-        return swap(jnp.where(even, high, low), axis, dist, 0), second
     first = swap(jnp.where(even, high, low), axis, dist, 0)
     return first, swap(jnp.where(even, low, high), axis, dist, 1)
 
@@ -69,11 +66,11 @@
 
 
 def each_row(count, row):
-    if count <= 4:
+    if count <= 6:
         for x in range(count):
             row(x)
         return
-    many = 4 if count % 4 == 0 else 2
+    many = max(k for k in range(1, 7) if count % k == 0)
 
     def rows(step, carry):
         for k in range(many):
@@ -416,15 +413,15 @@
     return jnp.concatenate([strip, rows.reshape((-1,) + tail)], axis=0)
 
 
-def frame(at, v, reach, beyond=0, blocks=None, rims=None, odd_first=False):
+def frame(at, v, reach, beyond=0, blocks=None, rims=None, strips=None):
     n = v.shape[0] - 2 * beyond
     tail = v.shape[-2:]
     own = v[beyond : beyond + n, beyond : beyond + n]
     extra = [blocks, blocks] if rims is None else [rims[-2:], rims[:2]]
-    low = v[beyond : beyond + reach, beyond : beyond + n]
-    high = v[beyond + n - reach : beyond + n, beyond : beyond + n]
+    inner = v[:, beyond : beyond + n]
+    low, high = strips or (inner[beyond : beyond + reach], inner[beyond + n - reach : beyond + n])
     low, high = with_rows(cells(low), extra[0], tail), with_rows(cells(high), extra[1], tail)
-    x_pieces = swap_ends(at, low, high, "gx", 1, odd_first)
+    x_pieces = swap_ends(at, low, high, "gx", 1)
     sides = in_order(at, *x_pieces, "gx")
     strips = [side[: reach * n].reshape((reach, n) + tail) for side in sides]
     rows = jnp.concatenate([strips[0], own, strips[1]], axis=0)
@@ -472,6 +469,7 @@
     at, rhs = lax.optimization_barrier((place(), rhs))
     right = jnp.transpose(rhs, (1, 2, 0, 3))
     n = right.shape[0]
+    strips = [jnp.transpose(rows, (1, 2, 0, 3)) for rows in (rhs[:, :HALO], rhs[:, n - HALO :])]
     tail = chans, depth = right.shape[2:]
     half, size = n // 2, n // 4
 
@@ -480,7 +478,7 @@
 
     x0, q0, b1, shift_wide, shift_one, shift_two = call(
         functools.partial(down_fine_kernel, n, grid_of(n)),
-        [right, *frame(at, right, HALO, 0, shift), shift],
+        [right, *frame(at, right, HALO, 0, shift, None, strips), shift],
         fields((n, n), (n, n), (half, half))
         + [(3 * n, 3 * n, depth), (3 * half, 3 * half, depth), (3 * size, 3 * size, depth)],
         fields((n + 6, n + 6), (n + 4, n + 4), (n + 2, n + 2)),
@@ -567,7 +565,7 @@
     )[0]
     x0 = call(
         functools.partial(up_last_kernel, half, (grid_of(half), grid_of(n)), offsets),
-        [x2, *frame(at, x2, 3, 1, odd_first=True), *sides, shift_one, around[2], around[1], shift_wide, x0, around[0]],
+        [x2, *frame(at, x2, 3, 1), *sides, shift_one, around[2], around[1], shift_wide, x0, around[0]],
         fields((n, n)),
         fields(
             (size + 6, size + 6), (half + 4, half + 4), (half + 8, half + 8), (half + 6, half + 6), (half + 4, half + 4),

time: 180 us -> 177 us (0.983)
  transfers between devices with their start and end apart: 25 -> 25, of which waited for: 16 -> 16; matrix products, arithmetic and copies ran while one was open for 0% -> 1% of each run, Pallas kernels for 1% -> 1%
where the time goes in v8:
time: 177 us
  starting transfers between devices  80.3 us (45%)
  blocking collectives  42.1 us (24%)
  waiting for transfers between devices  36.2 us (20%)
  Pallas kernels  11.2 us (6%)
  local copies, waits for them, and re-layouts  3.89 us (2%)
    ppermute x20, starting transfers between devices, swap(): return lax.ppermute(x, axis, pairs)  65.1 us
    ppermute x20, waiting for transfers between devices, swap(): return lax.ppermute(x, axis, pairs)  29.6 us
    all_gather x1, blocking collectives, body(): lax.all_gather(jnp.concatenate([b3, slot], axis=0)[None], 'gy', axis=0, t...  22.6 us
    all_gather x1, blocking collectives, body(): back = lax.all_gather(solved[None], 'gy', axis=0, tiled=True)  19.5 us
    ppermute x4, starting transfers between devices, by_core(): return lax.ppermute(x, ('gx', 'gy'), pairs)  14.6 us
    pallas_call x7, Pallas kernels, call(): pl.pallas_call(run, out_shape=[jax.ShapeDtypeStruct(out, jnp.float32) for...  11.2 us
    ppermute x4, waiting for transfers between devices, by_core(): return lax.ppermute(x, ('gx', 'gy'), pairs)  6.61 us
  transfers between devices with their start and end apart: 25, of which 16 were waited for; matrix products, arithmetic and copies ran while one was open for 1% of the time, Pallas kernels for 1%

profile of v8, /device:TPU:31, one launch (start us, length us, event | category | flops | bytes accessed | tf_op | source)
XLA Modules:
  0.0 176.5 jit_solution(11325596538007104067)
XLA Ops:
  1.3 4.5 %collective-permute-start.1 = (f32[27,24,128]{2,1,0:T(8,128)S(1)}, f32[27,24,128]{2,1,0:T(8,128)S(1)}, u32[]{:S(2)}, u32[]{:S(2)}) collective-permute-start(f32[27,24,128]{2,1,0:T(8,128)S(1)} %get-tuple-element.75), channel_id=1, source_target_pairs={{16,32},{32,16},{48,64},{64,48},{80,96},{96,80},{112,128},{128,112... | collective-permute-start | bytes 995336 | tf_op jit(solution)/shard_map/ppermute | solution.py:23
  5.8 1.9 %collective-permute-start = (f32[27,24,128]{2,1,0:T(8,128)S(1)}, f32[27,24,128]{2,1,0:T(8,128)S(1)}, u32[]{:S(2)}, u32[]{:S(2)}) collective-permute-start(f32[27,24,128]{2,1,0:T(8,128)S(1)} %get-tuple-element.76), channel_id=1, source_target_pairs={{0,16},{16,0},{32,48},{48,32},{64,80},{80,64},{96,112},{112,96},{1... | collective-permute-start | bytes 995336 | tf_op jit(solution)/shard_map/ppermute | solution.py:23
  8.2 7.1 %collective-permute-done.1.refs_2_ = f32[27,24,128]{2,1,0:T(8,128)S(1)} collective-permute-done((f32[27,24,128]{2,1,0:T(8,128)S(1)}, f32[27,24,128]{2,1,0:T(8,128)S(1)}, u32[]{:S(2)}, u32[]{:S(2)}) %collective-permute-start.1) | collective-permute-done | bytes 331808 | tf_op jit(solution)/shard_map/ppermute | solution.py:23
  16.3 5.8 %collective-permute-start.3 = (f32[38,24,128]{2,1,0:T(8,128)S(1)}, f32[38,24,128]{2,1,0:T(8,128)S(1)}, u32[]{:S(2)}, u32[]{:S(2)}) collective-permute-start(f32[38,24,128]{2,1,0:T(8,128)S(1)} %get-tuple-element.63), channel_id=1, source_target_pairs={{1,2},{2,1},{3,4},{4,3},{5,6},{6,5},{7,8},{8,7},{9,10},{10,9},{11,... | collective-permute-start | bytes 1400840 | tf_op jit(solution)/shard_map/ppermute | solution.py:23
  24.5 3.8 %collective-permute-done.3.refs_4_ = f32[38,24,128]{2,1,0:T(8,128)S(1)} collective-permute-done((f32[38,24,128]{2,1,0:T(8,128)S(1)}, f32[38,24,128]{2,1,0:T(8,128)S(1)}, u32[]{:S(2)}, u32[]{:S(2)}) %collective-permute-start.3) | collective-permute-done | bytes 466976 | tf_op jit(solution)/shard_map/ppermute | solution.py:23
  28.3 2.7 %down_fine.1 = (f32[8,8,24,128]{3,2,1,0:T(8,128)S(1)}, f32[8,8,24,128]{3,2,1,0:T(8,128)S(1)}, f32[4,4,24,128]{3,2,1,0:T(8,128)S(1)}, f32[24,24,128]{2,1,0:T(8,12...) custom-call(f32[8,8,24,128]{3,2,1,0:T(8,128)S(1)} %copy.40.refs_0_, ...), custom_call_target="tpu_custom_call" | custom-call | tf_op jit(solution)/shard_map/down_fine/pallas_call | solution.py:369
  31.1 4.3 %collective-permute-start.5 = (f32[13,24,128]{2,1,0:T(8,128)S(1)}, f32[13,24,128]{2,1,0:T(8,128)S(1)}, u32[]{:S(2)}, u32[]{:S(2)}) collective-permute-start(f32[13,24,128]{2,1,0:T(8,128)S(1)} %get-tuple-element.99), channel_id=1, source_target_pairs={{16,32},{32,16},{48,64},{64,48},{80,96},{96,80},{112,128},{128,112... | collective-permute-start | bytes 479240 | tf_op jit(solution)/shard_map/ppermute | solution.py:23
  37.3 3.1 %collective-permute-done.5.refs_2_ = f32[13,24,128]{2,1,0:T(8,128)S(1)} collective-permute-done((f32[13,24,128]{2,1,0:T(8,128)S(1)}, f32[13,24,128]{2,1,0:T(8,128)S(1)}, u32[]{:S(2)}, u32[]{:S(2)}) %collective-permute-start.5) | collective-permute-done | bytes 159776 | tf_op jit(solution)/shard_map/ppermute | solution.py:23
  41.8 6.2 %collective-permute-start.7 = (f32[19,24,128]{2,1,0:T(8,128)S(1)}, f32[19,24,128]{2,1,0:T(8,128)S(1)}, u32[]{:S(2)}, u32[]{:S(2)}) collective-permute-start(f32[19,24,128]{2,1,0:T(8,128)S(1)} %get-tuple-element.93), channel_id=1, source_target_pairs={{1,2},{2,1},{3,4},{4,3},{5,6},{6,5},{7,8},{8,7},{9,10},{10,9},{11,... | collective-permute-start | bytes 700424 | tf_op jit(solution)/shard_map/ppermute | solution.py:23
  48.0 1.9 %collective-permute-start.6 = (f32[19,24,128]{2,1,0:T(8,128)S(1)}, f32[19,24,128]{2,1,0:T(8,128)S(1)}, u32[]{:S(2)}, u32[]{:S(2)}) collective-permute-start(f32[19,24,128]{2,1,0:T(8,128)S(1)} %get-tuple-element.94), channel_id=1, source_target_pairs={{0,1},{1,0},{2,3},{3,2},{4,5},{5,4},{6,7},{7,6},{8,9},{9,8},{10,11... | collective-permute-start | bytes 700424 | tf_op jit(solution)/shard_map/ppermute | solution.py:23
  52.8 1.9 %collective-permute-start.8 = (f32[2,2,24,128]{3,2,0,1:T(8,128)S(1)}, f32[2,2,24,128]{3,2,0,1:T(8,128)S(1)}, u32[]{:S(2)}, u32[]{:S(2)}) collective-permute-start(f32[2,2,24,128]{3,2,0,1:T(8,128)S(1)} %copy.47), channel_id=1, source_target_pairs={{0,1},{1,0},{2,3},{3,2},{4,5},{5,4},{6,7},{7,6},{8,9},{9,8},{10,11... | collective-permute-start | bytes 147464 | tf_op jit(solution)/shard_map/ppermute | solution.py:23
  56.0 1.9 %collective-permute-start.10 = (f32[2,4,24,128]{3,2,0,1:T(8,128)S(1)}, f32[2,4,24,128]{3,2,0,1:T(8,128)S(1)}, u32[]{:S(2)}, u32[]{:S(2)}) collective-permute-start(f32[2,4,24,128]{3,2,0,1:T(8,128)S(1)} %pad_maximum_fusion.22), channel_id=1, source_target_pairs={{32,64},{64,32},{48,80},{80,48},{96,128},{128,96},{112,144},{144,1... | collective-permute-start | bytes 294920 | tf_op jit(solution)/shard_map/ppermute | solution.py:454
  57.9 5.3 %collective-permute-start.9 = (f32[2,4,24,128]{3,2,0,1:T(8,128)S(1)}, f32[2,4,24,128]{3,2,0,1:T(8,128)S(1)}, u32[]{:S(2)}, u32[]{:S(2)}) collective-permute-start(f32[2,4,24,128]{3,2,0,1:T(8,128)S(1)} %pad_maximum_fusion.22), channel_id=1, source_target_pairs={{0,16},{16,0},{32,48},{48,32},{64,80},{80,64},{96,112},{112,96},{1... | collective-permute-start | bytes 294920 | tf_op jit(solution)/shard_map/ppermute | solution.py:454
  63.3 3.5 %collective-permute-done.9 = f32[2,4,24,128]{3,2,0,1:T(8,128)S(1)} collective-permute-done((f32[2,4,24,128]{3,2,0,1:T(8,128)S(1)}, f32[2,4,24,128]{3,2,0,1:T(8,128)S(1)}, u32[]{:S(2)}, u32[]{:S(2)}) %collective-permute-start.9) | collective-permute-done | bytes 98336 | tf_op jit(solution)/shard_map/ppermute | solution.py:454
  66.8 2.2 %collective-permute-start.11 = (f32[16,24,128]{2,1,0:T(8,128)S(1)}, f32[16,24,128]{2,1,0:T(8,128)S(1)}, u32[]{:S(2)}, u32[]{:S(2)}) collective-permute-start(f32[16,24,128]{2,1,0:T(8,128)S(1)} %pad_maximum_fusion.12), channel_id=1, source_target_pairs={{0,1},{1,0},{2,3},{3,2},{4,5},{5,4},{6,7},{7,6},{8,9},{9,8},{10,11... | collective-permute-start | bytes 589832 | tf_op jit(solution)/shard_map/ppermute | solution.py:23
  70.4 4.2 %collective-permute-start.12 = (f32[20,24,128]{2,1,0:T(8,128)S(1)}, f32[20,24,128]{2,1,0:T(8,128)S(1)}, u32[]{:S(2)}, u32[]{:S(2)}) collective-permute-start(f32[20,24,128]{2,1,0:T(8,128)S(1)} %maximum_select_fusion), channel_id=1, source_target_pairs={{1,2},{2,1},{3,4},{4,3},{5,6},{6,5},{7,8},{8,7},{9,10},{10,9},{11,... | collective-permute-start | bytes 737288 | tf_op jit(solution)/shard_map/ppermute | solution.py:23
  75.3 3.1 %collective-permute-done.12.refs_1_ = f32[20,24,128]{2,1,0:T(8,128)S(1)} collective-permute-done((f32[20,24,128]{2,1,0:T(8,128)S(1)}, f32[20,24,128]{2,1,0:T(8,128)S(1)}, u32[]{:S(2)}, u32[]{:S(2)}) %collective-permute-start.12) | collective-permute-done | bytes 245792 | tf_op jit(solution)/shard_map/ppermute | solution.py:23
  79.5 5.0 %collective-permute-start.15 = (f32[46,24,128]{2,1,0:T(8,128)S(1)}, f32[46,24,128]{2,1,0:T(8,128)S(1)}, u32[]{:S(2)}, u32[]{:S(2)}) collective-permute-start(f32[46,24,128]{2,1,0:T(8,128)S(1)} %get-tuple-element.61), channel_id=1, source_target_pairs={{16,32},{32,16},{48,64},{64,48},{80,96},{96,80},{112,128},{128,112... | collective-permute-start | bytes 1695752 | tf_op jit(solution)/shard_map/ppermute | solution.py:23
  84.5 1.9 %collective-permute-start.14 = (f32[46,24,128]{2,1,0:T(8,128)S(1)}, f32[46,24,128]{2,1,0:T(8,128)S(1)}, u32[]{:S(2)}, u32[]{:S(2)}) collective-permute-start(f32[46,24,128]{2,1,0:T(8,128)S(1)} %get-tuple-element.62), channel_id=1, source_target_pairs={{0,16},{16,0},{32,48},{48,32},{64,80},{80,64},{96,112},{112,96},{1... | collective-permute-start | bytes 1695752 | tf_op jit(solution)/shard_map/ppermute | solution.py:23
  87.2 22.6 %all-gather = f32[512,128]{1,0:T(8,128)S(1)} all-gather(f32[32,128]{1,0:T(8,128)S(1)} %concatenate.126), channel_id=2, replica_groups=mesh['gx'=32,'gy'=16] {'gy'}, dimensions={0}, use_global_device_ids=true | all-gather | bytes 278528 | tf_op jit(solution)/shard_map/all_gather | solution.py:537
  110.5 2.4 %collective-permute-start.20 = (f32[68,24,128]{2,1,0:T(8,128)S(1)}, f32[68,24,128]{2,1,0:T(8,128)S(1)}, u32[]{:S(2)}, u32[]{:S(2)}) collective-permute-start(f32[68,24,128]{2,1,0:T(8,128)S(1)} %get-tuple-element.51), channel_id=1, source_target_pairs={{1,2},{2,1},{3,4},{4,3},{5,6},{6,5},{7,8},{8,7},{9,10},{10,9},{11,... | collective-permute-start | bytes 2506760 | tf_op jit(solution)/shard_map/ppermute | solution.py:23
  116.0 19.5 %all-gather.1 = f32[384,128]{1,0:T(8,128)S(1)} all-gather(f32[24,128]{1,0:T(8,128)S(1)} %solve.1), channel_id=3, replica_groups=mesh['gx'=32,'gy'=16] {'gy'}, dimensions={0}, use_global_device_ids=true | all-gather | bytes 208896 | tf_op jit(solution)/shard_map/all_gather | solution.py:556
  135.7 3.9 %collective-permute-start.16 = (f32[6,24,128]{2,1,0:T(8,128)S(1)}, f32[6,24,128]{2,1,0:T(8,128)S(1)}, u32[]{:S(2)}, u32[]{:S(2)}) collective-permute-start(f32[6,24,128]{2,1,0:T(8,128)S(1)} %pick.1.refs_0_), channel_id=1, source_target_pairs={{0,16},{16,0},{32,48},{48,32},{64,80},{80,64},{96,112},{112,96},{1... | collective-permute-start | bytes 221192 | tf_op jit(solution)/shard_map/ppermute | solution.py:454
  139.6 3.4 %collective-permute-start.17 = (f32[6,24,128]{2,1,0:T(8,128)S(1)}, f32[6,24,128]{2,1,0:T(8,128)S(1)}, u32[]{:S(2)}, u32[]{:S(2)}) collective-permute-start(f32[6,24,128]{2,1,0:T(8,128)S(1)} %pick.1.refs_0_), channel_id=1, source_target_pairs={{32,64},{64,32},{48,80},{80,48},{96,128},{128,96},{112,144},{144,1... | collective-permute-start | bytes 221192 | tf_op jit(solution)/shard_map/ppermute | solution.py:454
  144.1 2.1 %collective-permute-done.17 = f32[6,24,128]{2,1,0:T(8,128)S(1)} collective-permute-done((f32[6,24,128]{2,1,0:T(8,128)S(1)}, f32[6,24,128]{2,1,0:T(8,128)S(1)}, u32[]{:S(2)}, u32[]{:S(2)}) %collective-permute-start.17) | collective-permute-done | bytes 73760 | tf_op jit(solution)/shard_map/ppermute | solution.py:454
  146.2 5.3 %collective-permute-start.18 = (f32[12,24,128]{2,1,0:T(8,128)S(1)}, f32[12,24,128]{2,1,0:T(8,128)S(1)}, u32[]{:S(2)}, u32[]{:S(2)}) collective-permute-start(f32[12,24,128]{2,1,0:T(8,128)S(1)} %constant_dynamic-update-slice_fusion.6.refs_1_), channel_id=1, source_target_pairs={{0,1},{1,0},{2,3},{3,2},{4,5},{5,4},{6,7},{7,6},{8,9},{9,8},{10,11... | collective-permute-start | bytes 442376 | tf_op jit(solution)/shard_map/ppermute | solution.py:23
  153.5 1.9 %collective-permute-start.21 = (f32[6,24,128]{2,1,0:T(8,128)S(1)}, f32[6,24,128]{2,1,0:T(8,128)S(1)}, u32[]{:S(2)}, u32[]{:S(2)}) collective-permute-start(f32[6,24,128]{2,1,0:T(8,128)S(1)} %bitcast.299), channel_id=1, source_target_pairs={{0,16},{16,0},{32,48},{48,32},{64,80},{80,64},{96,112},{112,96},{1... | collective-permute-start | bytes 221192 | tf_op jit(solution)/shard_map/ppermute | solution.py:23
  155.4 3.9 %collective-permute-start.22 = (f32[6,24,128]{2,1,0:T(8,128)S(1)}, f32[6,24,128]{2,1,0:T(8,128)S(1)}, u32[]{:S(2)}, u32[]{:S(2)}) collective-permute-start(f32[6,24,128]{2,1,0:T(8,128)S(1)} %bitcast.298), channel_id=1, source_target_pairs={{16,32},{32,16},{48,64},{64,48},{80,96},{96,80},{112,128},{128,112... | collective-permute-start | bytes 221192 | tf_op jit(solution)/shard_map/ppermute | solution.py:23
  159.4 4.5 %collective-permute-done.22.refs_2_ = f32[6,24,128]{2,1,0:T(8,128)S(1)} collective-permute-done((f32[6,24,128]{2,1,0:T(8,128)S(1)}, f32[6,24,128]{2,1,0:T(8,128)S(1)}, u32[]{:S(2)}, u32[]{:S(2)}) %collective-permute-start.22) | collective-permute-done | bytes 73760 | tf_op jit(solution)/shard_map/ppermute | solution.py:23
  163.9 3.8 %collective-permute-start.24 = (f32[12,24,128]{2,1,0:T(8,128)S(1)}, f32[12,24,128]{2,1,0:T(8,128)S(1)}, u32[]{:S(2)}, u32[]{:S(2)}) collective-permute-start(f32[12,24,128]{2,1,0:T(8,128)S(1)} %get-tuple-element.101), channel_id=1, source_target_pairs={{1,2},{2,1},{3,4},{4,3},{5,6},{6,5},{7,8},{8,7},{9,10},{10,9},{11,... | collective-permute-start | bytes 442376 | tf_op jit(solution)/shard_map/ppermute | solution.py:23
  167.8 2.1 %collective-permute-start.23 = (f32[12,24,128]{2,1,0:T(8,128)S(1)}, f32[12,24,128]{2,1,0:T(8,128)S(1)}, u32[]{:S(2)}, u32[]{:S(2)}) collective-permute-start(f32[12,24,128]{2,1,0:T(8,128)S(1)} %get-tuple-element.102), channel_id=1, source_target_pairs={{0,1},{1,0},{2,3},{3,2},{4,5},{5,4},{6,7},{7,6},{8,9},{9,8},{10,11... | collective-permute-start | bytes 442376 | tf_op jit(solution)/shard_map/ppermute | solution.py:23
  171.1 4.4 %up_last.1 = f32[8,8,24,128]{3,2,1,0:T(8,128)S(1)} custom-call(f32[4,4,24,128]{3,2,1,0:T(8,128)S(1)} %up_block.1.refs_0_, f32[6,24,128]{2,1,0:T(8,128)S(1)} %collective-permute-done.21.refs_1_, f32[6,24,128]{2,1,0:T(8,128)S(1)} %collective-permute-done.22.refs_2_, f32[12,24,128]{2,1,0:T(8,128)S(1)} %collective-permute-done.23.refs_3_, ...), custom_call_target="tpu_custom_call" | custom-call | tf_op jit(solution)/shard_map/up_last/pallas_call | solution.py:369
  (140 shorter events, 24.5 us)
Async XLA Ops:
  0.0 1.2 copy-start.1
  1.1 6.6 %copy-start.2 = (f32[24,8,8,128]{3,2,1,0:T(8,128)S(1)}, f32[24,8,8,128]{3,2,1,0:T(8,128)}, u32[]{:S(2)}) copy-start(f32[24,8,8,128]{3,2,1,0:T(8,128)} %param.4) | copy-start | bytes 2359300
  1.3 14.0 %collective-permute-start.1 = (f32[27,24,128]{2,1,0:T(8,128)S(1)}, f32[27,24,128]{2,1,0:T(8,128)S(1)}, u32[]{:S(2)}, u32[]{:S(2)}) collective-permute-start(f32[27,24,128]{2,1,0:T(8,128)S(1)} %get-tuple-element.75), channel_id=1, source_target_pairs={{16,32},{32,16},{48,64},{64,48},{80,96},{96,80},{112,128},{128,112... | collective-permute-start | bytes 995336 | tf_op jit(solution)/shard_map/ppermute | solution.py:23
  5.8 10.2 %collective-permute-start = (f32[27,24,128]{2,1,0:T(8,128)S(1)}, f32[27,24,128]{2,1,0:T(8,128)S(1)}, u32[]{:S(2)}, u32[]{:S(2)}) collective-permute-start(f32[27,24,128]{2,1,0:T(8,128)S(1)} %get-tuple-element.76), channel_id=1, source_target_pairs={{0,16},{16,0},{32,48},{48,32},{64,80},{80,64},{96,112},{112,96},{1... | collective-permute-start | bytes 995336 | tf_op jit(solution)/shard_map/ppermute | solution.py:23
  16.3 12.0 %collective-permute-start.3 = (f32[38,24,128]{2,1,0:T(8,128)S(1)}, f32[38,24,128]{2,1,0:T(8,128)S(1)}, u32[]{:S(2)}, u32[]{:S(2)}) collective-permute-start(f32[38,24,128]{2,1,0:T(8,128)S(1)} %get-tuple-element.63), channel_id=1, source_target_pairs={{1,2},{2,1},{3,4},{4,3},{5,6},{6,5},{7,8},{8,7},{9,10},{10,9},{11,... | collective-permute-start | bytes 1400840 | tf_op jit(solution)/shard_map/ppermute | solution.py:23
  22.1 6.2 %collective-permute-start.2 = (f32[38,24,128]{2,1,0:T(8,128)S(1)}, f32[38,24,128]{2,1,0:T(8,128)S(1)}, u32[]{:S(2)}, u32[]{:S(2)}) collective-permute-start(f32[38,24,128]{2,1,0:T(8,128)S(1)} %get-tuple-element.64), channel_id=1, source_target_pairs={{0,1},{1,0},{2,3},{3,2},{4,5},{5,4},{6,7},{7,6},{8,9},{9,8},{10,11... | collective-permute-start | bytes 1400840 | tf_op jit(solution)/shard_map/ppermute | solution.py:23
  31.1 9.3 %collective-permute-start.5 = (f32[13,24,128]{2,1,0:T(8,128)S(1)}, f32[13,24,128]{2,1,0:T(8,128)S(1)}, u32[]{:S(2)}, u32[]{:S(2)}) collective-permute-start(f32[13,24,128]{2,1,0:T(8,128)S(1)} %get-tuple-element.99), channel_id=1, source_target_pairs={{16,32},{32,16},{48,64},{64,48},{80,96},{96,80},{112,128},{128,112... | collective-permute-start | bytes 479240 | tf_op jit(solution)/shard_map/ppermute | solution.py:23
  35.4 6.1 %collective-permute-start.4 = (f32[13,24,128]{2,1,0:T(8,128)S(1)}, f32[13,24,128]{2,1,0:T(8,128)S(1)}, u32[]{:S(2)}, u32[]{:S(2)}) collective-permute-start(f32[13,24,128]{2,1,0:T(8,128)S(1)} %get-tuple-element.100), channel_id=1, source_target_pairs={{0,16},{16,0},{32,48},{48,32},{64,80},{80,64},{96,112},{112,96},{1... | collective-permute-start | bytes 479240 | tf_op jit(solution)/shard_map/ppermute | solution.py:23
  41.8 10.0 %collective-permute-start.7 = (f32[19,24,128]{2,1,0:T(8,128)S(1)}, f32[19,24,128]{2,1,0:T(8,128)S(1)}, u32[]{:S(2)}, u32[]{:S(2)}) collective-permute-start(f32[19,24,128]{2,1,0:T(8,128)S(1)} %get-tuple-element.93), channel_id=1, source_target_pairs={{1,2},{2,1},{3,4},{4,3},{5,6},{6,5},{7,8},{8,7},{9,10},{10,9},{11,... | collective-permute-start | bytes 700424 | tf_op jit(solution)/shard_map/ppermute | solution.py:23
  48.0 3.7 %collective-permute-start.6 = (f32[19,24,128]{2,1,0:T(8,128)S(1)}, f32[19,24,128]{2,1,0:T(8,128)S(1)}, u32[]{:S(2)}, u32[]{:S(2)}) collective-permute-start(f32[19,24,128]{2,1,0:T(8,128)S(1)} %get-tuple-element.94), channel_id=1, source_target_pairs={{0,1},{1,0},{2,3},{3,2},{4,5},{5,4},{6,7},{7,6},{8,9},{9,8},{10,11... | collective-permute-start | bytes 700424 | tf_op jit(solution)/shard_map/ppermute | solution.py:23
  52.8 3.1 %collective-permute-start.8 = (f32[2,2,24,128]{3,2,0,1:T(8,128)S(1)}, f32[2,2,24,128]{3,2,0,1:T(8,128)S(1)}, u32[]{:S(2)}, u32[]{:S(2)}) collective-permute-start(f32[2,2,24,128]{3,2,0,1:T(8,128)S(1)} %copy.47), channel_id=1, source_target_pairs={{0,1},{1,0},{2,3},{3,2},{4,5},{5,4},{6,7},{7,6},{8,9},{9,8},{10,11... | collective-permute-start | bytes 147464 | tf_op jit(solution)/shard_map/ppermute | solution.py:23
  56.0 7.3 %collective-permute-start.10 = (f32[2,4,24,128]{3,2,0,1:T(8,128)S(1)}, f32[2,4,24,128]{3,2,0,1:T(8,128)S(1)}, u32[]{:S(2)}, u32[]{:S(2)}) collective-permute-start(f32[2,4,24,128]{3,2,0,1:T(8,128)S(1)} %pad_maximum_fusion.22), channel_id=1, source_target_pairs={{32,64},{64,32},{48,80},{80,48},{96,128},{128,96},{112,144},{144,1... | collective-permute-start | bytes 294920 | tf_op jit(solution)/shard_map/ppermute | solution.py:454
  57.9 8.8 %collective-permute-start.9 = (f32[2,4,24,128]{3,2,0,1:T(8,128)S(1)}, f32[2,4,24,128]{3,2,0,1:T(8,128)S(1)}, u32[]{:S(2)}, u32[]{:S(2)}) collective-permute-start(f32[2,4,24,128]{3,2,0,1:T(8,128)S(1)} %pad_maximum_fusion.22), channel_id=1, source_target_pairs={{0,16},{16,0},{32,48},{48,32},{64,80},{80,64},{96,112},{112,96},{1... | collective-permute-start | bytes 294920 | tf_op jit(solution)/shard_map/ppermute | solution.py:454
  66.8 3.3 %collective-permute-start.11 = (f32[16,24,128]{2,1,0:T(8,128)S(1)}, f32[16,24,128]{2,1,0:T(8,128)S(1)}, u32[]{:S(2)}, u32[]{:S(2)}) collective-permute-start(f32[16,24,128]{2,1,0:T(8,128)S(1)} %pad_maximum_fusion.12), channel_id=1, source_target_pairs={{0,1},{1,0},{2,3},{3,2},{4,5},{5,4},{6,7},{7,6},{8,9},{9,8},{10,11... | collective-permute-start | bytes 589832 | tf_op jit(solution)/shard_map/ppermute | solution.py:23
  70.4 8.0 %collective-permute-start.12 = (f32[20,24,128]{2,1,0:T(8,128)S(1)}, f32[20,24,128]{2,1,0:T(8,128)S(1)}, u32[]{:S(2)}, u32[]{:S(2)}) collective-permute-start(f32[20,24,128]{2,1,0:T(8,128)S(1)} %maximum_select_fusion), channel_id=1, source_target_pairs={{1,2},{2,1},{3,4},{4,3},{5,6},{6,5},{7,8},{8,7},{9,10},{10,9},{11,... | collective-permute-start | bytes 737288 | tf_op jit(solution)/shard_map/ppermute | solution.py:23
  74.5 0.7 collective-permute-start.13
  79.5 30.3 %collective-permute-start.15 = (f32[46,24,128]{2,1,0:T(8,128)S(1)}, f32[46,24,128]{2,1,0:T(8,128)S(1)}, u32[]{:S(2)}, u32[]{:S(2)}) collective-permute-start(f32[46,24,128]{2,1,0:T(8,128)S(1)} %get-tuple-element.61), channel_id=1, source_target_pairs={{16,32},{32,16},{48,64},{64,48},{80,96},{96,80},{112,128},{128,112... | collective-permute-start | bytes 1695752 | tf_op jit(solution)/shard_map/ppermute | solution.py:23
  84.5 25.2 %collective-permute-start.14 = (f32[46,24,128]{2,1,0:T(8,128)S(1)}, f32[46,24,128]{2,1,0:T(8,128)S(1)}, u32[]{:S(2)}, u32[]{:S(2)}) collective-permute-start(f32[46,24,128]{2,1,0:T(8,128)S(1)} %get-tuple-element.62), channel_id=1, source_target_pairs={{0,16},{16,0},{32,48},{48,32},{64,80},{80,64},{96,112},{112,96},{1... | collective-permute-start | bytes 1695752 | tf_op jit(solution)/shard_map/ppermute | solution.py:23
  110.4 4.5 %copy-start = (f32[1,1,128,2048]{3,2,1,0:T(8,128)S(1)}, f32[1,1,128,2048]{3,2,1,0:T(8,128)}, u32[]{:S(2)}) copy-start(f32[1,1,128,2048]{3,2,1,0:T(8,128)} %param.7) | copy-start | bytes 3145732
  110.5 42.0 %collective-permute-start.20 = (f32[68,24,128]{2,1,0:T(8,128)S(1)}, f32[68,24,128]{2,1,0:T(8,128)S(1)}, u32[]{:S(2)}, u32[]{:S(2)}) collective-permute-start(f32[68,24,128]{2,1,0:T(8,128)S(1)} %get-tuple-element.51), channel_id=1, source_target_pairs={{1,2},{2,1},{3,4},{4,3},{5,6},{6,5},{7,8},{8,7},{9,10},{10,9},{11,... | collective-permute-start | bytes 2506760 | tf_op jit(solution)/shard_map/ppermute | solution.py:23
  113.0 39.6 %collective-permute-start.19 = (f32[68,24,128]{2,1,0:T(8,128)S(1)}, f32[68,24,128]{2,1,0:T(8,128)S(1)}, u32[]{:S(2)}, u32[]{:S(2)}) collective-permute-start(f32[68,24,128]{2,1,0:T(8,128)S(1)} %get-tuple-element.52), channel_id=1, source_target_pairs={{0,1},{1,0},{2,3},{3,2},{4,5},{5,4},{6,7},{7,6},{8,9},{9,8},{10,11... | collective-permute-start | bytes 2506760 | tf_op jit(solution)/shard_map/ppermute | solution.py:23
  135.7 8.4 %collective-permute-start.16 = (f32[6,24,128]{2,1,0:T(8,128)S(1)}, f32[6,24,128]{2,1,0:T(8,128)S(1)}, u32[]{:S(2)}, u32[]{:S(2)}) collective-permute-start(f32[6,24,128]{2,1,0:T(8,128)S(1)} %pick.1.refs_0_), channel_id=1, source_target_pairs={{0,16},{16,0},{32,48},{48,32},{64,80},{80,64},{96,112},{112,96},{1... | collective-permute-start | bytes 221192 | tf_op jit(solution)/shard_map/ppermute | solution.py:454
  139.6 6.6 %collective-permute-start.17 = (f32[6,24,128]{2,1,0:T(8,128)S(1)}, f32[6,24,128]{2,1,0:T(8,128)S(1)}, u32[]{:S(2)}, u32[]{:S(2)}) collective-permute-start(f32[6,24,128]{2,1,0:T(8,128)S(1)} %pick.1.refs_0_), channel_id=1, source_target_pairs={{32,64},{64,32},{48,80},{80,48},{96,128},{128,96},{112,144},{144,1... | collective-permute-start | bytes 221192 | tf_op jit(solution)/shard_map/ppermute | solution.py:454
  146.2 6.3 %collective-permute-start.18 = (f32[12,24,128]{2,1,0:T(8,128)S(1)}, f32[12,24,128]{2,1,0:T(8,128)S(1)}, u32[]{:S(2)}, u32[]{:S(2)}) collective-permute-start(f32[12,24,128]{2,1,0:T(8,128)S(1)} %constant_dynamic-update-slice_fusion.6.refs_1_), channel_id=1, source_target_pairs={{0,1},{1,0},{2,3},{3,2},{4,5},{5,4},{6,7},{7,6},{8,9},{9,8},{10,11... | collective-permute-start | bytes 442376 | tf_op jit(solution)/shard_map/ppermute | solution.py:23
  153.5 5.9 %collective-permute-start.21 = (f32[6,24,128]{2,1,0:T(8,128)S(1)}, f32[6,24,128]{2,1,0:T(8,128)S(1)}, u32[]{:S(2)}, u32[]{:S(2)}) collective-permute-start(f32[6,24,128]{2,1,0:T(8,128)S(1)} %bitcast.299), channel_id=1, source_target_pairs={{0,16},{16,0},{32,48},{48,32},{64,80},{80,64},{96,112},{112,96},{1... | collective-permute-start | bytes 221192 | tf_op jit(solution)/shard_map/ppermute | solution.py:23
  155.4 8.4 %collective-permute-start.22 = (f32[6,24,128]{2,1,0:T(8,128)S(1)}, f32[6,24,128]{2,1,0:T(8,128)S(1)}, u32[]{:S(2)}, u32[]{:S(2)}) collective-permute-start(f32[6,24,128]{2,1,0:T(8,128)S(1)} %bitcast.298), channel_id=1, source_target_pairs={{16,32},{32,16},{48,64},{64,48},{80,96},{96,80},{112,128},{128,112... | collective-permute-start | bytes 221192 | tf_op jit(solution)/shard_map/ppermute | solution.py:23
  163.9 6.7 %collective-permute-start.24 = (f32[12,24,128]{2,1,0:T(8,128)S(1)}, f32[12,24,128]{2,1,0:T(8,128)S(1)}, u32[]{:S(2)}, u32[]{:S(2)}) collective-permute-start(f32[12,24,128]{2,1,0:T(8,128)S(1)} %get-tuple-element.101), channel_id=1, source_target_pairs={{1,2},{2,1},{3,4},{4,3},{5,6},{6,5},{7,8},{8,7},{9,10},{10,9},{11,... | collective-permute-start | bytes 442376 | tf_op jit(solution)/shard_map/ppermute | solution.py:23
  167.8 3.3 %collective-permute-start.23 = (f32[12,24,128]{2,1,0:T(8,128)S(1)}, f32[12,24,128]{2,1,0:T(8,128)S(1)}, u32[]{:S(2)}, u32[]{:S(2)}) collective-permute-start(f32[12,24,128]{2,1,0:T(8,128)S(1)} %get-tuple-element.102), channel_id=1, source_target_pairs={{0,1},{1,0},{2,3},{3,2},{4,5},{5,4},{6,7},{7,6},{8,9},{9,8},{10,11... | collective-permute-start | bytes 442376 | tf_op jit(solution)/shard_map/ppermute | solution.py:23
